TPU v7x, 32 devices: a whole 2x2x4 slice. The times are simulated.
32 devices in a mesh: cfg: 2 (over core), img: 4 (over y, x), seq: 4 (over z).
Axes of the slice: x: 2, y: 2, z: 4, core: 2. Of those that a mesh axis runs over, the one named last changes fastest.
Arguments:
- img_qkv: bfloat16 [2, 4, 512, 3, 2048], P('cfg', 'img', 'seq'), may hold values from -5 to 5
- txt_kv: bfloat16 [2, 4, 32, 2, 2048], P('cfg', 'img', 'seq'), may hold values from -5 to 5
- readout: bfloat16 [2048, 64], replicated, may hold values from -0.125 to 0.125
- old_velocity: float32 [4, 512, 64], P('img', 'seq'), may hold values from -6 to 6
- noise: float32 [4, 512, 64], P('img', 'seq'), may hold values from -5 to 5
- step_ratio: float32 [4], P('img'), may hold values from 0.2 to 0.8
- rewards: float32 [4], P('img'), may hold values from -6 to 6
- guidance: float32 [], replicated, may hold values from 1.5 to 3
Outputs:
- img_grad: bfloat16 [2, 4, 512, 3, 2048], P('cfg', 'img', 'seq')
- txt_grad: bfloat16 [2, 4, 32, 2, 2048], P('cfg', 'img', 'seq')
- readout_grad: float32 [2048, 64], replicated
- ratio: float32 [4], P('img')
All inputs are finite; a program needn't handle non-finite values.
Results may differ from a plain program's by a relative error of at most 0.009.
Values may be sent and summed in bfloat16 or wider, within the bound.
No kernel may reach another device: no remote copies, remote signals or barrier semaphores. Data moves between devices by JAX's collectives and lax.ppermute only.
A program may use at most 128 MiB of HBM per device.

v0:
```python
import jax
import jax.numpy as jnp
from jax import lax
from jax.sharding import PartitionSpec as P

HEADS = 16
HEAD_DIM = 128


def swapped(block, axis, apart):
    count = lax.axis_size(axis)
    route = []
    for low in range(count):
        high = low | 1 << apart
        if high != low and high < count:
            route += [(low, high), (high, low)]
    return lax.ppermute(block, axis, route)


def to_items(rows_whole, copies, groups, width):
    count = rows_whole.shape[0]
    split = rows_whole.reshape(copies, count // copies, groups, width)
    return split.transpose(2, 0, 1, 3).reshape(groups * copies, count // copies, width)


def from_items(items, copies, groups):
    sub_rows = items.shape[1]
    width = items.shape[2]
    split = items.reshape(groups, copies, sub_rows, width)
    return split.transpose(1, 2, 0, 3).reshape(copies * sub_rows, groups * width)


def repeat_items(rows_whole, copies, groups, width):
    count = rows_whole.shape[0]
    split = rows_whole.reshape(count, groups, width).transpose(1, 0, 2)
    return jnp.repeat(split, copies, axis=0)


def fold_items(items, copies, groups):
    count = items.shape[1]
    width = items.shape[2]
    summed = items.reshape(groups, copies, count, width).sum(axis=1)
    return summed.transpose(1, 0, 2).reshape(count, groups * width)


def block_count(total):
    count = max(1, total // 512)
    while total % count:
        count -= 1
    return count


def heads_view(x):
    return x.reshape(x.shape[0], x.shape[1] // HEAD_DIM, HEAD_DIM)


def attend_forward(queries, keys, values):
    blocks = block_count(queries.shape[0])
    scale = HEAD_DIM ** (-0.5)
    key_heads = heads_view(keys)
    value_heads = heads_view(values)
    query_blocks = heads_view(queries).reshape(blocks, -1, key_heads.shape[1], HEAD_DIM)

    def one_block(block):
        scores = (
            jnp.einsum("qhd,khd->hqk", block, key_heads, preferred_element_type=jnp.float32) * scale
        )
        top = jnp.max(scores, axis=-1, keepdims=True)
        raised = jnp.exp(scores - top)
        probs = (raised / jnp.sum(raised, axis=-1, keepdims=True)).astype(jnp.bfloat16)
        mixed = jnp.einsum("hqk,khd->qhd", probs, value_heads, preferred_element_type=jnp.float32)
        return (probs, mixed.astype(jnp.bfloat16))

    probs, mixed = lax.map(one_block, query_blocks)
    return (probs, mixed.reshape(queries.shape[0], queries.shape[1]))


def attend_backward(queries, keys, values, probs, grad_out):
    blocks = probs.shape[0]
    scale = HEAD_DIM ** (-0.5)
    key_heads = heads_view(keys)
    value_heads = heads_view(values)
    count = key_heads.shape[1]
    query_blocks = heads_view(queries).reshape(blocks, -1, count, HEAD_DIM)
    grad_blocks = heads_view(grad_out).reshape(blocks, -1, count, HEAD_DIM)

    def one_block(carry, inputs):
        block, grad_block, prob = inputs
        grad_probs = jnp.einsum(
            "qhd,khd->hqk", grad_block, value_heads, preferred_element_type=jnp.float32
        )
        weights = prob.astype(jnp.float32)
        delta = jnp.sum(weights * grad_probs, axis=-1, keepdims=True)
        grad_scores = (weights * (grad_probs - delta) * scale).astype(jnp.bfloat16)
        grad_query = jnp.einsum(
            "hqk,khd->qhd", grad_scores, key_heads, preferred_element_type=jnp.float32
        )
        grad_keys = carry[0] + jnp.einsum(
            "hqk,qhd->khd", grad_scores, block, preferred_element_type=jnp.float32
        )
        grad_values = carry[1] + jnp.einsum(
            "hqk,qhd->khd", prob, grad_block, preferred_element_type=jnp.float32
        )
        return ((grad_keys, grad_values), grad_query.astype(jnp.bfloat16))

    zeros = jnp.zeros(key_heads.shape, jnp.float32)
    totals, grad_query = lax.scan(one_block, (zeros, zeros), (query_blocks, grad_blocks, probs))
    return (
        grad_query.reshape(queries.shape),
        totals[0].reshape(keys.shape),
        totals[1].reshape(keys.shape),
    )


def surrogate_gain(ratio, advantage):
    clipped = jnp.clip(ratio, 0.8, 1.2)
    keep = ratio * advantage <= clipped * advantage
    return jnp.where(keep, -ratio * advantage, jnp.zeros_like(ratio))


def on_device(img_qkv, txt_kv, readout, old_velocity, noise, step_ratio, rewards, guidance):
    parts = lax.axis_size("seq")
    copies = max(1, parts // HEADS)
    groups = parts // copies
    width = readout.shape[0] // groups
    own = img_qkv[0, 0]
    text = txt_kv[0, 0]
    img_rows = own.shape[0]
    txt_rows = text.shape[0]
    keys = jnp.concatenate([text[:, 0], own[:, 1]], axis=0)
    values = jnp.concatenate([text[:, 1], own[:, 2]], axis=0)
    reward = rewards[0]
    reward_sums = lax.psum((reward, reward * reward), "img")
    images = lax.axis_size("img")
    mean = reward_sums[0] / images
    spread = jnp.sqrt(jnp.maximum(reward_sums[1] / images - mean * mean, 0.0))
    advantage = (reward - mean) / jnp.maximum(spread, 1.0)
    query_items = to_items(own[:, 0], copies, groups, width)
    key_items = repeat_items(keys, copies, groups, width)
    value_items = repeat_items(values, copies, groups, width)
    arrived = (
        lax.all_to_all(query_items, "seq", split_axis=0, concat_axis=1, tiled=True),
        lax.all_to_all(key_items, "seq", split_axis=0, concat_axis=1, tiled=True),
        lax.all_to_all(value_items, "seq", split_axis=0, concat_axis=1, tiled=True),
    )
    queries = arrived[0][0]
    head_keys = arrived[1][0]
    head_values = arrived[2][0]
    probs, mixed = attend_forward(queries, head_keys, head_values)
    returned = lax.all_to_all(
        mixed.reshape(parts, -1, width), "seq", split_axis=0, concat_axis=0, tiled=True
    )
    attended = from_items(returned, copies, groups)
    velocity = jnp.dot(attended, readout, preferred_element_type=jnp.float32)
    branch = lax.axis_index("cfg")
    rate = step_ratio[0]
    count = img_rows * parts * velocity.shape[1]
    partner = swapped(velocity, "cfg", 0)
    conditional = jnp.where(branch == 0, velocity, partner)
    unconditional = jnp.where(branch == 0, partner, velocity)
    guided = unconditional + guidance * (conditional - unconditional)
    deviation = rate * (guided - old_velocity[0])
    partial_sum = jnp.sum(noise[0] * deviation - 0.5 * deviation * deviation)
    log_ratio = lax.psum(partial_sum, "seq") / count
    ratio = jnp.exp(log_ratio)
    gain = surrogate_gain(ratio, advantage)
    grad_guided = gain * rate * (noise[0] - deviation)
    grad_velocity = jnp.where(branch == 0, guidance, 1.0 - guidance) * grad_guided
    readout_part = jnp.dot(
        attended.astype(jnp.float32).T, grad_velocity, precision=lax.Precision.HIGHEST
    )
    readout_grad = lax.psum(readout_part, ("cfg", "img", "seq"))
    grad_attended = jnp.dot(
        grad_velocity, readout.astype(jnp.float32).T, precision=lax.Precision.HIGHEST
    ).astype(jnp.bfloat16)
    grad_items = to_items(grad_attended, copies, groups, width)
    grad_out = lax.all_to_all(grad_items, "seq", split_axis=0, concat_axis=1, tiled=True)[0]
    grad_query, grad_keys, grad_values = attend_backward(
        queries, head_keys, head_values, probs, grad_out
    )
    query_home = lax.all_to_all(
        grad_query.reshape(parts, -1, width), "seq", split_axis=0, concat_axis=0, tiled=True
    )
    key_home = (
        lax.all_to_all(
            grad_keys.reshape(parts, -1, width).astype(jnp.bfloat16),
            "seq",
            split_axis=0,
            concat_axis=0,
            tiled=True,
        ).astype(jnp.float32),
        lax.all_to_all(
            grad_values.reshape(parts, -1, width).astype(jnp.bfloat16),
            "seq",
            split_axis=0,
            concat_axis=0,
            tiled=True,
        ).astype(jnp.float32),
    )
    query_grad = from_items(query_home, copies, groups)
    key_grad = fold_items(key_home[0], copies, groups)
    value_grad = fold_items(key_home[1], copies, groups)
    img_grad = jnp.stack(
        [
            query_grad,
            key_grad[txt_rows:].astype(jnp.bfloat16),
            value_grad[txt_rows:].astype(jnp.bfloat16),
        ],
        axis=1,
    )[None, None]
    txt_grad = jnp.stack([key_grad[:txt_rows], value_grad[:txt_rows]], axis=1).astype(jnp.bfloat16)[
        None, None
    ]
    return (img_grad, txt_grad, readout_grad, ratio.reshape(1))


def solution(mesh):
    return jax.shard_map(
        on_device,
        mesh=mesh,
        in_specs=(
            P("cfg", "img", "seq", None, None),
            P("cfg", "img", "seq", None, None),
            P(),
            P("img", "seq", None),
            P("img", "seq", None),
            P("img"),
            P("img"),
            P(),
        ),
        out_specs=(
            P("cfg", "img", "seq", None, None),
            P("cfg", "img", "seq", None, None),
            P(),
            P("img"),
        ),
        check_vma=False,
    )
```

profile of v0, /device:TPU:0, one launch (start us, length us, event | category | flops | bytes accessed | tf_op | source)
XLA Modules:
  0.0 333.7 jit_solution(14314312585268579537)
XLA Ops:
  7.2 1.5 fusion.45
  8.7 0.4 reshape_squeeze.12
  9.1 0.9 copy.95
  10.0 6.3 %all-to-all-start.1 = ((bf16[4,128,512]{2,1,0:T(8,128)(2,1)}), bf16[4,128,512]{2,1,0:T(8,128)(2,1)S(1)}, u32[]{:S(2)}, u32[]{:S(2)}) async-start(bf16[4,128,512]{2,1,0:T(8,128)(2,1)} %bitcast.89), calls=%async_computation.1 | async-start | bytes 1048576 | tf_op jit(solution)/shard_map/all_to_all | solution.py:142
  16.3 0.4 concatenate.25
  16.7 0.1 copy.55
  16.8 0.3 slice_reduce_fusion
  17.1 0.9 maximum_bitcast_fusion.1
  17.9 12.9 %all-to-all-done.1 = bf16[4,128,512]{2,1,0:T(8,128)(2,1)S(1)} async-done(((bf16[4,128,512]{2,1,0:T(8,128)(2,1)}), bf16[4,128,512]{2,1,0:T(8,128)(2,1)S(1)}, u32[]{:S(2)}, u32[]{:S(2)}) %all-to-all-start.1) | async-done | bytes 524320 | tf_op jit(solution)/shard_map/all_to_all | solution.py:142
  30.8 3.5 %all-to-all-start = ((bf16[4,136,512]{2,1,0:T(8,128)(2,1)}), bf16[4,136,512]{2,1,0:T(8,128)(2,1)S(1)}, u32[]{:S(2)}, u32[]{:S(2)}) async-start(bf16[4,136,512]{2,1,0:T(8,128)(2,1)} %maximum_bitcast_fusion.1), calls=%async_computation | async-start | bytes 1114112 | tf_op jit(solution)/shard_map/all_to_all | solution.py:143
  34.3 0.4 concatenate.28
  34.7 0.1 copy.60
  34.8 0.9 maximum_bitcast_fusion.2
  35.6 0.1 squeeze.39
  35.7 13.2 %all-to-all-done = bf16[4,136,512]{2,1,0:T(8,128)(2,1)S(1)} async-done(((bf16[4,136,512]{2,1,0:T(8,128)(2,1)}), bf16[4,136,512]{2,1,0:T(8,128)(2,1)S(1)}, u32[]{:S(2)}, u32[]{:S(2)}) %all-to-all-start) | async-done | bytes 557088 | tf_op jit(solution)/shard_map/all_to_all | solution.py:143
  48.9 4.1 %all-to-all-start.2 = ((bf16[4,136,512]{2,1,0:T(8,128)(2,1)}), bf16[4,136,512]{2,1,0:T(8,128)(2,1)}, u32[]{:S(2)}, u32[]{:S(2)}) async-start(bf16[4,136,512]{2,1,0:T(8,128)(2,1)} %maximum_bitcast_fusion.2), calls=%async_computation.2 | async-start | bytes 1114112 | tf_op jit(solution)/shard_map/all_to_all | solution.py:144
  53.1 0.1 reshape_squeeze.11
  53.2 0.7 fusion.21
  54.0 2.9 fusion.46
  56.9 0.6 divide_convert_fusion
  57.5 10.3 %all-to-all-done.2 = bf16[4,136,512]{2,1,0:T(8,128)(2,1)} async-done(((bf16[4,136,512]{2,1,0:T(8,128)(2,1)}), bf16[4,136,512]{2,1,0:T(8,128)(2,1)}, u32[]{:S(2)}, u32[]{:S(2)}) %all-to-all-start.2) | async-done | bytes 557088 | tf_op jit(solution)/shard_map/all_to_all | solution.py:144
  67.8 1.6 reshape_squeeze.13
  69.4 1.4 fusion.20
  70.8 2.0 reshape_reshape.8
  72.8 1.1 copy.62
  73.9 16.4 %all_to_all.56 = bf16[4,128,512]{1,2,0:T(8,128)(2,1)S(1)} all-to-all(bf16[4,128,512]{1,2,0:T(8,128)(2,1)S(1)} %copy.62), channel_id=1, replica_groups=mesh['cfg'=2,'img'=4,'seq'=4] {'seq'}, dimensions={0} | all-to-all | bytes 1048576 | tf_op jit(solution)/shard_map/all_to_all | solution.py:150
  90.3 0.8 copy-done.1
  91.1 0.2 fusion.47
  91.3 0.1 collective-permute-start
  92.1 10.6 %all-reduce = (f32[]{:T(128)}, f32[]{:T(128)}) all-reduce(f32[]{:T(128)} %bitcast.14, f32[]{:T(128)S(6)} %mul.86), channel_id=1, replica_groups=mesh['cfg'=2,'img'=4,'seq'=4] {'img'}, use_global_device_ids=true, to_apply=%region_4.0 | all-reduce | flops 2 | bytes 16 | tf_op jit(solution)/shard_map/psum | solution.py:133
  106.6 0.6 fusion.32
  107.2 10.4 %psum.28 = f32[]{:T(128)} all-reduce(f32[]{:T(128)} %get-tuple-element.65), channel_id=1, replica_groups=mesh['cfg'=2,'img'=4,'seq'=4] {'seq'}, use_global_device_ids=true, to_apply=%region_3.0 | all-reduce | flops 1 | bytes 8 | tf_op jit(solution)/shard_map/psum | solution.py:164
  118.4 1.4 convolution_convert_fusion
  119.8 2.2 reshape.138
  122.0 1.1 copy.94
  123.1 14.5 %all_to_all.57 = bf16[4,128,512]{2,1,0:T(8,128)(2,1)} all-to-all(bf16[4,128,512]{2,1,0:T(8,128)(2,1)S(1)} %bitcast.99), channel_id=1, replica_groups=mesh['cfg'=2,'img'=4,'seq'=4] {'seq'}, dimensions={0} | all-to-all | bytes 1048576 | tf_op jit(solution)/shard_map/all_to_all | solution.py:177
  137.6 2.0 squeeze.44
  139.6 3.8 %fusion.24 = f32[4,512,544]{1,2,0:T(8,128)} fusion(bf16[544,4,128]{2,1,0:T(4,128)(2,1)S(1)} %reshape_squeeze.13, bf16[512,4,128]{2,1,0:T(4,128)(2,1)} %squeeze.44), kind=kOutput, calls=%fused_computation.35 | convolution fusion | flops 285212672 | bytes 5537792 | tf_op jit(solution)/shard_map/while/body/eval_jaxpr/qhd,khd->hqk/dot_general | solution.py:89
  143.4 6.1 %fusion.17 = bf16[544,4,128]{2,0,1:T(8,128)(2,1)} fusion(bf16[4,512,544]{1,2,0:T(8,128)(2,1)S(1)} %divide_convert_fusion, f32[4,512,544]{1,2,0:T(8,128)} %fusion.24, bf16[512,4,128]{2,1,0:T(4,128)(2,1)} %copy-done.6), kind=kOutput, calls=%fused_computation.24 | convolution fusion | flops 293292576 | bytes 7766016 | tf_op jit(solution)/shard_map/while/body/eval_jaxpr/hqk,qhd->khd/dot_general | solution.py:98
  149.5 1.3 copy.69
  150.8 1.0 convert_element_type.91
  151.8 3.5 %all-to-all-start.6 = ((bf16[4,136,512]{2,1,0:T(8,128)(2,1)}), bf16[4,136,512]{2,1,0:T(8,128)(2,1)S(1)}, u32[]{:S(2)}, u32[]{:S(2)}) async-start(bf16[4,136,512]{2,1,0:T(8,128)(2,1)} %convert_element_type.91), calls=%async_computation.6 | async-start | bytes 1114112 | tf_op jit(solution)/shard_map/all_to_all | solution.py:185
  155.3 1.8 fusion.18
  157.1 1.1 copy.72
  158.2 2.2 convert_element_type.95
  160.4 8.0 %all-to-all-done.6 = bf16[4,136,512]{2,1,0:T(8,128)(2,1)S(1)} async-done(((bf16[4,136,512]{2,1,0:T(8,128)(2,1)}), bf16[4,136,512]{2,1,0:T(8,128)(2,1)S(1)}, u32[]{:S(2)}, u32[]{:S(2)}) %all-to-all-start.6) | async-done | bytes 557088 | tf_op jit(solution)/shard_map/all_to_all | solution.py:185
  168.4 0.8 copy-done.3
  169.2 4.3 %all-to-all-start.7 = ((bf16[4,136,512]{2,1,0:T(8,128)(2,1)}), bf16[4,136,512]{2,1,0:T(8,128)(2,1)}, u32[]{:S(2)}, u32[]{:S(2)}) async-start(bf16[4,136,512]{2,1,0:T(8,128)(2,1)} %convert_element_type.95), calls=%async_computation.7 | async-start | bytes 1114112 | tf_op jit(solution)/shard_map/all_to_all | solution.py:192
  173.6 5.5 %fusion.19 = bf16[512,4,128]{0,2,1:T(8,128)(2,1)S(1)} fusion(bf16[4,512,544]{1,2,0:T(8,128)(2,1)S(1)} %divide_convert_fusion, f32[4,512,544]{1,2,0:T(8,128)} %fusion.24, bf16[544,4,128]{2,1,0:T(4,128)(2,1)} %copy-done.5), kind=kOutput, calls=%fused_computation.26 | convolution fusion | flops 293276192 | bytes 7766016 | tf_op jit(solution)/shard_map/while/body/eval_jaxpr/hqk,khd->qhd/dot_general | solution.py:95
  179.2 0.1 reshape_reshape.9
  179.3 0.9 copy.67
  180.2 5.5 %all-to-all-done.7 = bf16[4,136,512]{2,1,0:T(8,128)(2,1)} async-done(((bf16[4,136,512]{2,1,0:T(8,128)(2,1)}), bf16[4,136,512]{2,1,0:T(8,128)(2,1)}, u32[]{:S(2)}, u32[]{:S(2)}) %all-to-all-start.7) | async-done | bytes 557088 | tf_op jit(solution)/shard_map/all_to_all | solution.py:192
  185.7 3.5 %all-to-all-start.5 = ((bf16[4,128,512]{1,2,0:T(8,128)(2,1)}), bf16[4,128,512]{1,2,0:T(8,128)(2,1)S(1)}, u32[]{:S(2)}, u32[]{:S(2)}) async-start(bf16[4,128,512]{1,2,0:T(8,128)(2,1)} %copy.67), calls=%async_computation.5 | async-start | bytes 1048576 | tf_op jit(solution)/shard_map/all_to_all | solution.py:181
  189.2 2.2 fusion.36
  191.5 0.8 slice.52
  192.3 1.1 slice.50
  193.4 0.7 copy.75
  194.1 0.3 copy.70
  194.4 0.3 copy.73
  194.7 7.1 %all-to-all-done.5 = bf16[4,128,512]{1,2,0:T(8,128)(2,1)S(1)} async-done(((bf16[4,128,512]{1,2,0:T(8,128)(2,1)}), bf16[4,128,512]{1,2,0:T(8,128)(2,1)S(1)}, u32[]{:S(2)}, u32[]{:S(2)}) %all-to-all-start.5) | async-done | bytes 524320 | tf_op jit(solution)/shard_map/all_to_all | solution.py:181
  201.7 0.2 maximum_bitcast_fusion
  201.9 1.6 copy.74
  203.5 120.4 %all-reduce.3.cloned.1.call-done = f32[2048,64]{0,1:T(8,128)} async-done(((f32[2048,64]{0,1:T(8,128)}), f32[2048,64]{0,1:T(8,128)}) %all-reduce.3.cloned.1.call-update) | async-done | bytes 524304 | tf_op jit(solution)/shard_map/psum | solution.py:172
  323.9 1.9 copy.100
  (26 shorter events, 0.2 us)
Async XLA Ops:
  7.2 83.9 %copy-start = (bf16[2048,64]{0,1:T(8,128)(2,1)S(1)}, bf16[2048,64]{0,1:T(8,128)(2,1)}, u32[]{:S(2)}) copy-start(bf16[2048,64]{0,1:T(8,128)(2,1)} %param.10) | copy-start | bytes 786436
  7.2 9.6 %copy-start.9 = (bf16[1,1,8,2,2048]{4,3,2,1,0:T(2,128)(2,1)S(1)}, bf16[1,1,8,2,2048]{4,3,2,1,0:T(2,128)(2,1)}, u32[]{:S(2)}) copy-start(bf16[1,1,8,2,2048]{4,3,2,1,0:T(2,128)(2,1)} %param.9) | copy-start | bytes 196612
  10.0 20.8 %all-to-all-start.1 = ((bf16[4,128,512]{2,1,0:T(8,128)(2,1)}), bf16[4,128,512]{2,1,0:T(8,128)(2,1)S(1)}, u32[]{:S(2)}, u32[]{:S(2)}) async-start(bf16[4,128,512]{2,1,0:T(8,128)(2,1)} %bitcast.89), calls=%async_computation.1 | async-start | bytes 1048576 | tf_op jit(solution)/shard_map/all_to_all | solution.py:142
  30.8 18.1 %all-to-all-start = ((bf16[4,136,512]{2,1,0:T(8,128)(2,1)}), bf16[4,136,512]{2,1,0:T(8,128)(2,1)S(1)}, u32[]{:S(2)}, u32[]{:S(2)}) async-start(bf16[4,136,512]{2,1,0:T(8,128)(2,1)} %maximum_bitcast_fusion.1), calls=%async_computation | async-start | bytes 1114112 | tf_op jit(solution)/shard_map/all_to_all | solution.py:143
  35.7 21.1 %copy-start.6 = (bf16[512,4,128]{2,1,0:T(4,128)(2,1)}, bf16[512,4,128]{2,1,0:T(4,128)(2,1)S(1)}, u32[]{:S(2)}) copy-start(bf16[512,4,128]{2,1,0:T(4,128)(2,1)S(1)} %squeeze.39) | copy-start | bytes 1572868
  48.9 18.9 %all-to-all-start.2 = ((bf16[4,136,512]{2,1,0:T(8,128)(2,1)}), bf16[4,136,512]{2,1,0:T(8,128)(2,1)}, u32[]{:S(2)}, u32[]{:S(2)}) async-start(bf16[4,136,512]{2,1,0:T(8,128)(2,1)} %maximum_bitcast_fusion.2), calls=%async_computation.2 | async-start | bytes 1114112 | tf_op jit(solution)/shard_map/all_to_all | solution.py:144
  53.2 3.6 %copy-start.5 = (bf16[544,4,128]{2,1,0:T(4,128)(2,1)}, bf16[544,4,128]{2,1,0:T(4,128)(2,1)S(1)}, u32[]{:S(2)}) copy-start(bf16[544,4,128]{2,1,0:T(4,128)(2,1)S(1)} %reshape_squeeze.11) | copy-start | bytes 1671172
  57.5 49.1 %copy-start.7 = (f32[1,128,64]{1,2,0:T(8,128)S(1)}, f32[1,128,64]{1,2,0:T(8,128)}, u32[]{:S(2)}) copy-start(f32[1,128,64]{1,2,0:T(8,128)} %param.12) | copy-start | bytes 98308
  57.5 49.1 %copy-start.10 = (f32[1,128,64]{1,2,0:T(8,128)S(1)}, f32[1,128,64]{1,2,0:T(8,128)}, u32[]{:S(2)}) copy-start(f32[1,128,64]{1,2,0:T(8,128)} %param.11) | copy-start | bytes 98308
  90.3 0.8 copy-start.1
  91.3 15.3 %collective-permute-start = (f32[128,64]{0,1:T(8,128)S(1)}, f32[128,64]{0,1:T(8,128)S(1)}, u32[]{:S(2)}, u32[]{:S(2)}) collective-permute-start(f32[128,64]{0,1:T(8,128)S(1)} %fusion.47), channel_id=1, source_target_pairs={{0,16},{16,0},{1,17},{17,1},{2,18},{18,2},{3,19},{19,3},{4,20},{20... | collective-permute-start | bytes 98312 | tf_op jit(solution)/shard_map/ppermute | solution.py:17
  107.2 36.2 %copy-start.8 = (f32[128,64]{0,1:T(8,128)}, f32[128,64]{0,1:T(8,128)S(1)}, u32[]{:S(2)}) copy-start(f32[128,64]{0,1:T(8,128)S(1)} %get-tuple-element.66) | copy-start | bytes 98308
  151.8 16.6 %all-to-all-start.6 = ((bf16[4,136,512]{2,1,0:T(8,128)(2,1)}), bf16[4,136,512]{2,1,0:T(8,128)(2,1)S(1)}, u32[]{:S(2)}, u32[]{:S(2)}) async-start(bf16[4,136,512]{2,1,0:T(8,128)(2,1)} %convert_element_type.91), calls=%async_computation.6 | async-start | bytes 1114112 | tf_op jit(solution)/shard_map/all_to_all | solution.py:185
  168.4 0.8 copy-start.3
  169.2 16.5 %all-to-all-start.7 = ((bf16[4,136,512]{2,1,0:T(8,128)(2,1)}), bf16[4,136,512]{2,1,0:T(8,128)(2,1)}, u32[]{:S(2)}, u32[]{:S(2)}) async-start(bf16[4,136,512]{2,1,0:T(8,128)(2,1)} %convert_element_type.95), calls=%async_computation.7 | async-start | bytes 1114112 | tf_op jit(solution)/shard_map/all_to_all | solution.py:192
  173.6 15.6 %copy-start.2 = (bf16[4,128,512]{1,2,0:T(8,128)(2,1)S(1)}, bf16[4,128,512]{1,2,0:T(8,128)(2,1)}, u32[]{:S(2)}) copy-start(bf16[4,128,512]{1,2,0:T(8,128)(2,1)} %copy-done.1) | copy-start | bytes 1572868
  179.1 12.3 %copy-start.4 = (bf16[4,136,512]{2,1,0:T(8,128)(2,1)S(1)}, bf16[4,136,512]{2,1,0:T(8,128)(2,1)}, u32[]{:S(2)}) copy-start(bf16[4,136,512]{2,1,0:T(8,128)(2,1)} %copy-done.3) | copy-start | bytes 1671172
  185.7 16.0 %all-to-all-start.5 = ((bf16[4,128,512]{1,2,0:T(8,128)(2,1)}), bf16[4,128,512]{1,2,0:T(8,128)(2,1)S(1)}, u32[]{:S(2)}, u32[]{:S(2)}) async-start(bf16[4,128,512]{1,2,0:T(8,128)(2,1)} %copy.67), calls=%async_computation.5 | async-start | bytes 1048576 | tf_op jit(solution)/shard_map/all_to_all | solution.py:181
  189.2 134.7 %all-reduce.3.cloned.1.call-start = ((), (), s32[]{:S(2)}) async-start(), calls=%async_computation.8 | async-start | bytes 1048576 | tf_op jit(solution)/shard_map/psum | solution.py:172
Sparse Core Ops, SparseCore 0:
  195.3 128.5 all-reduce.2
where the time goes:
time: 335 us; the launch traced here: 334 us
  waiting for transfers between devices  177 us (53%)
  blocking collectives  51.8 us (15%)
  local copies, waits for them, and re-layouts  29.1 us (9%)
  starting transfers between devices  25.3 us (8%)
  matrix products  23.2 us (7%)
  between operations  20.8 us (6%)
  other arithmetic  5.98 us (2%)
    psum x1, waiting for transfers between devices, on_device(): readout_grad = lax.psum(readout_part, ('cfg', 'img', 'seq'))  120 us
    all_to_all x1, blocking collectives, on_device(): lax.all_to_all(mixed.reshape(parts, -1, width), 'seq', split_axis=0, conc...  16.4 us
    all_to_all x1, blocking collectives, on_device(): lax.all_to_all(grad_items, 'seq', split_axis=0, concat_axis=1, tiled=True)  14.5 us
    all_to_all x1, waiting for transfers between devices, on_device(): lax.all_to_all(key_items, 'seq', split_axis=0, concat_axis=1, tiled=True)  13.2 us
    all_to_all x1, waiting for transfers between devices, on_device(): lax.all_to_all(query_items, 'seq', split_axis=0, concat_axis=1, tiled=True)  12.9 us
    psum x1, blocking collectives, on_device(): reward_sums = lax.psum((reward, reward * reward), 'img')  10.6 us
    psum x1, blocking collectives, on_device(): log_ratio = lax.psum(partial_sum, 'seq') / count  10.4 us
    all_to_all x1, waiting for transfers between devices, on_device(): lax.all_to_all(value_items, 'seq', split_axis=0, concat_axis=1, tiled=True)  10.3 us
  transfers between devices with their start and end apart: 8, of which 7 were waited for; matrix products, arithmetic and copies ran while one was open for 8% of the time, Pallas kernels for 0%

commit v1 on v0

v1 whole, which is shorter than its diff:
```python
import functools

import jax
import jax.numpy as jnp
from jax import lax
from jax.experimental import pallas as pl
from jax.experimental.pallas import tpu as pltpu
from jax.sharding import PartitionSpec as P

HEADS = 16
HEAD_DIM = 128
SCALE = HEAD_DIM ** (-0.5)
F32 = jnp.float32
BF16 = jnp.bfloat16
PARAMS = pltpu.CompilerParams(vmem_limit_bytes=40 * 1024 * 1024)
SMEM = pl.BlockSpec(memory_space=pltpu.SMEM)


def dot(a, b):
    return jnp.dot(a, b, preferred_element_type=F32)


def dot_nt(a, b):
    return lax.dot_general(a, b, (((1,), (1,)), ((), ())), preferred_element_type=F32)


def dot_tn(a, b):
    return lax.dot_general(a, b, (((0,), (0,)), ((), ())), preferred_element_type=F32)


def whole(shape):
    return pl.BlockSpec(shape, lambda *_: (0,) * len(shape))


def at(refs, slot):
    return refs[slot].at[0] if len(refs) > 1 else refs[0].at[slot]


def cols(start, size):
    return pl.ds(pl.multiple_of(start, 128), size)


def tree_sum(terms):
    while len(terms) > 1:
        terms = [terms[k] + terms[k + 1] for k in range(0, len(terms), 2)]
    return terms[0]


def mirror(x, axis, apart):
    count = lax.axis_size(axis)
    return lax.ppermute(x, axis, [(i, i ^ apart) for i in range(count)])


class Sizes:
    def __init__(self, img_rows, txt_rows, features, channels):
        self.parts = lax.axis_size("seq")
        self.copies = max(1, self.parts // HEADS)
        self.groups = self.parts // self.copies
        self.features = features
        self.ch = channels
        self.width = features // self.groups
        self.heads = self.width // HEAD_DIM
        self.rows = img_rows
        self.txt = txt_rows
        self.sub = img_rows // self.copies
        self.img_keys = self.parts * img_rows
        self.keys = self.img_keys + self.parts * txt_rows
        self.queries = self.parts * self.sub
        self.block_rows = self.sub + self.rows + 2 * self.txt
        self.mirrored = self.parts in (1, 2, 4, 8) and self.copies == 1
        self.lists = self.parts if self.mirrored else 1
        self.each = self.parts // self.lists
        block = self.queries
        while block % 256 == 0 and self.keys * block > 600_000:
            block //= 2
        self.q_block = block
        self.q_blocks = self.queries // block

    def head_specs(self, rows, width):
        return [
            pl.BlockSpec((self.each, rows, width), lambda h, b: (0, 0, h))
            for _ in range(self.lists)
        ]

    def shapes(self, rows, width, dtype):
        return [
            jax.ShapeDtypeStruct((self.each, rows, width), dtype) for _ in range(self.lists)
        ]

    def specs(self, rows, width):
        return [whole((self.each, rows, width)) for _ in range(self.lists)]


def exchange(size, blocks):
    if size.mirrored:
        return [blocks[0]] + [mirror(blocks[k], "seq", k) for k in range(1, size.parts)]
    return [lax.all_to_all(blocks[0], "seq", split_axis=0, concat_axis=0, tiled=True)]


def pack_kernel(size, ints, qk, text, *outs):
    for slot in range(size.parts):
        dest = ints[0] ^ slot
        group = dest // size.copies
        place = cols(group * size.width, size.width)
        out = at(outs, slot)
        if size.copies == 1:
            out[: size.sub] = qk[0, :, place]
        else:
            first = pl.multiple_of((dest % size.copies) * size.sub, 16)
            out[: size.sub] = qk[0, pl.ds(first, size.sub), place]
        out[size.sub : size.sub + size.rows] = qk[1, :, place]
        out[size.sub + size.rows :] = text[:, place]


def pack(size, ints, slots, text):
    return pl.pallas_call(
        functools.partial(pack_kernel, size),
        grid=(1,),
        in_specs=[SMEM, whole((2,) + slots.shape[1:]), whole(text.shape)],
        out_specs=size.specs(size.block_rows, size.width),
        out_shape=size.shapes(size.block_rows, size.width, BF16),
        compiler_params=PARAMS,
        name="pack_queries_keys",
    )(ints, slots, text)


def project_kernel(size, ints, floats, value, readout, noise, old, mixed_out, *outs):
    for slot in range(size.parts):
        group = (ints[0] ^ slot) // size.copies
        out = at(outs, slot)
        for head in range(size.heads):
            place = cols(group * size.width + head * HEAD_DIM, HEAD_DIM)
            projected = dot(value[0, :, place], readout[place, :])
            out[:, head * size.rows : (head + 1) * size.rows] = projected.T.astype(BF16)
    mixed = noise[...] + floats[0] * old[...]
    squares = jnp.sum(noise[...] * noise[...], axis=(0, 1), keepdims=True)
    mixed_out[: size.ch] = mixed.T
    mixed_out[size.ch :] = jnp.broadcast_to(squares, (8, size.rows))


def project(size, ints, floats, slots, readout, noise, old):
    outs = pl.pallas_call(
        functools.partial(project_kernel, size),
        grid=(1,),
        in_specs=[
            SMEM,
            SMEM,
            pl.BlockSpec((1,) + slots.shape[1:], lambda *_: (2, 0, 0)),
            whole(readout.shape),
            whole(noise.shape),
            whole(old.shape),
        ],
        out_specs=[whole((size.ch + 8, size.rows))] + size.specs(size.ch, size.heads * size.rows),
        out_shape=[jax.ShapeDtypeStruct((size.ch + 8, size.rows), F32)]
        + size.shapes(size.ch, size.heads * size.rows, BF16),
        compiler_params=PARAMS,
        name="project_values",
    )(ints, floats, slots, readout, noise, old)
    return outs[0], outs[1:]


def gather_queries(size, blocks, queries):
    for slot in range(size.parts):
        queries[slot * size.sub : (slot + 1) * size.sub] = at(blocks, slot)[: size.sub]


def text_rows(size, blocks, second):
    first = size.sub + size.rows
    found = []
    for slot in range(size.parts):
        pair = at(blocks, slot)[first : first + 2 * size.txt].astype(F32)
        found.append(pair[size.txt :] if second else pair[: size.txt])
    return jnp.concatenate(found, axis=0).astype(BF16)


def gather_keys(size, blocks, keys):
    for slot in range(size.parts):
        part = at(blocks, slot)[size.sub : size.sub + size.rows]
        keys[slot * size.rows : (slot + 1) * size.rows] = part
    keys[size.img_keys :] = text_rows(size, blocks, False)


def probs_kernel(size, *refs):
    blocks = refs[: size.lists]
    probs, keys, queries = refs[size.lists :]
    step = pl.program_id(1)

    @pl.when(step == 0)
    def _():
        gather_queries(size, blocks, queries)
        gather_keys(size, blocks, keys)

    first = pl.multiple_of(step * size.q_block, 128)
    scores = dot_nt(keys[...], queries[pl.ds(first, size.q_block), :]) * SCALE
    top = jnp.max(scores, axis=0, keepdims=True)
    raised = jnp.exp(scores - top)
    total = jnp.sum(raised, axis=0, keepdims=True)
    probs[0] = (raised * (1.0 / total)).astype(BF16)


def probabilities(size, blocks):
    return pl.pallas_call(
        functools.partial(probs_kernel, size),
        grid=(size.heads, size.q_blocks),
        in_specs=size.head_specs(size.block_rows, HEAD_DIM),
        out_specs=pl.BlockSpec((1, size.keys, size.q_block), lambda h, b: (h, 0, b)),
        out_shape=jax.ShapeDtypeStruct((size.heads, size.keys, size.queries), BF16),
        scratch_shapes=[
            pltpu.VMEM((size.keys, HEAD_DIM), BF16),
            pltpu.VMEM((size.queries, HEAD_DIM), BF16),
        ],
        compiler_params=PARAMS,
        name="attention_probs",
    )(*blocks)


def joined_projection(size, projected):
    return jnp.concatenate([at(projected, slot)[...] for slot in range(size.parts)], axis=1)


def guided_kernel(size, ints, floats, *refs):
    blocks = refs[: size.lists]
    projected = refs[size.lists : 2 * size.lists]
    readout, probs, out = refs[2 * size.lists :]
    head = pl.program_id(1)
    place = cols(ints[1] * size.width + head * HEAD_DIM, HEAD_DIM)
    text = dot(text_rows(size, blocks, True), readout[place, :]).astype(BF16)
    image = joined_projection(size, projected)
    part = dot(image, probs[0, : size.img_keys]) + dot_tn(text, probs[0, size.img_keys :])
    part = part * floats[1]

    @pl.when(head == 0)
    def _():
        out[...] = part

    @pl.when(head > 0)
    def _():
        out[...] += part


def guided_part(size, ints, floats, blocks, projected, readout, probs):
    def swap(spec):
        index = spec.index_map
        return pl.BlockSpec(spec.block_shape, lambda b, h: index(h, b))

    return pl.pallas_call(
        functools.partial(guided_kernel, size),
        grid=(size.q_blocks, size.heads),
        in_specs=[SMEM, SMEM]
        + [swap(s) for s in size.head_specs(size.block_rows, HEAD_DIM)]
        + [swap(s) for s in size.head_specs(size.ch, size.rows)]
        + [
            whole(readout.shape),
            pl.BlockSpec((1, size.keys, size.q_block), lambda b, h: (h, 0, b)),
        ],
        out_specs=pl.BlockSpec((size.ch, size.q_block), lambda b, h: (0, b)),
        out_shape=jax.ShapeDtypeStruct((size.ch, size.queries), F32),
        compiler_params=PARAMS,
        name="guided_part",
    )(ints, floats, *blocks, *projected, readout, probs)


def surrogate_gain(ratio, advantage):
    clipped = jnp.clip(ratio, 0.8, 1.2)
    keep = ratio * advantage <= clipped * advantage
    return jnp.where(keep, -ratio * advantage, jnp.zeros_like(ratio))


def grad_values_kernel(size, floats, *refs):
    if size.mirrored:
        guided_parts = refs[: size.parts]
        mixed = refs[size.parts : 2 * size.parts]
        refs = refs[2 * size.parts :]
    else:
        given, refs = refs[0], refs[1:]
    probs, grad_out, ratio_out = refs[:3]
    outs = refs[3 : 3 + size.lists]
    total = refs[3 + size.lists]
    head, step = pl.program_id(0), pl.program_id(1)

    @pl.when((head == 0) & (step == 0))
    def _():
        if size.mirrored:
            rest = []
            for slot in range(size.parts):
                parts = []
                for apart in range(size.parts):
                    other = slot ^ apart
                    part = guided_parts[apart][:, other * size.sub : (other + 1) * size.sub]
                    parts.append(part.astype(F32))
                rest.append(mixed[slot][: size.ch] - floats[0] * tree_sum(parts))
            norm = tree_sum([jnp.sum(x * x, axis=(0, 1), keepdims=True) for x in rest])
            squares = tree_sum([x[size.ch : size.ch + 1, :1] for x in mixed])
            count = size.queries * size.ch
            ratio = jnp.exp((squares - norm) * (0.5 / count))
            gain = surrogate_gain(ratio, jnp.full((1, 1), floats[2], F32))
            factor = gain * (floats[0] * floats[1])
            for slot in range(size.parts):
                place = slice(slot * size.sub, (slot + 1) * size.sub)
                grad_out[:, place] = (rest[slot] * factor).astype(BF16)
            ratio_out[...] = jnp.broadcast_to(ratio, ratio_out.shape)
        else:
            grad_out[...] = given[...]
            ratio_out[...] = jnp.zeros(ratio_out.shape, F32)

    first = pl.multiple_of(step * size.q_block, 128)
    part = dot_nt(grad_out[:, pl.ds(first, size.q_block)], probs[0])
    if size.q_blocks == 1:
        done = part
    else:

        @pl.when(step == 0)
        def _():
            total[...] = part

        @pl.when(step > 0)
        def _():
            total[...] += part

        done = total[...]
    for slot in range(size.parts):
        at(outs, slot)[...] = done[:, slot * size.rows : (slot + 1) * size.rows].astype(BF16)


def grad_values(size, floats, given, probs):
    specs = [whole(x.shape) for x in given]
    outs = pl.pallas_call(
        functools.partial(grad_values_kernel, size),
        grid=(size.heads, size.q_blocks),
        in_specs=[SMEM]
        + specs
        + [pl.BlockSpec((1, size.img_keys, size.q_block), lambda h, b: (h, 0, b))],
        out_specs=[whole((size.ch, size.queries)), whole((8, 128))]
        + size.head_specs(size.ch, size.rows),
        out_shape=[
            jax.ShapeDtypeStruct((size.ch, size.queries), BF16),
            jax.ShapeDtypeStruct((8, 128), F32),
        ]
        + size.shapes(size.ch, size.heads * size.rows, BF16),
        scratch_shapes=[pltpu.VMEM((size.ch, size.img_keys), F32)],
        compiler_params=PARAMS,
        name="grad_values",
    )(floats, *given, probs)
    return outs[0], outs[1], outs[2:]


def backward_kernel(size, ints, *refs):
    blocks = refs[: size.lists]
    projected = refs[size.lists : 2 * size.lists]
    readout, probs_ref, grad_ref, text_out = refs[2 * size.lists : 2 * size.lists + 4]
    outs = refs[2 * size.lists + 4 : 3 * size.lists + 4]
    keys, queries, grad_keys, grad_queries, grad_text = refs[3 * size.lists + 4 :]
    head, step = pl.program_id(0), pl.program_id(1)

    @pl.when(step == 0)
    def _():
        gather_queries(size, blocks, queries)
        gather_keys(size, blocks, keys)

    place = cols(ints[1] * size.width + head * HEAD_DIM, HEAD_DIM)
    first = pl.multiple_of(step * size.q_block, 128)
    text_values = text_rows(size, blocks, True)
    text = dot(text_values, readout[place, :]).astype(BF16)
    image = joined_projection(size, projected)
    grad = grad_ref[:, pl.ds(first, size.q_block)]
    probs = probs_ref[0]
    weights = probs.astype(F32)
    grad_probs = jnp.concatenate([dot_tn(image, grad), dot(text, grad)], axis=0)
    delta = jnp.sum(weights * grad_probs, axis=0, keepdims=True)
    grad_scores = (weights * (grad_probs - delta) * SCALE).astype(BF16)
    key_part = dot(grad_scores, queries[pl.ds(first, size.q_block), :])
    text_part = dot_nt(probs[size.img_keys :], grad)
    query_part = dot_tn(keys[...], grad_scores).T

    @pl.when(step == 0)
    def _():
        grad_keys[...] = key_part
        grad_text[...] = text_part

    @pl.when(step > 0)
    def _():
        grad_keys[...] += key_part
        grad_text[...] += text_part

    grad_queries[pl.ds(first, size.q_block), :] = query_part.astype(BF16)

    @pl.when(step == size.q_blocks - 1)
    def _():
        summed = grad_text[...].astype(BF16)
        value_text = dot_nt(summed, readout[place, :])
        text_out[...] = dot_tn(summed, text_values)
        for slot in range(size.parts):
            out = at(outs, slot)
            out[: size.sub] = grad_queries[slot * size.sub : (slot + 1) * size.sub]
            out[size.sub : size.sub + size.rows] = grad_keys[
                slot * size.rows : (slot + 1) * size.rows
            ].astype(BF16)
            start = size.img_keys + slot * size.txt
            pair = [
                grad_keys[start : start + size.txt],
                value_text[slot * size.txt : (slot + 1) * size.txt],
            ]
            out[size.sub + size.rows :] = jnp.concatenate(pair, axis=0).astype(BF16)


def backward(size, ints, blocks, projected, readout, probs, grad):
    outs = pl.pallas_call(
        functools.partial(backward_kernel, size),
        grid=(size.heads, size.q_blocks),
        in_specs=[SMEM]
        + size.head_specs(size.block_rows, HEAD_DIM)
        + size.head_specs(size.ch, size.rows)
        + [
            whole(readout.shape),
            pl.BlockSpec((1, size.keys, size.q_block), lambda h, b: (h, 0, b)),
            whole(grad.shape),
        ],
        out_specs=[pl.BlockSpec((size.ch, HEAD_DIM), lambda h, b: (0, h))]
        + size.head_specs(size.block_rows, HEAD_DIM),
        out_shape=[jax.ShapeDtypeStruct((size.ch, size.width), F32)]
        + size.shapes(size.block_rows, size.width, BF16),
        scratch_shapes=[
            pltpu.VMEM((size.keys, HEAD_DIM), BF16),
            pltpu.VMEM((size.queries, HEAD_DIM), BF16),
            pltpu.VMEM((size.keys, HEAD_DIM), F32),
            pltpu.VMEM((size.queries, HEAD_DIM), BF16),
            pltpu.VMEM((size.parts * size.txt, size.ch), F32),
        ],
        compiler_params=PARAMS,
        name="attention_backward",
    )(ints, *blocks, *projected, readout, probs, grad)
    return outs[0], outs[1:]


def home_values_kernel(size, pieces, ints, *refs):
    blocks = refs[: size.lists]
    value, readout, text, grad_out, part_out = refs[size.lists :]
    piece_width = size.features // pieces

    def target(start):
        piece = (start // piece_width) ^ ints[2]
        return piece * piece_width + start % piece_width

    for group in range(size.groups):
        held = [
            at(blocks, group * size.copies + copy)[...].astype(F32) for copy in range(size.copies)
        ]
        summed = sum(held[1:], held[0])
        owner = ints[0] ^ group
        for head in range(size.heads):
            start = owner * size.width + head * HEAD_DIM
            place = cols(start, HEAD_DIM)
            part = summed[:, head * size.rows : (head + 1) * size.rows]
            grad_out[:, place] = dot_nt(part.T.astype(BF16), readout[place, :]).astype(BF16)
            product = dot(part.astype(BF16), value[0, :, place])
            part_out[:, cols(target(start), HEAD_DIM)] = product
    for head in range(size.heads):
        start = ints[1] * size.width + head * HEAD_DIM
        part_out[:, cols(target(start), HEAD_DIM)] += text[
            :, head * HEAD_DIM : (head + 1) * HEAD_DIM
        ]


def home_values(size, pieces, ints, blocks, slots, readout, text):
    shape = slots.shape[1:]
    return pl.pallas_call(
        functools.partial(home_values_kernel, size, pieces),
        grid=(1,),
        in_specs=[SMEM]
        + size.specs(size.ch, size.heads * size.rows)
        + [
            pl.BlockSpec((1,) + shape, lambda *_: (2, 0, 0)),
            whole(readout.shape),
            whole(text.shape),
        ],
        out_specs=[whole(shape), whole((size.ch, size.features))],
        out_shape=[
            jax.ShapeDtypeStruct(shape, BF16),
            jax.ShapeDtypeStruct((size.ch, size.features), F32),
        ],
        compiler_params=PARAMS,
        name="home_values",
    )(ints, *blocks, slots, readout, text)


def home_kernel(size, ints, *refs):
    blocks = refs[: size.lists]
    out, text_out = refs[size.lists :]
    for group in range(size.groups):
        place = cols((ints[0] ^ group) * size.width, size.width)
        held = [at(blocks, group * size.copies + copy) for copy in range(size.copies)]
        for copy in range(size.copies):
            out[0, copy * size.sub : (copy + 1) * size.sub, place] = held[copy][: size.sub]
        if size.copies == 1:
            out[1, :, place] = held[0][size.sub : size.sub + size.rows]
            text_out[:, place] = held[0][size.sub + size.rows :]
        else:
            rest = sum([x[size.sub :].astype(F32) for x in held]).astype(BF16)
            out[1, :, place] = rest[: size.rows]
            text_out[:, place] = rest[size.rows :]


def home(size, ints, blocks):
    return pl.pallas_call(
        functools.partial(home_kernel, size),
        grid=(1,),
        in_specs=[SMEM] + size.specs(size.block_rows, size.width),
        out_specs=[
            whole((2, size.rows, size.features)),
            whole((2 * size.txt, size.features)),
        ],
        out_shape=[
            jax.ShapeDtypeStruct((2, size.rows, size.features), BF16),
            jax.ShapeDtypeStruct((2 * size.txt, size.features), BF16),
        ],
        compiler_params=PARAMS,
        name="home_queries_keys",
    )(ints, *blocks)


def turn_kernel(ints, *refs):
    pieces, out = refs[:-1], refs[-1]
    per = pieces[0].shape[1]
    for slot, piece in enumerate(pieces):
        first = pl.multiple_of((slot ^ ints[2]) * per, 128)
        out[pl.ds(first, per), :] = piece[...].astype(F32).T


def sum_readout(size, ints, part):
    branches, images = lax.axis_size("cfg"), lax.axis_size("img")
    half = part.shape[1] // branches
    own = part[:, :half] + mirror(part[:, half:], "cfg", 1)
    per = half // images
    sent = own.astype(BF16)
    mine = own[:, :per]
    for k in range(1, images):
        mine = mine + mirror(sent[:, k * per : (k + 1) * per], "img", k).astype(F32)
    sent = mine.astype(BF16)
    held = [sent] + [mirror(sent, "seq", k) for k in range(1, size.parts)]
    total = tree_sum([x.astype(F32) for x in held]).astype(BF16)
    found = [total] + [mirror(total, "img", k) for k in range(1, images)]
    found = found + [mirror(x, "cfg", 1) for x in found]
    return pl.pallas_call(
        turn_kernel,
        grid=(1,),
        in_specs=[SMEM] + [whole(x.shape) for x in found],
        out_specs=whole((part.shape[1], part.shape[0])),
        out_shape=jax.ShapeDtypeStruct((part.shape[1], part.shape[0]), F32),
        compiler_params=PARAMS,
        name="turn_readout_grad",
    )(ints, *found)


def on_device(img_qkv, txt_kv, readout, old_velocity, noise, step_ratio, rewards, guidance):
    features, channels = readout.shape
    size = Sizes(img_qkv.shape[2], txt_kv.shape[2], features, channels)
    branches, images = lax.axis_size("cfg"), lax.axis_size("img")
    pieces = branches * images
    split = size.mirrored and branches == 2 and images in (1, 2, 4, 8)
    branch = lax.axis_index("cfg")
    place = lax.axis_index("seq")
    piece = branch * images + lax.axis_index("img")
    ints = jnp.stack(
        [
            place if size.mirrored else jnp.zeros_like(place),
            place // size.copies,
            piece if split else jnp.zeros_like(piece),
        ]
    ).astype(jnp.int32)
    slots = img_qkv[0, 0].transpose(1, 0, 2)
    text = txt_kv[0, 0].transpose(1, 0, 2).reshape(2 * size.txt, features)
    blocks = exchange(size, pack(size, ints, slots, text))

    reward = rewards[0]
    if images in (2, 4, 8):
        every = [reward] + [mirror(rewards, "img", k)[0] for k in range(1, images)]
        mean = tree_sum(every) / images
        square = tree_sum([x * x for x in every]) / images
    else:
        mean = lax.psum(reward, "img") / images
        square = lax.psum(reward * reward, "img") / images
    spread = jnp.sqrt(jnp.maximum(square - mean * mean, 0.0))
    advantage = (reward - mean) / jnp.maximum(spread, 1.0)
    rate = step_ratio[0]
    weight = jnp.where(branch == 0, guidance, 1.0 - guidance)
    early = jnp.stack([rate, weight])
    mixed, projected = project(size, ints, early, slots, readout, noise[0], old_velocity[0])
    projected = exchange(size, projected)
    floats = jnp.stack([rate, weight, advantage])

    probs = probabilities(size, blocks)
    part = guided_part(size, ints, early, blocks, projected, readout, probs)
    summed = part + mirror(part, "cfg", 1)
    if size.mirrored:
        all_mixed = [mixed] + [mirror(mixed, "seq", k) for k in range(1, size.parts)]
        sent = summed.astype(BF16)
        given = [sent] + [mirror(sent, "seq", k) for k in range(1, size.parts)] + all_mixed
    else:
        copy = place % size.copies
        chosen = jnp.arange(size.copies).reshape(-1, 1, 1) == copy
        guided = lax.psum(jnp.where(chosen, summed[None], 0.0), "seq")
        guided = lax.dynamic_index_in_dim(guided, copy, 0, False)
        all_mixed = lax.all_gather(mixed, "seq", axis=0)
        squares = jnp.sum(all_mixed[:, channels, 0])
        near = lax.dynamic_slice_in_dim(all_mixed[:, :channels], copy * size.sub, size.sub, 2)
        near = near.transpose(1, 0, 2).reshape(channels, size.queries)
        left = near - rate * guided
        norm = lax.psum(jnp.sum(left * left), "seq") / size.groups
        ratio = jnp.exp((squares - norm) * (0.5 / (size.parts * size.rows * channels)))
        gain = surrogate_gain(ratio, advantage)
        given = [(left * (gain * (rate * weight))).astype(BF16)]
    grad, found_ratio, value_blocks = grad_values(size, floats, given, probs)
    if size.mirrored:
        ratio = found_ratio[0, 0]
    value_home = exchange(size, value_blocks)
    text_part, grad_blocks = backward(size, ints, blocks, projected, readout, probs, grad)
    grad_home = exchange(size, grad_blocks)
    value_grad, readout_part = home_values(
        size, pieces if split else 1, ints, value_home, slots, readout, text_part
    )
    if split:
        readout_grad = sum_readout(size, ints, readout_part)
    else:
        readout_grad = lax.psum(readout_part, ("cfg", "img", "seq")).T
    token_grads, text_grads = home(size, ints, grad_home)
    img_grad = jnp.stack([token_grads[0], token_grads[1], value_grad], axis=1)[None, None]
    txt_grad = text_grads.reshape(2, size.txt, features).transpose(1, 0, 2)[None, None]
    return (img_grad, txt_grad, readout_grad, ratio.reshape(1))


def solution(mesh):
    return jax.shard_map(
        on_device,
        mesh=mesh,
        in_specs=(
            P("cfg", "img", "seq", None, None),
            P("cfg", "img", "seq", None, None),
            P(),
            P("img", "seq", None),
            P("img", "seq", None),
            P("img"),
            P("img"),
            P(),
        ),
        out_specs=(
            P("cfg", "img", "seq", None, None),
            P("cfg", "img", "seq", None, None),
            P(),
            P("img"),
        ),
        check_vma=False,
    )
```

time: 335 us -> 129 us (0.39)
  waiting for transfers between devices: 177 us -> 41.6 us
  blocking collectives: 51.8 us -> 0 us
  matrix products: 23.2 us -> 0 us
  starting transfers between devices: 25.3 us -> 47.9 us
  local copies, waits for them, and re-layouts: 29.1 us -> 9.5 us
  Pallas kernels: 0 us -> 18.3 us
  between operations: 20.8 us -> 8.46 us
  other arithmetic: 5.98 us -> 2.6 us
    psum x1 -> x0, waiting for transfers between devices: 120 us -> none  [on_device(): readout_grad = lax.psum(readout_part, ('cfg', 'img', 'seq'))]
    all_to_all x6 -> x0, waiting for transfers between devices: 57 us -> none  [the longest x1 13.2 us: on_device(): lax.all_to_all(key_items, 'seq', split_axis=0, concat_axis=1, tiled=True)]
    ppermute x1 -> x36, starting transfers between devices: 0.07 us -> 47.9 us  [mirror(): return lax.ppermute(x, axis, [(i, i ^ apart) for i in range(count)])]
    ppermute x1 -> x36, waiting for transfers between devices: 0.01 us -> 41.6 us  [mirror(): return lax.ppermute(x, axis, [(i, i ^ apart) for i in range(count)])]
    all_to_all x2 -> x0, blocking collectives: 30.9 us -> none  [the longest x1 16.4 us: on_device(): lax.all_to_all(mixed.reshape(parts, -1, width), 'seq', split_axis=0, conc...]
    all_to_all x6 -> x0, starting transfers between devices: 25.2 us -> none  [the longest x1 6.32 us: on_device(): lax.all_to_all(query_items, 'seq', split_axis=0, concat_axis=1, tiled=True)]
    dot_general x9 -> x0, matrix products: 23.2 us -> none  [the longest x1 6.05 us: one_block(): jnp.einsum('hqk,qhd->khd', grad_scores, block, preferred_element_type=jnp...]
    psum x2 -> x0, blocking collectives: 21 us -> none  [the longest x1 10.6 us: on_device(): reward_sums = lax.psum((reward, reward * reward), 'img')]
  transfers between devices with their start and end apart: 8 -> 36, of which waited for: 7 -> 12; matrix products, arithmetic and copies ran while one was open for 8% -> 4% of each run, Pallas kernels for 0% -> 8%
where the time goes in v1:
time: 129 us; the launch traced here: 128 us
  starting transfers between devices  47.9 us (37%)
  waiting for transfers between devices  41.6 us (32%)
  Pallas kernels  18.3 us (14%)
  local copies, waits for them, and re-layouts  9.5 us (7%)
  between operations  8.46 us (7%)
  other arithmetic  2.6 us (2%)
    ppermute x36, starting transfers between devices, mirror(): return lax.ppermute(x, axis, [(i, i ^ apart) for i in range(count)])  47.9 us
    ppermute x36, waiting for transfers between devices, mirror(): return lax.ppermute(x, axis, [(i, i ^ apart) for i in range(count)])  41.6 us
    unnamed x42, local copies, waits for them, and re-layouts  7.33 us
    pallas_call x1, Pallas kernels, backward(): pl.pallas_call(functools.partial(backward_kernel, size), grid=(size.heads...  5.19 us
    pallas_call x1, Pallas kernels, probabilities(): pl.pallas_call(functools.partial(probs_kernel, size), grid=(size.heads, s...  2.93 us
    pallas_call x1, Pallas kernels, guided_part(): pl.pallas_call(functools.partial(guided_kernel, size), grid=(size.q_block...  2.6 us
  transfers between devices with their start and end apart: 36, of which 12 were waited for; matrix products, arithmetic and copies ran while one was open for 4% of the time, Pallas kernels for 8%

profile of v1, /device:TPU:0, one launch (start us, length us, event | category | flops | bytes accessed | tf_op | source)
XLA Modules:
  0.0 128.4 jit_solution(13703201104350189855)
XLA Ops:
  0.7 0.9 copy.24
  1.5 0.1 pad_add_fusion.ints
  1.6 1.4 %copy-done = bf16[1,1,128,3,2048]{4,2,3,1,0:T(8,128)(2,1)S(1)} copy-done((bf16[1,1,128,3,2048]{4,2,3,1,0:T(8,128)(2,1)S(1)}, bf16[1,1,128,3,2048]{4,2,3,1,0:T(8,128)(2,1)}, u32[]{:S(2)}) %copy-start) | copy-done | bytes 1572888
  3.0 1.5 %pack_queries_keys.1 = (bf16[1,272,512]{2,1,0:T(8,128)(2,1)S(1)}, bf16[1,272,512]{2,1,0:T(8,128)(2,1)}, bf16[1,272,512]{2,1,0:T(8,128)(2,1)}, bf16[1,272,512]{2,1,0:T(8,128)(2,1)}) custom-call(s32[3]{0:T(128)S(1)} %pad_add_fusion.ints, bf16[3,128,2048]{2,1,0:T(8,128)(2,1)S(1)} %bitcast.37, bf16[16,2048]{1,0:T(8,128)(2,1)S(1)} %bitcast.43), custom_call_target="tpu_custom_call" | custom-call | tf_op jit(solution)/shard_map/pack_queries_keys/pallas_call | solution.py:116
  4.5 3.0 %collective-permute-start = (bf16[1,272,512]{2,1,0:T(8,128)(2,1)}, bf16[1,272,512]{2,1,0:T(8,128)(2,1)S(1)}, u32[]{:S(2)}, u32[]{:S(2)}) collective-permute-start(bf16[1,272,512]{2,1,0:T(8,128)(2,1)} %get-tuple-element.29), channel_id=1, source_target_pairs={{0,1},{1,0},{2,3},{3,2},{4,5},{5,4},{6,7},{7,6},{8,9},{9,8},{10,11... | collective-permute-start | bytes 835592 | tf_op jit(solution)/shard_map/ppermute | solution.py:51
  7.6 2.6 %collective-permute-start.1 = (bf16[1,272,512]{2,1,0:T(8,128)(2,1)}, bf16[1,272,512]{2,1,0:T(8,128)(2,1)S(1)}, u32[]{:S(2)}, u32[]{:S(2)}) collective-permute-start(bf16[1,272,512]{2,1,0:T(8,128)(2,1)} %get-tuple-element.30), channel_id=1, source_target_pairs={{0,2},{1,3},{2,0},{3,1},{4,6},{5,7},{6,4},{7,5},{8,10},{9,11},{10,... | collective-permute-start | bytes 835592 | tf_op jit(solution)/shard_map/ppermute | solution.py:51
  11.5 0.1 copy.14
  11.6 0.1 copy.13
  11.7 1.2 copy.15.readout.refs_8_.refs_5_
  12.9 0.1 pad_maximum_fusion.floats
  13.0 1.0 project_values.1
  14.0 1.0 collective-permute-start.3
  14.9 3.5 %collective-permute-start.4 = (bf16[1,64,512]{2,1,0:T(8,128)(2,1)S(1)}, bf16[1,64,512]{2,1,0:T(8,128)(2,1)S(1)}, u32[]{:S(2)}, u32[]{:S(2)}) collective-permute-start(bf16[1,64,512]{2,1,0:T(8,128)(2,1)S(1)} %get-tuple-element.34), channel_id=1, source_target_pairs={{0,2},{1,3},{2,0},{3,1},{4,6},{5,7},{6,4},{7,5},{8,10},{9,11},{10,... | collective-permute-start | bytes 196616 | tf_op jit(solution)/shard_map/ppermute | solution.py:51
  18.4 1.9 %collective-permute-done.refs_1_ = bf16[1,272,512]{2,1,0:T(8,128)(2,1)S(1)} collective-permute-done((bf16[1,272,512]{2,1,0:T(8,128)(2,1)}, bf16[1,272,512]{2,1,0:T(8,128)(2,1)S(1)}, u32[]{:S(2)}, u32[]{:S(2)}) %collective-permute-start) | collective-permute-done | bytes 278560 | tf_op jit(solution)/shard_map/ppermute | solution.py:51
  20.3 3.8 %collective-permute-start.5 = (bf16[1,64,512]{2,1,0:T(8,128)(2,1)S(1)}, bf16[1,64,512]{2,1,0:T(8,128)(2,1)S(1)}, u32[]{:S(2)}, u32[]{:S(2)}) collective-permute-start(bf16[1,64,512]{2,1,0:T(8,128)(2,1)S(1)} %get-tuple-element.35), channel_id=1, source_target_pairs={{0,3},{1,2},{2,1},{3,0},{4,7},{5,6},{6,5},{7,4},{8,11},{9,10},{10,... | collective-permute-start | bytes 196616 | tf_op jit(solution)/shard_map/ppermute | solution.py:51
  24.2 8.8 %collective-permute-done.1.refs_2_ = bf16[1,272,512]{2,1,0:T(8,128)(2,1)S(1)} collective-permute-done((bf16[1,272,512]{2,1,0:T(8,128)(2,1)}, bf16[1,272,512]{2,1,0:T(8,128)(2,1)S(1)}, u32[]{:S(2)}, u32[]{:S(2)}) %collective-permute-start.1) | collective-permute-done | bytes 278560 | tf_op jit(solution)/shard_map/ppermute | solution.py:51
  33.0 0.7 copy-done.3
  33.7 0.7 copy-done.7
  34.4 1.0 copy-done.4
  35.4 1.0 copy-done.8
  36.3 2.9 %attention_probs.1.refs_9_.refs_8_ = bf16[4,544,512]{2,1,0:T(8,128)(2,1)S(1)} custom-call(bf16[1,272,512]{2,1,0:T(8,128)(2,1)S(1)} %get-tuple-element.28.refs_0_, bf16[1,272,512]{2,1,0:T(8,128)(2,1)S(1)} %collective-permute-done.refs_1_, bf16[1,272,512]{2,1,0:T(8,128)(2,1)S(1)} %copy-done.4, bf16[1,272,512]{2,1,0:T(8,128)(2,1)S(1)} %copy-done.8), custom_call_target="tpu_custom_call" | custom-call | tf_op jit(solution)/shard_map/attention_probs/pallas_call | solution.py:202
  39.3 0.4 collective-permute-done.4.refs_6_
  39.7 2.6 %guided_part.1 = f32[64,512]{1,0:T(8,128)S(1)} custom-call(s32[3]{0:T(128)S(1)} %pad_add_fusion.ints, f32[2]{0:T(128)S(1)} %pad_maximum_fusion.floats, bf16[1,272,512]{2,1,0:T(8,128)(2,1)S(1)} %get-tuple-element.28.refs_0_, bf16[1,272,512]{2,1,0:T(8,128)(2,1)S(1)} %collective-permute-done.refs_1_, bf16[1,272,512]{2,1,0:T(8,128)(2,1)S(1)} %copy-done.5, ...), custom_call_target="tpu_custom_call" | custom-call | tf_op jit(solution)/shard_map/guided_part/pallas_call | solution.py:246
  42.4 1.6 %collective-permute-start.6 = (f32[1]{0:T(128)}, f32[1]{0:T(128)}, u32[]{:S(2)}, u32[]{:S(2)}) collective-permute-start(f32[1]{0:T(128)} %param.14), channel_id=1, source_target_pairs={{0,4},{4,0},{8,12},{12,8},{1,5},{5,1},{9,13},{13,9},{2,6},{6,2},{1... | collective-permute-start | bytes 20 | tf_op jit(solution)/shard_map/ppermute | solution.py:51
  44.0 1.5 %collective-permute-start.8 = (f32[1]{0:T(128)}, f32[1]{0:T(128)}, u32[]{:S(2)}, u32[]{:S(2)}) collective-permute-start(f32[1]{0:T(128)} %param.14), channel_id=1, source_target_pairs={{0,12},{4,8},{8,4},{12,0},{1,13},{5,9},{9,5},{13,1},{2,14},{6,10},... | collective-permute-start | bytes 20 | tf_op jit(solution)/shard_map/ppermute | solution.py:51
  45.4 0.5 collective-permute-start.7
  46.0 2.5 %collective-permute-start.15 = (f32[72,128]{1,0:T(8,128)S(1)}, f32[72,128]{1,0:T(8,128)}, u32[]{:S(2)}, u32[]{:S(2)}) collective-permute-start(f32[72,128]{1,0:T(8,128)S(1)} %get-tuple-element.36.refs_4_), channel_id=1, source_target_pairs={{0,3},{1,2},{2,1},{3,0},{4,7},{5,6},{6,5},{7,4},{8,11},{9,10},{10,... | collective-permute-start | bytes 110600 | tf_op jit(solution)/shard_map/ppermute | solution.py:51
  49.1 4.5 %collective-permute-start.14 = (f32[72,128]{1,0:T(8,128)S(1)}, f32[72,128]{1,0:T(8,128)}, u32[]{:S(2)}, u32[]{:S(2)}) collective-permute-start(f32[72,128]{1,0:T(8,128)S(1)} %get-tuple-element.36.refs_4_), channel_id=1, source_target_pairs={{0,2},{1,3},{2,0},{3,1},{4,6},{5,7},{6,4},{7,5},{8,10},{9,11},{10,... | collective-permute-start | bytes 110600 | tf_op jit(solution)/shard_map/ppermute | solution.py:51
  55.3 0.2 collective-permute-start.13
  59.4 1.0 add_convert_fusion.refs_0_
  60.4 2.4 %collective-permute-start.12 = (bf16[64,512]{1,0:T(8,128)(2,1)S(1)}, bf16[64,512]{1,0:T(8,128)(2,1)S(1)}, u32[]{:S(2)}, u32[]{:S(2)}) collective-permute-start(bf16[64,512]{1,0:T(8,128)(2,1)S(1)} %add_convert_fusion.refs_0_), channel_id=1, source_target_pairs={{0,3},{1,2},{2,1},{3,0},{4,7},{5,6},{6,5},{7,4},{8,11},{9,10},{10,... | collective-permute-start | bytes 196616 | tf_op jit(solution)/shard_map/ppermute | solution.py:51
  62.8 1.0 collective-permute-start.11
  63.8 1.1 collective-permute-start.10
  64.8 0.1 pad_maximum_fusion.1.floats
  64.9 2.3 %collective-permute-done.12.refs_3_ = bf16[64,512]{1,0:T(8,128)(2,1)S(1)} collective-permute-done((bf16[64,512]{1,0:T(8,128)(2,1)S(1)}, bf16[64,512]{1,0:T(8,128)(2,1)S(1)}, u32[]{:S(2)}, u32[]{:S(2)}) %collective-permute-start.12) | collective-permute-done | bytes 65568 | tf_op jit(solution)/shard_map/ppermute | solution.py:51
  67.2 2.1 %collective-permute-done.11.refs_2_ = bf16[64,512]{1,0:T(8,128)(2,1)S(1)} collective-permute-done((bf16[64,512]{1,0:T(8,128)(2,1)S(1)}, bf16[64,512]{1,0:T(8,128)(2,1)S(1)}, u32[]{:S(2)}, u32[]{:S(2)}) %collective-permute-start.11) | collective-permute-done | bytes 65568 | tf_op jit(solution)/shard_map/ppermute | solution.py:51
  69.3 2.4 %grad_values.1 = (bf16[64,512]{1,0:T(8,128)(2,1)S(1)}, f32[8,128]{1,0:T(8,128)S(1)}, bf16[1,64,512]{2,1,0:T(8,128)(2,1)S(1)}, bf16[1,64,512]{2,1,0:T(8,128)(2,1)...) custom-call(f32[3]{0:T(128)S(1)} %pad_maximum_fusion.1.floats, ...), custom_call_target="tpu_custom_call" | custom-call | tf_op jit(solution)/shard_map/grad_values/pallas_call | solution.py:327
  71.8 2.8 %collective-permute-start.20 = (bf16[1,64,512]{2,1,0:T(8,128)(2,1)S(1)}, bf16[1,64,512]{2,1,0:T(8,128)(2,1)S(1)}, u32[]{:S(2)}, u32[]{:S(2)}) collective-permute-start(bf16[1,64,512]{2,1,0:T(8,128)(2,1)S(1)} %get-tuple-element.45), channel_id=1, source_target_pairs={{0,2},{1,3},{2,0},{3,1},{4,6},{5,7},{6,4},{7,5},{8,10},{9,11},{10,... | collective-permute-start | bytes 196616 | tf_op jit(solution)/shard_map/ppermute | solution.py:51
  74.6 1.6 %collective-permute-start.21 = (bf16[1,64,512]{2,1,0:T(8,128)(2,1)S(1)}, bf16[1,64,512]{2,1,0:T(8,128)(2,1)S(1)}, u32[]{:S(2)}, u32[]{:S(2)}) collective-permute-start(bf16[1,64,512]{2,1,0:T(8,128)(2,1)S(1)} %get-tuple-element.46), channel_id=1, source_target_pairs={{0,3},{1,2},{2,1},{3,0},{4,7},{5,6},{6,5},{7,4},{8,11},{9,10},{10,... | collective-permute-start | bytes 196616 | tf_op jit(solution)/shard_map/ppermute | solution.py:51
  76.2 5.2 %attention_backward.1 = (f32[64,512]{1,0:T(8,128)S(1)}, bf16[1,272,512]{2,1,0:T(8,128)(2,1)S(1)}, bf16[1,272,512]{2,1,0:T(8,128)(2,1)S(1)}, bf16[1,272,512]{2,1,0:T(8,128)(2,1)S(1)}, bf16[1,272,512]{2,1,0:T(8,128)(2,1)S(1)}) custom-call(s32[3]{0:T(128)S(1)} %pad_add_fusion.ints, bf16[1,272,512]{2,1,0:T(8,128)(2,1)S(1)} %get-tuple-element.28.refs_0_, ...), custom_call_target="tpu_custom_call" | custom-call | tf_op jit(solution)/shard_map/attention_backward/pallas_call | solution.py:407
  81.4 1.3 %home_values.1 = (bf16[128,2048]{1,0:T(8,128)(2,1)S(1)}, f32[64,2048]{1,0:T(8,128)S(1)}) custom-call(s32[3]{0:T(128)S(1)} %pad_add_fusion.ints, bf16[1,64,512]{2,1,0:T(8,128)(2,1)S(1)} %get-tuple-element.43.refs_0_, bf16[1,64,512]{2,1,0:T(8,128)(2,1)S(1)} %collective-permute-done.19.refs_1_, bf16[1,64,512]{2,1,0:T(8,128)(2,1)S(1)} %collective-permute-done.20.refs_2_, ...), custom_call_target="tpu_custom_call" | custom-call | tf_op jit(solution)/shard_map/home_values/pallas_call | solution.py:466
  82.8 1.5 %collective-permute-done.22 = f32[64,1024]{1,0:T(8,128)S(1)} collective-permute-done((f32[64,1024]{1,0:T(8,128)S(1)}, f32[64,1024]{1,0:T(8,128)S(1)}, u32[]{:S(2)}, u32[]{:S(2)}) %collective-permute-start.22) | collective-permute-done | bytes 262176 | tf_op jit(solution)/shard_map/ppermute | solution.py:51
  84.4 1.6 %collective-permute-start.23 = (bf16[64,256]{1,0:T(8,128)(2,1)S(1)}, bf16[64,256]{1,0:T(8,128)(2,1)S(1)}, u32[]{:S(2)}, u32[]{:S(2)}) collective-permute-start(bf16[64,256]{1,0:T(8,128)(2,1)S(1)} %get-tuple-element.60), channel_id=1, source_target_pairs={{0,4},{4,0},{8,12},{12,8},{1,5},{5,1},{9,13},{13,9},{2,6},{6,2},{1... | collective-permute-start | bytes 98312 | tf_op jit(solution)/shard_map/ppermute | solution.py:51
  86.0 1.5 %collective-permute-start.25 = (bf16[64,256]{1,0:T(8,128)(2,1)S(1)}, bf16[64,256]{1,0:T(8,128)(2,1)S(1)}, u32[]{:S(2)}, u32[]{:S(2)}) collective-permute-start(bf16[64,256]{1,0:T(8,128)(2,1)S(1)} %get-tuple-element.61), channel_id=1, source_target_pairs={{0,12},{4,8},{8,4},{12,0},{1,13},{5,9},{9,5},{13,1},{2,14},{6,10},... | collective-permute-start | bytes 98312 | tf_op jit(solution)/shard_map/ppermute | solution.py:51
  87.5 0.5 collective-permute-start.24
  88.0 2.8 %collective-permute-start.17 = (bf16[1,272,512]{2,1,0:T(8,128)(2,1)S(1)}, bf16[1,272,512]{2,1,0:T(8,128)(2,1)S(1)}, u32[]{:S(2)}, u32[]{:S(2)}) collective-permute-start(bf16[1,272,512]{2,1,0:T(8,128)(2,1)S(1)} %get-tuple-element.40), channel_id=1, source_target_pairs={{0,2},{1,3},{2,0},{3,1},{4,6},{5,7},{6,4},{7,5},{8,10},{9,11},{10,... | collective-permute-start | bytes 835592 | tf_op jit(solution)/shard_map/ppermute | solution.py:51
  90.8 1.6 %collective-permute-start.18 = (bf16[1,272,512]{2,1,0:T(8,128)(2,1)S(1)}, bf16[1,272,512]{2,1,0:T(8,128)(2,1)S(1)}, u32[]{:S(2)}, u32[]{:S(2)}) collective-permute-start(bf16[1,272,512]{2,1,0:T(8,128)(2,1)S(1)} %get-tuple-element.41), channel_id=1, source_target_pairs={{0,3},{1,2},{2,1},{3,0},{4,7},{5,6},{6,5},{7,4},{8,11},{9,10},{10,... | collective-permute-start | bytes 835592 | tf_op jit(solution)/shard_map/ppermute | solution.py:51
  92.4 2.3 %collective-permute-start.28 = (bf16[64,256]{1,0:T(8,128)(2,1)S(1)}, bf16[64,256]{1,0:T(8,128)(2,1)S(1)}, u32[]{:S(2)}, u32[]{:S(2)}) collective-permute-start(bf16[64,256]{1,0:T(8,128)(2,1)S(1)} %fusion.2), channel_id=1, source_target_pairs={{0,3},{1,2},{2,1},{3,0},{4,7},{5,6},{6,5},{7,4},{8,11},{9,10},{10,... | collective-permute-start | bytes 98312 | tf_op jit(solution)/shard_map/ppermute | solution.py:51
  94.7 0.2 collective-permute-start.27
  94.9 3.7 %collective-permute-done.16.refs_1_ = bf16[1,272,512]{2,1,0:T(8,128)(2,1)S(1)} collective-permute-done((bf16[1,272,512]{2,1,0:T(8,128)(2,1)S(1)}, bf16[1,272,512]{2,1,0:T(8,128)(2,1)S(1)}, u32[]{:S(2)}, u32[]{:S(2)}) %collective-permute-start.16) | collective-permute-done | bytes 278560 | tf_op jit(solution)/shard_map/ppermute | solution.py:51
  98.6 0.5 slice.35
  99.1 12.7 %collective-permute-done.17.refs_2_ = bf16[1,272,512]{2,1,0:T(8,128)(2,1)S(1)} collective-permute-done((bf16[1,272,512]{2,1,0:T(8,128)(2,1)S(1)}, bf16[1,272,512]{2,1,0:T(8,128)(2,1)S(1)}, u32[]{:S(2)}, u32[]{:S(2)}) %collective-permute-start.17) | collective-permute-done | bytes 278560 | tf_op jit(solution)/shard_map/ppermute | solution.py:51
  111.8 0.6 home_queries_keys.1
  112.5 5.0 %collective-permute-done.27 = bf16[64,256]{1,0:T(8,128)(2,1)S(1)} collective-permute-done((bf16[64,256]{1,0:T(8,128)(2,1)S(1)}, bf16[64,256]{1,0:T(8,128)(2,1)S(1)}, u32[]{:S(2)}, u32[]{:S(2)}) %collective-permute-start.27) | collective-permute-done | bytes 32800 | tf_op jit(solution)/shard_map/ppermute | solution.py:51
  117.5 2.5 %collective-permute-start.31 = (bf16[64,256]{1,0:T(8,128)(2,1)S(1)}, bf16[64,256]{1,0:T(8,128)(2,1)S(1)}, u32[]{:S(2)}, u32[]{:S(2)}) collective-permute-start(bf16[64,256]{1,0:T(8,128)(2,1)S(1)} %add_convert_fusion.1.refs_0_), channel_id=1, source_target_pairs={{0,12},{4,8},{8,4},{12,0},{1,13},{5,9},{9,5},{13,1},{2,14},{6,10},... | collective-permute-start | bytes 98312 | tf_op jit(solution)/shard_map/ppermute | solution.py:51
  120.0 0.5 collective-permute-start.30
  120.5 0.6 collective-permute-start.29
  121.3 1.2 collective-permute-done.31.refs_3_
  122.4 1.5 %collective-permute-done.30.refs_2_ = bf16[64,256]{1,0:T(8,128)(2,1)S(1)} collective-permute-done((bf16[64,256]{1,0:T(8,128)(2,1)S(1)}, bf16[64,256]{1,0:T(8,128)(2,1)S(1)}, u32[]{:S(2)}, u32[]{:S(2)}) %collective-permute-start.30) | collective-permute-done | bytes 32800 | tf_op jit(solution)/shard_map/ppermute | solution.py:51
  123.9 0.5 collective-permute-done.29.refs_1_
  124.5 1.3 %maximum_bitcast_fusion = bf16[1,1,128,3,2048]{4,2,3,1,0:T(8,128)(2,1)} fusion(bf16[128,1,2048]{2,0,1:T(8,128)(2,1)S(1)} %bitcast.40, bf16[128,1,2048]{2,0,1:T(8,128)(2,1)S(1)} %get-tuple-element.59, bf16[128,1,2048]{2,0,1:T(8,128)(2,1)S(1)} %get-tuple-element.58), kind=kLoop, calls=%fused_computation | loop fusion | flops 1572864 | bytes 3145728 | tf_op jit(solution)/shard_map/broadcast_in_dim | solution.py:626
  125.8 0.7 copy.23
  126.5 0.8 turn_readout_grad.1
  127.3 1.1 copy.20
  (73 shorter events, 0.6 us)
Async XLA Ops:
  0.6 10.8 %copy-start.17 = (f32[1,128,64]{1,2,0:T(8,128)S(1)}, f32[1,128,64]{1,2,0:T(8,128)}, u32[]{:S(2)}) copy-start(f32[1,128,64]{1,2,0:T(8,128)} %param.11) | copy-start | bytes 98308
  0.6 10.9 %copy-start.18 = (f32[1,128,64]{1,2,0:T(8,128)S(1)}, f32[1,128,64]{1,2,0:T(8,128)}, u32[]{:S(2)}) copy-start(f32[1,128,64]{1,2,0:T(8,128)} %param.12) | copy-start | bytes 98308
  1.6 1.4 %copy-start = (bf16[1,1,128,3,2048]{4,2,3,1,0:T(8,128)(2,1)S(1)}, bf16[1,1,128,3,2048]{4,2,3,1,0:T(8,128)(2,1)}, u32[]{:S(2)}) copy-start(bf16[1,1,128,3,2048]{4,2,3,1,0:T(8,128)(2,1)} %param.8) | copy-start | bytes 4718596
  3.0 10.0 %copy-start.1 = (bf16[1,1,128,3,2048]{4,2,3,1,0:T(8,128)(2,1)S(1)}, bf16[1,1,128,3,2048]{4,2,3,1,0:T(8,128)(2,1)}, u32[]{:S(2)}) copy-start(bf16[1,1,128,3,2048]{4,2,3,1,0:T(8,128)(2,1)} %param.8) | copy-start | bytes 4718596
  4.5 15.8 %collective-permute-start = (bf16[1,272,512]{2,1,0:T(8,128)(2,1)}, bf16[1,272,512]{2,1,0:T(8,128)(2,1)S(1)}, u32[]{:S(2)}, u32[]{:S(2)}) collective-permute-start(bf16[1,272,512]{2,1,0:T(8,128)(2,1)} %get-tuple-element.29), channel_id=1, source_target_pairs={{0,1},{1,0},{2,3},{3,2},{4,5},{5,4},{6,7},{7,6},{8,9},{9,8},{10,11... | collective-permute-start | bytes 835592 | tf_op jit(solution)/shard_map/ppermute | solution.py:51
  7.6 25.4 %collective-permute-start.1 = (bf16[1,272,512]{2,1,0:T(8,128)(2,1)}, bf16[1,272,512]{2,1,0:T(8,128)(2,1)S(1)}, u32[]{:S(2)}, u32[]{:S(2)}) collective-permute-start(bf16[1,272,512]{2,1,0:T(8,128)(2,1)} %get-tuple-element.30), channel_id=1, source_target_pairs={{0,2},{1,3},{2,0},{3,1},{4,6},{5,7},{6,4},{7,5},{8,10},{9,11},{10,... | collective-permute-start | bytes 835592 | tf_op jit(solution)/shard_map/ppermute | solution.py:51
  10.2 23.6 %collective-permute-start.2 = (bf16[1,272,512]{2,1,0:T(8,128)(2,1)}, bf16[1,272,512]{2,1,0:T(8,128)(2,1)S(1)}, u32[]{:S(2)}, u32[]{:S(2)}) collective-permute-start(bf16[1,272,512]{2,1,0:T(8,128)(2,1)} %get-tuple-element.31), channel_id=1, source_target_pairs={{0,3},{1,2},{2,1},{3,0},{4,7},{5,6},{6,5},{7,4},{8,11},{9,10},{10,... | collective-permute-start | bytes 835592 | tf_op jit(solution)/shard_map/ppermute | solution.py:51
  14.0 25.3 %collective-permute-start.3 = (bf16[1,64,512]{2,1,0:T(8,128)(2,1)S(1)}, bf16[1,64,512]{2,1,0:T(8,128)(2,1)S(1)}, u32[]{:S(2)}, u32[]{:S(2)}) collective-permute-start(bf16[1,64,512]{2,1,0:T(8,128)(2,1)S(1)} %get-tuple-element.33), channel_id=1, source_target_pairs={{0,1},{1,0},{2,3},{3,2},{4,5},{5,4},{6,7},{7,6},{8,9},{9,8},{10,11... | collective-permute-start | bytes 196616 | tf_op jit(solution)/shard_map/ppermute | solution.py:51
  14.9 24.7 %collective-permute-start.4 = (bf16[1,64,512]{2,1,0:T(8,128)(2,1)S(1)}, bf16[1,64,512]{2,1,0:T(8,128)(2,1)S(1)}, u32[]{:S(2)}, u32[]{:S(2)}) collective-permute-start(bf16[1,64,512]{2,1,0:T(8,128)(2,1)S(1)} %get-tuple-element.34), channel_id=1, source_target_pairs={{0,2},{1,3},{2,0},{3,1},{4,6},{5,7},{6,4},{7,5},{8,10},{9,11},{10,... | collective-permute-start | bytes 196616 | tf_op jit(solution)/shard_map/ppermute | solution.py:51
  20.3 19.3 %collective-permute-start.5 = (bf16[1,64,512]{2,1,0:T(8,128)(2,1)S(1)}, bf16[1,64,512]{2,1,0:T(8,128)(2,1)S(1)}, u32[]{:S(2)}, u32[]{:S(2)}) collective-permute-start(bf16[1,64,512]{2,1,0:T(8,128)(2,1)S(1)} %get-tuple-element.35), channel_id=1, source_target_pairs={{0,3},{1,2},{2,1},{3,0},{4,7},{5,6},{6,5},{7,4},{8,11},{9,10},{10,... | collective-permute-start | bytes 196616 | tf_op jit(solution)/shard_map/ppermute | solution.py:51
  33.0 0.7 copy-start.3
  33.7 0.7 copy-start.7
  34.4 1.0 copy-start.4
  35.4 1.0 copy-start.8
  36.3 3.3 %copy-start.5 = (bf16[1,272,512]{2,1,0:T(8,128)(2,1)S(1)}, bf16[1,272,512]{2,1,0:T(8,128)(2,1)}, u32[]{:S(2)}) copy-start(bf16[1,272,512]{2,1,0:T(8,128)(2,1)} %copy-done.3) | copy-start | bytes 835588
  36.3 3.3 %copy-start.9 = (bf16[1,272,512]{2,1,0:T(8,128)(2,1)S(1)}, bf16[1,272,512]{2,1,0:T(8,128)(2,1)}, u32[]{:S(2)}) copy-start(bf16[1,272,512]{2,1,0:T(8,128)(2,1)} %copy-done.7) | copy-start | bytes 835588
  39.3 3.0 %copy-start.11 = (bf16[1,64,512]{2,1,0:T(8,128)(2,1)}, bf16[1,64,512]{2,1,0:T(8,128)(2,1)S(1)}, u32[]{:S(2)}) copy-start(bf16[1,64,512]{2,1,0:T(8,128)(2,1)S(1)} %collective-permute-done.3.refs_5_) | copy-start | bytes 196612
  39.7 2.6 %copy-start.13 = (bf16[1,64,512]{2,1,0:T(8,128)(2,1)}, bf16[1,64,512]{2,1,0:T(8,128)(2,1)S(1)}, u32[]{:S(2)}) copy-start(bf16[1,64,512]{2,1,0:T(8,128)(2,1)S(1)} %collective-permute-done.4.refs_6_) | copy-start | bytes 196612
  39.7 2.7 %copy-start.15 = (bf16[1,64,512]{2,1,0:T(8,128)(2,1)}, bf16[1,64,512]{2,1,0:T(8,128)(2,1)S(1)}, u32[]{:S(2)}) copy-start(bf16[1,64,512]{2,1,0:T(8,128)(2,1)S(1)} %collective-permute-done.5.refs_7_) | copy-start | bytes 196612
  42.3 17.1 %collective-permute-start.9 = (f32[64,512]{1,0:T(8,128)S(1)}, f32[64,512]{1,0:T(8,128)}, u32[]{:S(2)}, u32[]{:S(2)}) collective-permute-start(f32[64,512]{1,0:T(8,128)S(1)} %guided_part.1), channel_id=1, source_target_pairs={{0,16},{16,0},{1,17},{17,1},{2,18},{18,2},{3,19},{19,3},{4,20},{20... | collective-permute-start | bytes 393224 | tf_op jit(solution)/shard_map/ppermute | solution.py:51
  42.4 6.7 %collective-permute-start.6 = (f32[1]{0:T(128)}, f32[1]{0:T(128)}, u32[]{:S(2)}, u32[]{:S(2)}) collective-permute-start(f32[1]{0:T(128)} %param.14), channel_id=1, source_target_pairs={{0,4},{4,0},{8,12},{12,8},{1,5},{5,1},{9,13},{13,9},{2,6},{6,2},{1... | collective-permute-start | bytes 20 | tf_op jit(solution)/shard_map/ppermute | solution.py:51
  44.0 11.3 %collective-permute-start.8 = (f32[1]{0:T(128)}, f32[1]{0:T(128)}, u32[]{:S(2)}, u32[]{:S(2)}) collective-permute-start(f32[1]{0:T(128)} %param.14), channel_id=1, source_target_pairs={{0,12},{4,8},{8,4},{12,0},{1,13},{5,9},{9,5},{13,1},{2,14},{6,10},... | collective-permute-start | bytes 20 | tf_op jit(solution)/shard_map/ppermute | solution.py:51
  45.4 10.1 %collective-permute-start.7 = (f32[1]{0:T(128)}, f32[1]{0:T(128)}, u32[]{:S(2)}, u32[]{:S(2)}) collective-permute-start(f32[1]{0:T(128)} %param.14), channel_id=1, source_target_pairs={{0,8},{4,12},{8,0},{12,4},{1,9},{5,13},{9,1},{13,5},{2,10},{6,14},... | collective-permute-start | bytes 20 | tf_op jit(solution)/shard_map/ppermute | solution.py:51
  46.0 17.8 %collective-permute-start.15 = (f32[72,128]{1,0:T(8,128)S(1)}, f32[72,128]{1,0:T(8,128)}, u32[]{:S(2)}, u32[]{:S(2)}) collective-permute-start(f32[72,128]{1,0:T(8,128)S(1)} %get-tuple-element.36.refs_4_), channel_id=1, source_target_pairs={{0,3},{1,2},{2,1},{3,0},{4,7},{5,6},{6,5},{7,4},{8,11},{9,10},{10,... | collective-permute-start | bytes 110600 | tf_op jit(solution)/shard_map/ppermute | solution.py:51
  49.1 15.8 %collective-permute-start.14 = (f32[72,128]{1,0:T(8,128)S(1)}, f32[72,128]{1,0:T(8,128)}, u32[]{:S(2)}, u32[]{:S(2)}) collective-permute-start(f32[72,128]{1,0:T(8,128)S(1)} %get-tuple-element.36.refs_4_), channel_id=1, source_target_pairs={{0,2},{1,3},{2,0},{3,1},{4,6},{5,7},{6,4},{7,5},{8,10},{9,11},{10,... | collective-permute-start | bytes 110600 | tf_op jit(solution)/shard_map/ppermute | solution.py:51
  55.3 9.6 %collective-permute-start.13 = (f32[72,128]{1,0:T(8,128)S(1)}, f32[72,128]{1,0:T(8,128)}, u32[]{:S(2)}, u32[]{:S(2)}) collective-permute-start(f32[72,128]{1,0:T(8,128)S(1)} %get-tuple-element.36.refs_4_), channel_id=1, source_target_pairs={{0,1},{1,0},{2,3},{3,2},{4,5},{5,4},{6,7},{7,6},{8,9},{9,8},{10,11... | collective-permute-start | bytes 110600 | tf_op jit(solution)/shard_map/ppermute | solution.py:51
  59.3 16.8 %copy-start.6 = (bf16[1,272,512]{2,1,0:T(8,128)(2,1)S(1)}, bf16[1,272,512]{2,1,0:T(8,128)(2,1)}, u32[]{:S(2)}) copy-start(bf16[1,272,512]{2,1,0:T(8,128)(2,1)} %copy-done.3) | copy-start | bytes 835588
  59.3 16.8 %copy-start.10 = (bf16[1,272,512]{2,1,0:T(8,128)(2,1)S(1)}, bf16[1,272,512]{2,1,0:T(8,128)(2,1)}, u32[]{:S(2)}) copy-start(bf16[1,272,512]{2,1,0:T(8,128)(2,1)} %copy-done.7) | copy-start | bytes 835588
  59.3 16.8 %copy-start.12 = (bf16[1,64,512]{2,1,0:T(8,128)(2,1)S(1)}, bf16[1,64,512]{2,1,0:T(8,128)(2,1)}, u32[]{:S(2)}) copy-start(bf16[1,64,512]{2,1,0:T(8,128)(2,1)} %copy-done.11) | copy-start | bytes 196612
  59.4 16.8 %copy-start.14 = (bf16[1,64,512]{2,1,0:T(8,128)(2,1)S(1)}, bf16[1,64,512]{2,1,0:T(8,128)(2,1)}, u32[]{:S(2)}) copy-start(bf16[1,64,512]{2,1,0:T(8,128)(2,1)} %copy-done.13) | copy-start | bytes 196612
  59.4 16.8 %copy-start.16 = (bf16[1,64,512]{2,1,0:T(8,128)(2,1)S(1)}, bf16[1,64,512]{2,1,0:T(8,128)(2,1)}, u32[]{:S(2)}) copy-start(bf16[1,64,512]{2,1,0:T(8,128)(2,1)} %copy-done.15) | copy-start | bytes 196612
  60.4 6.8 %collective-permute-start.12 = (bf16[64,512]{1,0:T(8,128)(2,1)S(1)}, bf16[64,512]{1,0:T(8,128)(2,1)S(1)}, u32[]{:S(2)}, u32[]{:S(2)}) collective-permute-start(bf16[64,512]{1,0:T(8,128)(2,1)S(1)} %add_convert_fusion.refs_0_), channel_id=1, source_target_pairs={{0,3},{1,2},{2,1},{3,0},{4,7},{5,6},{6,5},{7,4},{8,11},{9,10},{10,... | collective-permute-start | bytes 196616 | tf_op jit(solution)/shard_map/ppermute | solution.py:51
  62.8 6.5 %collective-permute-start.11 = (bf16[64,512]{1,0:T(8,128)(2,1)S(1)}, bf16[64,512]{1,0:T(8,128)(2,1)S(1)}, u32[]{:S(2)}, u32[]{:S(2)}) collective-permute-start(bf16[64,512]{1,0:T(8,128)(2,1)S(1)} %add_convert_fusion.refs_0_), channel_id=1, source_target_pairs={{0,2},{1,3},{2,0},{3,1},{4,6},{5,7},{6,4},{7,5},{8,10},{9,11},{10,... | collective-permute-start | bytes 196616 | tf_op jit(solution)/shard_map/ppermute | solution.py:51
  63.8 5.5 %collective-permute-start.10 = (bf16[64,512]{1,0:T(8,128)(2,1)S(1)}, bf16[64,512]{1,0:T(8,128)(2,1)S(1)}, u32[]{:S(2)}, u32[]{:S(2)}) collective-permute-start(bf16[64,512]{1,0:T(8,128)(2,1)S(1)} %add_convert_fusion.refs_0_), channel_id=1, source_target_pairs={{0,1},{1,0},{2,3},{3,2},{4,5},{5,4},{6,7},{7,6},{8,9},{9,8},{10,11... | collective-permute-start | bytes 196616 | tf_op jit(solution)/shard_map/ppermute | solution.py:51
  71.7 9.7 %collective-permute-start.19 = (bf16[1,64,512]{2,1,0:T(8,128)(2,1)S(1)}, bf16[1,64,512]{2,1,0:T(8,128)(2,1)S(1)}, u32[]{:S(2)}, u32[]{:S(2)}) collective-permute-start(bf16[1,64,512]{2,1,0:T(8,128)(2,1)S(1)} %get-tuple-element.44), channel_id=1, source_target_pairs={{0,1},{1,0},{2,3},{3,2},{4,5},{5,4},{6,7},{7,6},{8,9},{9,8},{10,11... | collective-permute-start | bytes 196616 | tf_op jit(solution)/shard_map/ppermute | solution.py:51
  71.8 9.6 %collective-permute-start.20 = (bf16[1,64,512]{2,1,0:T(8,128)(2,1)S(1)}, bf16[1,64,512]{2,1,0:T(8,128)(2,1)S(1)}, u32[]{:S(2)}, u32[]{:S(2)}) collective-permute-start(bf16[1,64,512]{2,1,0:T(8,128)(2,1)S(1)} %get-tuple-element.45), channel_id=1, source_target_pairs={{0,2},{1,3},{2,0},{3,1},{4,6},{5,7},{6,4},{7,5},{8,10},{9,11},{10,... | collective-permute-start | bytes 196616 | tf_op jit(solution)/shard_map/ppermute | solution.py:51
  74.6 6.8 %collective-permute-start.21 = (bf16[1,64,512]{2,1,0:T(8,128)(2,1)S(1)}, bf16[1,64,512]{2,1,0:T(8,128)(2,1)S(1)}, u32[]{:S(2)}, u32[]{:S(2)}) collective-permute-start(bf16[1,64,512]{2,1,0:T(8,128)(2,1)S(1)} %get-tuple-element.46), channel_id=1, source_target_pairs={{0,3},{1,2},{2,1},{3,0},{4,7},{5,6},{6,5},{7,4},{8,11},{9,10},{10,... | collective-permute-start | bytes 196616 | tf_op jit(solution)/shard_map/ppermute | solution.py:51
  76.2 5.2 %copy-start.2 = (bf16[1,1,128,3,2048]{4,2,3,1,0:T(8,128)(2,1)S(1)}, bf16[1,1,128,3,2048]{4,2,3,1,0:T(8,128)(2,1)}, u32[]{:S(2)}) copy-start(bf16[1,1,128,3,2048]{4,2,3,1,0:T(8,128)(2,1)} %param.8) | copy-start | bytes 4718596
  82.7 1.6 %collective-permute-start.22 = (f32[64,1024]{1,0:T(8,128)S(1)}, f32[64,1024]{1,0:T(8,128)S(1)}, u32[]{:S(2)}, u32[]{:S(2)}) collective-permute-start(f32[64,1024]{1,0:T(8,128)S(1)} %slice.30), channel_id=1, source_target_pairs={{0,16},{16,0},{1,17},{17,1},{2,18},{18,2},{3,19},{19,3},{4,20},{20... | collective-permute-start | bytes 786440 | tf_op jit(solution)/shard_map/ppermute | solution.py:51
  84.4 6.4 %collective-permute-start.23 = (bf16[64,256]{1,0:T(8,128)(2,1)S(1)}, bf16[64,256]{1,0:T(8,128)(2,1)S(1)}, u32[]{:S(2)}, u32[]{:S(2)}) collective-permute-start(bf16[64,256]{1,0:T(8,128)(2,1)S(1)} %get-tuple-element.60), channel_id=1, source_target_pairs={{0,4},{4,0},{8,12},{12,8},{1,5},{5,1},{9,13},{13,9},{2,6},{6,2},{1... | collective-permute-start | bytes 98312 | tf_op jit(solution)/shard_map/ppermute | solution.py:51
  86.0 12.6 %collective-permute-start.16 = (bf16[1,272,512]{2,1,0:T(8,128)(2,1)S(1)}, bf16[1,272,512]{2,1,0:T(8,128)(2,1)S(1)}, u32[]{:S(2)}, u32[]{:S(2)}) collective-permute-start(bf16[1,272,512]{2,1,0:T(8,128)(2,1)S(1)} %get-tuple-element.39), channel_id=1, source_target_pairs={{0,1},{1,0},{2,3},{3,2},{4,5},{5,4},{6,7},{7,6},{8,9},{9,8},{10,11... | collective-permute-start | bytes 835592 | tf_op jit(solution)/shard_map/ppermute | solution.py:51
  86.0 6.4 %collective-permute-start.25 = (bf16[64,256]{1,0:T(8,128)(2,1)S(1)}, bf16[64,256]{1,0:T(8,128)(2,1)S(1)}, u32[]{:S(2)}, u32[]{:S(2)}) collective-permute-start(bf16[64,256]{1,0:T(8,128)(2,1)S(1)} %get-tuple-element.61), channel_id=1, source_target_pairs={{0,12},{4,8},{8,4},{12,0},{1,13},{5,9},{9,5},{13,1},{2,14},{6,10},... | collective-permute-start | bytes 98312 | tf_op jit(solution)/shard_map/ppermute | solution.py:51
  87.5 4.9 %collective-permute-start.24 = (bf16[64,256]{1,0:T(8,128)(2,1)S(1)}, bf16[64,256]{1,0:T(8,128)(2,1)S(1)}, u32[]{:S(2)}, u32[]{:S(2)}) collective-permute-start(bf16[64,256]{1,0:T(8,128)(2,1)S(1)} %get-tuple-element.62), channel_id=1, source_target_pairs={{0,8},{4,12},{8,0},{12,4},{1,9},{5,13},{9,1},{13,5},{2,10},{6,14},... | collective-permute-start | bytes 98312 | tf_op jit(solution)/shard_map/ppermute | solution.py:51
  88.0 23.9 %collective-permute-start.17 = (bf16[1,272,512]{2,1,0:T(8,128)(2,1)S(1)}, bf16[1,272,512]{2,1,0:T(8,128)(2,1)S(1)}, u32[]{:S(2)}, u32[]{:S(2)}) collective-permute-start(bf16[1,272,512]{2,1,0:T(8,128)(2,1)S(1)} %get-tuple-element.40), channel_id=1, source_target_pairs={{0,2},{1,3},{2,0},{3,1},{4,6},{5,7},{6,4},{7,5},{8,10},{9,11},{10,... | collective-permute-start | bytes 835592 | tf_op jit(solution)/shard_map/ppermute | solution.py:51
  90.8 21.1 %collective-permute-start.18 = (bf16[1,272,512]{2,1,0:T(8,128)(2,1)S(1)}, bf16[1,272,512]{2,1,0:T(8,128)(2,1)S(1)}, u32[]{:S(2)}, u32[]{:S(2)}) collective-permute-start(bf16[1,272,512]{2,1,0:T(8,128)(2,1)S(1)} %get-tuple-element.41), channel_id=1, source_target_pairs={{0,3},{1,2},{2,1},{3,0},{4,7},{5,6},{6,5},{7,4},{8,11},{9,10},{10,... | collective-permute-start | bytes 835592 | tf_op jit(solution)/shard_map/ppermute | solution.py:51
  92.4 20.1 %collective-permute-start.28 = (bf16[64,256]{1,0:T(8,128)(2,1)S(1)}, bf16[64,256]{1,0:T(8,128)(2,1)S(1)}, u32[]{:S(2)}, u32[]{:S(2)}) collective-permute-start(bf16[64,256]{1,0:T(8,128)(2,1)S(1)} %fusion.2), channel_id=1, source_target_pairs={{0,3},{1,2},{2,1},{3,0},{4,7},{5,6},{6,5},{7,4},{8,11},{9,10},{10,... | collective-permute-start | bytes 98312 | tf_op jit(solution)/shard_map/ppermute | solution.py:51
  94.7 22.8 %collective-permute-start.27 = (bf16[64,256]{1,0:T(8,128)(2,1)S(1)}, bf16[64,256]{1,0:T(8,128)(2,1)S(1)}, u32[]{:S(2)}, u32[]{:S(2)}) collective-permute-start(bf16[64,256]{1,0:T(8,128)(2,1)S(1)} %fusion.2), channel_id=1, source_target_pairs={{0,2},{1,3},{2,0},{3,1},{4,6},{5,7},{6,4},{7,5},{8,10},{9,11},{10,... | collective-permute-start | bytes 98312 | tf_op jit(solution)/shard_map/ppermute | solution.py:51
  98.6 18.9 %collective-permute-start.26 = (bf16[64,256]{1,0:T(8,128)(2,1)S(1)}, bf16[64,256]{1,0:T(8,128)(2,1)S(1)}, u32[]{:S(2)}, u32[]{:S(2)}) collective-permute-start(bf16[64,256]{1,0:T(8,128)(2,1)S(1)} %fusion.2), channel_id=1, source_target_pairs={{0,1},{1,0},{2,3},{3,2},{4,5},{5,4},{6,7},{7,6},{8,9},{9,8},{10,11... | collective-permute-start | bytes 98312 | tf_op jit(solution)/shard_map/ppermute | solution.py:51
  117.5 4.9 %collective-permute-start.31 = (bf16[64,256]{1,0:T(8,128)(2,1)S(1)}, bf16[64,256]{1,0:T(8,128)(2,1)S(1)}, u32[]{:S(2)}, u32[]{:S(2)}) collective-permute-start(bf16[64,256]{1,0:T(8,128)(2,1)S(1)} %add_convert_fusion.1.refs_0_), channel_id=1, source_target_pairs={{0,12},{4,8},{8,4},{12,0},{1,13},{5,9},{9,5},{13,1},{2,14},{6,10},... | collective-permute-start | bytes 98312 | tf_op jit(solution)/shard_map/ppermute | solution.py:51
  120.0 3.9 %collective-permute-start.30 = (bf16[64,256]{1,0:T(8,128)(2,1)S(1)}, bf16[64,256]{1,0:T(8,128)(2,1)S(1)}, u32[]{:S(2)}, u32[]{:S(2)}) collective-permute-start(bf16[64,256]{1,0:T(8,128)(2,1)S(1)} %add_convert_fusion.1.refs_0_), channel_id=1, source_target_pairs={{0,8},{4,12},{8,0},{12,4},{1,9},{5,13},{9,1},{13,5},{2,10},{6,14},... | collective-permute-start | bytes 98312 | tf_op jit(solution)/shard_map/ppermute | solution.py:51
  120.5 3.9 %collective-permute-start.29 = (bf16[64,256]{1,0:T(8,128)(2,1)S(1)}, bf16[64,256]{1,0:T(8,128)(2,1)S(1)}, u32[]{:S(2)}, u32[]{:S(2)}) collective-permute-start(bf16[64,256]{1,0:T(8,128)(2,1)S(1)} %add_convert_fusion.1.refs_0_), channel_id=1, source_target_pairs={{0,4},{4,0},{8,12},{12,8},{1,5},{5,1},{9,13},{13,9},{2,6},{6,2},{1... | collective-permute-start | bytes 98312 | tf_op jit(solution)/shard_map/ppermute | solution.py:51
  121.2 5.3 %collective-permute-start.32 = (bf16[64,256]{1,0:T(8,128)(2,1)S(1)}, bf16[64,256]{1,0:T(8,128)(2,1)S(1)}, u32[]{:S(2)}, u32[]{:S(2)}) collective-permute-start(bf16[64,256]{1,0:T(8,128)(2,1)S(1)} %add_convert_fusion.1.refs_0_), channel_id=1, source_target_pairs={{0,16},{16,0},{1,17},{17,1},{2,18},{18,2},{3,19},{19,3},{4,20},{20... | collective-permute-start | bytes 98312 | tf_op jit(solution)/shard_map/ppermute | solution.py:51
  122.4 4.0 %collective-permute-start.35 = (bf16[64,256]{1,0:T(8,128)(2,1)S(1)}, bf16[64,256]{1,0:T(8,128)(2,1)S(1)}, u32[]{:S(2)}, u32[]{:S(2)}) collective-permute-start(bf16[64,256]{1,0:T(8,128)(2,1)S(1)} %collective-permute-done.31.refs_3_), channel_id=1, source_target_pairs={{0,16},{16,0},{1,17},{17,1},{2,18},{18,2},{3,19},{19,3},{4,20},{20... | collective-permute-start | bytes 98312 | tf_op jit(solution)/shard_map/ppermute | solution.py:51
  123.9 2.5 %collective-permute-start.34 = (bf16[64,256]{1,0:T(8,128)(2,1)S(1)}, bf16[64,256]{1,0:T(8,128)(2,1)S(1)}, u32[]{:S(2)}, u32[]{:S(2)}) collective-permute-start(bf16[64,256]{1,0:T(8,128)(2,1)S(1)} %collective-permute-done.30.refs_2_), channel_id=1, source_target_pairs={{0,16},{16,0},{1,17},{17,1},{2,18},{18,2},{3,19},{19,3},{4,20},{20... | collective-permute-start | bytes 98312 | tf_op jit(solution)/shard_map/ppermute | solution.py:51
  124.5 2.0 %collective-permute-start.33 = (bf16[64,256]{1,0:T(8,128)(2,1)S(1)}, bf16[64,256]{1,0:T(8,128)(2,1)S(1)}, u32[]{:S(2)}, u32[]{:S(2)}) collective-permute-start(bf16[64,256]{1,0:T(8,128)(2,1)S(1)} %collective-permute-done.29.refs_1_), channel_id=1, source_target_pairs={{0,16},{16,0},{1,17},{17,1},{2,18},{18,2},{3,19},{19,3},{4,20},{20... | collective-permute-start | bytes 98312 | tf_op jit(solution)/shard_map/ppermute | solution.py:51

commit v2 on v0

v2 whole, which is shorter than its diff:
```python
import functools
import math

import jax
import jax.numpy as jnp
from jax import lax
from jax.experimental import pallas as pl
from jax.experimental.pallas import tpu as pltpu
from jax.sharding import PartitionSpec as P

HEADS = 16
HEAD_DIM = 128
SCALE = HEAD_DIM ** (-0.5)
EXP2_SCALE = SCALE * math.log2(math.e)
F32 = jnp.float32
BF16 = jnp.bfloat16
MIB = 1024 * 1024
SMEM = pl.BlockSpec(memory_space=pltpu.SMEM)
ANY = pl.BlockSpec(memory_space=pl.ANY)


def dot(a, b):
    return jnp.dot(a, b, preferred_element_type=F32)


def dot_nt(a, b):
    return lax.dot_general(a, b, (((1,), (1,)), ((), ())), preferred_element_type=F32)


def dot_tn(a, b):
    return lax.dot_general(a, b, (((0,), (0,)), ((), ())), preferred_element_type=F32)


def whole(shape):
    return pl.BlockSpec(shape, lambda *_: (0,) * len(shape))


def at(refs, slot):
    return refs[slot].at[0] if len(refs) > 1 else refs[0].at[slot]


def cols(start, size):
    return pl.ds(pl.multiple_of(start, 128), size)


def tree_sum(terms):
    while len(terms) > 1:
        terms = [terms[k] + terms[k + 1] for k in range(0, len(terms), 2)]
    return terms[0]


def mirror(x, axis, apart):
    count = lax.axis_size(axis)
    return lax.ppermute(x, axis, [(i, i ^ apart) for i in range(count)])


class Sizes:
    def __init__(self, img_rows, txt_rows, features, channels):
        self.parts = lax.axis_size("seq")
        self.images = lax.axis_size("img")
        self.copies = max(1, self.parts // HEADS)
        self.groups = self.parts // self.copies
        self.features = features
        self.ch = channels
        self.width = features // self.groups
        self.heads = self.width // HEAD_DIM
        self.rows = img_rows
        self.txt = txt_rows
        self.sub = img_rows // self.copies
        self.img_keys = self.parts * img_rows
        self.keys = self.img_keys + self.parts * txt_rows
        self.queries = self.parts * self.sub
        self.mirrored = self.parts in (1, 2, 4, 8) and self.copies == 1
        self.lists = self.parts if self.mirrored else 1
        self.each = self.parts // self.lists
        self.at_keys = self.sub
        self.at_values = self.sub + self.rows
        self.at_text = self.sub + 2 * self.rows
        self.at_mixed = self.at_text + 2 * self.txt
        self.folds = self.width // (2 * self.rows)
        self.per_fold = self.ch // max(1, self.folds)
        self.at_squares = self.at_mixed + (self.per_fold if self.folds else 2 * self.ch)
        self.sent_rows = self.at_squares + 16
        self.at_pair = self.sub + self.rows
        self.at_small = self.at_pair + 2 * self.txt
        self.home_rows = self.at_small + self.ch
        block = self.queries
        while block % 256 == 0 and self.keys * block > 600_000:
            block //= 2
        self.q_block = block
        self.q_blocks = self.queries // block
        limit = (16 if self.mirrored else 48) * MIB
        self.params = pltpu.CompilerParams(vmem_limit_bytes=limit)

    def tiles(self):
        edges = list(range(0, self.img_keys, self.rows)) + [self.img_keys, self.keys]
        return list(zip(edges[:-1], edges[1:]))

    def shapes(self, rows):
        shape = (self.each, rows, self.width)
        return [jax.ShapeDtypeStruct(shape, BF16) for _ in range(self.lists)]

    def specs(self, rows):
        return [whole((self.each, rows, self.width)) for _ in range(self.lists)]

    def head_specs(self, rows, index):
        return [
            pl.BlockSpec((self.each, rows, HEAD_DIM), lambda *g: (0, 0, index(*g)))
            for _ in range(self.lists)
        ]

    def base(self):
        place = lax.axis_index("seq")
        return place if self.mirrored else jnp.zeros_like(place)

    def group(self):
        return lax.axis_index("seq") // self.copies


def exchange(size, blocks):
    if size.mirrored:
        return [blocks[0]] + [mirror(blocks[k], "seq", k) for k in range(1, size.parts)]
    return [lax.all_to_all(blocks[0], "seq", split_axis=0, concat_axis=0, tiled=True)]


def branch_weight(guidance):
    return jnp.where(lax.axis_index("cfg") == 0, guidance, 1.0 - guidance)


def pack_kernel(size, rate, slots, text, noise, old, readout, *refs):
    outs = refs[: size.lists]
    held, block, arrived, left = refs[size.lists :]
    incoming = []
    places = []
    for slot in range(size.parts):
        dest = size.base() ^ slot
        place = cols((dest // size.copies) * size.width, size.width)
        places.append(place)
        if size.copies == 1:
            queries = slots.at[0, :, place]
        else:
            first = pl.multiple_of((dest % size.copies) * size.sub, 16)
            queries = slots.at[0, pl.ds(first, size.sub), place]
        ends = (
            (queries, block.at[slot, pl.ds(0, size.sub)]),
            (slots.at[1, :, place], block.at[slot, pl.ds(size.at_keys, size.rows)]),
            (slots.at[2, :, place], block.at[slot, pl.ds(size.at_values, size.rows)]),
        )
        copies = [
            pltpu.make_async_copy(source, target, arrived.at[slot, index])
            for index, (source, target) in enumerate(ends)
        ]
        for copy in copies:
            copy.start()
        incoming.append(copies)
    held[...] = readout[:, cols(size.group() * size.width, size.width)]
    mixed = noise[...] + rate[0] * old[...]
    high = mixed.astype(BF16)
    low = (mixed - high.astype(F32)).astype(BF16)
    squares = jnp.sum(noise[...] * noise[...], axis=(0, 1), keepdims=True)
    near = squares.astype(BF16).astype(F32)
    far = (squares - near).astype(BF16).astype(F32)
    row = lax.broadcasted_iota(jnp.int32, (16, size.width), 0)
    three = jnp.where(row == 0, near, jnp.where(row == 1, far, squares - near - far))
    outgoing = []
    for slot in range(size.parts):
        pair = text[:, :, places[slot]].astype(F32)
        pair = jnp.concatenate([pair[:, 0], pair[:, 1]], axis=0)
        block[slot, size.at_text : size.at_mixed] = pair.astype(BF16)
        if size.folds:
            for fold in range(size.folds):
                part = slice(fold * size.per_fold, (fold + 1) * size.per_fold)
                lane = 2 * fold * size.rows
                block[slot, size.at_mixed : size.at_squares, lane : lane + size.rows] = high[part]
                lane = lane + size.rows
                block[slot, size.at_mixed : size.at_squares, lane : lane + size.rows] = low[part]
        else:
            middle = size.at_mixed + size.ch
            block[slot, size.at_mixed : middle, : size.rows] = high
            block[slot, middle : size.at_squares, : size.rows] = low
        block[slot, size.at_squares :] = three.astype(BF16)
        for copy in incoming[slot]:
            copy.wait()
        outgoing.append(pltpu.make_async_copy(block.at[slot], at(outs, slot), left.at[slot]))
        outgoing[-1].start()
    for copy in outgoing:
        copy.wait()


def pack(size, rate, slots, text, noise, old, readout):
    outs = pl.pallas_call(
        functools.partial(pack_kernel, size),
        in_specs=[SMEM, ANY]
        + [whole(x.shape) for x in (text, noise, old, readout)],
        out_specs=[ANY] * size.lists + [whole((size.ch, size.width))],
        out_shape=size.shapes(size.sent_rows)
        + [jax.ShapeDtypeStruct((size.ch, size.width), BF16)],
        scratch_shapes=[
            pltpu.VMEM((size.parts, size.sent_rows, size.width), BF16),
            pltpu.SemaphoreType.DMA((size.parts, 3)),
            pltpu.SemaphoreType.DMA((size.parts,)),
        ],
        grid=(1,),
        compiler_params=pltpu.CompilerParams(vmem_limit_bytes=60 * MIB),
        name="pack_tokens",
    )(rate, slots, text, noise, old, readout)
    return outs[:-1], outs[-1]


def text_rows(size, blocks, second):
    found = []
    for slot in range(size.parts):
        pair = at(blocks, slot)[size.at_text : size.at_text + 2 * size.txt].astype(F32)
        found.append(pair[size.txt :] if second else pair[: size.txt])
    return jnp.concatenate(found, axis=0).astype(BF16)


def gather_queries(size, blocks, queries):
    for slot in range(size.parts):
        queries[slot * size.sub : (slot + 1) * size.sub] = at(blocks, slot)[: size.sub]


def gather_keys(size, blocks, first, second, keys):
    for slot in range(size.parts):
        part = at(blocks, slot)[first : first + size.rows]
        keys[slot * size.rows : (slot + 1) * size.rows] = part
    keys[size.img_keys :] = text_rows(size, blocks, second)


def folded(x, combine):
    return combine(x.reshape(x.shape[0] // 8, 8, x.shape[1]), axis=0)


def forward_kernel(size, guidance, *refs):
    blocks = refs[: size.lists]
    readout, raised, each, inverse, out, scores, keys, values, queries = refs[size.lists :]
    step, head = pl.program_id(0), pl.program_id(1)
    gather_queries(size, blocks, queries)
    gather_keys(size, blocks, size.at_keys, False, keys)
    gather_keys(size, blocks, size.at_values, True, values)
    query = queries[pl.ds(pl.multiple_of(step * size.q_block, 128), size.q_block), :]
    peaks = []
    for lo, hi in size.tiles():
        tile = dot_nt(keys[lo:hi], query)
        scores[lo:hi] = tile
        peaks.append(folded(tile, jnp.max))
    top = jnp.max(functools.reduce(jnp.maximum, peaks), axis=0, keepdims=True)
    sums = []
    for lo, hi in size.tiles():
        tile = jnp.exp2((scores[lo:hi] - top) * EXP2_SCALE)
        sums.append(folded(tile, jnp.sum))
        raised[0, lo:hi] = tile.astype(BF16)
    inverted = 1.0 / jnp.sum(sum(sums[1:], sums[0]), axis=0, keepdims=True)
    held = readout[:, cols(head * HEAD_DIM, HEAD_DIM)]
    projected = dot_nt(held, values[...]).astype(BF16)
    velocity = dot(projected, raised[0]) * inverted
    each[0] = velocity
    inverse[0] = inverted
    part = velocity * branch_weight(guidance[0])

    @pl.when(head == 0)
    def _():
        out[...] = part

    @pl.when(head > 0)
    def _():
        out[...] += part


def forward(size, guidance, blocks, readout):
    return pl.pallas_call(
        functools.partial(forward_kernel, size),
        grid=(size.q_blocks, size.heads),
        in_specs=[SMEM]
        + size.head_specs(size.sent_rows, lambda b, h: h)
        + [whole(readout.shape)],
        out_specs=[
            pl.BlockSpec((1, size.keys, size.q_block), lambda b, h: (h, 0, b)),
            pl.BlockSpec((1, size.ch, size.q_block), lambda b, h: (h, 0, b)),
            pl.BlockSpec((1, 1, size.q_block), lambda b, h: (h, 0, b)),
            pl.BlockSpec((size.ch, size.q_block), lambda b, h: (0, b)),
        ],
        out_shape=[
            jax.ShapeDtypeStruct((size.heads, size.keys, size.queries), BF16),
            jax.ShapeDtypeStruct((size.heads, size.ch, size.queries), F32),
            jax.ShapeDtypeStruct((size.heads, 1, size.queries), F32),
            jax.ShapeDtypeStruct((size.ch, size.queries), F32),
        ],
        scratch_shapes=[
            pltpu.VMEM((size.keys, size.q_block), F32),
            pltpu.VMEM((size.keys, HEAD_DIM), BF16),
            pltpu.VMEM((size.keys, HEAD_DIM), BF16),
            pltpu.VMEM((size.queries, HEAD_DIM), BF16),
        ],
        compiler_params=size.params,
        name="attention_forward",
    )(guidance, *blocks, readout)


def surrogate_gain(ratio, advantage):
    clipped = jnp.clip(ratio, 0.8, 1.2)
    keep = ratio * advantage <= clipped * advantage
    return jnp.where(keep, -ratio * advantage, jnp.zeros_like(ratio))


def relative_reward(every, own):
    count = len(every)
    mean = sum(every[1:], every[0]) / count
    square = sum([x * x for x in every[1:]], every[0] * every[0]) / count
    spread = jnp.sqrt(jnp.maximum(square - mean * mean, 0.0))
    return (own - mean) / jnp.maximum(spread, 1.0)


def split_mixed(size, block):
    start = size.at_mixed
    if not size.folds:
        both = block[start : size.at_squares, : size.rows].astype(F32)
        return both[: size.ch] + both[size.ch :]
    found = []
    for fold in range(size.folds):
        lane = 2 * fold * size.rows
        near = block[start : size.at_squares, lane : lane + 2 * size.rows].astype(F32)
        found.append(near[:, : size.rows] + near[:, size.rows :])
    return jnp.concatenate(found, axis=0)


def split_squares(size, block):
    three = block[size.at_squares :, : size.rows].astype(F32)
    return three[:1, :1] + three[1:2, :1] + three[2:3, :1]


def velocity_grad(size, rate, guidance, stats, guided_parts, mixed, grad, ratio_out):
    rest = []
    for slot in range(size.parts):
        parts = []
        for apart in range(size.parts):
            other = slot ^ apart
            part = guided_parts[apart][:, other * size.sub : (other + 1) * size.sub]
            parts.append(part.astype(F32))
        rest.append(split_mixed(size, at(mixed, slot)) - rate[0] * tree_sum(parts))
    norm = tree_sum([jnp.sum(x * x, axis=(0, 1), keepdims=True) for x in rest])
    own = lax.axis_index("img")

    def spread(value):
        return jnp.full((1, 1), value, F32)

    every = [spread(stats[k]) for k in range(size.images)]
    advantage = relative_reward(every, spread(stats[own]))
    squares = tree_sum([split_squares(size, at(mixed, slot)) for slot in range(size.parts)])
    ratio = jnp.exp((squares - norm) * (0.5 / (size.queries * size.ch)))
    gain = surrogate_gain(ratio, advantage)
    factor = gain * (rate[0] * branch_weight(guidance[0]))
    for slot in range(size.parts):
        grad[:, slot * size.sub : (slot + 1) * size.sub] = rest[slot] * factor
    ratio_out[...] = ratio


def backward_kernel(size, *refs):
    if size.mirrored:
        rate, guidance, stats = refs[:3]
        guided_parts = refs[3 : 3 + size.parts]
        mixed = refs[3 + size.parts : 3 + size.parts + size.lists]
        refs = refs[3 + size.parts + size.lists :]
    else:
        given, refs = refs[0], refs[1:]
    blocks = refs[: size.lists]
    readout, raised, each, inverse, ratio_out, readout_out = refs[size.lists : size.lists + 6]
    outs = refs[size.lists + 6 : 2 * size.lists + 6]
    grad_ref, scores, keys, values, queries, grad_keys, grad_queries, small = refs[
        2 * size.lists + 6 :
    ]
    head, step = pl.program_id(0), pl.program_id(1)

    @pl.when((head == 0) & (step == 0))
    def _():
        if size.mirrored:
            velocity_grad(
                size, rate, guidance, stats, guided_parts, mixed, grad_ref, ratio_out
            )
        else:
            grad_ref[...] = given[...]
            ratio_out[...] = jnp.zeros(ratio_out.shape, F32)

    @pl.when(step == 0)
    def _():
        gather_queries(size, blocks, queries)
        gather_keys(size, blocks, size.at_keys, False, keys)
        gather_keys(size, blocks, size.at_values, True, values)

    first = pl.multiple_of(step * size.q_block, 128)
    held = readout[:, cols(head * HEAD_DIM, HEAD_DIM)]
    projected = dot_nt(values[...], held).astype(BF16)
    grad = (grad_ref[:, pl.ds(first, size.q_block)] * inverse[0]).astype(BF16)
    delta = jnp.sum(grad.astype(F32) * each[0], axis=0, keepdims=True)
    for lo, hi in size.tiles():
        tile = dot(projected[lo:hi], grad) - delta
        scores[lo:hi] = (raised[0, lo:hi].astype(F32) * tile).astype(BF16)
    key_part = dot(scores[...], queries[pl.ds(first, size.q_block), :]) * SCALE
    query_part = dot_tn(keys[...], scores[...]) * SCALE
    grad_queries[pl.ds(first, size.q_block), :] = query_part.T.astype(BF16)
    small_part = dot_nt(grad, raised[0])
    if size.q_blocks == 1:
        grad_keys[...] = key_part
        small[...] = small_part
    else:

        @pl.when(step == 0)
        def _():
            grad_keys[...] = key_part
            small[...] = small_part

        @pl.when(step > 0)
        def _():
            grad_keys[...] += key_part
            small[...] += small_part

    @pl.when(step == size.q_blocks - 1)
    def _():
        little = small[...].astype(BF16)
        readout_out[...] = dot(little, values[...])
        value_text = dot_tn(little[:, size.img_keys :], held)
        for slot in range(size.parts):
            out = at(outs, slot)
            near = slice(slot * size.rows, (slot + 1) * size.rows)
            out[: size.sub] = grad_queries[slot * size.sub : (slot + 1) * size.sub]
            out[size.sub : size.sub + size.rows] = grad_keys[near].astype(BF16)
            start = size.img_keys + slot * size.txt
            pair = [
                grad_keys[start : start + size.txt],
                value_text[slot * size.txt : (slot + 1) * size.txt],
            ]
            out[size.at_pair : size.at_small] = jnp.concatenate(pair, axis=0).astype(BF16)
            out[size.at_small :] = little[:, near]


def backward(size, given, blocks, readout, saved):
    if size.mirrored:
        rate, guidance, stats, guided = given
        first = [rate, guidance, stats] + guided + list(blocks)
        specs = [SMEM] * 3 + [whole(x.shape) for x in guided]
        mixed = pl.BlockSpec((1, size.sent_rows, size.width), lambda *_: (0, 0, 0))
        specs = specs + [mixed] * size.lists
    else:
        first, specs = [given], [whole(given.shape)]
    raised, each, inverse = saved
    outs = pl.pallas_call(
        functools.partial(backward_kernel, size),
        grid=(size.heads, size.q_blocks),
        in_specs=specs
        + size.head_specs(size.sent_rows, lambda h, b: h)
        + [
            whole(readout.shape),
            pl.BlockSpec((1, size.keys, size.q_block), lambda h, b: (h, 0, b)),
            pl.BlockSpec((1, size.ch, size.q_block), lambda h, b: (h, 0, b)),
            pl.BlockSpec((1, 1, size.q_block), lambda h, b: (h, 0, b)),
        ],
        out_specs=[whole((1, 1)), pl.BlockSpec((size.ch, HEAD_DIM), lambda h, b: (0, h))]
        + size.head_specs(size.home_rows, lambda h, b: h),
        out_shape=[
            jax.ShapeDtypeStruct((1, 1), F32),
            jax.ShapeDtypeStruct((size.ch, size.width), F32),
        ]
        + size.shapes(size.home_rows),
        scratch_shapes=[
            pltpu.VMEM((size.ch, size.queries), F32),
            pltpu.VMEM((size.keys, size.q_block), BF16),
            pltpu.VMEM((size.keys, HEAD_DIM), BF16),
            pltpu.VMEM((size.keys, HEAD_DIM), BF16),
            pltpu.VMEM((size.queries, HEAD_DIM), BF16),
            pltpu.VMEM((size.keys, HEAD_DIM), F32),
            pltpu.VMEM((size.queries, HEAD_DIM), BF16),
            pltpu.VMEM((size.ch, size.keys), F32),
        ],
        compiler_params=size.params,
        name="attention_backward",
    )(*first, *blocks, readout, raised, each, inverse)
    return outs[0], outs[1], outs[2:]


def home_kernel(size, readout, *refs):
    blocks = refs[: size.lists]
    out, text_out = refs[size.lists :]
    for group in range(size.groups):
        start = (size.base() ^ group) * size.width
        place = cols(start, size.width)
        held = [at(blocks, group * size.copies + copy) for copy in range(size.copies)]
        for copy in range(size.copies):
            out[0, copy * size.sub : (copy + 1) * size.sub, place] = held[copy][: size.sub]
        if size.copies == 1:
            rest = held[0][size.sub :]
        else:
            rest = sum([x[size.sub :].astype(F32) for x in held]).astype(BF16)
        out[1, :, place] = rest[: size.rows]
        pair = rest[size.rows : size.rows + 2 * size.txt].astype(F32)
        pair = jnp.stack([pair[: size.txt], pair[size.txt :]], axis=1)
        text_out[:, :, place] = pair.astype(BF16)
        for head in range(size.heads):
            near = cols(start + head * HEAD_DIM, HEAD_DIM)
            little = rest[size.rows + 2 * size.txt :, head * size.rows : (head + 1) * size.rows]
            out[2, :, near] = dot_tn(little, readout[:, near]).astype(BF16)


def home(size, readout, blocks):
    shapes = ((3, size.rows, size.features), (size.txt, 2, size.features))
    return pl.pallas_call(
        functools.partial(home_kernel, size),
        grid=(1,),
        in_specs=[whole(readout.shape)] + size.specs(size.home_rows),
        out_specs=[whole(x) for x in shapes],
        out_shape=[jax.ShapeDtypeStruct(x, BF16) for x in shapes],
        compiler_params=size.params,
        name="home_tokens",
    )(readout, *blocks)


def place_kernel(size, *refs):
    found, out = refs[:-1], refs[-1]
    for slot in range(size.parts):
        place = cols((size.base() ^ slot) * size.width, size.width)
        out[:, place] = found[slot][...].astype(F32)


def sum_readout(size, part):
    sent = (part + mirror(part, "cfg", 1)).astype(BF16)
    held = lax.all_gather(sent, "img", axis=0)
    total = tree_sum([held[k].astype(F32) for k in range(size.images)]).astype(BF16)
    found = [total] + [mirror(total, "seq", k) for k in range(1, size.parts)]
    return pl.pallas_call(
        functools.partial(place_kernel, size),
        grid=(1,),
        in_specs=[whole(x.shape) for x in found],
        out_specs=whole((size.ch, size.features)),
        out_shape=jax.ShapeDtypeStruct((size.ch, size.features), F32),
        compiler_params=size.params,
        name="place_readout_grad",
    )(*found)


def on_device(img_qkv, txt_kv, readout, old_velocity, noise, step_ratio, rewards, guidance):
    features, channels = readout.shape
    size = Sizes(img_qkv.shape[2], txt_kv.shape[2], features, channels)
    place = lax.axis_index("seq")
    own = lax.axis_index("img")
    slots = img_qkv[0, 0].transpose(1, 0, 2)
    wide = readout.T
    strength = guidance.reshape(1)
    extra = (noise[0].T, old_velocity[0].T, wide)
    packed, held = pack(size, step_ratio, slots, txt_kv[0, 0], *extra)
    blocks = exchange(size, packed)

    mine = jnp.arange(size.images) == own
    stats = lax.psum(jnp.where(mine, rewards[0], 0.0), "img")
    stats, blocks = lax.optimization_barrier((stats, blocks))

    *saved, part = forward(size, strength, blocks, held)
    summed = part + mirror(part, "cfg", 1)
    if size.mirrored:
        sent = summed.astype(BF16)
        guided = [sent] + [mirror(sent, "seq", k) for k in range(1, size.parts)]
        given = (step_ratio, strength, stats, guided)
    else:
        copy = place % size.copies
        rate = step_ratio[0]
        chosen = jnp.arange(size.copies).reshape(-1, 1, 1) == copy
        guided = lax.psum(jnp.where(chosen, summed[None], 0.0), "seq")
        guided = lax.dynamic_index_in_dim(guided, copy, 0, False)
        mixed = jax.vmap(lambda block: split_mixed(size, block))(blocks[0])
        near = lax.dynamic_slice_in_dim(mixed, copy * size.sub, size.sub, 2)
        near = near.transpose(1, 0, 2).reshape(channels, size.queries)
        left = near - rate * guided
        norm = lax.psum(jnp.sum(left * left), "seq") / size.groups
        squares = jnp.sum(jax.vmap(lambda block: split_squares(size, block))(blocks[0]))
        every = [stats[k] for k in range(size.images)]
        advantage = relative_reward(every, rewards[0])
        count = size.parts * size.rows * channels
        ratio = jnp.exp((squares - norm) * (0.5 / count))
        gain = surrogate_gain(ratio, advantage)
        given = left * (gain * (rate * branch_weight(guidance)))
    found, readout_part, sent = backward(size, given, blocks, held, saved)
    if size.mirrored:
        ratio = found
    homes = exchange(size, sent)
    if size.mirrored and lax.axis_size("cfg") == 2 and size.images in (1, 2, 4, 8):
        readout_grad = sum_readout(size, readout_part).T
    else:
        full = jnp.zeros((channels, features), F32)
        start = size.group() * size.width
        full = lax.dynamic_update_slice_in_dim(full, readout_part, start, 1)
        readout_grad = lax.psum(full, ("cfg", "img", "seq")).T
    token_grads, text_grads = home(size, wide, homes)
    img_grad = token_grads.transpose(1, 0, 2)[None, None]
    return (img_grad, text_grads[None, None], readout_grad, ratio.reshape(1))


def solution(mesh):
    return jax.shard_map(
        on_device,
        mesh=mesh,
        in_specs=(
            P("cfg", "img", "seq", None, None),
            P("cfg", "img", "seq", None, None),
            P(),
            P("img", "seq", None),
            P("img", "seq", None),
            P("img"),
            P("img"),
            P(),
        ),
        out_specs=(
            P("cfg", "img", "seq", None, None),
            P("cfg", "img", "seq", None, None),
            P(),
            P("img"),
        ),
        check_vma=False,
    )
```

time: 335 us -> 115 us (0.34)
  waiting for transfers between devices: 177 us -> 40.2 us
  blocking collectives: 51.8 us -> 19.1 us
  local copies, waits for them, and re-layouts: 29.1 us -> 1.86 us
  matrix products: 23.2 us -> 0 us
  between operations: 20.8 us -> 2.66 us
  Pallas kernels: 0 us -> 15.8 us
  starting transfers between devices: 25.3 us -> 35.1 us
  other arithmetic: 5.98 us -> 0.08 us
    psum x1 -> x0, waiting for transfers between devices: 120 us -> none  [on_device(): readout_grad = lax.psum(readout_part, ('cfg', 'img', 'seq'))]
    all_to_all x6 -> x0, waiting for transfers between devices: 57 us -> none  [the longest x1 13.2 us: on_device(): lax.all_to_all(key_items, 'seq', split_axis=0, concat_axis=1, tiled=True)]
    ppermute x1 -> x14, waiting for transfers between devices: 0.01 us -> 40.2 us  [mirror(): return lax.ppermute(x, axis, [(i, i ^ apart) for i in range(count)])]
    ppermute x1 -> x14, starting transfers between devices: 0.07 us -> 35.1 us  [mirror(): return lax.ppermute(x, axis, [(i, i ^ apart) for i in range(count)])]
    all_to_all x2 -> x0, blocking collectives: 30.9 us -> none  [the longest x1 16.4 us: on_device(): lax.all_to_all(mixed.reshape(parts, -1, width), 'seq', split_axis=0, conc...]
    all_to_all x6 -> x0, starting transfers between devices: 25.2 us -> none  [the longest x1 6.32 us: on_device(): lax.all_to_all(query_items, 'seq', split_axis=0, concat_axis=1, tiled=True)]
    dot_general x9 -> x0, matrix products: 23.2 us -> none  [the longest x1 6.05 us: one_block(): jnp.einsum('hqk,qhd->khd', grad_scores, block, preferred_element_type=jnp...]
    pallas_call x0 -> x5, Pallas kernels: none -> 15.8 us  [the longest x1 5.96 us: backward(): pl.pallas_call(functools.partial(backward_kernel, size), grid=(size.heads...]
  transfers between devices with their start and end apart: 8 -> 14, of which waited for: 7 -> 8; matrix products, arithmetic and copies ran while one was open for 8% -> 0% of each run, Pallas kernels for 0% -> 1%
where the time goes in v2:
time: 115 us
  waiting for transfers between devices  40.2 us (35%)
  starting transfers between devices  35.1 us (31%)
  blocking collectives  19.1 us (17%)
  Pallas kernels  15.8 us (14%)
  between operations  2.66 us (2%)
  local copies, waits for them, and re-layouts  1.86 us (2%)
    ppermute x14, waiting for transfers between devices, mirror(): return lax.ppermute(x, axis, [(i, i ^ apart) for i in range(count)])  40.2 us
    ppermute x14, starting transfers between devices, mirror(): return lax.ppermute(x, axis, [(i, i ^ apart) for i in range(count)])  35.1 us
    psum x1, blocking collectives, on_device(): stats = lax.psum(jnp.where(mine, rewards[0], 0.0), 'img')  10.1 us
    all_gather x1, blocking collectives, sum_readout(): held = lax.all_gather(sent, 'img', axis=0)  8.97 us
    pallas_call x1, Pallas kernels, backward(): pl.pallas_call(functools.partial(backward_kernel, size), grid=(size.heads...  5.96 us
    pallas_call x1, Pallas kernels, pack(): pl.pallas_call(functools.partial(pack_kernel, size), in_specs=[SMEM, ANY]...  4.07 us
    pallas_call x1, Pallas kernels, forward(): pl.pallas_call(functools.partial(forward_kernel, size), grid=(size.q_bloc...  3.42 us
  transfers between devices with their start and end apart: 14, of which 8 were waited for; matrix products, arithmetic and copies ran while one was open for 0% of the time, Pallas kernels for 1%

profile of v2, /device:TPU:0, one launch (start us, length us, event | category | flops | bytes accessed | tf_op | source)
XLA Modules:
  0.0 114.8 jit_solution(15179004381947522861)
XLA Ops:
  1.3 4.1 %pack_tokens.1 = (bf16[1,448,512]{2,1,0:T(8,128)(2,1)}, bf16[1,448,512]{2,1,0:T(8,128)(2,1)}, bf16[1,448,512]{2,1,0:T(8,128)(2,1)}, bf16[1,448,512]{2,1,0:T(8,128)(2,1)}, bf16[64,512]{1,0:T(8,128)(2,1)}) custom-call(f32[1]{0:T(128)S(6)} %copy.12.rate.refs_0_, bf16[3,128,2048]{2,1,0:T(8,128)(2,1)} %bitcast.24, bf16[8,2,2048]{2,1,0:T(2,128)(2,1)} %bitcast.26, ...), custom_call_target="tpu_custom_call" | custom-call | tf_op jit(solution)/shard_map/pack_tokens/pallas_call | solution.py:191
  5.4 3.1 %collective-permute-start = (bf16[1,448,512]{2,1,0:T(8,128)(2,1)}, bf16[1,448,512]{2,1,0:T(8,128)(2,1)S(1)}, u32[]{:S(2)}, u32[]{:S(2)}) collective-permute-start(bf16[1,448,512]{2,1,0:T(8,128)(2,1)} %get-tuple-element.27), channel_id=1, source_target_pairs={{0,1},{1,0},{2,3},{3,2},{4,5},{5,4},{6,7},{7,6},{8,9},{9,8},{10,11... | collective-permute-start | bytes 1376264 | tf_op jit(solution)/shard_map/ppermute | solution.py:54
  8.4 2.6 %collective-permute-start.1 = (bf16[1,448,512]{2,1,0:T(8,128)(2,1)}, bf16[1,448,512]{2,1,0:T(8,128)(2,1)S(1)}, u32[]{:S(2)}, u32[]{:S(2)}) collective-permute-start(bf16[1,448,512]{2,1,0:T(8,128)(2,1)} %get-tuple-element.28), channel_id=1, source_target_pairs={{0,2},{1,3},{2,0},{3,1},{4,6},{5,7},{6,4},{7,5},{8,10},{9,11},{10,... | collective-permute-start | bytes 1376264 | tf_op jit(solution)/shard_map/ppermute | solution.py:54
  11.0 0.0 collective-permute-start.2
  11.7 10.1 %psum.7.refs_2_ = f32[4]{0:T(128)S(1)} all-reduce(f32[4]{0:T(128)S(1)} %compare_select_fusion), channel_id=1, replica_groups=mesh['cfg'=2,'img'=4,'seq'=4] {'img'}, use_global_device_ids=true, to_apply=%region_0.1 | all-reduce | flops 4 | bytes 32 | tf_op jit(solution)/shard_map/psum | solution.py:552
  22.5 5.8 %collective-permute-done.refs_1_.refs_8_.refs_12_ = bf16[1,448,512]{2,1,0:T(8,128)(2,1)S(1)} collective-permute-done((bf16[1,448,512]{2,1,0:T(8,128)(2,1)}, bf16[1,448,512]{2,1,0:T(8,128)(2,1)S(1)}, u32[]{:S(2)}, u32[]{:S(2)}) %collective-permute-start) | collective-permute-done | bytes 458784 | tf_op jit(solution)/shard_map/ppermute | solution.py:54
  28.2 14.4 %collective-permute-done.1.refs_2_.refs_9_.refs_13_ = bf16[1,448,512]{2,1,0:T(8,128)(2,1)S(1)} collective-permute-done((bf16[1,448,512]{2,1,0:T(8,128)(2,1)}, bf16[1,448,512]{2,1,0:T(8,128)(2,1)S(1)}, u32[]{:S(2)}, u32[]{:S(2)}) %collective-permute-start.1) | collective-permute-done | bytes 458784 | tf_op jit(solution)/shard_map/ppermute | solution.py:54
  42.7 0.0 collective-permute-done.2.refs_3_.refs_10_.refs_14_
  42.7 0.0 copy-start
  42.7 1.0 copy-done
  43.7 0.0 copy-start.2
  43.7 0.8 copy-done.2
  44.5 3.4 %attention_forward.1 = (bf16[4,544,512]{2,1,0:T(8,128)(2,1)S(1)}, f32[4,64,512]{2,1,0:T(8,128)S(1)}, f32[4,1,512]{2,1,0:T(1,128)S(1)}, f32[64,512]{1,0:T(8,128)S(1)}) custom-call(f32[1]{0:T(128)} %bitcast.20.guidance, bf16[1,448,512]{2,1,0:T(8,128)(2,1)S(1)} %copy-done, bf16[1,448,512]{2,1,0:T(8,128)(2,1)S(1)} %collective-permute-done.refs_1_.refs_8_.refs_12_, ...), custom_call_target="tpu_custom_call" | custom-call | tf_op jit(solution)/shard_map/attention_forward/pallas_call | solution.py:271
  48.0 0.1 collective-permute-start.3
  48.0 1.3 %collective-permute-done.3 = f32[64,512]{1,0:T(8,128)S(1)} collective-permute-done((f32[64,512]{1,0:T(8,128)S(1)}, f32[64,512]{1,0:T(8,128)S(1)}, u32[]{:S(2)}, u32[]{:S(2)}) %collective-permute-start.3) | collective-permute-done | bytes 131104 | tf_op jit(solution)/shard_map/ppermute | solution.py:54
  49.4 2.5 %collective-permute-start.6 = (bf16[64,512]{1,0:T(8,128)(2,1)S(1)}, bf16[64,512]{1,0:T(8,128)(2,1)S(1)}, u32[]{:S(2)}, u32[]{:S(2)}) collective-permute-start(bf16[64,512]{1,0:T(8,128)(2,1)S(1)} %add_convert_fusion.2.refs_3_), channel_id=1, source_target_pairs={{0,3},{1,2},{2,1},{3,0},{4,7},{5,6},{6,5},{7,4},{8,11},{9,10},{10,... | collective-permute-start | bytes 196616 | tf_op jit(solution)/shard_map/ppermute | solution.py:54
  51.9 8.0 %collective-permute-start.5 = (bf16[64,512]{1,0:T(8,128)(2,1)S(1)}, bf16[64,512]{1,0:T(8,128)(2,1)S(1)}, u32[]{:S(2)}, u32[]{:S(2)}) collective-permute-start(bf16[64,512]{1,0:T(8,128)(2,1)S(1)} %add_convert_fusion.2.refs_3_), channel_id=1, source_target_pairs={{0,2},{1,3},{2,0},{3,1},{4,6},{5,7},{6,4},{7,5},{8,10},{9,11},{10,... | collective-permute-start | bytes 196616 | tf_op jit(solution)/shard_map/ppermute | solution.py:54
  59.9 0.1 collective-permute-start.4
  60.0 0.0 collective-permute-done.6.refs_6_
  60.0 4.3 %collective-permute-done.5.refs_5_ = bf16[64,512]{1,0:T(8,128)(2,1)S(1)} collective-permute-done((bf16[64,512]{1,0:T(8,128)(2,1)S(1)}, bf16[64,512]{1,0:T(8,128)(2,1)S(1)}, u32[]{:S(2)}, u32[]{:S(2)}) %collective-permute-start.5) | collective-permute-done | bytes 65568 | tf_op jit(solution)/shard_map/ppermute | solution.py:54
  64.3 0.4 collective-permute-done.4.refs_4_
  64.7 6.0 %attention_backward.1 = (f32[1,1]{1,0:T(1,128)}, f32[64,512]{1,0:T(8,128)S(1)}, bf16[1,336,512]{2,1,0:T(8,128)(2,1)S(1)}, bf16[1,336,512]{2,1,0:T(8,128)(2,1)S(1...) custom-call(f32[1]{0:T(128)S(6)} %copy.12.rate.refs_0_, f32[1]{0:T(128)} %bitcast.21.refs_1_, ...), custom_call_target="tpu_custom_call" | custom-call | tf_op jit(solution)/shard_map/attention_backward/pallas_call | solution.py:446
  70.6 0.0 copy-start.1
  70.6 0.0 collective-permute-start.10
  70.7 0.8 collective-permute-start.7
  71.5 2.6 %collective-permute-start.8 = (bf16[1,336,512]{2,1,0:T(8,128)(2,1)S(1)}, bf16[1,336,512]{2,1,0:T(8,128)(2,1)S(1)}, u32[]{:S(2)}, u32[]{:S(2)}) collective-permute-start(bf16[1,336,512]{2,1,0:T(8,128)(2,1)S(1)} %get-tuple-element.42), channel_id=1, source_target_pairs={{0,2},{1,3},{2,0},{3,1},{4,6},{5,7},{6,4},{7,5},{8,10},{9,11},{10,... | collective-permute-start | bytes 1032200 | tf_op jit(solution)/shard_map/ppermute | solution.py:54
  74.1 1.1 collective-permute-start.9
  75.1 0.0 collective-permute-done.10
  75.1 9.0 %all-gather = bf16[256,512]{1,0:T(8,128)(2,1)S(1)} all-gather(bf16[64,512]{1,0:T(8,128)(2,1)S(1)} %add_convert_fusion.1), channel_id=2, replica_groups=mesh['cfg'=2,'img'=4,'seq'=4] {'img'}, dimensions={0}, use_global_device_ids=true | all-gather | bytes 327680 | tf_op jit(solution)/shard_map/all_gather | solution.py:525
  84.1 2.8 %collective-permute-start.13 = (bf16[64,512]{1,0:T(8,128)(2,1)S(1)}, bf16[64,512]{1,0:T(8,128)(2,1)S(1)}, u32[]{:S(2)}, u32[]{:S(2)}) collective-permute-start(bf16[64,512]{1,0:T(8,128)(2,1)S(1)} %add_convert_fusion.refs_0_), channel_id=1, source_target_pairs={{0,3},{1,2},{2,1},{3,0},{4,7},{5,6},{6,5},{7,4},{8,11},{9,10},{10,... | collective-permute-start | bytes 196616 | tf_op jit(solution)/shard_map/ppermute | solution.py:54
  87.0 0.0 collective-permute-start.12
  87.0 11.7 %collective-permute-done.13.refs_3_ = bf16[64,512]{1,0:T(8,128)(2,1)S(1)} collective-permute-done((bf16[64,512]{1,0:T(8,128)(2,1)S(1)}, bf16[64,512]{1,0:T(8,128)(2,1)S(1)}, u32[]{:S(2)}, u32[]{:S(2)}) %collective-permute-start.13) | collective-permute-done | bytes 65568 | tf_op jit(solution)/shard_map/ppermute | solution.py:54
  98.7 11.4 %collective-permute-start.11 = (bf16[64,512]{1,0:T(8,128)(2,1)S(1)}, bf16[64,512]{1,0:T(8,128)(2,1)S(1)}, u32[]{:S(2)}, u32[]{:S(2)}) collective-permute-start(bf16[64,512]{1,0:T(8,128)(2,1)S(1)} %add_convert_fusion.refs_0_), channel_id=1, source_target_pairs={{0,1},{1,0},{2,3},{3,2},{4,5},{5,4},{6,7},{7,6},{8,9},{9,8},{10,11... | collective-permute-start | bytes 196616 | tf_op jit(solution)/shard_map/ppermute | solution.py:54
  110.2 0.2 collective-permute-done.12.refs_2_
  110.4 2.0 %collective-permute-done.11.refs_1_ = bf16[64,512]{1,0:T(8,128)(2,1)S(1)} collective-permute-done((bf16[64,512]{1,0:T(8,128)(2,1)S(1)}, bf16[64,512]{1,0:T(8,128)(2,1)S(1)}, u32[]{:S(2)}, u32[]{:S(2)}) %collective-permute-start.11) | collective-permute-done | bytes 65568 | tf_op jit(solution)/shard_map/ppermute | solution.py:54
  112.4 0.8 place_readout_grad.1
  113.2 0.0 collective-permute-done.7.refs_1_
  113.3 0.0 collective-permute-done.8.refs_2_
  113.3 0.0 collective-permute-done.9.refs_3_
  113.3 0.0 copy-done.1
  113.3 1.6 %home_tokens.1 = (bf16[3,128,2048]{2,1,0:T(8,128)(2,1)}, bf16[8,2,2048]{2,1,0:T(2,128)(2,1)}) custom-call(bf16[64,2048]{1,0:T(8,128)(2,1)S(1)} %bitcast.23, bf16[1,336,512]{2,1,0:T(8,128)(2,1)S(1)} %get-tuple-element.40.refs_0_, bf16[1,336,512]{2,1,0:T(8,128)(2,1)S(1)} %collective-permute-done.7.refs_1_, ...), custom_call_target="tpu_custom_call" | custom-call | tf_op jit(solution)/shard_map/home_tokens/pallas_call | solution.py:505
  (4 shorter events, 0.1 us)
Async XLA Ops:
  5.4 22.9 %collective-permute-start = (bf16[1,448,512]{2,1,0:T(8,128)(2,1)}, bf16[1,448,512]{2,1,0:T(8,128)(2,1)S(1)}, u32[]{:S(2)}, u32[]{:S(2)}) collective-permute-start(bf16[1,448,512]{2,1,0:T(8,128)(2,1)} %get-tuple-element.27), channel_id=1, source_target_pairs={{0,1},{1,0},{2,3},{3,2},{4,5},{5,4},{6,7},{7,6},{8,9},{9,8},{10,11... | collective-permute-start | bytes 1376264 | tf_op jit(solution)/shard_map/ppermute | solution.py:54
  8.4 34.2 %collective-permute-start.1 = (bf16[1,448,512]{2,1,0:T(8,128)(2,1)}, bf16[1,448,512]{2,1,0:T(8,128)(2,1)S(1)}, u32[]{:S(2)}, u32[]{:S(2)}) collective-permute-start(bf16[1,448,512]{2,1,0:T(8,128)(2,1)} %get-tuple-element.28), channel_id=1, source_target_pairs={{0,2},{1,3},{2,0},{3,1},{4,6},{5,7},{6,4},{7,5},{8,10},{9,11},{10,... | collective-permute-start | bytes 1376264 | tf_op jit(solution)/shard_map/ppermute | solution.py:54
  11.0 31.6 %collective-permute-start.2 = (bf16[1,448,512]{2,1,0:T(8,128)(2,1)}, bf16[1,448,512]{2,1,0:T(8,128)(2,1)S(1)}, u32[]{:S(2)}, u32[]{:S(2)}) collective-permute-start(bf16[1,448,512]{2,1,0:T(8,128)(2,1)} %get-tuple-element.29), channel_id=1, source_target_pairs={{0,3},{1,2},{2,1},{3,0},{4,7},{5,6},{6,5},{7,4},{8,11},{9,10},{10,... | collective-permute-start | bytes 1376264 | tf_op jit(solution)/shard_map/ppermute | solution.py:54
  42.7 1.0 copy-start
  43.7 0.8 copy-start.2
  48.0 1.4 %collective-permute-start.3 = (f32[64,512]{1,0:T(8,128)S(1)}, f32[64,512]{1,0:T(8,128)S(1)}, u32[]{:S(2)}, u32[]{:S(2)}) collective-permute-start(f32[64,512]{1,0:T(8,128)S(1)} %get-tuple-element.36), channel_id=1, source_target_pairs={{0,16},{16,0},{1,17},{17,1},{2,18},{18,2},{3,19},{19,3},{4,20},{20... | collective-permute-start | bytes 393224 | tf_op jit(solution)/shard_map/ppermute | solution.py:54
  49.4 10.6 %collective-permute-start.6 = (bf16[64,512]{1,0:T(8,128)(2,1)S(1)}, bf16[64,512]{1,0:T(8,128)(2,1)S(1)}, u32[]{:S(2)}, u32[]{:S(2)}) collective-permute-start(bf16[64,512]{1,0:T(8,128)(2,1)S(1)} %add_convert_fusion.2.refs_3_), channel_id=1, source_target_pairs={{0,3},{1,2},{2,1},{3,0},{4,7},{5,6},{6,5},{7,4},{8,11},{9,10},{10,... | collective-permute-start | bytes 196616 | tf_op jit(solution)/shard_map/ppermute | solution.py:54
  51.9 12.4 %collective-permute-start.5 = (bf16[64,512]{1,0:T(8,128)(2,1)S(1)}, bf16[64,512]{1,0:T(8,128)(2,1)S(1)}, u32[]{:S(2)}, u32[]{:S(2)}) collective-permute-start(bf16[64,512]{1,0:T(8,128)(2,1)S(1)} %add_convert_fusion.2.refs_3_), channel_id=1, source_target_pairs={{0,2},{1,3},{2,0},{3,1},{4,6},{5,7},{6,4},{7,5},{8,10},{9,11},{10,... | collective-permute-start | bytes 196616 | tf_op jit(solution)/shard_map/ppermute | solution.py:54
  59.9 4.8 %collective-permute-start.4 = (bf16[64,512]{1,0:T(8,128)(2,1)S(1)}, bf16[64,512]{1,0:T(8,128)(2,1)S(1)}, u32[]{:S(2)}, u32[]{:S(2)}) collective-permute-start(bf16[64,512]{1,0:T(8,128)(2,1)S(1)} %add_convert_fusion.2.refs_3_), channel_id=1, source_target_pairs={{0,1},{1,0},{2,3},{3,2},{4,5},{5,4},{6,7},{7,6},{8,9},{9,8},{10,11... | collective-permute-start | bytes 196616 | tf_op jit(solution)/shard_map/ppermute | solution.py:54
  70.6 42.6 %copy-start.1 = (bf16[2048,64]{0,1:T(8,128)(2,1)S(1)}, bf16[2048,64]{0,1:T(8,128)(2,1)}, u32[]{:S(2)}) copy-start(bf16[2048,64]{0,1:T(8,128)(2,1)} %param.10) | copy-start | bytes 786436
  70.6 4.5 %collective-permute-start.10 = (f32[64,512]{1,0:T(8,128)S(1)}, f32[64,512]{1,0:T(8,128)S(1)}, u32[]{:S(2)}, u32[]{:S(2)}) collective-permute-start(f32[64,512]{1,0:T(8,128)S(1)} %get-tuple-element.46), channel_id=1, source_target_pairs={{0,16},{16,0},{1,17},{17,1},{2,18},{18,2},{3,19},{19,3},{4,20},{20... | collective-permute-start | bytes 393224 | tf_op jit(solution)/shard_map/ppermute | solution.py:54
  70.7 42.6 %collective-permute-start.7 = (bf16[1,336,512]{2,1,0:T(8,128)(2,1)S(1)}, bf16[1,336,512]{2,1,0:T(8,128)(2,1)S(1)}, u32[]{:S(2)}, u32[]{:S(2)}) collective-permute-start(bf16[1,336,512]{2,1,0:T(8,128)(2,1)S(1)} %get-tuple-element.41), channel_id=1, source_target_pairs={{0,1},{1,0},{2,3},{3,2},{4,5},{5,4},{6,7},{7,6},{8,9},{9,8},{10,11... | collective-permute-start | bytes 1032200 | tf_op jit(solution)/shard_map/ppermute | solution.py:54
  71.5 41.8 %collective-permute-start.8 = (bf16[1,336,512]{2,1,0:T(8,128)(2,1)S(1)}, bf16[1,336,512]{2,1,0:T(8,128)(2,1)S(1)}, u32[]{:S(2)}, u32[]{:S(2)}) collective-permute-start(bf16[1,336,512]{2,1,0:T(8,128)(2,1)S(1)} %get-tuple-element.42), channel_id=1, source_target_pairs={{0,2},{1,3},{2,0},{3,1},{4,6},{5,7},{6,4},{7,5},{8,10},{9,11},{10,... | collective-permute-start | bytes 1032200 | tf_op jit(solution)/shard_map/ppermute | solution.py:54
  74.1 39.2 %collective-permute-start.9 = (bf16[1,336,512]{2,1,0:T(8,128)(2,1)S(1)}, bf16[1,336,512]{2,1,0:T(8,128)(2,1)S(1)}, u32[]{:S(2)}, u32[]{:S(2)}) collective-permute-start(bf16[1,336,512]{2,1,0:T(8,128)(2,1)S(1)} %get-tuple-element.43), channel_id=1, source_target_pairs={{0,3},{1,2},{2,1},{3,0},{4,7},{5,6},{6,5},{7,4},{8,11},{9,10},{10,... | collective-permute-start | bytes 1032200 | tf_op jit(solution)/shard_map/ppermute | solution.py:54
  84.1 14.6 %collective-permute-start.13 = (bf16[64,512]{1,0:T(8,128)(2,1)S(1)}, bf16[64,512]{1,0:T(8,128)(2,1)S(1)}, u32[]{:S(2)}, u32[]{:S(2)}) collective-permute-start(bf16[64,512]{1,0:T(8,128)(2,1)S(1)} %add_convert_fusion.refs_0_), channel_id=1, source_target_pairs={{0,3},{1,2},{2,1},{3,0},{4,7},{5,6},{6,5},{7,4},{8,11},{9,10},{10,... | collective-permute-start | bytes 196616 | tf_op jit(solution)/shard_map/ppermute | solution.py:54
  87.0 23.4 %collective-permute-start.12 = (bf16[64,512]{1,0:T(8,128)(2,1)S(1)}, bf16[64,512]{1,0:T(8,128)(2,1)S(1)}, u32[]{:S(2)}, u32[]{:S(2)}) collective-permute-start(bf16[64,512]{1,0:T(8,128)(2,1)S(1)} %add_convert_fusion.refs_0_), channel_id=1, source_target_pairs={{0,2},{1,3},{2,0},{3,1},{4,6},{5,7},{6,4},{7,5},{8,10},{9,11},{10,... | collective-permute-start | bytes 196616 | tf_op jit(solution)/shard_map/ppermute | solution.py:54
  98.7 13.7 %collective-permute-start.11 = (bf16[64,512]{1,0:T(8,128)(2,1)S(1)}, bf16[64,512]{1,0:T(8,128)(2,1)S(1)}, u32[]{:S(2)}, u32[]{:S(2)}) collective-permute-start(bf16[64,512]{1,0:T(8,128)(2,1)S(1)} %add_convert_fusion.refs_0_), channel_id=1, source_target_pairs={{0,1},{1,0},{2,3},{3,2},{4,5},{5,4},{6,7},{7,6},{8,9},{9,8},{10,11... | collective-permute-start | bytes 196616 | tf_op jit(solution)/shard_map/ppermute | solution.py:54

commit v3 on v2

--- a/solution.py
+++ b/solution.py
@@ -76,11 +76,7 @@
         self.at_keys = self.sub
         self.at_values = self.sub + self.rows
         self.at_text = self.sub + 2 * self.rows
-        self.at_mixed = self.at_text + 2 * self.txt
-        self.folds = self.width // (2 * self.rows)
-        self.per_fold = self.ch // max(1, self.folds)
-        self.at_squares = self.at_mixed + (self.per_fold if self.folds else 2 * self.ch)
-        self.sent_rows = self.at_squares + 16
+        self.sent_rows = self.at_text + 2 * self.txt
         self.at_pair = self.sub + self.rows
         self.at_small = self.at_pair + 2 * self.txt
         self.home_rows = self.at_small + self.ch
@@ -90,18 +86,23 @@
         self.q_block = block
         self.q_blocks = self.queries // block
         limit = (16 if self.mirrored else 48) * MIB
+        self.late = 1 if self.mirrored and self.heads > 1 else 0
         self.params = pltpu.CompilerParams(vmem_limit_bytes=limit)
 
     def tiles(self):
         edges = list(range(0, self.img_keys, self.rows)) + [self.img_keys, self.keys]
         return list(zip(edges[:-1], edges[1:]))
 
-    def shapes(self, rows):
-        shape = (self.each, rows, self.width)
+    def shapes(self, rows, width):
+        shape = (self.each, rows, width)
         return [jax.ShapeDtypeStruct(shape, BF16) for _ in range(self.lists)]
 
-    def specs(self, rows):
-        return [whole((self.each, rows, self.width)) for _ in range(self.lists)]
+    def specs(self, rows, width):
+        return [whole((self.each, rows, width)) for _ in range(self.lists)]
+
+    def home_widths(self):
+        widths = [(self.heads - self.late) * HEAD_DIM]
+        return widths + [self.late * HEAD_DIM] * (self.late > 0)
 
     def head_specs(self, rows, index):
         return [
@@ -117,9 +118,14 @@
         return lax.axis_index("seq") // self.copies
 
 
+def spread(size, blocks):
+    found = [mirror(blocks[k], "seq", k) for k in reversed(range(1, size.parts))]
+    return [blocks[0]] + found[::-1]
+
+
 def exchange(size, blocks):
     if size.mirrored:
-        return [blocks[0]] + [mirror(blocks[k], "seq", k) for k in range(1, size.parts)]
+        return spread(size, blocks)
     return [lax.all_to_all(blocks[0], "seq", split_axis=0, concat_axis=0, tiled=True)]
 
 
@@ -127,12 +133,12 @@
     return jnp.where(lax.axis_index("cfg") == 0, guidance, 1.0 - guidance)
 
 
-def pack_kernel(size, rate, slots, text, noise, old, readout, *refs):
+def pack_kernel(size, slots, text, *refs):
     outs = refs[: size.lists]
-    held, block, arrived, left = refs[size.lists :]
+    words, block, arrived, left, read = refs[size.lists :]
     incoming = []
     places = []
-    for slot in range(size.parts):
+    for slot in reversed(range(size.parts)):
         dest = size.base() ^ slot
         place = cols((dest // size.copies) * size.width, size.width)
         places.append(place)
@@ -150,36 +156,19 @@
             pltpu.make_async_copy(source, target, arrived.at[slot, index])
             for index, (source, target) in enumerate(ends)
         ]
+        if not incoming:
+            fetch = pltpu.make_async_copy(text, words, read)
+            fetch.start()
         for copy in copies:
             copy.start()
         incoming.append(copies)
-    held[...] = readout[:, cols(size.group() * size.width, size.width)]
-    mixed = noise[...] + rate[0] * old[...]
-    high = mixed.astype(BF16)
-    low = (mixed - high.astype(F32)).astype(BF16)
-    squares = jnp.sum(noise[...] * noise[...], axis=(0, 1), keepdims=True)
-    near = squares.astype(BF16).astype(F32)
-    far = (squares - near).astype(BF16).astype(F32)
-    row = lax.broadcasted_iota(jnp.int32, (16, size.width), 0)
-    three = jnp.where(row == 0, near, jnp.where(row == 1, far, squares - near - far))
+    fetch.wait()
     outgoing = []
-    for slot in range(size.parts):
-        pair = text[:, :, places[slot]].astype(F32)
+    for slot, place, copies in zip(reversed(range(size.parts)), places, incoming):
+        pair = words[:, :, place].astype(F32)
         pair = jnp.concatenate([pair[:, 0], pair[:, 1]], axis=0)
-        block[slot, size.at_text : size.at_mixed] = pair.astype(BF16)
-        if size.folds:
-            for fold in range(size.folds):
-                part = slice(fold * size.per_fold, (fold + 1) * size.per_fold)
-                lane = 2 * fold * size.rows
-                block[slot, size.at_mixed : size.at_squares, lane : lane + size.rows] = high[part]
-                lane = lane + size.rows
-                block[slot, size.at_mixed : size.at_squares, lane : lane + size.rows] = low[part]
-        else:
-            middle = size.at_mixed + size.ch
-            block[slot, size.at_mixed : middle, : size.rows] = high
-            block[slot, middle : size.at_squares, : size.rows] = low
-        block[slot, size.at_squares :] = three.astype(BF16)
-        for copy in incoming[slot]:
+        block[slot, size.at_text :] = pair.astype(BF16)
+        for copy in copies:
             copy.wait()
         outgoing.append(pltpu.make_async_copy(block.at[slot], at(outs, slot), left.at[slot]))
         outgoing[-1].start()
@@ -187,24 +176,22 @@
         copy.wait()
 
 
-def pack(size, rate, slots, text, noise, old, readout):
-    outs = pl.pallas_call(
+def pack(size, slots, text):
+    return pl.pallas_call(
         functools.partial(pack_kernel, size),
-        in_specs=[SMEM, ANY]
-        + [whole(x.shape) for x in (text, noise, old, readout)],
-        out_specs=[ANY] * size.lists + [whole((size.ch, size.width))],
-        out_shape=size.shapes(size.sent_rows)
-        + [jax.ShapeDtypeStruct((size.ch, size.width), BF16)],
+        in_specs=[ANY, ANY],
+        out_specs=[ANY] * size.lists,
+        out_shape=size.shapes(size.sent_rows, size.width),
         scratch_shapes=[
+            pltpu.VMEM(text.shape, BF16),
             pltpu.VMEM((size.parts, size.sent_rows, size.width), BF16),
             pltpu.SemaphoreType.DMA((size.parts, 3)),
             pltpu.SemaphoreType.DMA((size.parts,)),
+            pltpu.SemaphoreType.DMA,
         ],
-        grid=(1,),
         compiler_params=pltpu.CompilerParams(vmem_limit_bytes=60 * MIB),
         name="pack_tokens",
-    )(rate, slots, text, noise, old, readout)
-    return outs[:-1], outs[-1]
+    )(slots, text)
 
 
 def text_rows(size, blocks, second):
@@ -251,7 +238,7 @@
         sums.append(folded(tile, jnp.sum))
         raised[0, lo:hi] = tile.astype(BF16)
     inverted = 1.0 / jnp.sum(sum(sums[1:], sums[0]), axis=0, keepdims=True)
-    held = readout[:, cols(head * HEAD_DIM, HEAD_DIM)]
+    held = readout[:, cols(size.group() * size.width + head * HEAD_DIM, HEAD_DIM)]
     projected = dot_nt(held, values[...]).astype(BF16)
     velocity = dot(projected, raised[0]) * inverted
     each[0] = velocity
@@ -311,43 +298,61 @@
     return (own - mean) / jnp.maximum(spread, 1.0)
 
 
-def split_mixed(size, block):
-    start = size.at_mixed
-    if not size.folds:
-        both = block[start : size.at_squares, : size.rows].astype(F32)
-        return both[: size.ch] + both[size.ch :]
-    found = []
-    for fold in range(size.folds):
-        lane = 2 * fold * size.rows
-        near = block[start : size.at_squares, lane : lane + 2 * size.rows].astype(F32)
-        found.append(near[:, : size.rows] + near[:, size.rows :])
-    return jnp.concatenate(found, axis=0)
-
-
-def split_squares(size, block):
-    three = block[size.at_squares :, : size.rows].astype(F32)
-    return three[:1, :1] + three[1:2, :1] + three[2:3, :1]
-
-
-def velocity_grad(size, rate, guidance, stats, guided_parts, mixed, grad, ratio_out):
-    rest = []
+def combine_kernel(size, rate, part, other, noise, old, out):
+    out[:, : size.queries] = (part[...] + other[...]).astype(BF16)
+    own = part[:, : size.sub] + other[:, : size.sub]
+    own = own - (old[...] + noise[...] * (1.0 / rate[0]))
+    high = own.astype(BF16)
+    low = own - high.astype(F32)
+    squares = jnp.sum(noise[...] * noise[...], axis=(0, 1), keepdims=True)
+    near = squares.astype(BF16).astype(F32)
+    far = (squares - near).astype(BF16).astype(F32)
+    for index, value in enumerate((near, far, squares - near - far)):
+        low = jnp.where(is_place(low.shape, index), value, low)
+    out[:, : size.sub] = high
+    out[:, size.queries :] = low.astype(BF16)
+
+
+def is_place(shape, index):
+    row = lax.broadcasted_iota(jnp.int32, shape, 0)
+    lane = lax.broadcasted_iota(jnp.int32, shape, 1)
+    return (row == 0) & (lane == index)
+
+
+def combine(size, rate, part, other, noise, old):
+    arrays = (part, other, noise, old)
+    shape = (size.ch, size.queries + size.sub)
+    return pl.pallas_call(
+        functools.partial(combine_kernel, size),
+        grid=(1,),
+        in_specs=[SMEM] + [whole(x.shape) for x in arrays],
+        out_specs=whole(shape),
+        out_shape=jax.ShapeDtypeStruct(shape, BF16),
+        compiler_params=size.params,
+        name="combine_branches",
+    )(rate, *arrays)
+
+
+def velocity_grad(size, rate, guidance, stats, gathered, grad, ratio_out):
+    rest, squares = [], []
     for slot in range(size.parts):
         parts = []
         for apart in range(size.parts):
             other = slot ^ apart
-            part = guided_parts[apart][:, other * size.sub : (other + 1) * size.sub]
-            parts.append(part.astype(F32))
-        rest.append(split_mixed(size, at(mixed, slot)) - rate[0] * tree_sum(parts))
+            part = gathered[apart][:, other * size.sub : (other + 1) * size.sub].astype(F32)
+            if apart == slot:
+                low = gathered[apart][:, size.queries :].astype(F32)
+                squares.append(low[:1, :1] + low[:1, 1:2] + low[:1, 2:3])
+                for index in range(3):
+                    low = jnp.where(is_place(low.shape, index), 0.0, low)
+                part = part + low
+            parts.append(part)
+        rest.append(tree_sum(parts) * -rate[0])
     norm = tree_sum([jnp.sum(x * x, axis=(0, 1), keepdims=True) for x in rest])
     own = lax.axis_index("img")
-
-    def spread(value):
-        return jnp.full((1, 1), value, F32)
-
-    every = [spread(stats[k]) for k in range(size.images)]
-    advantage = relative_reward(every, spread(stats[own]))
-    squares = tree_sum([split_squares(size, at(mixed, slot)) for slot in range(size.parts)])
-    ratio = jnp.exp((squares - norm) * (0.5 / (size.queries * size.ch)))
+    every = [jnp.full((1, 1), stats[k], F32) for k in range(size.images)]
+    advantage = relative_reward(every, jnp.full((1, 1), stats[own], F32))
+    ratio = jnp.exp((tree_sum(squares) - norm) * (0.5 / (size.queries * size.ch)))
     gain = surrogate_gain(ratio, advantage)
     factor = gain * (rate[0] * branch_weight(guidance[0]))
     for slot in range(size.parts):
@@ -358,25 +363,23 @@
 def backward_kernel(size, *refs):
     if size.mirrored:
         rate, guidance, stats = refs[:3]
-        guided_parts = refs[3 : 3 + size.parts]
-        mixed = refs[3 + size.parts : 3 + size.parts + size.lists]
-        refs = refs[3 + size.parts + size.lists :]
+        gathered = refs[3 : 3 + size.parts]
+        refs = refs[3 + size.parts :]
     else:
         given, refs = refs[0], refs[1:]
     blocks = refs[: size.lists]
     readout, raised, each, inverse, ratio_out, readout_out = refs[size.lists : size.lists + 6]
-    outs = refs[size.lists + 6 : 2 * size.lists + 6]
-    grad_ref, scores, keys, values, queries, grad_keys, grad_queries, small = refs[
-        2 * size.lists + 6 :
-    ]
+    refs = refs[size.lists + 6 :]
+    outs, refs = refs[: size.lists], refs[size.lists :]
+    if size.late:
+        late_outs, refs = refs[: size.lists], refs[size.lists :]
+    grad_ref, scores, keys, values, queries, grad_keys, grad_queries, small = refs
     head, step = pl.program_id(0), pl.program_id(1)
 
     @pl.when((head == 0) & (step == 0))
     def _():
         if size.mirrored:
-            velocity_grad(
-                size, rate, guidance, stats, guided_parts, mixed, grad_ref, ratio_out
-            )
+            velocity_grad(size, rate, guidance, stats, gathered, grad_ref, ratio_out)
         else:
             grad_ref[...] = given[...]
             ratio_out[...] = jnp.zeros(ratio_out.shape, F32)
@@ -388,7 +391,7 @@
         gather_keys(size, blocks, size.at_values, True, values)
 
     first = pl.multiple_of(step * size.q_block, 128)
-    held = readout[:, cols(head * HEAD_DIM, HEAD_DIM)]
+    held = readout[:, cols(size.group() * size.width + head * HEAD_DIM, HEAD_DIM)]
     projected = dot_nt(values[...], held).astype(BF16)
     grad = (grad_ref[:, pl.ds(first, size.q_block)] * inverse[0]).astype(BF16)
     delta = jnp.sum(grad.astype(F32) * each[0], axis=0, keepdims=True)
@@ -419,30 +422,48 @@
         little = small[...].astype(BF16)
         readout_out[...] = dot(little, values[...])
         value_text = dot_tn(little[:, size.img_keys :], held)
-        for slot in range(size.parts):
-            out = at(outs, slot)
-            near = slice(slot * size.rows, (slot + 1) * size.rows)
-            out[: size.sub] = grad_queries[slot * size.sub : (slot + 1) * size.sub]
-            out[size.sub : size.sub + size.rows] = grad_keys[near].astype(BF16)
-            start = size.img_keys + slot * size.txt
-            pair = [
-                grad_keys[start : start + size.txt],
-                value_text[slot * size.txt : (slot + 1) * size.txt],
-            ]
-            out[size.at_pair : size.at_small] = jnp.concatenate(pair, axis=0).astype(BF16)
-            out[size.at_small :] = little[:, near]
+
+        def write(targets):
+            for slot in range(size.parts):
+                out = at(targets, slot)
+                near = slice(slot * size.rows, (slot + 1) * size.rows)
+                out[: size.sub] = grad_queries[slot * size.sub : (slot + 1) * size.sub]
+                out[size.sub : size.sub + size.rows] = grad_keys[near].astype(BF16)
+                start = size.img_keys + slot * size.txt
+                pair = [
+                    grad_keys[start : start + size.txt],
+                    value_text[slot * size.txt : (slot + 1) * size.txt],
+                ]
+                out[size.at_pair : size.at_small] = jnp.concatenate(pair, axis=0).astype(BF16)
+                out[size.at_small :] = little[:, near]
+
+        if size.late:
+            early = size.heads - size.late
+
+            @pl.when(head < early)
+            def _():
+                write(outs)
+
+            @pl.when(head >= early)
+            def _():
+                write(late_outs)
+
+        else:
+            write(outs)
 
 
 def backward(size, given, blocks, readout, saved):
     if size.mirrored:
-        rate, guidance, stats, guided = given
-        first = [rate, guidance, stats] + guided + list(blocks)
-        specs = [SMEM] * 3 + [whole(x.shape) for x in guided]
-        mixed = pl.BlockSpec((1, size.sent_rows, size.width), lambda *_: (0, 0, 0))
-        specs = specs + [mixed] * size.lists
+        rate, guidance, stats, gathered = given
+        first = [rate, guidance, stats] + gathered
+        specs = [SMEM] * 3 + [whole(x.shape) for x in gathered]
     else:
         first, specs = [given], [whole(given.shape)]
     raised, each, inverse = saved
+    early = size.heads - size.late
+    home_specs = size.head_specs(size.home_rows, lambda h, b: jnp.minimum(h, early - 1))
+    if size.late:
+        home_specs += size.head_specs(size.home_rows, lambda h, b: jnp.maximum(h - early, 0))
     outs = pl.pallas_call(
         functools.partial(backward_kernel, size),
         grid=(size.heads, size.q_blocks),
@@ -455,12 +476,12 @@
             pl.BlockSpec((1, 1, size.q_block), lambda h, b: (h, 0, b)),
         ],
         out_specs=[whole((1, 1)), pl.BlockSpec((size.ch, HEAD_DIM), lambda h, b: (0, h))]
-        + size.head_specs(size.home_rows, lambda h, b: h),
+        + home_specs,
         out_shape=[
             jax.ShapeDtypeStruct((1, 1), F32),
             jax.ShapeDtypeStruct((size.ch, size.width), F32),
         ]
-        + size.shapes(size.home_rows),
+        + [x for width in size.home_widths() for x in size.shapes(size.home_rows, width)],
         scratch_shapes=[
             pltpu.VMEM((size.ch, size.queries), F32),
             pltpu.VMEM((size.keys, size.q_block), BF16),
@@ -474,43 +495,49 @@
         compiler_params=size.params,
         name="attention_backward",
     )(*first, *blocks, readout, raised, each, inverse)
-    return outs[0], outs[1], outs[2:]
+    sent = outs[2:]
+    return outs[0], outs[1], [sent[k : k + size.lists] for k in range(0, len(sent), size.lists)]
 
 
 def home_kernel(size, readout, *refs):
-    blocks = refs[: size.lists]
-    out, text_out = refs[size.lists :]
-    for group in range(size.groups):
-        start = (size.base() ^ group) * size.width
-        place = cols(start, size.width)
-        held = [at(blocks, group * size.copies + copy) for copy in range(size.copies)]
-        for copy in range(size.copies):
-            out[0, copy * size.sub : (copy + 1) * size.sub, place] = held[copy][: size.sub]
-        if size.copies == 1:
-            rest = held[0][size.sub :]
-        else:
-            rest = sum([x[size.sub :].astype(F32) for x in held]).astype(BF16)
-        out[1, :, place] = rest[: size.rows]
-        pair = rest[size.rows : size.rows + 2 * size.txt].astype(F32)
-        pair = jnp.stack([pair[: size.txt], pair[size.txt :]], axis=1)
-        text_out[:, :, place] = pair.astype(BF16)
-        for head in range(size.heads):
-            near = cols(start + head * HEAD_DIM, HEAD_DIM)
-            little = rest[size.rows + 2 * size.txt :, head * size.rows : (head + 1) * size.rows]
-            out[2, :, near] = dot_tn(little, readout[:, near]).astype(BF16)
-
-
-def home(size, readout, blocks):
+    out, text_out = refs[-2:]
+    offset = 0
+    for index, width in enumerate(size.home_widths()):
+        blocks = refs[index * size.lists : (index + 1) * size.lists]
+        for group in range(size.groups):
+            start = (size.base() ^ group) * size.width + offset
+            place = cols(start, width)
+            held = [at(blocks, group * size.copies + copy) for copy in range(size.copies)]
+            for copy in range(size.copies):
+                out[0, copy * size.sub : (copy + 1) * size.sub, place] = held[copy][: size.sub]
+            if size.copies == 1:
+                rest = held[0][size.sub :]
+            else:
+                rest = sum([x[size.sub :].astype(F32) for x in held]).astype(BF16)
+            out[1, :, place] = rest[: size.rows]
+            pair = rest[size.rows : size.rows + 2 * size.txt].astype(F32)
+            pair = jnp.stack([pair[: size.txt], pair[size.txt :]], axis=1)
+            text_out[:, :, place] = pair.astype(BF16)
+            for head in range(width // HEAD_DIM):
+                near = cols(start + head * HEAD_DIM, HEAD_DIM)
+                lanes = slice(head * size.rows, (head + 1) * size.rows)
+                little = rest[size.rows + 2 * size.txt :, lanes]
+                out[2, :, near] = dot_tn(little, readout[:, near]).astype(BF16)
+        offset += width
+
+
+def home(size, readout, homes):
     shapes = ((3, size.rows, size.features), (size.txt, 2, size.features))
+    specs = [x for width in size.home_widths() for x in size.specs(size.home_rows, width)]
     return pl.pallas_call(
         functools.partial(home_kernel, size),
         grid=(1,),
-        in_specs=[whole(readout.shape)] + size.specs(size.home_rows),
+        in_specs=[whole(readout.shape)] + specs,
         out_specs=[whole(x) for x in shapes],
         out_shape=[jax.ShapeDtypeStruct(x, BF16) for x in shapes],
         compiler_params=size.params,
         name="home_tokens",
-    )(readout, *blocks)
+    )(readout, *[x for blocks in homes for x in blocks])
 
 
 def place_kernel(size, *refs):
@@ -523,8 +550,10 @@
 def sum_readout(size, part):
     sent = (part + mirror(part, "cfg", 1)).astype(BF16)
     held = lax.all_gather(sent, "img", axis=0)
-    total = tree_sum([held[k].astype(F32) for k in range(size.images)]).astype(BF16)
-    found = [total] + [mirror(total, "seq", k) for k in range(1, size.parts)]
+    return tree_sum([held[k].astype(F32) for k in range(size.images)]).astype(BF16)
+
+
+def place_readout(size, found):
     return pl.pallas_call(
         functools.partial(place_kernel, size),
         grid=(1,),
@@ -544,50 +573,58 @@
     slots = img_qkv[0, 0].transpose(1, 0, 2)
     wide = readout.T
     strength = guidance.reshape(1)
-    extra = (noise[0].T, old_velocity[0].T, wide)
-    packed, held = pack(size, step_ratio, slots, txt_kv[0, 0], *extra)
-    blocks = exchange(size, packed)
+    noise_wide, old_wide = noise[0].T, old_velocity[0].T
+    blocks = exchange(size, pack(size, slots, txt_kv[0, 0]))
 
     mine = jnp.arange(size.images) == own
     stats = lax.psum(jnp.where(mine, rewards[0], 0.0), "img")
     stats, blocks = lax.optimization_barrier((stats, blocks))
 
-    *saved, part = forward(size, strength, blocks, held)
-    summed = part + mirror(part, "cfg", 1)
+    *saved, part = forward(size, strength, blocks, wide)
+    other = mirror(part, "cfg", 1)
     if size.mirrored:
-        sent = summed.astype(BF16)
-        guided = [sent] + [mirror(sent, "seq", k) for k in range(1, size.parts)]
-        given = (step_ratio, strength, stats, guided)
+        sent = combine(size, step_ratio, part, other, noise_wide, old_wide)
+        gathered = spread(size, [sent] * size.parts)
+        given = (step_ratio, strength, stats, gathered)
     else:
         copy = place % size.copies
         rate = step_ratio[0]
         chosen = jnp.arange(size.copies).reshape(-1, 1, 1) == copy
-        guided = lax.psum(jnp.where(chosen, summed[None], 0.0), "seq")
+        guided = lax.psum(jnp.where(chosen, (part + other)[None], 0.0), "seq")
         guided = lax.dynamic_index_in_dim(guided, copy, 0, False)
-        mixed = jax.vmap(lambda block: split_mixed(size, block))(blocks[0])
+        mixed = lax.all_gather(noise_wide + rate * old_wide, "seq", axis=0)
         near = lax.dynamic_slice_in_dim(mixed, copy * size.sub, size.sub, 2)
         near = near.transpose(1, 0, 2).reshape(channels, size.queries)
         left = near - rate * guided
         norm = lax.psum(jnp.sum(left * left), "seq") / size.groups
-        squares = jnp.sum(jax.vmap(lambda block: split_squares(size, block))(blocks[0]))
+        squares = lax.psum(jnp.sum(noise * noise), "seq")
         every = [stats[k] for k in range(size.images)]
         advantage = relative_reward(every, rewards[0])
         count = size.parts * size.rows * channels
         ratio = jnp.exp((squares - norm) * (0.5 / count))
         gain = surrogate_gain(ratio, advantage)
         given = left * (gain * (rate * branch_weight(guidance)))
-    found, readout_part, sent = backward(size, given, blocks, held, saved)
+    found, readout_part, sent = backward(size, given, blocks, wide, saved)
     if size.mirrored:
         ratio = found
-    homes = exchange(size, sent)
     if size.mirrored and lax.axis_size("cfg") == 2 and size.images in (1, 2, 4, 8):
-        readout_grad = sum_readout(size, readout_part).T
+        homes = [exchange(size, sent[0])]
+        total = sum_readout(size, readout_part)
+        if size.late:
+            total, late = lax.optimization_barrier((total, sent[1]))
+        every = spread(size, [total] * size.parts)
+        if size.late:
+            homes.append(exchange(size, late))
+        token_grads, text_grads = home(size, wide, homes)
+        token_grads, every = lax.optimization_barrier((token_grads, every))
+        readout_grad = place_readout(size, every).T
     else:
+        homes = [exchange(size, x) for x in sent]
+        token_grads, text_grads = home(size, wide, homes)
         full = jnp.zeros((channels, features), F32)
         start = size.group() * size.width
         full = lax.dynamic_update_slice_in_dim(full, readout_part, start, 1)
         readout_grad = lax.psum(full, ("cfg", "img", "seq")).T
-    token_grads, text_grads = home(size, wide, homes)
     img_grad = token_grads.transpose(1, 0, 2)[None, None]
     return (img_grad, text_grads[None, None], readout_grad, ratio.reshape(1))
 

time: 115 us -> 107 us (0.930)
  starting transfers between devices: 35.1 us -> 30.1 us
  waiting for transfers between devices: 40.2 us -> 38.8 us
    ppermute x14 -> x17, starting transfers between devices: 35.1 us -> 30.1 us  [mirror(): return lax.ppermute(x, axis, [(i, i ^ apart) for i in range(count)])]
    ppermute x14 -> x17, waiting for transfers between devices: 40.2 us -> 38.8 us  [mirror(): return lax.ppermute(x, axis, [(i, i ^ apart) for i in range(count)])]
    pallas_call x2 -> x3, Pallas kernels: 4.9 us -> 3.71 us  [the longest x1 2.75 us: pack(): pl.pallas_call(functools.partial(pack_kernel, size), in_specs=[ANY, ANY],...]
  transfers between devices with their start and end apart: 14 -> 17, of which waited for: 8 -> 9; matrix products, arithmetic and copies ran while one was open for 0% -> 0% of each run, Pallas kernels for 1% -> 2%
where the time goes in v3:
time: 107 us
  waiting for transfers between devices  38.8 us (36%)
  starting transfers between devices  30.1 us (28%)
  blocking collectives  19.1 us (18%)
  Pallas kernels  15 us (14%)
  between operations  2.68 us (3%)
    ppermute x17, waiting for transfers between devices, mirror(): return lax.ppermute(x, axis, [(i, i ^ apart) for i in range(count)])  38.8 us
    ppermute x17, starting transfers between devices, mirror(): return lax.ppermute(x, axis, [(i, i ^ apart) for i in range(count)])  30.1 us
    psum x1, blocking collectives, on_device(): stats = lax.psum(jnp.where(mine, rewards[0], 0.0), 'img')  10.1 us
    all_gather x1, blocking collectives, sum_readout(): held = lax.all_gather(sent, 'img', axis=0)  9.01 us
    pallas_call x1, Pallas kernels, backward(): pl.pallas_call(functools.partial(backward_kernel, size), grid=(size.heads...  6.25 us
    pallas_call x1, Pallas kernels, forward(): pl.pallas_call(functools.partial(forward_kernel, size), grid=(size.q_bloc...  3.38 us
    pallas_call x1, Pallas kernels, pack(): pl.pallas_call(functools.partial(pack_kernel, size), in_specs=[ANY, ANY],...  2.75 us
  transfers between devices with their start and end apart: 17, of which 9 were waited for; matrix products, arithmetic and copies ran while one was open for 0% of the time, Pallas kernels for 2%

profile of v3, /device:TPU:0, one launch (start us, length us, event | category | flops | bytes accessed | tf_op | source)
XLA Modules:
  0.0 106.8 jit_solution(17008058910963627775)
XLA Ops:
  0.6 0.0 copy-start
  0.6 0.0 copy-start.3
  0.7 0.0 copy-start.4
  0.7 2.7 %pack_tokens.1 = (bf16[1,400,512]{2,1,0:T(8,128)(2,1)}, bf16[1,400,512]{2,1,0:T(8,128)(2,1)}, bf16[1,400,512]{2,1,0:T(8,128)(2,1)}, bf16[1,400,512]{2,1,0:T(8,128)(2,1)}) custom-call(bf16[3,128,2048]{2,1,0:T(8,128)(2,1)} %bitcast.27, bf16[8,2,2048]{2,1,0:T(2,128)(2,1)} %bitcast.29), custom_call_target="tpu_custom_call" | custom-call | tf_op jit(solution)/shard_map/pack_tokens/pallas_call | solution.py:180
  3.4 3.1 %collective-permute-start = (bf16[1,400,512]{2,1,0:T(8,128)(2,1)}, bf16[1,400,512]{2,1,0:T(8,128)(2,1)S(1)}, u32[]{:S(2)}, u32[]{:S(2)}) collective-permute-start(bf16[1,400,512]{2,1,0:T(8,128)(2,1)} %get-tuple-element.40), channel_id=1, source_target_pairs={{0,1},{1,0},{2,3},{3,2},{4,5},{5,4},{6,7},{7,6},{8,9},{9,8},{10,11... | collective-permute-start | bytes 1228808 | tf_op jit(solution)/shard_map/ppermute | solution.py:54
  6.5 2.6 %collective-permute-start.1 = (bf16[1,400,512]{2,1,0:T(8,128)(2,1)}, bf16[1,400,512]{2,1,0:T(8,128)(2,1)S(1)}, u32[]{:S(2)}, u32[]{:S(2)}) collective-permute-start(bf16[1,400,512]{2,1,0:T(8,128)(2,1)} %get-tuple-element.41), channel_id=1, source_target_pairs={{0,2},{1,3},{2,0},{3,1},{4,6},{5,7},{6,4},{7,5},{8,10},{9,11},{10,... | collective-permute-start | bytes 1228808 | tf_op jit(solution)/shard_map/ppermute | solution.py:54
  9.1 0.0 collective-permute-start.2
  9.8 10.1 %psum.7.refs_2_ = f32[4]{0:T(128)S(1)} all-reduce(f32[4]{0:T(128)S(1)} %compare_select_fusion), channel_id=1, replica_groups=mesh['cfg'=2,'img'=4,'seq'=4] {'img'}, use_global_device_ids=true, to_apply=%region_0.1 | all-reduce | flops 4 | bytes 32 | tf_op jit(solution)/shard_map/psum | solution.py:580
  20.5 3.6 %collective-permute-done.refs_1_.refs_8_ = bf16[1,400,512]{2,1,0:T(8,128)(2,1)S(1)} collective-permute-done((bf16[1,400,512]{2,1,0:T(8,128)(2,1)}, bf16[1,400,512]{2,1,0:T(8,128)(2,1)S(1)}, u32[]{:S(2)}, u32[]{:S(2)}) %collective-permute-start) | collective-permute-done | bytes 409632 | tf_op jit(solution)/shard_map/ppermute | solution.py:54
  24.2 13.4 %collective-permute-done.1.refs_2_.refs_9_ = bf16[1,400,512]{2,1,0:T(8,128)(2,1)S(1)} collective-permute-done((bf16[1,400,512]{2,1,0:T(8,128)(2,1)}, bf16[1,400,512]{2,1,0:T(8,128)(2,1)S(1)}, u32[]{:S(2)}, u32[]{:S(2)}) %collective-permute-start.1) | collective-permute-done | bytes 409632 | tf_op jit(solution)/shard_map/ppermute | solution.py:54
  37.6 0.0 collective-permute-done.2.refs_3_.refs_10_
  37.6 0.0 copy-done
  37.6 0.0 copy-start.1
  37.6 1.0 copy-done.1
  38.6 0.0 copy-start.2
  38.6 3.4 %attention_forward.1 = (bf16[4,544,512]{2,1,0:T(8,128)(2,1)S(1)}, f32[4,64,512]{2,1,0:T(8,128)S(1)}, f32[4,1,512]{2,1,0:T(1,128)S(1)}, f32[64,512]{1,0:T(8,128)S(1)}) custom-call(f32[1]{0:T(128)} %bitcast.20.guidance, bf16[1,400,512]{2,1,0:T(8,128)(2,1)S(1)} %copy-done.1, bf16[1,400,512]{2,1,0:T(8,128)(2,1)S(1)} %collective-permute-done.refs_1_.refs_8_, ...), custom_call_target="tpu_custom_call" | custom-call | tf_op jit(solution)/shard_map/attention_forward/pallas_call | solution.py:258
  42.0 0.1 collective-permute-start.3
  42.7 0.7 collective-permute-done.3.other
  43.4 0.0 copy-done.3
  43.4 0.0 copy-done.4
  43.4 0.1 combine_branches.1.refs_3_
  43.5 2.5 %collective-permute-start.6 = (bf16[64,640]{1,0:T(8,128)(2,1)S(1)}, bf16[64,640]{1,0:T(8,128)(2,1)S(1)}, u32[]{:S(2)}, u32[]{:S(2)}) collective-permute-start(bf16[64,640]{1,0:T(8,128)(2,1)S(1)} %combine_branches.1.refs_3_), channel_id=1, source_target_pairs={{0,3},{1,2},{2,1},{3,0},{4,7},{5,6},{6,5},{7,4},{8,11},{9,10},{10,... | collective-permute-start | bytes 245768 | tf_op jit(solution)/shard_map/ppermute | solution.py:54
  46.0 6.9 %collective-permute-start.5 = (bf16[64,640]{1,0:T(8,128)(2,1)S(1)}, bf16[64,640]{1,0:T(8,128)(2,1)S(1)}, u32[]{:S(2)}, u32[]{:S(2)}) collective-permute-start(bf16[64,640]{1,0:T(8,128)(2,1)S(1)} %combine_branches.1.refs_3_), channel_id=1, source_target_pairs={{0,2},{1,3},{2,0},{3,1},{4,6},{5,7},{6,4},{7,5},{8,10},{9,11},{10,... | collective-permute-start | bytes 245768 | tf_op jit(solution)/shard_map/ppermute | solution.py:54
  53.0 0.1 collective-permute-start.4
  53.1 0.0 collective-permute-done.6.refs_6_
  53.1 5.9 %collective-permute-done.5.refs_5_ = bf16[64,640]{1,0:T(8,128)(2,1)S(1)} collective-permute-done((bf16[64,640]{1,0:T(8,128)(2,1)S(1)}, bf16[64,640]{1,0:T(8,128)(2,1)S(1)}, u32[]{:S(2)}, u32[]{:S(2)}) %collective-permute-start.5) | collective-permute-done | bytes 81952 | tf_op jit(solution)/shard_map/ppermute | solution.py:54
  58.9 0.0 collective-permute-done.4.refs_4_
  58.9 0.0 copy-done.2
  58.9 6.3 %attention_backward.1 = (f32[1,1]{1,0:T(1,128)}, f32[64,512]{1,0:T(8,128)S(1)}, bf16[1,336,384]{2,1,0:T(8,128)(2,1)S(1)}, bf16[1,336,384]{2,1,0:T(8,128)(2,1)S(1...) custom-call(f32[1]{0:T(128)S(6)} %copy.12.rate.refs_0_, ...), custom_call_target="tpu_custom_call" | custom-call | tf_op jit(solution)/shard_map/attention_backward/pallas_call | solution.py:467
  65.2 0.0 collective-permute-start.10
  65.2 0.1 collective-permute-start.7
  65.3 2.9 %collective-permute-start.8 = (bf16[1,336,384]{2,1,0:T(8,128)(2,1)S(1)}, bf16[1,336,384]{2,1,0:T(8,128)(2,1)S(1)}, u32[]{:S(2)}, u32[]{:S(2)}) collective-permute-start(bf16[1,336,384]{2,1,0:T(8,128)(2,1)S(1)} %get-tuple-element.54), channel_id=1, source_target_pairs={{0,2},{1,3},{2,0},{3,1},{4,6},{5,7},{6,4},{7,5},{8,10},{9,11},{10,... | collective-permute-start | bytes 774152 | tf_op jit(solution)/shard_map/ppermute | solution.py:54
  68.2 1.3 %collective-permute-start.9 = (bf16[1,336,384]{2,1,0:T(8,128)(2,1)S(1)}, bf16[1,336,384]{2,1,0:T(8,128)(2,1)S(1)}, u32[]{:S(2)}, u32[]{:S(2)}) collective-permute-start(bf16[1,336,384]{2,1,0:T(8,128)(2,1)S(1)} %get-tuple-element.55), channel_id=1, source_target_pairs={{0,3},{1,2},{2,1},{3,0},{4,7},{5,6},{6,5},{7,4},{8,11},{9,10},{10,... | collective-permute-start | bytes 774152 | tf_op jit(solution)/shard_map/ppermute | solution.py:54
  69.6 0.0 collective-permute-done.10
  69.6 9.0 %all-gather = bf16[256,512]{1,0:T(8,128)(2,1)S(1)} all-gather(bf16[64,512]{1,0:T(8,128)(2,1)S(1)} %add_convert_fusion.1), channel_id=2, replica_groups=mesh['cfg'=2,'img'=4,'seq'=4] {'img'}, dimensions={0}, use_global_device_ids=true | all-gather | bytes 327680 | tf_op jit(solution)/shard_map/all_gather | solution.py:552
  78.7 0.1 collective-permute-start.11
  78.7 3.0 %collective-permute-start.12 = (bf16[1,336,128]{2,1,0:T(8,128)(2,1)S(1)}, bf16[1,336,128]{2,1,0:T(8,128)(2,1)S(1)}, u32[]{:S(2)}, u32[]{:S(2)}) collective-permute-start(bf16[1,336,128]{2,1,0:T(8,128)(2,1)S(1)} %get-tuple-element.63), channel_id=1, source_target_pairs={{0,2},{1,3},{2,0},{3,1},{4,6},{5,7},{6,4},{7,5},{8,10},{9,11},{10,... | collective-permute-start | bytes 258056 | tf_op jit(solution)/shard_map/ppermute | solution.py:54
  81.8 5.5 %collective-permute-done.11.refs_5_ = bf16[1,336,128]{2,1,0:T(8,128)(2,1)S(1)} collective-permute-done((bf16[1,336,128]{2,1,0:T(8,128)(2,1)S(1)}, bf16[1,336,128]{2,1,0:T(8,128)(2,1)S(1)}, u32[]{:S(2)}, u32[]{:S(2)}) %collective-permute-start.11) | collective-permute-done | bytes 86048 | tf_op jit(solution)/shard_map/ppermute | solution.py:54
  87.3 2.9 %collective-permute-start.13 = (bf16[1,336,128]{2,1,0:T(8,128)(2,1)S(1)}, bf16[1,336,128]{2,1,0:T(8,128)(2,1)S(1)}, u32[]{:S(2)}, u32[]{:S(2)}) collective-permute-start(bf16[1,336,128]{2,1,0:T(8,128)(2,1)S(1)} %get-tuple-element.64), channel_id=1, source_target_pairs={{0,3},{1,2},{2,1},{3,0},{4,7},{5,6},{6,5},{7,4},{8,11},{9,10},{10,... | collective-permute-start | bytes 258056 | tf_op jit(solution)/shard_map/ppermute | solution.py:54
  90.2 7.3 %collective-permute-done.12.refs_6_ = bf16[1,336,128]{2,1,0:T(8,128)(2,1)S(1)} collective-permute-done((bf16[1,336,128]{2,1,0:T(8,128)(2,1)S(1)}, bf16[1,336,128]{2,1,0:T(8,128)(2,1)S(1)}, u32[]{:S(2)}, u32[]{:S(2)}) %collective-permute-start.12) | collective-permute-done | bytes 86048 | tf_op jit(solution)/shard_map/ppermute | solution.py:54
  97.5 2.3 %collective-permute-start.16 = (bf16[64,512]{1,0:T(8,128)(2,1)S(1)}, bf16[64,512]{1,0:T(8,128)(2,1)S(1)}, u32[]{:S(2)}, u32[]{:S(2)}) collective-permute-start(bf16[64,512]{1,0:T(8,128)(2,1)S(1)} %add_convert_fusion.refs_0_), channel_id=1, source_target_pairs={{0,3},{1,2},{2,1},{3,0},{4,7},{5,6},{6,5},{7,4},{8,11},{9,10},{10,... | collective-permute-start | bytes 196616 | tf_op jit(solution)/shard_map/ppermute | solution.py:54
  99.8 0.0 collective-permute-done.13.refs_7_
  99.8 0.9 collective-permute-start.15
  100.8 0.0 collective-permute-done.7.refs_1_
  100.8 1.1 %collective-permute-start.14 = (bf16[64,512]{1,0:T(8,128)(2,1)S(1)}, bf16[64,512]{1,0:T(8,128)(2,1)S(1)}, u32[]{:S(2)}, u32[]{:S(2)}) collective-permute-start(bf16[64,512]{1,0:T(8,128)(2,1)S(1)} %add_convert_fusion.refs_0_), channel_id=1, source_target_pairs={{0,1},{1,0},{2,3},{3,2},{4,5},{5,4},{6,7},{7,6},{8,9},{9,8},{10,11... | collective-permute-start | bytes 196616 | tf_op jit(solution)/shard_map/ppermute | solution.py:54
  101.9 0.0 collective-permute-done.8.refs_2_
  101.9 0.0 collective-permute-done.9.refs_3_
  101.9 1.6 %home_tokens.1 = (bf16[3,128,2048]{2,1,0:T(8,128)(2,1)}, bf16[8,2,2048]{2,1,0:T(2,128)(2,1)}) custom-call(bf16[64,2048]{1,0:T(8,128)(2,1)S(1)} %bitcast.24, bf16[1,336,384]{2,1,0:T(8,128)(2,1)S(1)} %get-tuple-element.52.refs_0_, bf16[1,336,384]{2,1,0:T(8,128)(2,1)S(1)} %collective-permute-done.7.refs_1_, ...), custom_call_target="tpu_custom_call" | custom-call | tf_op jit(solution)/shard_map/home_tokens/pallas_call | solution.py:532
  103.5 0.2 collective-permute-done.16.refs_3_
  103.7 2.0 %collective-permute-done.15.refs_2_ = bf16[64,512]{1,0:T(8,128)(2,1)S(1)} collective-permute-done((bf16[64,512]{1,0:T(8,128)(2,1)S(1)}, bf16[64,512]{1,0:T(8,128)(2,1)S(1)}, u32[]{:S(2)}, u32[]{:S(2)}) %collective-permute-start.15) | collective-permute-done | bytes 65568 | tf_op jit(solution)/shard_map/ppermute | solution.py:54
  105.7 0.3 collective-permute-done.14.refs_1_
  105.9 0.8 place_readout_grad.1
  (3 shorter events, 0.1 us)
Async XLA Ops:
  0.6 36.9 %copy-start = (bf16[2048,64]{0,1:T(8,128)(2,1)S(1)}, bf16[2048,64]{0,1:T(8,128)(2,1)}, u32[]{:S(2)}) copy-start(bf16[2048,64]{0,1:T(8,128)(2,1)} %param.10) | copy-start | bytes 786436
  0.6 42.7 %copy-start.3 = (f32[1,128,64]{1,2,0:T(8,128)S(1)}, f32[1,128,64]{1,2,0:T(8,128)}, u32[]{:S(2)}) copy-start(f32[1,128,64]{1,2,0:T(8,128)} %param.12) | copy-start | bytes 98308
  0.7 42.7 %copy-start.4 = (f32[1,128,64]{1,2,0:T(8,128)S(1)}, f32[1,128,64]{1,2,0:T(8,128)}, u32[]{:S(2)}) copy-start(f32[1,128,64]{1,2,0:T(8,128)} %param.11) | copy-start | bytes 98308
  3.4 20.8 %collective-permute-start = (bf16[1,400,512]{2,1,0:T(8,128)(2,1)}, bf16[1,400,512]{2,1,0:T(8,128)(2,1)S(1)}, u32[]{:S(2)}, u32[]{:S(2)}) collective-permute-start(bf16[1,400,512]{2,1,0:T(8,128)(2,1)} %get-tuple-element.40), channel_id=1, source_target_pairs={{0,1},{1,0},{2,3},{3,2},{4,5},{5,4},{6,7},{7,6},{8,9},{9,8},{10,11... | collective-permute-start | bytes 1228808 | tf_op jit(solution)/shard_map/ppermute | solution.py:54
  6.5 31.1 %collective-permute-start.1 = (bf16[1,400,512]{2,1,0:T(8,128)(2,1)}, bf16[1,400,512]{2,1,0:T(8,128)(2,1)S(1)}, u32[]{:S(2)}, u32[]{:S(2)}) collective-permute-start(bf16[1,400,512]{2,1,0:T(8,128)(2,1)} %get-tuple-element.41), channel_id=1, source_target_pairs={{0,2},{1,3},{2,0},{3,1},{4,6},{5,7},{6,4},{7,5},{8,10},{9,11},{10,... | collective-permute-start | bytes 1228808 | tf_op jit(solution)/shard_map/ppermute | solution.py:54
  9.1 28.5 %collective-permute-start.2 = (bf16[1,400,512]{2,1,0:T(8,128)(2,1)}, bf16[1,400,512]{2,1,0:T(8,128)(2,1)S(1)}, u32[]{:S(2)}, u32[]{:S(2)}) collective-permute-start(bf16[1,400,512]{2,1,0:T(8,128)(2,1)} %get-tuple-element.42), channel_id=1, source_target_pairs={{0,3},{1,2},{2,1},{3,0},{4,7},{5,6},{6,5},{7,4},{8,11},{9,10},{10,... | collective-permute-start | bytes 1228808 | tf_op jit(solution)/shard_map/ppermute | solution.py:54
  37.6 1.0 copy-start.1
  38.6 20.4 %copy-start.2 = (bf16[1,400,512]{2,1,0:T(8,128)(2,1)S(1)}, bf16[1,400,512]{2,1,0:T(8,128)(2,1)}, u32[]{:S(2)}) copy-start(bf16[1,400,512]{2,1,0:T(8,128)(2,1)} %get-tuple-element.44.refs_0_.refs_7_) | copy-start | bytes 1228804
  42.0 1.4 %collective-permute-start.3 = (f32[64,512]{1,0:T(8,128)S(1)}, f32[64,512]{1,0:T(8,128)S(1)}, u32[]{:S(2)}, u32[]{:S(2)}) collective-permute-start(f32[64,512]{1,0:T(8,128)S(1)} %get-tuple-element.48.part), channel_id=1, source_target_pairs={{0,16},{16,0},{1,17},{17,1},{2,18},{18,2},{3,19},{19,3},{4,20},{20... | collective-permute-start | bytes 393224 | tf_op jit(solution)/shard_map/ppermute | solution.py:54
  43.5 9.6 %collective-permute-start.6 = (bf16[64,640]{1,0:T(8,128)(2,1)S(1)}, bf16[64,640]{1,0:T(8,128)(2,1)S(1)}, u32[]{:S(2)}, u32[]{:S(2)}) collective-permute-start(bf16[64,640]{1,0:T(8,128)(2,1)S(1)} %combine_branches.1.refs_3_), channel_id=1, source_target_pairs={{0,3},{1,2},{2,1},{3,0},{4,7},{5,6},{6,5},{7,4},{8,11},{9,10},{10,... | collective-permute-start | bytes 245768 | tf_op jit(solution)/shard_map/ppermute | solution.py:54
  46.0 12.9 %collective-permute-start.5 = (bf16[64,640]{1,0:T(8,128)(2,1)S(1)}, bf16[64,640]{1,0:T(8,128)(2,1)S(1)}, u32[]{:S(2)}, u32[]{:S(2)}) collective-permute-start(bf16[64,640]{1,0:T(8,128)(2,1)S(1)} %combine_branches.1.refs_3_), channel_id=1, source_target_pairs={{0,2},{1,3},{2,0},{3,1},{4,6},{5,7},{6,4},{7,5},{8,10},{9,11},{10,... | collective-permute-start | bytes 245768 | tf_op jit(solution)/shard_map/ppermute | solution.py:54
  53.0 6.0 %collective-permute-start.4 = (bf16[64,640]{1,0:T(8,128)(2,1)S(1)}, bf16[64,640]{1,0:T(8,128)(2,1)S(1)}, u32[]{:S(2)}, u32[]{:S(2)}) collective-permute-start(bf16[64,640]{1,0:T(8,128)(2,1)S(1)} %combine_branches.1.refs_3_), channel_id=1, source_target_pairs={{0,1},{1,0},{2,3},{3,2},{4,5},{5,4},{6,7},{7,6},{8,9},{9,8},{10,11... | collective-permute-start | bytes 245768 | tf_op jit(solution)/shard_map/ppermute | solution.py:54
  65.2 4.4 %collective-permute-start.10 = (f32[64,512]{1,0:T(8,128)S(1)}, f32[64,512]{1,0:T(8,128)S(1)}, u32[]{:S(2)}, u32[]{:S(2)}) collective-permute-start(f32[64,512]{1,0:T(8,128)S(1)} %get-tuple-element.56), channel_id=1, source_target_pairs={{0,16},{16,0},{1,17},{17,1},{2,18},{18,2},{3,19},{19,3},{4,20},{20... | collective-permute-start | bytes 393224 | tf_op jit(solution)/shard_map/ppermute | solution.py:54
  65.2 35.6 %collective-permute-start.7 = (bf16[1,336,384]{2,1,0:T(8,128)(2,1)S(1)}, bf16[1,336,384]{2,1,0:T(8,128)(2,1)S(1)}, u32[]{:S(2)}, u32[]{:S(2)}) collective-permute-start(bf16[1,336,384]{2,1,0:T(8,128)(2,1)S(1)} %get-tuple-element.53), channel_id=1, source_target_pairs={{0,1},{1,0},{2,3},{3,2},{4,5},{5,4},{6,7},{7,6},{8,9},{9,8},{10,11... | collective-permute-start | bytes 774152 | tf_op jit(solution)/shard_map/ppermute | solution.py:54
  65.3 36.5 %collective-permute-start.8 = (bf16[1,336,384]{2,1,0:T(8,128)(2,1)S(1)}, bf16[1,336,384]{2,1,0:T(8,128)(2,1)S(1)}, u32[]{:S(2)}, u32[]{:S(2)}) collective-permute-start(bf16[1,336,384]{2,1,0:T(8,128)(2,1)S(1)} %get-tuple-element.54), channel_id=1, source_target_pairs={{0,2},{1,3},{2,0},{3,1},{4,6},{5,7},{6,4},{7,5},{8,10},{9,11},{10,... | collective-permute-start | bytes 774152 | tf_op jit(solution)/shard_map/ppermute | solution.py:54
  68.2 33.6 %collective-permute-start.9 = (bf16[1,336,384]{2,1,0:T(8,128)(2,1)S(1)}, bf16[1,336,384]{2,1,0:T(8,128)(2,1)S(1)}, u32[]{:S(2)}, u32[]{:S(2)}) collective-permute-start(bf16[1,336,384]{2,1,0:T(8,128)(2,1)S(1)} %get-tuple-element.55), channel_id=1, source_target_pairs={{0,3},{1,2},{2,1},{3,0},{4,7},{5,6},{6,5},{7,4},{8,11},{9,10},{10,... | collective-permute-start | bytes 774152 | tf_op jit(solution)/shard_map/ppermute | solution.py:54
  78.7 8.6 %collective-permute-start.11 = (bf16[1,336,128]{2,1,0:T(8,128)(2,1)S(1)}, bf16[1,336,128]{2,1,0:T(8,128)(2,1)S(1)}, u32[]{:S(2)}, u32[]{:S(2)}) collective-permute-start(bf16[1,336,128]{2,1,0:T(8,128)(2,1)S(1)} %get-tuple-element.62), channel_id=1, source_target_pairs={{0,1},{1,0},{2,3},{3,2},{4,5},{5,4},{6,7},{7,6},{8,9},{9,8},{10,11... | collective-permute-start | bytes 258056 | tf_op jit(solution)/shard_map/ppermute | solution.py:54
  78.7 18.7 %collective-permute-start.12 = (bf16[1,336,128]{2,1,0:T(8,128)(2,1)S(1)}, bf16[1,336,128]{2,1,0:T(8,128)(2,1)S(1)}, u32[]{:S(2)}, u32[]{:S(2)}) collective-permute-start(bf16[1,336,128]{2,1,0:T(8,128)(2,1)S(1)} %get-tuple-element.63), channel_id=1, source_target_pairs={{0,2},{1,3},{2,0},{3,1},{4,6},{5,7},{6,4},{7,5},{8,10},{9,11},{10,... | collective-permute-start | bytes 258056 | tf_op jit(solution)/shard_map/ppermute | solution.py:54
  87.3 12.6 %collective-permute-start.13 = (bf16[1,336,128]{2,1,0:T(8,128)(2,1)S(1)}, bf16[1,336,128]{2,1,0:T(8,128)(2,1)S(1)}, u32[]{:S(2)}, u32[]{:S(2)}) collective-permute-start(bf16[1,336,128]{2,1,0:T(8,128)(2,1)S(1)} %get-tuple-element.64), channel_id=1, source_target_pairs={{0,3},{1,2},{2,1},{3,0},{4,7},{5,6},{6,5},{7,4},{8,11},{9,10},{10,... | collective-permute-start | bytes 258056 | tf_op jit(solution)/shard_map/ppermute | solution.py:54
  97.5 6.2 %collective-permute-start.16 = (bf16[64,512]{1,0:T(8,128)(2,1)S(1)}, bf16[64,512]{1,0:T(8,128)(2,1)S(1)}, u32[]{:S(2)}, u32[]{:S(2)}) collective-permute-start(bf16[64,512]{1,0:T(8,128)(2,1)S(1)} %add_convert_fusion.refs_0_), channel_id=1, source_target_pairs={{0,3},{1,2},{2,1},{3,0},{4,7},{5,6},{6,5},{7,4},{8,11},{9,10},{10,... | collective-permute-start | bytes 196616 | tf_op jit(solution)/shard_map/ppermute | solution.py:54
  99.8 5.9 %collective-permute-start.15 = (bf16[64,512]{1,0:T(8,128)(2,1)S(1)}, bf16[64,512]{1,0:T(8,128)(2,1)S(1)}, u32[]{:S(2)}, u32[]{:S(2)}) collective-permute-start(bf16[64,512]{1,0:T(8,128)(2,1)S(1)} %add_convert_fusion.refs_0_), channel_id=1, source_target_pairs={{0,2},{1,3},{2,0},{3,1},{4,6},{5,7},{6,4},{7,5},{8,10},{9,11},{10,... | collective-permute-start | bytes 196616 | tf_op jit(solution)/shard_map/ppermute | solution.py:54
  100.8 5.2 %collective-permute-start.14 = (bf16[64,512]{1,0:T(8,128)(2,1)S(1)}, bf16[64,512]{1,0:T(8,128)(2,1)S(1)}, u32[]{:S(2)}, u32[]{:S(2)}) collective-permute-start(bf16[64,512]{1,0:T(8,128)(2,1)S(1)} %add_convert_fusion.refs_0_), channel_id=1, source_target_pairs={{0,1},{1,0},{2,3},{3,2},{4,5},{5,4},{6,7},{7,6},{8,9},{9,8},{10,11... | collective-permute-start | bytes 196616 | tf_op jit(solution)/shard_map/ppermute | solution.py:54

commit v4 on v3

--- a/solution.py
+++ b/solution.py
@@ -70,7 +70,9 @@
         self.img_keys = self.parts * img_rows
         self.keys = self.img_keys + self.parts * txt_rows
         self.queries = self.parts * self.sub
-        self.mirrored = self.parts in (1, 2, 4, 8) and self.copies == 1
+        power = self.images & (self.images - 1) == 0
+        self.mirrored = self.parts in (2, 4, 8) and self.copies == 1
+        self.mirrored = self.mirrored and self.heads > 1 and power and lax.axis_size("cfg") == 2
         self.lists = self.parts if self.mirrored else 1
         self.each = self.parts // self.lists
         self.at_keys = self.sub
@@ -86,7 +88,8 @@
         self.q_block = block
         self.q_blocks = self.queries // block
         limit = (16 if self.mirrored else 48) * MIB
-        self.late = 1 if self.mirrored and self.heads > 1 else 0
+        self.halves = 2 if self.mirrored else 1
+        self.late = 1 if self.mirrored else 0
         self.params = pltpu.CompilerParams(vmem_limit_bytes=limit)
 
     def tiles(self):
@@ -133,12 +136,13 @@
     return jnp.where(lax.axis_index("cfg") == 0, guidance, 1.0 - guidance)
 
 
-def pack_kernel(size, slots, text, *refs):
-    outs = refs[: size.lists]
-    words, block, arrived, left, read = refs[size.lists :]
+def pack_kernel(size, which, slots, text, *refs):
+    count = len(which) if size.mirrored else 1
+    outs = refs[:count]
+    words, block, arrived, left, read = refs[count:]
     incoming = []
     places = []
-    for slot in reversed(range(size.parts)):
+    for spot, slot in enumerate(which):
         dest = size.base() ^ slot
         place = cols((dest // size.copies) * size.width, size.width)
         places.append(place)
@@ -148,12 +152,12 @@
             first = pl.multiple_of((dest % size.copies) * size.sub, 16)
             queries = slots.at[0, pl.ds(first, size.sub), place]
         ends = (
-            (queries, block.at[slot, pl.ds(0, size.sub)]),
-            (slots.at[1, :, place], block.at[slot, pl.ds(size.at_keys, size.rows)]),
-            (slots.at[2, :, place], block.at[slot, pl.ds(size.at_values, size.rows)]),
+            (queries, block.at[spot, pl.ds(0, size.sub)]),
+            (slots.at[1, :, place], block.at[spot, pl.ds(size.at_keys, size.rows)]),
+            (slots.at[2, :, place], block.at[spot, pl.ds(size.at_values, size.rows)]),
         )
         copies = [
-            pltpu.make_async_copy(source, target, arrived.at[slot, index])
+            pltpu.make_async_copy(source, target, arrived.at[spot, index])
             for index, (source, target) in enumerate(ends)
         ]
         if not incoming:
@@ -164,32 +168,35 @@
         incoming.append(copies)
     fetch.wait()
     outgoing = []
-    for slot, place, copies in zip(reversed(range(size.parts)), places, incoming):
+    for spot, (place, copies) in enumerate(zip(places, incoming)):
         pair = words[:, :, place].astype(F32)
         pair = jnp.concatenate([pair[:, 0], pair[:, 1]], axis=0)
-        block[slot, size.at_text :] = pair.astype(BF16)
+        block[spot, size.at_text :] = pair.astype(BF16)
         for copy in copies:
             copy.wait()
-        outgoing.append(pltpu.make_async_copy(block.at[slot], at(outs, slot), left.at[slot]))
+        out = outs[spot].at[0] if size.mirrored else outs[0].at[spot]
+        outgoing.append(pltpu.make_async_copy(block.at[spot], out, left.at[spot]))
         outgoing[-1].start()
     for copy in outgoing:
         copy.wait()
 
 
-def pack(size, slots, text):
+def pack(size, slots, text, which, limit):
+    count = len(which)
+    shapes = size.shapes(size.sent_rows, size.width)[: count if size.mirrored else 1]
     return pl.pallas_call(
-        functools.partial(pack_kernel, size),
+        functools.partial(pack_kernel, size, which),
         in_specs=[ANY, ANY],
-        out_specs=[ANY] * size.lists,
-        out_shape=size.shapes(size.sent_rows, size.width),
+        out_specs=[ANY] * len(shapes),
+        out_shape=shapes,
         scratch_shapes=[
             pltpu.VMEM(text.shape, BF16),
-            pltpu.VMEM((size.parts, size.sent_rows, size.width), BF16),
-            pltpu.SemaphoreType.DMA((size.parts, 3)),
-            pltpu.SemaphoreType.DMA((size.parts,)),
+            pltpu.VMEM((count, size.sent_rows, size.width), BF16),
+            pltpu.SemaphoreType.DMA((count, 3)),
+            pltpu.SemaphoreType.DMA((count,)),
             pltpu.SemaphoreType.DMA,
         ],
-        compiler_params=pltpu.CompilerParams(vmem_limit_bytes=60 * MIB),
+        compiler_params=pltpu.CompilerParams(vmem_limit_bytes=limit),
         name="pack_tokens",
     )(slots, text)
 
@@ -220,7 +227,9 @@
 
 def forward_kernel(size, guidance, *refs):
     blocks = refs[: size.lists]
-    readout, raised, each, inverse, out, scores, keys, values, queries = refs[size.lists :]
+    readout, raised, each, inverse = refs[size.lists : size.lists + 4]
+    outs = refs[size.lists + 4 : size.lists + 4 + size.halves]
+    total, scores, keys, values, queries = refs[size.lists + 4 + size.halves :]
     step, head = pl.program_id(0), pl.program_id(1)
     gather_queries(size, blocks, queries)
     gather_keys(size, blocks, size.at_keys, False, keys)
@@ -247,11 +256,23 @@
 
     @pl.when(head == 0)
     def _():
-        out[...] = part
+        total[...] = part
 
     @pl.when(head > 0)
     def _():
-        out[...] += part
+        total[...] += part
+
+    @pl.when(head == size.heads - 1)
+    def _():
+        for half, out in enumerate(outs):
+            out[...] = total[half_rows(size, half)]
+
+
+def half_rows(size, half):
+    per = size.ch // size.halves
+    if size.halves == 1:
+        return pl.ds(0, per)
+    return pl.ds(pl.multiple_of((lax.axis_index("cfg") ^ half) * per, per), per)
 
 
 def forward(size, guidance, blocks, readout):
@@ -265,15 +286,17 @@
             pl.BlockSpec((1, size.keys, size.q_block), lambda b, h: (h, 0, b)),
             pl.BlockSpec((1, size.ch, size.q_block), lambda b, h: (h, 0, b)),
             pl.BlockSpec((1, 1, size.q_block), lambda b, h: (h, 0, b)),
-            pl.BlockSpec((size.ch, size.q_block), lambda b, h: (0, b)),
-        ],
+        ]
+        + [pl.BlockSpec((size.ch // size.halves, size.q_block), lambda b, h: (0, b))]
+        * size.halves,
         out_shape=[
             jax.ShapeDtypeStruct((size.heads, size.keys, size.queries), BF16),
             jax.ShapeDtypeStruct((size.heads, size.ch, size.queries), F32),
             jax.ShapeDtypeStruct((size.heads, 1, size.queries), F32),
-            jax.ShapeDtypeStruct((size.ch, size.queries), F32),
-        ],
+        ]
+        + [jax.ShapeDtypeStruct((size.ch // size.halves, size.queries), F32)] * size.halves,
         scratch_shapes=[
+            pltpu.VMEM((size.ch, size.q_block), F32),
             pltpu.VMEM((size.keys, size.q_block), F32),
             pltpu.VMEM((size.keys, HEAD_DIM), BF16),
             pltpu.VMEM((size.keys, HEAD_DIM), BF16),
@@ -299,12 +322,13 @@
 
 
 def combine_kernel(size, rate, part, other, noise, old, out):
+    rows = half_rows(size, 0)
     out[:, : size.queries] = (part[...] + other[...]).astype(BF16)
     own = part[:, : size.sub] + other[:, : size.sub]
-    own = own - (old[...] + noise[...] * (1.0 / rate[0]))
+    own = own - (old[rows] + noise[rows] * (1.0 / rate[0]))
     high = own.astype(BF16)
     low = own - high.astype(F32)
-    squares = jnp.sum(noise[...] * noise[...], axis=(0, 1), keepdims=True)
+    squares = jnp.sum(noise[rows] * noise[rows], axis=(0, 1), keepdims=True)
     near = squares.astype(BF16).astype(F32)
     far = (squares - near).astype(BF16).astype(F32)
     for index, value in enumerate((near, far, squares - near - far)):
@@ -321,7 +345,7 @@
 
 def combine(size, rate, part, other, noise, old):
     arrays = (part, other, noise, old)
-    shape = (size.ch, size.queries + size.sub)
+    shape = (size.ch // size.halves, size.queries + size.sub)
     return pl.pallas_call(
         functools.partial(combine_kernel, size),
         grid=(1,),
@@ -333,8 +357,10 @@
     )(rate, *arrays)
 
 
-def velocity_grad(size, rate, guidance, stats, gathered, grad, ratio_out):
-    rest, squares = [], []
+def gather_guided_kernel(size, *refs):
+    gathered, out = refs[:-1], refs[-1]
+    per = size.ch // size.halves
+    squares, norms = [], []
     for slot in range(size.parts):
         parts = []
         for apart in range(size.parts):
@@ -347,24 +373,47 @@
                     low = jnp.where(is_place(low.shape, index), 0.0, low)
                 part = part + low
             parts.append(part)
-        rest.append(tree_sum(parts) * -rate[0])
-    norm = tree_sum([jnp.sum(x * x, axis=(0, 1), keepdims=True) for x in rest])
+        left = tree_sum(parts)
+        norms.append(jnp.sum(left * left, axis=(0, 1), keepdims=True))
+        out[:per, slot * size.sub : (slot + 1) * size.sub] = left
+    row = lax.broadcasted_iota(jnp.int32, (8, size.queries), 0)
+    out[per:] = jnp.where(row == 0, tree_sum(squares), tree_sum(norms))
+
+
+def gather_guided(size, gathered):
+    shape = (size.ch // size.halves + 8, size.queries)
+    return pl.pallas_call(
+        functools.partial(gather_guided_kernel, size),
+        grid=(1,),
+        in_specs=[whole(x.shape) for x in gathered],
+        out_specs=whole(shape),
+        out_shape=jax.ShapeDtypeStruct(shape, F32),
+        compiler_params=size.params,
+        name="gather_guided",
+    )(*gathered)
+
+
+def velocity_grad(size, rate, guidance, stats, moved, grad, ratio_out):
+    per = size.ch // size.halves
+    norm = tree_sum([x[per + 1 : per + 2, :1] for x in moved])
+    squares = tree_sum([x[per : per + 1, :1] for x in moved])
     own = lax.axis_index("img")
     every = [jnp.full((1, 1), stats[k], F32) for k in range(size.images)]
     advantage = relative_reward(every, jnp.full((1, 1), stats[own], F32))
-    ratio = jnp.exp((tree_sum(squares) - norm) * (0.5 / (size.queries * size.ch)))
+    exponent = (squares - norm * (rate[0] * rate[0])) * (0.5 / (size.queries * size.ch))
+    ratio = jnp.exp(exponent)
     gain = surrogate_gain(ratio, advantage)
-    factor = gain * (rate[0] * branch_weight(guidance[0]))
-    for slot in range(size.parts):
-        grad[:, slot * size.sub : (slot + 1) * size.sub] = rest[slot] * factor
+    factor = gain * (-rate[0] * rate[0] * branch_weight(guidance[0]))
+    for half, x in enumerate(moved):
+        grad[half_rows(size, half)] = x[:per] * factor
     ratio_out[...] = ratio
 
 
 def backward_kernel(size, *refs):
     if size.mirrored:
         rate, guidance, stats = refs[:3]
-        gathered = refs[3 : 3 + size.parts]
-        refs = refs[3 + size.parts :]
+        moved = refs[3 : 3 + size.halves]
+        refs = refs[3 + size.halves :]
     else:
         given, refs = refs[0], refs[1:]
     blocks = refs[: size.lists]
@@ -379,7 +428,7 @@
     @pl.when((head == 0) & (step == 0))
     def _():
         if size.mirrored:
-            velocity_grad(size, rate, guidance, stats, gathered, grad_ref, ratio_out)
+            velocity_grad(size, rate, guidance, stats, moved, grad_ref, ratio_out)
         else:
             grad_ref[...] = given[...]
             ratio_out[...] = jnp.zeros(ratio_out.shape, F32)
@@ -454,9 +503,9 @@
 
 def backward(size, given, blocks, readout, saved):
     if size.mirrored:
-        rate, guidance, stats, gathered = given
-        first = [rate, guidance, stats] + gathered
-        specs = [SMEM] * 3 + [whole(x.shape) for x in gathered]
+        rate, guidance, stats, moved = given
+        first = [rate, guidance, stats] + moved
+        specs = [SMEM] * 3 + [whole(x.shape) for x in moved]
     else:
         first, specs = [given], [whole(given.shape)]
     raised, each, inverse = saved
@@ -511,7 +560,7 @@
             for copy in range(size.copies):
                 out[0, copy * size.sub : (copy + 1) * size.sub, place] = held[copy][: size.sub]
             if size.copies == 1:
-                rest = held[0][size.sub :]
+                rest = held[0][size.sub : size.home_rows]
             else:
                 rest = sum([x[size.sub :].astype(F32) for x in held]).astype(BF16)
             out[1, :, place] = rest[: size.rows]
@@ -527,30 +576,57 @@
 
 
 def home(size, readout, homes):
-    shapes = ((3, size.rows, size.features), (size.txt, 2, size.features))
-    specs = [x for width in size.home_widths() for x in size.specs(size.home_rows, width)]
+    shapes = [(3, size.rows, size.features), (size.txt, 2, size.features)]
+    outs = [jax.ShapeDtypeStruct(x, BF16) for x in shapes]
+    specs = [whole(x.shape) for blocks in homes for x in blocks]
     return pl.pallas_call(
         functools.partial(home_kernel, size),
         grid=(1,),
         in_specs=[whole(readout.shape)] + specs,
-        out_specs=[whole(x) for x in shapes],
-        out_shape=[jax.ShapeDtypeStruct(x, BF16) for x in shapes],
+        out_specs=[whole(x.shape) for x in outs],
+        out_shape=outs,
         compiler_params=size.params,
         name="home_tokens",
     )(readout, *[x for blocks in homes for x in blocks])
 
 
-def place_kernel(size, *refs):
-    found, out = refs[:-1], refs[-1]
-    for slot in range(size.parts):
-        place = cols((size.base() ^ slot) * size.width, size.width)
-        out[:, place] = found[slot][...].astype(F32)
-
-
-def sum_readout(size, part):
+def join_readout_kernel(size, held, *refs):
+    blocks, outs = refs[: size.parts], refs[size.parts :]
+    rows = half_rows(size, 0)
+    per = size.ch // size.halves
+    total = tree_sum([held[k, rows].astype(F32) for k in range(size.images)]).astype(BF16)
+    for block, out in zip(blocks, outs):
+        out[0, : size.home_rows] = block[0]
+        for head in range(size.heads):
+            first = size.home_rows + head * per
+            out[0, first : first + per] = total[:, head * HEAD_DIM : (head + 1) * HEAD_DIM]
+
+
+def join_readout(size, part, blocks):
     sent = (part + mirror(part, "cfg", 1)).astype(BF16)
     held = lax.all_gather(sent, "img", axis=0)
-    return tree_sum([held[k].astype(F32) for k in range(size.images)]).astype(BF16)
+    shape = (1, size.home_rows + size.heads * size.ch // size.halves, HEAD_DIM)
+    return pl.pallas_call(
+        functools.partial(join_readout_kernel, size),
+        grid=(1,),
+        in_specs=[whole(held.shape)] + [whole(x.shape) for x in blocks],
+        out_specs=[whole(shape)] * size.parts,
+        out_shape=[jax.ShapeDtypeStruct(shape, BF16)] * size.parts,
+        compiler_params=size.params,
+        name="join_readout_grad",
+    )(held, *blocks)
+
+
+def place_kernel(size, *refs):
+    out = refs[-1]
+    per = size.ch // size.halves
+    for half in range(size.halves):
+        for slot in range(size.parts):
+            found = refs[half * size.parts + slot]
+            for head in range(size.heads):
+                lanes = cols((size.base() ^ slot) * size.width + head * HEAD_DIM, HEAD_DIM)
+                first = size.home_rows + head * per
+                out[half_rows(size, half), lanes] = found[0, first : first + per].astype(F32)
 
 
 def place_readout(size, found):
@@ -574,19 +650,30 @@
     wide = readout.T
     strength = guidance.reshape(1)
     noise_wide, old_wide = noise[0].T, old_velocity[0].T
-    blocks = exchange(size, pack(size, slots, txt_kv[0, 0]))
+    text = txt_kv[0, 0]
+    if size.mirrored:
+        away = list(range(1, size.parts))
+        sent = pack(size, slots, text, away, 60 * MIB)
+        blocks = [mirror(block, "seq", k) for k, block in zip(away, sent)]
+    else:
+        blocks = exchange(size, pack(size, slots, text, list(range(size.parts)), 48 * MIB))
 
     mine = jnp.arange(size.images) == own
     stats = lax.psum(jnp.where(mine, rewards[0], 0.0), "img")
-    stats, blocks = lax.optimization_barrier((stats, blocks))
+    if size.mirrored:
+        stats, near, words = lax.optimization_barrier((stats, slots, text))
+        blocks = list(pack(size, near, words, [0], 16 * MIB)) + blocks
+        blocks = lax.optimization_barrier(blocks)
 
     *saved, part = forward(size, strength, blocks, wide)
-    other = mirror(part, "cfg", 1)
     if size.mirrored:
-        sent = combine(size, step_ratio, part, other, noise_wide, old_wide)
-        gathered = spread(size, [sent] * size.parts)
-        given = (step_ratio, strength, stats, gathered)
+        saved, kept, part = saved[:3], saved[3], part
+        other = mirror(part, "cfg", 1)
+        sent = combine(size, step_ratio, kept, other, noise_wide, old_wide)
+        guided = gather_guided(size, spread(size, [sent] * size.parts))
+        given = (step_ratio, strength, stats, [guided, mirror(guided, "cfg", 1)])
     else:
+        other = mirror(part, "cfg", 1)
         copy = place % size.copies
         rate = step_ratio[0]
         chosen = jnp.arange(size.copies).reshape(-1, 1, 1) == copy
@@ -607,17 +694,14 @@
     found, readout_part, sent = backward(size, given, blocks, wide, saved)
     if size.mirrored:
         ratio = found
-    if size.mirrored and lax.axis_size("cfg") == 2 and size.images in (1, 2, 4, 8):
+    if size.late:
         homes = [exchange(size, sent[0])]
-        total = sum_readout(size, readout_part)
-        if size.late:
-            total, late = lax.optimization_barrier((total, sent[1]))
-        every = spread(size, [total] * size.parts)
-        if size.late:
-            homes.append(exchange(size, late))
+        homes.append(exchange(size, join_readout(size, readout_part, sent[1])))
+        joined = homes[1]
+        found = joined + [mirror(x, "cfg", 1) for x in joined]
         token_grads, text_grads = home(size, wide, homes)
-        token_grads, every = lax.optimization_barrier((token_grads, every))
-        readout_grad = place_readout(size, every).T
+        token_grads, found = lax.optimization_barrier((token_grads, found))
+        readout_grad = place_readout(size, found).T
     else:
         homes = [exchange(size, x) for x in sent]
         token_grads, text_grads = home(size, wide, homes)

time: 107 us -> 103 us (0.963)
  starting transfers between devices: 30.1 us -> 24.7 us
  waiting for transfers between devices: 38.8 us -> 40.6 us
    ppermute x17 -> x19, starting transfers between devices: 30.1 us -> 24.7 us  [mirror(): return lax.ppermute(x, axis, [(i, i ^ apart) for i in range(count)])]
    ppermute x17 -> x19, waiting for transfers between devices: 38.8 us -> 40.6 us  [mirror(): return lax.ppermute(x, axis, [(i, i ^ apart) for i in range(count)])]
    pallas_call x1 -> x4, Pallas kernels: 2.75 us -> 3.16 us  [the longest x2 2.97 us: pack(): pl.pallas_call(functools.partial(pack_kernel, size, which), in_specs=[ANY...]
  transfers between devices with their start and end apart: 17 -> 19, of which waited for: 9 -> 8; matrix products, arithmetic and copies ran while one was open for 0% -> 0% of each run, Pallas kernels for 2% -> 2%
where the time goes in v4:
time: 103 us
  waiting for transfers between devices  40.6 us (39%)
  starting transfers between devices  24.7 us (24%)
  blocking collectives  19.1 us (19%)
  Pallas kernels  15.3 us (15%)
  between operations  2.74 us (3%)
    ppermute x19, waiting for transfers between devices, mirror(): return lax.ppermute(x, axis, [(i, i ^ apart) for i in range(count)])  40.6 us
    ppermute x19, starting transfers between devices, mirror(): return lax.ppermute(x, axis, [(i, i ^ apart) for i in range(count)])  24.7 us
    psum x1, blocking collectives, on_device(): stats = lax.psum(jnp.where(mine, rewards[0], 0.0), 'img')  10.1 us
    all_gather x1, blocking collectives, join_readout(): held = lax.all_gather(sent, 'img', axis=0)  9 us
    pallas_call x1, Pallas kernels, backward(): pl.pallas_call(functools.partial(backward_kernel, size), grid=(size.heads...  6.11 us
    pallas_call x1, Pallas kernels, forward(): pl.pallas_call(functools.partial(forward_kernel, size), grid=(size.q_bloc...  3.41 us
    pallas_call x2, Pallas kernels, pack(): pl.pallas_call(functools.partial(pack_kernel, size, which), in_specs=[ANY...  2.97 us
  transfers between devices with their start and end apart: 19, of which 8 were waited for; matrix products, arithmetic and copies ran while one was open for 0% of the time, Pallas kernels for 2%

profile of v4, /device:TPU:0, one launch (start us, length us, event | category | flops | bytes accessed | tf_op | source)
XLA Modules:
  0.0 102.5 jit_solution(16468950033261954851)
XLA Ops:
  0.6 0.0 copy-start.2
  0.6 0.0 copy-start
  0.7 0.0 copy-start.1
  0.7 2.6 %pack_tokens.3 = (bf16[1,400,512]{2,1,0:T(8,128)(2,1)}, bf16[1,400,512]{2,1,0:T(8,128)(2,1)}, bf16[1,400,512]{2,1,0:T(8,128)(2,1)}) custom-call(bf16[3,128,2048]{2,1,0:T(8,128)(2,1)} %bitcast.23, bf16[8,2,2048]{2,1,0:T(2,128)(2,1)} %bitcast.29), custom_call_target="tpu_custom_call" | custom-call | tf_op jit(solution)/shard_map/pack_tokens/pallas_call | solution.py:187
  3.2 3.1 %collective-permute-start = (bf16[1,400,512]{2,1,0:T(8,128)(2,1)}, bf16[1,400,512]{2,1,0:T(8,128)(2,1)S(1)}, u32[]{:S(2)}, u32[]{:S(2)}) collective-permute-start(bf16[1,400,512]{2,1,0:T(8,128)(2,1)} %get-tuple-element.47), channel_id=1, source_target_pairs={{0,1},{1,0},{2,3},{3,2},{4,5},{5,4},{6,7},{7,6},{8,9},{9,8},{10,11... | collective-permute-start | bytes 1228808 | tf_op jit(solution)/shard_map/ppermute | solution.py:54
  6.3 2.6 %collective-permute-start.1 = (bf16[1,400,512]{2,1,0:T(8,128)(2,1)}, bf16[1,400,512]{2,1,0:T(8,128)(2,1)S(1)}, u32[]{:S(2)}, u32[]{:S(2)}) collective-permute-start(bf16[1,400,512]{2,1,0:T(8,128)(2,1)} %get-tuple-element.48), channel_id=1, source_target_pairs={{0,2},{1,3},{2,0},{3,1},{4,6},{5,7},{6,4},{7,5},{8,10},{9,11},{10,... | collective-permute-start | bytes 1228808 | tf_op jit(solution)/shard_map/ppermute | solution.py:54
  8.9 0.0 collective-permute-start.2
  9.6 10.1 %psum.7.refs_2_ = f32[4]{0:T(128)S(1)} all-reduce(f32[4]{0:T(128)S(1)} %compare_select_fusion), channel_id=1, replica_groups=mesh['cfg'=2,'img'=4,'seq'=4] {'img'}, use_global_device_ids=true, to_apply=%region_0.1 | all-reduce | flops 4 | bytes 32 | tf_op jit(solution)/shard_map/psum | solution.py:662
  20.3 0.0 copy-done.2
  20.4 0.0 copy-done
  20.4 0.0 copy-start.3
  20.4 0.0 copy-start.4
  20.4 0.4 pack_tokens.2.refs_0_.refs_5_
  20.8 3.2 %collective-permute-done.refs_1_.refs_6_ = bf16[1,400,512]{2,1,0:T(8,128)(2,1)S(1)} collective-permute-done((bf16[1,400,512]{2,1,0:T(8,128)(2,1)}, bf16[1,400,512]{2,1,0:T(8,128)(2,1)S(1)}, u32[]{:S(2)}, u32[]{:S(2)}) %collective-permute-start) | collective-permute-done | bytes 409632 | tf_op jit(solution)/shard_map/ppermute | solution.py:54
  24.0 13.4 %collective-permute-done.1.refs_2_.refs_7_ = bf16[1,400,512]{2,1,0:T(8,128)(2,1)S(1)} collective-permute-done((bf16[1,400,512]{2,1,0:T(8,128)(2,1)}, bf16[1,400,512]{2,1,0:T(8,128)(2,1)S(1)}, u32[]{:S(2)}, u32[]{:S(2)}) %collective-permute-start.1) | collective-permute-done | bytes 409632 | tf_op jit(solution)/shard_map/ppermute | solution.py:54
  37.4 0.0 collective-permute-done.2.refs_3_.refs_8_
  37.4 0.0 copy-done.1
  37.4 3.4 %attention_forward.1 = (bf16[4,544,512]{2,1,0:T(8,128)(2,1)S(1)}, f32[4,64,512]{2,1,0:T(8,128)S(1)}, f32[4,1,512]{2,1,0:T(1,128)S(1)}, f32[32,512]{1,0:T(8,128)S(1)}, f32[32,512]{1,0:T(8,128)S(1)}) custom-call(f32[1]{0:T(128)} %bitcast.21.guidance, bf16[1,400,512]{2,1,0:T(8,128)(2,1)S(1)} %pack_tokens.2.refs_0_.refs_5_, ...), custom_call_target="tpu_custom_call" | custom-call | tf_op jit(solution)/shard_map/attention_forward/pallas_call | solution.py:279
  40.8 0.1 collective-permute-start.3
  41.5 0.6 collective-permute-done.3.other
  42.1 0.0 copy-done.3
  42.1 0.0 copy-done.4
  42.1 0.1 combine_branches.1.refs_0_
  42.3 2.5 %collective-permute-start.6 = (bf16[32,640]{1,0:T(8,128)(2,1)S(1)}, bf16[32,640]{1,0:T(8,128)(2,1)S(1)}, u32[]{:S(2)}, u32[]{:S(2)}) collective-permute-start(bf16[32,640]{1,0:T(8,128)(2,1)S(1)} %combine_branches.1.refs_0_), channel_id=1, source_target_pairs={{0,3},{1,2},{2,1},{3,0},{4,7},{5,6},{6,5},{7,4},{8,11},{9,10},{10,... | collective-permute-start | bytes 122888 | tf_op jit(solution)/shard_map/ppermute | solution.py:54
  44.8 6.9 %collective-permute-start.5 = (bf16[32,640]{1,0:T(8,128)(2,1)S(1)}, bf16[32,640]{1,0:T(8,128)(2,1)S(1)}, u32[]{:S(2)}, u32[]{:S(2)}) collective-permute-start(bf16[32,640]{1,0:T(8,128)(2,1)S(1)} %combine_branches.1.refs_0_), channel_id=1, source_target_pairs={{0,2},{1,3},{2,0},{3,1},{4,6},{5,7},{6,4},{7,5},{8,10},{9,11},{10,... | collective-permute-start | bytes 122888 | tf_op jit(solution)/shard_map/ppermute | solution.py:54
  51.7 0.1 collective-permute-start.4
  51.8 0.0 collective-permute-done.6.refs_3_
  51.8 2.4 %collective-permute-done.5.refs_2_ = bf16[32,640]{1,0:T(8,128)(2,1)S(1)} collective-permute-done((bf16[32,640]{1,0:T(8,128)(2,1)S(1)}, bf16[32,640]{1,0:T(8,128)(2,1)S(1)}, u32[]{:S(2)}, u32[]{:S(2)}) %collective-permute-start.5) | collective-permute-done | bytes 40992 | tf_op jit(solution)/shard_map/ppermute | solution.py:54
  54.2 1.5 %collective-permute-done.4.refs_1_ = bf16[32,640]{1,0:T(8,128)(2,1)S(1)} collective-permute-done((bf16[32,640]{1,0:T(8,128)(2,1)S(1)}, bf16[32,640]{1,0:T(8,128)(2,1)S(1)}, u32[]{:S(2)}, u32[]{:S(2)}) %collective-permute-start.4) | collective-permute-done | bytes 40992 | tf_op jit(solution)/shard_map/ppermute | solution.py:54
  55.7 0.2 gather_guided.1.refs_3_
  55.9 0.1 collective-permute-start.7
  55.9 1.3 %collective-permute-done.7.refs_4_ = f32[40,512]{1,0:T(8,128)S(1)} collective-permute-done((f32[40,512]{1,0:T(8,128)S(1)}, f32[40,512]{1,0:T(8,128)S(1)}, u32[]{:S(2)}, u32[]{:S(2)}) %collective-permute-start.7) | collective-permute-done | bytes 81952 | tf_op jit(solution)/shard_map/ppermute | solution.py:54
  57.2 6.1 %attention_backward.1 = (f32[1,1]{1,0:T(1,128)}, f32[64,512]{1,0:T(8,128)S(1)}, bf16[1,336,384]{2,1,0:T(8,128)(2,1)S(1)}, bf16[1,336,384]{2,1,0:T(8,128)(2,1)S(1...) custom-call(f32[1]{0:T(128)S(6)} %copy.12.rate.refs_0_, ...), custom_call_target="tpu_custom_call" | custom-call | tf_op jit(solution)/shard_map/attention_backward/pallas_call | solution.py:516
  63.3 0.2 collective-permute-start.11
  63.5 1.0 %collective-permute-start.8 = (bf16[1,336,384]{2,1,0:T(8,128)(2,1)S(1)}, bf16[1,336,384]{2,1,0:T(8,128)(2,1)S(1)}, u32[]{:S(2)}, u32[]{:S(2)}) collective-permute-start(bf16[1,336,384]{2,1,0:T(8,128)(2,1)S(1)} %get-tuple-element.60), channel_id=1, source_target_pairs={{0,1},{1,0},{2,3},{3,2},{4,5},{5,4},{6,7},{7,6},{8,9},{9,8},{10,11... | collective-permute-start | bytes 774152 | tf_op jit(solution)/shard_map/ppermute | solution.py:54
  64.5 2.0 %collective-permute-start.9 = (bf16[1,336,384]{2,1,0:T(8,128)(2,1)S(1)}, bf16[1,336,384]{2,1,0:T(8,128)(2,1)S(1)}, u32[]{:S(2)}, u32[]{:S(2)}) collective-permute-start(bf16[1,336,384]{2,1,0:T(8,128)(2,1)S(1)} %get-tuple-element.61), channel_id=1, source_target_pairs={{0,2},{1,3},{2,0},{3,1},{4,6},{5,7},{6,4},{7,5},{8,10},{9,11},{10,... | collective-permute-start | bytes 774152 | tf_op jit(solution)/shard_map/ppermute | solution.py:54
  66.5 0.0 collective-permute-done.11
  66.5 9.0 %all-gather = bf16[256,512]{1,0:T(8,128)(2,1)S(1)} all-gather(bf16[64,512]{1,0:T(8,128)(2,1)S(1)} %add_convert_fusion), channel_id=2, replica_groups=mesh['cfg'=2,'img'=4,'seq'=4] {'img'}, dimensions={0}, use_global_device_ids=true | all-gather | bytes 327680 | tf_op jit(solution)/shard_map/all_gather | solution.py:607
  75.6 0.5 collective-permute-start.12
  76.1 1.9 %collective-permute-start.10 = (bf16[1,336,384]{2,1,0:T(8,128)(2,1)S(1)}, bf16[1,336,384]{2,1,0:T(8,128)(2,1)S(1)}, u32[]{:S(2)}, u32[]{:S(2)}) collective-permute-start(bf16[1,336,384]{2,1,0:T(8,128)(2,1)S(1)} %get-tuple-element.62), channel_id=1, source_target_pairs={{0,3},{1,2},{2,1},{3,0},{4,7},{5,6},{6,5},{7,4},{8,11},{9,10},{10,... | collective-permute-start | bytes 774152 | tf_op jit(solution)/shard_map/ppermute | solution.py:54
  78.0 1.1 %collective-permute-start.13 = (bf16[1,464,128]{2,1,0:T(8,128)(2,1)S(1)}, bf16[1,464,128]{2,1,0:T(8,128)(2,1)S(1)}, u32[]{:S(2)}, u32[]{:S(2)}) collective-permute-start(bf16[1,464,128]{2,1,0:T(8,128)(2,1)S(1)} %get-tuple-element.70), channel_id=1, source_target_pairs={{0,2},{1,3},{2,0},{3,1},{4,6},{5,7},{6,4},{7,5},{8,10},{9,11},{10,... | collective-permute-start | bytes 356360 | tf_op jit(solution)/shard_map/ppermute | solution.py:54
  79.1 2.6 %collective-permute-done.12.refs_5_.refs_1_ = bf16[1,464,128]{2,1,0:T(8,128)(2,1)S(1)} collective-permute-done((bf16[1,464,128]{2,1,0:T(8,128)(2,1)S(1)}, bf16[1,464,128]{2,1,0:T(8,128)(2,1)S(1)}, u32[]{:S(2)}, u32[]{:S(2)}) %collective-permute-start.12) | collective-permute-done | bytes 118816 | tf_op jit(solution)/shard_map/ppermute | solution.py:54
  81.8 1.5 %collective-permute-start.14 = (bf16[1,464,128]{2,1,0:T(8,128)(2,1)S(1)}, bf16[1,464,128]{2,1,0:T(8,128)(2,1)S(1)}, u32[]{:S(2)}, u32[]{:S(2)}) collective-permute-start(bf16[1,464,128]{2,1,0:T(8,128)(2,1)S(1)} %get-tuple-element.71), channel_id=1, source_target_pairs={{0,3},{1,2},{2,1},{3,0},{4,7},{5,6},{6,5},{7,4},{8,11},{9,10},{10,... | collective-permute-start | bytes 356360 | tf_op jit(solution)/shard_map/ppermute | solution.py:54
  83.3 15.7 %collective-permute-done.13.refs_6_.refs_2_ = bf16[1,464,128]{2,1,0:T(8,128)(2,1)S(1)} collective-permute-done((bf16[1,464,128]{2,1,0:T(8,128)(2,1)S(1)}, bf16[1,464,128]{2,1,0:T(8,128)(2,1)S(1)}, u32[]{:S(2)}, u32[]{:S(2)}) %collective-permute-start.13) | collective-permute-done | bytes 118816 | tf_op jit(solution)/shard_map/ppermute | solution.py:54
  99.0 0.0 collective-permute-start.15
  99.0 0.0 collective-permute-done.14.refs_7_.refs_3_
  99.0 0.5 collective-permute-start.16
  99.5 0.0 collective-permute-done.8.refs_1_
  99.5 0.1 collective-permute-start.17
  99.6 0.0 collective-permute-done.9.refs_2_
  99.6 0.4 collective-permute-start.18
  100.0 0.0 collective-permute-done.10.refs_3_
  100.0 1.6 %home_tokens.1 = (bf16[3,128,2048]{2,1,0:T(8,128)(2,1)}, bf16[8,2,2048]{2,1,0:T(2,128)(2,1)}) custom-call(bf16[64,2048]{1,0:T(8,128)(2,1)S(1)} %bitcast.27, bf16[1,336,384]{2,1,0:T(8,128)(2,1)S(1)} %get-tuple-element.59.refs_0_, bf16[1,336,384]{2,1,0:T(8,128)(2,1)S(1)} %collective-permute-done.8.refs_1_, ...), custom_call_target="tpu_custom_call" | custom-call | tf_op jit(solution)/shard_map/home_tokens/pallas_call | solution.py:582
  101.6 0.0 collective-permute-done.15.refs_4_
  101.7 0.0 collective-permute-done.16.refs_5_
  101.7 0.0 collective-permute-done.17.refs_6_
  101.7 0.0 collective-permute-done.18.refs_7_
  101.7 0.9 place_readout_grad.1
  (3 shorter events, 0.1 us)
Async XLA Ops:
  0.6 19.7 %copy-start.2 = (bf16[1,1,8,2,2048]{4,3,2,1,0:T(2,128)(2,1)S(1)}, bf16[1,1,8,2,2048]{4,3,2,1,0:T(2,128)(2,1)}, u32[]{:S(2)}) copy-start(bf16[1,1,8,2,2048]{4,3,2,1,0:T(2,128)(2,1)} %param.9) | copy-start | bytes 196612
  0.6 19.7 %copy-start = (bf16[1,1,128,3,2048]{4,2,3,1,0:T(8,128)(2,1)S(1)}, bf16[1,1,128,3,2048]{4,2,3,1,0:T(8,128)(2,1)}, u32[]{:S(2)}) copy-start(bf16[1,1,128,3,2048]{4,2,3,1,0:T(8,128)(2,1)} %param.8) | copy-start | bytes 4718596
  0.7 36.7 %copy-start.1 = (bf16[2048,64]{0,1:T(8,128)(2,1)S(1)}, bf16[2048,64]{0,1:T(8,128)(2,1)}, u32[]{:S(2)}) copy-start(bf16[2048,64]{0,1:T(8,128)(2,1)} %param.10) | copy-start | bytes 786436
  3.2 20.8 %collective-permute-start = (bf16[1,400,512]{2,1,0:T(8,128)(2,1)}, bf16[1,400,512]{2,1,0:T(8,128)(2,1)S(1)}, u32[]{:S(2)}, u32[]{:S(2)}) collective-permute-start(bf16[1,400,512]{2,1,0:T(8,128)(2,1)} %get-tuple-element.47), channel_id=1, source_target_pairs={{0,1},{1,0},{2,3},{3,2},{4,5},{5,4},{6,7},{7,6},{8,9},{9,8},{10,11... | collective-permute-start | bytes 1228808 | tf_op jit(solution)/shard_map/ppermute | solution.py:54
  6.3 31.1 %collective-permute-start.1 = (bf16[1,400,512]{2,1,0:T(8,128)(2,1)}, bf16[1,400,512]{2,1,0:T(8,128)(2,1)S(1)}, u32[]{:S(2)}, u32[]{:S(2)}) collective-permute-start(bf16[1,400,512]{2,1,0:T(8,128)(2,1)} %get-tuple-element.48), channel_id=1, source_target_pairs={{0,2},{1,3},{2,0},{3,1},{4,6},{5,7},{6,4},{7,5},{8,10},{9,11},{10,... | collective-permute-start | bytes 1228808 | tf_op jit(solution)/shard_map/ppermute | solution.py:54
  8.9 28.5 %collective-permute-start.2 = (bf16[1,400,512]{2,1,0:T(8,128)(2,1)}, bf16[1,400,512]{2,1,0:T(8,128)(2,1)S(1)}, u32[]{:S(2)}, u32[]{:S(2)}) collective-permute-start(bf16[1,400,512]{2,1,0:T(8,128)(2,1)} %get-tuple-element.49), channel_id=1, source_target_pairs={{0,3},{1,2},{2,1},{3,0},{4,7},{5,6},{6,5},{7,4},{8,11},{9,10},{10,... | collective-permute-start | bytes 1228808 | tf_op jit(solution)/shard_map/ppermute | solution.py:54
  20.4 21.7 %copy-start.3 = (f32[1,128,64]{1,2,0:T(8,128)S(1)}, f32[1,128,64]{1,2,0:T(8,128)}, u32[]{:S(2)}) copy-start(f32[1,128,64]{1,2,0:T(8,128)} %param.12) | copy-start | bytes 98308
  20.4 21.7 %copy-start.4 = (f32[1,128,64]{1,2,0:T(8,128)S(1)}, f32[1,128,64]{1,2,0:T(8,128)}, u32[]{:S(2)}) copy-start(f32[1,128,64]{1,2,0:T(8,128)} %param.11) | copy-start | bytes 98308
  40.8 1.3 %collective-permute-start.3 = (f32[32,512]{1,0:T(8,128)S(1)}, f32[32,512]{1,0:T(8,128)S(1)}, u32[]{:S(2)}, u32[]{:S(2)}) collective-permute-start(f32[32,512]{1,0:T(8,128)S(1)} %get-tuple-element.55), channel_id=1, source_target_pairs={{0,16},{16,0},{1,17},{17,1},{2,18},{18,2},{3,19},{19,3},{4,20},{20... | collective-permute-start | bytes 196616 | tf_op jit(solution)/shard_map/ppermute | solution.py:54
  42.3 9.6 %collective-permute-start.6 = (bf16[32,640]{1,0:T(8,128)(2,1)S(1)}, bf16[32,640]{1,0:T(8,128)(2,1)S(1)}, u32[]{:S(2)}, u32[]{:S(2)}) collective-permute-start(bf16[32,640]{1,0:T(8,128)(2,1)S(1)} %combine_branches.1.refs_0_), channel_id=1, source_target_pairs={{0,3},{1,2},{2,1},{3,0},{4,7},{5,6},{6,5},{7,4},{8,11},{9,10},{10,... | collective-permute-start | bytes 122888 | tf_op jit(solution)/shard_map/ppermute | solution.py:54
  44.8 9.4 %collective-permute-start.5 = (bf16[32,640]{1,0:T(8,128)(2,1)S(1)}, bf16[32,640]{1,0:T(8,128)(2,1)S(1)}, u32[]{:S(2)}, u32[]{:S(2)}) collective-permute-start(bf16[32,640]{1,0:T(8,128)(2,1)S(1)} %combine_branches.1.refs_0_), channel_id=1, source_target_pairs={{0,2},{1,3},{2,0},{3,1},{4,6},{5,7},{6,4},{7,5},{8,10},{9,11},{10,... | collective-permute-start | bytes 122888 | tf_op jit(solution)/shard_map/ppermute | solution.py:54
  51.7 4.0 %collective-permute-start.4 = (bf16[32,640]{1,0:T(8,128)(2,1)S(1)}, bf16[32,640]{1,0:T(8,128)(2,1)S(1)}, u32[]{:S(2)}, u32[]{:S(2)}) collective-permute-start(bf16[32,640]{1,0:T(8,128)(2,1)S(1)} %combine_branches.1.refs_0_), channel_id=1, source_target_pairs={{0,1},{1,0},{2,3},{3,2},{4,5},{5,4},{6,7},{7,6},{8,9},{9,8},{10,11... | collective-permute-start | bytes 122888 | tf_op jit(solution)/shard_map/ppermute | solution.py:54
  55.9 1.3 %collective-permute-start.7 = (f32[40,512]{1,0:T(8,128)S(1)}, f32[40,512]{1,0:T(8,128)S(1)}, u32[]{:S(2)}, u32[]{:S(2)}) collective-permute-start(f32[40,512]{1,0:T(8,128)S(1)} %gather_guided.1.refs_3_), channel_id=1, source_target_pairs={{0,16},{16,0},{1,17},{17,1},{2,18},{18,2},{3,19},{19,3},{4,20},{20... | collective-permute-start | bytes 245768 | tf_op jit(solution)/shard_map/ppermute | solution.py:54
  63.3 3.2 %collective-permute-start.11 = (f32[64,512]{1,0:T(8,128)S(1)}, f32[64,512]{1,0:T(8,128)S(1)}, u32[]{:S(2)}, u32[]{:S(2)}) collective-permute-start(f32[64,512]{1,0:T(8,128)S(1)} %get-tuple-element.63), channel_id=1, source_target_pairs={{0,16},{16,0},{1,17},{17,1},{2,18},{18,2},{3,19},{19,3},{4,20},{20... | collective-permute-start | bytes 393224 | tf_op jit(solution)/shard_map/ppermute | solution.py:54
  63.5 36.0 %collective-permute-start.8 = (bf16[1,336,384]{2,1,0:T(8,128)(2,1)S(1)}, bf16[1,336,384]{2,1,0:T(8,128)(2,1)S(1)}, u32[]{:S(2)}, u32[]{:S(2)}) collective-permute-start(bf16[1,336,384]{2,1,0:T(8,128)(2,1)S(1)} %get-tuple-element.60), channel_id=1, source_target_pairs={{0,1},{1,0},{2,3},{3,2},{4,5},{5,4},{6,7},{7,6},{8,9},{9,8},{10,11... | collective-permute-start | bytes 774152 | tf_op jit(solution)/shard_map/ppermute | solution.py:54
  64.5 35.1 %collective-permute-start.9 = (bf16[1,336,384]{2,1,0:T(8,128)(2,1)S(1)}, bf16[1,336,384]{2,1,0:T(8,128)(2,1)S(1)}, u32[]{:S(2)}, u32[]{:S(2)}) collective-permute-start(bf16[1,336,384]{2,1,0:T(8,128)(2,1)S(1)} %get-tuple-element.61), channel_id=1, source_target_pairs={{0,2},{1,3},{2,0},{3,1},{4,6},{5,7},{6,4},{7,5},{8,10},{9,11},{10,... | collective-permute-start | bytes 774152 | tf_op jit(solution)/shard_map/ppermute | solution.py:54
  75.6 6.2 %collective-permute-start.12 = (bf16[1,464,128]{2,1,0:T(8,128)(2,1)S(1)}, bf16[1,464,128]{2,1,0:T(8,128)(2,1)S(1)}, u32[]{:S(2)}, u32[]{:S(2)}) collective-permute-start(bf16[1,464,128]{2,1,0:T(8,128)(2,1)S(1)} %get-tuple-element.69), channel_id=1, source_target_pairs={{0,1},{1,0},{2,3},{3,2},{4,5},{5,4},{6,7},{7,6},{8,9},{9,8},{10,11... | collective-permute-start | bytes 356360 | tf_op jit(solution)/shard_map/ppermute | solution.py:54
  76.1 23.9 %collective-permute-start.10 = (bf16[1,336,384]{2,1,0:T(8,128)(2,1)S(1)}, bf16[1,336,384]{2,1,0:T(8,128)(2,1)S(1)}, u32[]{:S(2)}, u32[]{:S(2)}) collective-permute-start(bf16[1,336,384]{2,1,0:T(8,128)(2,1)S(1)} %get-tuple-element.62), channel_id=1, source_target_pairs={{0,3},{1,2},{2,1},{3,0},{4,7},{5,6},{6,5},{7,4},{8,11},{9,10},{10,... | collective-permute-start | bytes 774152 | tf_op jit(solution)/shard_map/ppermute | solution.py:54
  78.0 20.9 %collective-permute-start.13 = (bf16[1,464,128]{2,1,0:T(8,128)(2,1)S(1)}, bf16[1,464,128]{2,1,0:T(8,128)(2,1)S(1)}, u32[]{:S(2)}, u32[]{:S(2)}) collective-permute-start(bf16[1,464,128]{2,1,0:T(8,128)(2,1)S(1)} %get-tuple-element.70), channel_id=1, source_target_pairs={{0,2},{1,3},{2,0},{3,1},{4,6},{5,7},{6,4},{7,5},{8,10},{9,11},{10,... | collective-permute-start | bytes 356360 | tf_op jit(solution)/shard_map/ppermute | solution.py:54
  81.8 17.2 %collective-permute-start.14 = (bf16[1,464,128]{2,1,0:T(8,128)(2,1)S(1)}, bf16[1,464,128]{2,1,0:T(8,128)(2,1)S(1)}, u32[]{:S(2)}, u32[]{:S(2)}) collective-permute-start(bf16[1,464,128]{2,1,0:T(8,128)(2,1)S(1)} %get-tuple-element.71), channel_id=1, source_target_pairs={{0,3},{1,2},{2,1},{3,0},{4,7},{5,6},{6,5},{7,4},{8,11},{9,10},{10,... | collective-permute-start | bytes 356360 | tf_op jit(solution)/shard_map/ppermute | solution.py:54
  99.0 2.7 %collective-permute-start.15 = (bf16[1,464,128]{2,1,0:T(8,128)(2,1)S(1)}, bf16[1,464,128]{2,1,0:T(8,128)(2,1)S(1)}, u32[]{:S(2)}, u32[]{:S(2)}) collective-permute-start(bf16[1,464,128]{2,1,0:T(8,128)(2,1)S(1)} %get-tuple-element.75.refs_4_.refs_0_), channel_id=1, source_target_pairs={{0,16},{16,0},{1,17},{17,1},{2,18},{18,2},{3,19},{19,3},{4,20},{20... | collective-permute-start | bytes 356360 | tf_op jit(solution)/shard_map/ppermute | solution.py:54
  99.0 2.7 %collective-permute-start.16 = (bf16[1,464,128]{2,1,0:T(8,128)(2,1)S(1)}, bf16[1,464,128]{2,1,0:T(8,128)(2,1)S(1)}, u32[]{:S(2)}, u32[]{:S(2)}) collective-permute-start(bf16[1,464,128]{2,1,0:T(8,128)(2,1)S(1)} %collective-permute-done.12.refs_5_.refs_1_), channel_id=1, source_target_pairs={{0,16},{16,0},{1,17},{17,1},{2,18},{18,2},{3,19},{19,3},{4,20},{20... | collective-permute-start | bytes 356360 | tf_op jit(solution)/shard_map/ppermute | solution.py:54
  99.5 2.2 %collective-permute-start.17 = (bf16[1,464,128]{2,1,0:T(8,128)(2,1)S(1)}, bf16[1,464,128]{2,1,0:T(8,128)(2,1)S(1)}, u32[]{:S(2)}, u32[]{:S(2)}) collective-permute-start(bf16[1,464,128]{2,1,0:T(8,128)(2,1)S(1)} %collective-permute-done.13.refs_6_.refs_2_), channel_id=1, source_target_pairs={{0,16},{16,0},{1,17},{17,1},{2,18},{18,2},{3,19},{19,3},{4,20},{20... | collective-permute-start | bytes 356360 | tf_op jit(solution)/shard_map/ppermute | solution.py:54
  99.6 2.1 %collective-permute-start.18 = (bf16[1,464,128]{2,1,0:T(8,128)(2,1)S(1)}, bf16[1,464,128]{2,1,0:T(8,128)(2,1)S(1)}, u32[]{:S(2)}, u32[]{:S(2)}) collective-permute-start(bf16[1,464,128]{2,1,0:T(8,128)(2,1)S(1)} %collective-permute-done.14.refs_7_.refs_3_), channel_id=1, source_target_pairs={{0,16},{16,0},{1,17},{17,1},{2,18},{18,2},{3,19},{19,3},{4,20},{20... | collective-permute-start | bytes 356360 | tf_op jit(solution)/shard_map/ppermute | solution.py:54

commit v5 on v4

--- a/solution.py
+++ b/solution.py
@@ -107,11 +107,16 @@
         widths = [(self.heads - self.late) * HEAD_DIM]
         return widths + [self.late * HEAD_DIM] * (self.late > 0)
 
-    def head_specs(self, rows, index):
-        return [
-            pl.BlockSpec((self.each, rows, HEAD_DIM), lambda *g: (0, 0, index(*g)))
-            for _ in range(self.lists)
-        ]
+    def grid(self):
+        return {} if self.mirrored else {"grid": (self.q_blocks,)}
+
+    def full(self, shape):
+        return pl.BlockSpec(memory_space=pltpu.VMEM) if self.mirrored else whole(shape)
+
+    def by_queries(self, *lead):
+        if self.mirrored:
+            return pl.BlockSpec(memory_space=pltpu.VMEM)
+        return pl.BlockSpec(lead + (self.q_block,), lambda b: (0,) * len(lead) + (b,))
 
     def base(self):
         place = lax.axis_index("seq")
@@ -201,24 +206,41 @@
     )(slots, text)
 
 
-def text_rows(size, blocks, second):
+def lanes_of(head):
+    return slice(head * HEAD_DIM, (head + 1) * HEAD_DIM)
+
+
+def text_rows(size, blocks, head, second):
     found = []
     for slot in range(size.parts):
-        pair = at(blocks, slot)[size.at_text : size.at_text + 2 * size.txt].astype(F32)
+        block = at(blocks, slot)
+        pair = block[size.at_text : size.at_text + 2 * size.txt, lanes_of(head)].astype(F32)
         found.append(pair[size.txt :] if second else pair[: size.txt])
     return jnp.concatenate(found, axis=0).astype(BF16)
 
 
-def gather_queries(size, blocks, queries):
-    for slot in range(size.parts):
-        queries[slot * size.sub : (slot + 1) * size.sub] = at(blocks, slot)[: size.sub]
-
-
-def gather_keys(size, blocks, first, second, keys):
-    for slot in range(size.parts):
-        part = at(blocks, slot)[first : first + size.rows]
-        keys[slot * size.rows : (slot + 1) * size.rows] = part
-    keys[size.img_keys :] = text_rows(size, blocks, second)
+def rows_of(size, blocks, head, first, count):
+    return [at(blocks, slot)[first : first + count, lanes_of(head)] for slot in range(size.parts)]
+
+
+def keys_of(size, blocks, head):
+    found = rows_of(size, blocks, head, size.at_keys, size.rows)
+    return found + [text_rows(size, blocks, head, False)]
+
+
+def values_of(size, blocks, head):
+    found = rows_of(size, blocks, head, size.at_values, size.rows)
+    return found + [text_rows(size, blocks, head, True)]
+
+
+def queries_of(size, blocks, head, step):
+    if size.q_blocks == 1:
+        return jnp.concatenate(rows_of(size, blocks, head, 0, size.sub), axis=0)
+    count = size.q_block // size.sub
+    found = [
+        blocks[0][step * count + k, : size.sub, lanes_of(head)] for k in range(count)
+    ]
+    return jnp.concatenate(found, axis=0)
 
 
 def folded(x, combine):
@@ -229,43 +251,34 @@
     blocks = refs[: size.lists]
     readout, raised, each, inverse = refs[size.lists : size.lists + 4]
     outs = refs[size.lists + 4 : size.lists + 4 + size.halves]
-    total, scores, keys, values, queries = refs[size.lists + 4 + size.halves :]
-    step, head = pl.program_id(0), pl.program_id(1)
-    gather_queries(size, blocks, queries)
-    gather_keys(size, blocks, size.at_keys, False, keys)
-    gather_keys(size, blocks, size.at_values, True, values)
-    query = queries[pl.ds(pl.multiple_of(step * size.q_block, 128), size.q_block), :]
-    peaks = []
-    for lo, hi in size.tiles():
-        tile = dot_nt(keys[lo:hi], query)
-        scores[lo:hi] = tile
-        peaks.append(folded(tile, jnp.max))
-    top = jnp.max(functools.reduce(jnp.maximum, peaks), axis=0, keepdims=True)
-    sums = []
-    for lo, hi in size.tiles():
-        tile = jnp.exp2((scores[lo:hi] - top) * EXP2_SCALE)
-        sums.append(folded(tile, jnp.sum))
-        raised[0, lo:hi] = tile.astype(BF16)
-    inverted = 1.0 / jnp.sum(sum(sums[1:], sums[0]), axis=0, keepdims=True)
-    held = readout[:, cols(size.group() * size.width + head * HEAD_DIM, HEAD_DIM)]
-    projected = dot_nt(held, values[...]).astype(BF16)
-    velocity = dot(projected, raised[0]) * inverted
-    each[0] = velocity
-    inverse[0] = inverted
-    part = velocity * branch_weight(guidance[0])
-
-    @pl.when(head == 0)
-    def _():
-        total[...] = part
-
-    @pl.when(head > 0)
-    def _():
-        total[...] += part
-
-    @pl.when(head == size.heads - 1)
-    def _():
-        for half, out in enumerate(outs):
-            out[...] = total[half_rows(size, half)]
+    total, scores = refs[size.lists + 4 + size.halves :]
+    step = 0 if size.mirrored else pl.program_id(0)
+    weight = branch_weight(guidance[0])
+    velocities = []
+    for head in range(size.heads):
+        query = queries_of(size, blocks, head, step)
+        peaks = []
+        for (lo, hi), key in zip(size.tiles(), keys_of(size, blocks, head)):
+            tile = dot_nt(key, query)
+            scores[head, lo:hi] = tile
+            peaks.append(folded(tile, jnp.max))
+        top = jnp.max(functools.reduce(jnp.maximum, peaks), axis=0, keepdims=True)
+        sums = []
+        for lo, hi in size.tiles():
+            tile = jnp.exp2((scores[head, lo:hi] - top) * EXP2_SCALE)
+            sums.append(folded(tile, jnp.sum))
+            raised[head, lo:hi] = tile.astype(BF16)
+        inverted = 1.0 / jnp.sum(sum(sums[1:], sums[0]), axis=0, keepdims=True)
+        held = readout[:, cols(size.group() * size.width + head * HEAD_DIM, HEAD_DIM)]
+        projected = [dot_nt(held, value) for value in values_of(size, blocks, head)]
+        projected = jnp.concatenate(projected, axis=1).astype(BF16)
+        velocity = dot(projected, raised[head]) * inverted
+        each[head] = velocity
+        inverse[head] = inverted
+        velocities.append(velocity)
+    total[...] = sum(velocities[1:], velocities[0]) * weight
+    for half, out in enumerate(outs):
+        out[...] = total[half_rows(size, half)]
 
 
 def half_rows(size, half):
@@ -276,34 +289,29 @@
 
 
 def forward(size, guidance, blocks, readout):
+    per = size.ch // size.halves
     return pl.pallas_call(
         functools.partial(forward_kernel, size),
-        grid=(size.q_blocks, size.heads),
-        in_specs=[SMEM]
-        + size.head_specs(size.sent_rows, lambda b, h: h)
-        + [whole(readout.shape)],
+        in_specs=[SMEM] + [size.full(x.shape) for x in blocks] + [size.full(readout.shape)],
         out_specs=[
-            pl.BlockSpec((1, size.keys, size.q_block), lambda b, h: (h, 0, b)),
-            pl.BlockSpec((1, size.ch, size.q_block), lambda b, h: (h, 0, b)),
-            pl.BlockSpec((1, 1, size.q_block), lambda b, h: (h, 0, b)),
+            size.by_queries(size.heads, size.keys),
+            size.by_queries(size.heads, size.ch),
+            size.by_queries(size.heads, 1),
         ]
-        + [pl.BlockSpec((size.ch // size.halves, size.q_block), lambda b, h: (0, b))]
-        * size.halves,
+        + [size.by_queries(per)] * size.halves,
         out_shape=[
             jax.ShapeDtypeStruct((size.heads, size.keys, size.queries), BF16),
             jax.ShapeDtypeStruct((size.heads, size.ch, size.queries), F32),
             jax.ShapeDtypeStruct((size.heads, 1, size.queries), F32),
         ]
-        + [jax.ShapeDtypeStruct((size.ch // size.halves, size.queries), F32)] * size.halves,
+        + [jax.ShapeDtypeStruct((per, size.queries), F32)] * size.halves,
         scratch_shapes=[
             pltpu.VMEM((size.ch, size.q_block), F32),
-            pltpu.VMEM((size.keys, size.q_block), F32),
-            pltpu.VMEM((size.keys, HEAD_DIM), BF16),
-            pltpu.VMEM((size.keys, HEAD_DIM), BF16),
-            pltpu.VMEM((size.queries, HEAD_DIM), BF16),
+            pltpu.VMEM((size.heads, size.keys, size.q_block), F32),
         ],
         compiler_params=size.params,
         name="attention_forward",
+        **size.grid(),
     )(guidance, *blocks, readout)
 
 
@@ -422,127 +430,108 @@
     outs, refs = refs[: size.lists], refs[size.lists :]
     if size.late:
         late_outs, refs = refs[: size.lists], refs[size.lists :]
-    grad_ref, scores, keys, values, queries, grad_keys, grad_queries, small = refs
-    head, step = pl.program_id(0), pl.program_id(1)
-
-    @pl.when((head == 0) & (step == 0))
-    def _():
-        if size.mirrored:
-            velocity_grad(size, rate, guidance, stats, moved, grad_ref, ratio_out)
-        else:
-            grad_ref[...] = given[...]
-            ratio_out[...] = jnp.zeros(ratio_out.shape, F32)
-
-    @pl.when(step == 0)
-    def _():
-        gather_queries(size, blocks, queries)
-        gather_keys(size, blocks, size.at_keys, False, keys)
-        gather_keys(size, blocks, size.at_values, True, values)
-
-    first = pl.multiple_of(step * size.q_block, 128)
-    held = readout[:, cols(size.group() * size.width + head * HEAD_DIM, HEAD_DIM)]
-    projected = dot_nt(values[...], held).astype(BF16)
-    grad = (grad_ref[:, pl.ds(first, size.q_block)] * inverse[0]).astype(BF16)
-    delta = jnp.sum(grad.astype(F32) * each[0], axis=0, keepdims=True)
-    for lo, hi in size.tiles():
-        tile = dot(projected[lo:hi], grad) - delta
-        scores[lo:hi] = (raised[0, lo:hi].astype(F32) * tile).astype(BF16)
-    key_part = dot(scores[...], queries[pl.ds(first, size.q_block), :]) * SCALE
-    query_part = dot_tn(keys[...], scores[...]) * SCALE
-    grad_queries[pl.ds(first, size.q_block), :] = query_part.T.astype(BF16)
-    small_part = dot_nt(grad, raised[0])
-    if size.q_blocks == 1:
-        grad_keys[...] = key_part
-        small[...] = small_part
+    grad_ref, scores, grad_keys, grad_queries, small = refs
+    step = 0 if size.mirrored else pl.program_id(0)
+    if size.mirrored:
+        velocity_grad(size, rate, guidance, stats, moved, grad_ref, ratio_out)
     else:
+        grad_ref[...] = given[...]
+        ratio_out[...] = jnp.zeros(ratio_out.shape, F32)
+
+    def add(ref, value):
+        if size.q_blocks == 1:
+            ref[...] = value
+            return
 
         @pl.when(step == 0)
         def _():
-            grad_keys[...] = key_part
-            small[...] = small_part
+            ref[...] = value
 
         @pl.when(step > 0)
         def _():
-            grad_keys[...] += key_part
-            small[...] += small_part
-
-    @pl.when(step == size.q_blocks - 1)
-    def _():
-        little = small[...].astype(BF16)
-        readout_out[...] = dot(little, values[...])
-        value_text = dot_tn(little[:, size.img_keys :], held)
-
-        def write(targets):
+            ref[...] += value
+
+    early = size.heads - size.late
+    for head in range(size.heads):
+        targets, lanes = (outs, lanes_of(head)) if head < early else (late_outs, lanes_of(head - early))
+        query = queries_of(size, blocks, head, step)
+        keys = keys_of(size, blocks, head)
+        values = values_of(size, blocks, head)
+        held = readout[:, cols(size.group() * size.width + head * HEAD_DIM, HEAD_DIM)]
+        grad = (grad_ref[...] * inverse[head]).astype(BF16)
+        delta = jnp.sum(grad.astype(F32) * each[head], axis=0, keepdims=True)
+        little = dot_nt(raised[head], grad).T
+        add(small.at[head], little)
+        projected = dot_nt(jnp.concatenate(values, axis=0), held).astype(BF16)
+        tile = dot(projected, grad) - delta
+        scores[head] = (raised[head].astype(F32) * tile).astype(BF16)
+        add(grad_keys.at[head], dot(scores[head], query) * SCALE)
+        found = dot_tn(jnp.concatenate(keys, axis=0), scores[head]) * SCALE
+        if size.mirrored:
+            grad_queries[head] = found.astype(BF16).T
+        else:
+            first = pl.multiple_of(step * size.q_block, 128)
+            grad_queries[head, pl.ds(first, size.q_block)] = found.astype(BF16).T
+
+        def write():
+            little = small[head].astype(BF16)
+            readout_out[:, lanes_of(head)] = dot(little, jnp.concatenate(values, axis=0))
+            value_text = dot_tn(little[:, size.img_keys :], held)
             for slot in range(size.parts):
                 out = at(targets, slot)
                 near = slice(slot * size.rows, (slot + 1) * size.rows)
-                out[: size.sub] = grad_queries[slot * size.sub : (slot + 1) * size.sub]
-                out[size.sub : size.sub + size.rows] = grad_keys[near].astype(BF16)
+                out[: size.sub, lanes] = grad_queries[head, slot * size.sub : (slot + 1) * size.sub]
+                out[size.sub : size.sub + size.rows, lanes] = grad_keys[head, near].astype(BF16)
                 start = size.img_keys + slot * size.txt
                 pair = [
-                    grad_keys[start : start + size.txt],
+                    grad_keys[head, start : start + size.txt],
                     value_text[slot * size.txt : (slot + 1) * size.txt],
                 ]
-                out[size.at_pair : size.at_small] = jnp.concatenate(pair, axis=0).astype(BF16)
-                out[size.at_small :] = little[:, near]
-
-        if size.late:
-            early = size.heads - size.late
-
-            @pl.when(head < early)
-            def _():
-                write(outs)
-
-            @pl.when(head >= early)
-            def _():
-                write(late_outs)
-
+                pair = jnp.concatenate(pair, axis=0).astype(BF16)
+                out[size.at_pair : size.at_small, lanes] = pair
+                out[size.at_small :, lanes] = little[:, near]
+
+        if size.mirrored:
+            write()
         else:
-            write(outs)
+            pl.when(step == size.q_blocks - 1)(write)
 
 
 def backward(size, given, blocks, readout, saved):
     if size.mirrored:
         rate, guidance, stats, moved = given
         first = [rate, guidance, stats] + moved
-        specs = [SMEM] * 3 + [whole(x.shape) for x in moved]
+        specs = [SMEM] * 3 + [size.full(x.shape) for x in moved]
     else:
-        first, specs = [given], [whole(given.shape)]
+        first, specs = [given], [size.by_queries(size.ch)]
     raised, each, inverse = saved
-    early = size.heads - size.late
-    home_specs = size.head_specs(size.home_rows, lambda h, b: jnp.minimum(h, early - 1))
-    if size.late:
-        home_specs += size.head_specs(size.home_rows, lambda h, b: jnp.maximum(h - early, 0))
+    shapes = [x for width in size.home_widths() for x in size.shapes(size.home_rows, width)]
+    shapes = [
+        jax.ShapeDtypeStruct((1, 1), F32),
+        jax.ShapeDtypeStruct((size.ch, size.width), F32),
+    ] + shapes
     outs = pl.pallas_call(
         functools.partial(backward_kernel, size),
-        grid=(size.heads, size.q_blocks),
         in_specs=specs
-        + size.head_specs(size.sent_rows, lambda h, b: h)
+        + [size.full(x.shape) for x in blocks]
         + [
-            whole(readout.shape),
-            pl.BlockSpec((1, size.keys, size.q_block), lambda h, b: (h, 0, b)),
-            pl.BlockSpec((1, size.ch, size.q_block), lambda h, b: (h, 0, b)),
-            pl.BlockSpec((1, 1, size.q_block), lambda h, b: (h, 0, b)),
+            size.full(readout.shape),
+            size.by_queries(size.heads, size.keys),
+            size.by_queries(size.heads, size.ch),
+            size.by_queries(size.heads, 1),
         ],
-        out_specs=[whole((1, 1)), pl.BlockSpec((size.ch, HEAD_DIM), lambda h, b: (0, h))]
-        + home_specs,
-        out_shape=[
-            jax.ShapeDtypeStruct((1, 1), F32),
-            jax.ShapeDtypeStruct((size.ch, size.width), F32),
-        ]
-        + [x for width in size.home_widths() for x in size.shapes(size.home_rows, width)],
+        out_specs=[size.full(x.shape) for x in shapes],
+        out_shape=shapes,
         scratch_shapes=[
-            pltpu.VMEM((size.ch, size.queries), F32),
-            pltpu.VMEM((size.keys, size.q_block), BF16),
-            pltpu.VMEM((size.keys, HEAD_DIM), BF16),
-            pltpu.VMEM((size.keys, HEAD_DIM), BF16),
-            pltpu.VMEM((size.queries, HEAD_DIM), BF16),
-            pltpu.VMEM((size.keys, HEAD_DIM), F32),
-            pltpu.VMEM((size.queries, HEAD_DIM), BF16),
-            pltpu.VMEM((size.ch, size.keys), F32),
+            pltpu.VMEM((size.ch, size.q_block), F32),
+            pltpu.VMEM((size.heads, size.keys, size.q_block), BF16),
+            pltpu.VMEM((size.heads, size.keys, HEAD_DIM), F32),
+            pltpu.VMEM((size.heads, size.queries, HEAD_DIM), BF16),
+            pltpu.VMEM((size.heads, size.ch, size.keys), F32),
         ],
         compiler_params=size.params,
         name="attention_backward",
+        **size.grid(),
     )(*first, *blocks, readout, raised, each, inverse)
     sent = outs[2:]
     return outs[0], outs[1], [sent[k : k + size.lists] for k in range(0, len(sent), size.lists)]

time: 103 us -> 99.6 us (0.967)
  Pallas kernels: 15.3 us -> 12.2 us
    pallas_call x2, Pallas kernels: 9.52 us -> 6.37 us  [the longest x1 3.86 us: backward(): pl.pallas_call(functools.partial(backward_kernel, size), in_specs=specs +...]
where the time goes in v5:
time: 99.6 us; the launch traced here: 99.4 us
  waiting for transfers between devices  40.6 us (41%)
  starting transfers between devices  24.7 us (25%)
  blocking collectives  19.1 us (19%)
  Pallas kernels  12.2 us (12%)
  between operations  2.74 us (3%)
    ppermute x19, waiting for transfers between devices, mirror(): return lax.ppermute(x, axis, [(i, i ^ apart) for i in range(count)])  40.6 us
    ppermute x19, starting transfers between devices, mirror(): return lax.ppermute(x, axis, [(i, i ^ apart) for i in range(count)])  24.7 us
    psum x1, blocking collectives, on_device(): stats = lax.psum(jnp.where(mine, rewards[0], 0.0), 'img')  10.1 us
    all_gather x1, blocking collectives, join_readout(): held = lax.all_gather(sent, 'img', axis=0)  9.01 us
    pallas_call x1, Pallas kernels, backward(): pl.pallas_call(functools.partial(backward_kernel, size), in_specs=specs +...  3.86 us
    pallas_call x2, Pallas kernels, pack(): pl.pallas_call(functools.partial(pack_kernel, size, which), in_specs=[ANY...  2.97 us
    pallas_call x1, Pallas kernels, forward(): pl.pallas_call(functools.partial(forward_kernel, size), in_specs=[SMEM] +...  2.5 us
  transfers between devices with their start and end apart: 19, of which 8 were waited for; matrix products, arithmetic and copies ran while one was open for 0% of the time, Pallas kernels for 2%

profile of v5, /device:TPU:0, one launch (start us, length us, event | category | flops | bytes accessed | tf_op | source)
XLA Modules:
  0.0 99.4 jit_solution(3936494824126269641)
XLA Ops:
  0.6 0.0 copy-start.2
  0.6 0.0 copy-start
  0.7 0.0 copy-start.1
  0.7 2.6 %pack_tokens.3 = (bf16[1,400,512]{2,1,0:T(8,128)(2,1)}, bf16[1,400,512]{2,1,0:T(8,128)(2,1)}, bf16[1,400,512]{2,1,0:T(8,128)(2,1)}) custom-call(bf16[3,128,2048]{2,1,0:T(8,128)(2,1)} %bitcast.23, bf16[8,2,2048]{2,1,0:T(2,128)(2,1)} %bitcast.29), custom_call_target="tpu_custom_call" | custom-call | tf_op jit(solution)/shard_map/pack_tokens/pallas_call | solution.py:192
  3.2 3.1 %collective-permute-start = (bf16[1,400,512]{2,1,0:T(8,128)(2,1)}, bf16[1,400,512]{2,1,0:T(8,128)(2,1)S(1)}, u32[]{:S(2)}, u32[]{:S(2)}) collective-permute-start(bf16[1,400,512]{2,1,0:T(8,128)(2,1)} %get-tuple-element.47), channel_id=1, source_target_pairs={{0,1},{1,0},{2,3},{3,2},{4,5},{5,4},{6,7},{7,6},{8,9},{9,8},{10,11... | collective-permute-start | bytes 1228808 | tf_op jit(solution)/shard_map/ppermute | solution.py:54
  6.3 2.6 %collective-permute-start.1 = (bf16[1,400,512]{2,1,0:T(8,128)(2,1)}, bf16[1,400,512]{2,1,0:T(8,128)(2,1)S(1)}, u32[]{:S(2)}, u32[]{:S(2)}) collective-permute-start(bf16[1,400,512]{2,1,0:T(8,128)(2,1)} %get-tuple-element.48), channel_id=1, source_target_pairs={{0,2},{1,3},{2,0},{3,1},{4,6},{5,7},{6,4},{7,5},{8,10},{9,11},{10,... | collective-permute-start | bytes 1228808 | tf_op jit(solution)/shard_map/ppermute | solution.py:54
  8.9 0.0 collective-permute-start.2
  9.6 10.1 %psum.7.refs_2_ = f32[4]{0:T(128)S(1)} all-reduce(f32[4]{0:T(128)S(1)} %compare_select_fusion), channel_id=1, replica_groups=mesh['cfg'=2,'img'=4,'seq'=4] {'img'}, use_global_device_ids=true, to_apply=%region_0.1 | all-reduce | flops 4 | bytes 32 | tf_op jit(solution)/shard_map/psum | solution.py:651
  20.3 0.0 copy-done.2
  20.4 0.0 copy-done
  20.4 0.0 copy-start.3
  20.4 0.0 copy-start.4
  20.4 0.4 pack_tokens.2.refs_0_.refs_5_
  20.8 3.2 %collective-permute-done.refs_1_.refs_6_ = bf16[1,400,512]{2,1,0:T(8,128)(2,1)S(1)} collective-permute-done((bf16[1,400,512]{2,1,0:T(8,128)(2,1)}, bf16[1,400,512]{2,1,0:T(8,128)(2,1)S(1)}, u32[]{:S(2)}, u32[]{:S(2)}) %collective-permute-start) | collective-permute-done | bytes 409632 | tf_op jit(solution)/shard_map/ppermute | solution.py:54
  24.0 13.4 %collective-permute-done.1.refs_2_.refs_7_ = bf16[1,400,512]{2,1,0:T(8,128)(2,1)S(1)} collective-permute-done((bf16[1,400,512]{2,1,0:T(8,128)(2,1)}, bf16[1,400,512]{2,1,0:T(8,128)(2,1)S(1)}, u32[]{:S(2)}, u32[]{:S(2)}) %collective-permute-start.1) | collective-permute-done | bytes 409632 | tf_op jit(solution)/shard_map/ppermute | solution.py:54
  37.4 0.0 collective-permute-done.2.refs_3_.refs_8_
  37.4 0.0 copy-done.1
  37.4 2.5 %attention_forward.1 = (bf16[4,544,512]{2,1,0:T(8,128)(2,1)S(1)}, f32[4,64,512]{2,1,0:T(8,128)S(1)}, f32[4,1,512]{2,1,0:T(1,128)S(1)}, f32[32,512]{1,0:T(8,128)S(1)}, f32[32,512]{1,0:T(8,128)S(1)}) custom-call(f32[1]{0:T(128)} %bitcast.21.guidance, bf16[1,400,512]{2,1,0:T(8,128)(2,1)S(1)} %pack_tokens.2.refs_0_.refs_5_, ...), custom_call_target="tpu_custom_call" | custom-call | tf_op jit(solution)/shard_map/attention_forward/pallas_call | solution.py:293
  39.9 0.1 collective-permute-start.3
  40.6 0.6 collective-permute-done.3.other
  41.2 0.0 copy-done.3
  41.2 0.0 copy-done.4
  41.2 0.1 combine_branches.1.refs_0_
  41.4 2.5 %collective-permute-start.6 = (bf16[32,640]{1,0:T(8,128)(2,1)S(1)}, bf16[32,640]{1,0:T(8,128)(2,1)S(1)}, u32[]{:S(2)}, u32[]{:S(2)}) collective-permute-start(bf16[32,640]{1,0:T(8,128)(2,1)S(1)} %combine_branches.1.refs_0_), channel_id=1, source_target_pairs={{0,3},{1,2},{2,1},{3,0},{4,7},{5,6},{6,5},{7,4},{8,11},{9,10},{10,... | collective-permute-start | bytes 122888 | tf_op jit(solution)/shard_map/ppermute | solution.py:54
  43.9 6.9 %collective-permute-start.5 = (bf16[32,640]{1,0:T(8,128)(2,1)S(1)}, bf16[32,640]{1,0:T(8,128)(2,1)S(1)}, u32[]{:S(2)}, u32[]{:S(2)}) collective-permute-start(bf16[32,640]{1,0:T(8,128)(2,1)S(1)} %combine_branches.1.refs_0_), channel_id=1, source_target_pairs={{0,2},{1,3},{2,0},{3,1},{4,6},{5,7},{6,4},{7,5},{8,10},{9,11},{10,... | collective-permute-start | bytes 122888 | tf_op jit(solution)/shard_map/ppermute | solution.py:54
  50.8 0.1 collective-permute-start.4
  50.9 0.0 collective-permute-done.6.refs_3_
  50.9 2.4 %collective-permute-done.5.refs_2_ = bf16[32,640]{1,0:T(8,128)(2,1)S(1)} collective-permute-done((bf16[32,640]{1,0:T(8,128)(2,1)S(1)}, bf16[32,640]{1,0:T(8,128)(2,1)S(1)}, u32[]{:S(2)}, u32[]{:S(2)}) %collective-permute-start.5) | collective-permute-done | bytes 40992 | tf_op jit(solution)/shard_map/ppermute | solution.py:54
  53.3 1.5 %collective-permute-done.4.refs_1_ = bf16[32,640]{1,0:T(8,128)(2,1)S(1)} collective-permute-done((bf16[32,640]{1,0:T(8,128)(2,1)S(1)}, bf16[32,640]{1,0:T(8,128)(2,1)S(1)}, u32[]{:S(2)}, u32[]{:S(2)}) %collective-permute-start.4) | collective-permute-done | bytes 40992 | tf_op jit(solution)/shard_map/ppermute | solution.py:54
  54.8 0.2 gather_guided.1.refs_3_
  55.0 0.1 collective-permute-start.7
  55.0 1.3 %collective-permute-done.7.refs_4_ = f32[40,512]{1,0:T(8,128)S(1)} collective-permute-done((f32[40,512]{1,0:T(8,128)S(1)}, f32[40,512]{1,0:T(8,128)S(1)}, u32[]{:S(2)}, u32[]{:S(2)}) %collective-permute-start.7) | collective-permute-done | bytes 81952 | tf_op jit(solution)/shard_map/ppermute | solution.py:54
  56.3 3.9 %attention_backward.1 = (f32[1,1]{1,0:T(1,128)}, f32[64,512]{1,0:T(8,128)S(1)}, bf16[1,336,384]{2,1,0:T(8,128)(2,1)S(1)}, bf16[1,336,384]{2,1,0:T(8,128)(2,1)S(1...) custom-call(f32[1]{0:T(128)S(6)} %copy.12.rate.refs_0_, ...), custom_call_target="tpu_custom_call" | custom-call | tf_op jit(solution)/shard_map/attention_backward/pallas_call | solution.py:513
  60.2 0.2 collective-permute-start.11
  60.3 1.0 %collective-permute-start.8 = (bf16[1,336,384]{2,1,0:T(8,128)(2,1)S(1)}, bf16[1,336,384]{2,1,0:T(8,128)(2,1)S(1)}, u32[]{:S(2)}, u32[]{:S(2)}) collective-permute-start(bf16[1,336,384]{2,1,0:T(8,128)(2,1)S(1)} %get-tuple-element.60), channel_id=1, source_target_pairs={{0,1},{1,0},{2,3},{3,2},{4,5},{5,4},{6,7},{7,6},{8,9},{9,8},{10,11... | collective-permute-start | bytes 774152 | tf_op jit(solution)/shard_map/ppermute | solution.py:54
  61.3 2.0 %collective-permute-start.9 = (bf16[1,336,384]{2,1,0:T(8,128)(2,1)S(1)}, bf16[1,336,384]{2,1,0:T(8,128)(2,1)S(1)}, u32[]{:S(2)}, u32[]{:S(2)}) collective-permute-start(bf16[1,336,384]{2,1,0:T(8,128)(2,1)S(1)} %get-tuple-element.61), channel_id=1, source_target_pairs={{0,2},{1,3},{2,0},{3,1},{4,6},{5,7},{6,4},{7,5},{8,10},{9,11},{10,... | collective-permute-start | bytes 774152 | tf_op jit(solution)/shard_map/ppermute | solution.py:54
  63.4 0.0 collective-permute-done.11
  63.4 9.0 %all-gather = bf16[256,512]{1,0:T(8,128)(2,1)S(1)} all-gather(bf16[64,512]{1,0:T(8,128)(2,1)S(1)} %add_convert_fusion), channel_id=2, replica_groups=mesh['cfg'=2,'img'=4,'seq'=4] {'img'}, dimensions={0}, use_global_device_ids=true | all-gather | bytes 327680 | tf_op jit(solution)/shard_map/all_gather | solution.py:596
  72.4 0.5 collective-permute-start.12
  72.9 1.9 %collective-permute-start.10 = (bf16[1,336,384]{2,1,0:T(8,128)(2,1)S(1)}, bf16[1,336,384]{2,1,0:T(8,128)(2,1)S(1)}, u32[]{:S(2)}, u32[]{:S(2)}) collective-permute-start(bf16[1,336,384]{2,1,0:T(8,128)(2,1)S(1)} %get-tuple-element.62), channel_id=1, source_target_pairs={{0,3},{1,2},{2,1},{3,0},{4,7},{5,6},{6,5},{7,4},{8,11},{9,10},{10,... | collective-permute-start | bytes 774152 | tf_op jit(solution)/shard_map/ppermute | solution.py:54
  74.9 1.1 %collective-permute-start.13 = (bf16[1,464,128]{2,1,0:T(8,128)(2,1)S(1)}, bf16[1,464,128]{2,1,0:T(8,128)(2,1)S(1)}, u32[]{:S(2)}, u32[]{:S(2)}) collective-permute-start(bf16[1,464,128]{2,1,0:T(8,128)(2,1)S(1)} %get-tuple-element.70), channel_id=1, source_target_pairs={{0,2},{1,3},{2,0},{3,1},{4,6},{5,7},{6,4},{7,5},{8,10},{9,11},{10,... | collective-permute-start | bytes 356360 | tf_op jit(solution)/shard_map/ppermute | solution.py:54
  76.0 2.6 %collective-permute-done.12.refs_5_.refs_1_ = bf16[1,464,128]{2,1,0:T(8,128)(2,1)S(1)} collective-permute-done((bf16[1,464,128]{2,1,0:T(8,128)(2,1)S(1)}, bf16[1,464,128]{2,1,0:T(8,128)(2,1)S(1)}, u32[]{:S(2)}, u32[]{:S(2)}) %collective-permute-start.12) | collective-permute-done | bytes 118816 | tf_op jit(solution)/shard_map/ppermute | solution.py:54
  78.6 1.5 %collective-permute-start.14 = (bf16[1,464,128]{2,1,0:T(8,128)(2,1)S(1)}, bf16[1,464,128]{2,1,0:T(8,128)(2,1)S(1)}, u32[]{:S(2)}, u32[]{:S(2)}) collective-permute-start(bf16[1,464,128]{2,1,0:T(8,128)(2,1)S(1)} %get-tuple-element.71), channel_id=1, source_target_pairs={{0,3},{1,2},{2,1},{3,0},{4,7},{5,6},{6,5},{7,4},{8,11},{9,10},{10,... | collective-permute-start | bytes 356360 | tf_op jit(solution)/shard_map/ppermute | solution.py:54
  80.2 15.7 %collective-permute-done.13.refs_6_.refs_2_ = bf16[1,464,128]{2,1,0:T(8,128)(2,1)S(1)} collective-permute-done((bf16[1,464,128]{2,1,0:T(8,128)(2,1)S(1)}, bf16[1,464,128]{2,1,0:T(8,128)(2,1)S(1)}, u32[]{:S(2)}, u32[]{:S(2)}) %collective-permute-start.13) | collective-permute-done | bytes 118816 | tf_op jit(solution)/shard_map/ppermute | solution.py:54
  95.8 0.0 collective-permute-start.15
  95.8 0.0 collective-permute-done.14.refs_7_.refs_3_
  95.8 0.5 collective-permute-start.16
  96.3 0.0 collective-permute-done.8.refs_1_
  96.3 0.1 collective-permute-start.17
  96.4 0.0 collective-permute-done.9.refs_2_
  96.4 0.4 collective-permute-start.18
  96.9 0.0 collective-permute-done.10.refs_3_
  96.9 1.6 %home_tokens.1 = (bf16[3,128,2048]{2,1,0:T(8,128)(2,1)}, bf16[8,2,2048]{2,1,0:T(2,128)(2,1)}) custom-call(bf16[64,2048]{1,0:T(8,128)(2,1)S(1)} %bitcast.27, bf16[1,336,384]{2,1,0:T(8,128)(2,1)S(1)} %get-tuple-element.59.refs_0_, bf16[1,336,384]{2,1,0:T(8,128)(2,1)S(1)} %collective-permute-done.8.refs_1_, ...), custom_call_target="tpu_custom_call" | custom-call | tf_op jit(solution)/shard_map/home_tokens/pallas_call | solution.py:571
  98.5 0.0 collective-permute-done.15.refs_4_
  98.5 0.0 collective-permute-done.16.refs_5_
  98.5 0.0 collective-permute-done.17.refs_6_
  98.5 0.0 collective-permute-done.18.refs_7_
  98.5 0.9 place_readout_grad.1
  (3 shorter events, 0.1 us)
Async XLA Ops:
  0.6 19.7 %copy-start.2 = (bf16[1,1,8,2,2048]{4,3,2,1,0:T(2,128)(2,1)S(1)}, bf16[1,1,8,2,2048]{4,3,2,1,0:T(2,128)(2,1)}, u32[]{:S(2)}) copy-start(bf16[1,1,8,2,2048]{4,3,2,1,0:T(2,128)(2,1)} %param.9) | copy-start | bytes 196612
  0.6 19.7 %copy-start = (bf16[1,1,128,3,2048]{4,2,3,1,0:T(8,128)(2,1)S(1)}, bf16[1,1,128,3,2048]{4,2,3,1,0:T(8,128)(2,1)}, u32[]{:S(2)}) copy-start(bf16[1,1,128,3,2048]{4,2,3,1,0:T(8,128)(2,1)} %param.8) | copy-start | bytes 4718596
  0.7 36.7 %copy-start.1 = (bf16[2048,64]{0,1:T(8,128)(2,1)S(1)}, bf16[2048,64]{0,1:T(8,128)(2,1)}, u32[]{:S(2)}) copy-start(bf16[2048,64]{0,1:T(8,128)(2,1)} %param.10) | copy-start | bytes 786436
  3.2 20.8 %collective-permute-start = (bf16[1,400,512]{2,1,0:T(8,128)(2,1)}, bf16[1,400,512]{2,1,0:T(8,128)(2,1)S(1)}, u32[]{:S(2)}, u32[]{:S(2)}) collective-permute-start(bf16[1,400,512]{2,1,0:T(8,128)(2,1)} %get-tuple-element.47), channel_id=1, source_target_pairs={{0,1},{1,0},{2,3},{3,2},{4,5},{5,4},{6,7},{7,6},{8,9},{9,8},{10,11... | collective-permute-start | bytes 1228808 | tf_op jit(solution)/shard_map/ppermute | solution.py:54
  6.3 31.1 %collective-permute-start.1 = (bf16[1,400,512]{2,1,0:T(8,128)(2,1)}, bf16[1,400,512]{2,1,0:T(8,128)(2,1)S(1)}, u32[]{:S(2)}, u32[]{:S(2)}) collective-permute-start(bf16[1,400,512]{2,1,0:T(8,128)(2,1)} %get-tuple-element.48), channel_id=1, source_target_pairs={{0,2},{1,3},{2,0},{3,1},{4,6},{5,7},{6,4},{7,5},{8,10},{9,11},{10,... | collective-permute-start | bytes 1228808 | tf_op jit(solution)/shard_map/ppermute | solution.py:54
  8.9 28.5 %collective-permute-start.2 = (bf16[1,400,512]{2,1,0:T(8,128)(2,1)}, bf16[1,400,512]{2,1,0:T(8,128)(2,1)S(1)}, u32[]{:S(2)}, u32[]{:S(2)}) collective-permute-start(bf16[1,400,512]{2,1,0:T(8,128)(2,1)} %get-tuple-element.49), channel_id=1, source_target_pairs={{0,3},{1,2},{2,1},{3,0},{4,7},{5,6},{6,5},{7,4},{8,11},{9,10},{10,... | collective-permute-start | bytes 1228808 | tf_op jit(solution)/shard_map/ppermute | solution.py:54
  20.4 20.8 %copy-start.3 = (f32[1,128,64]{1,2,0:T(8,128)S(1)}, f32[1,128,64]{1,2,0:T(8,128)}, u32[]{:S(2)}) copy-start(f32[1,128,64]{1,2,0:T(8,128)} %param.12) | copy-start | bytes 98308
  20.4 20.8 %copy-start.4 = (f32[1,128,64]{1,2,0:T(8,128)S(1)}, f32[1,128,64]{1,2,0:T(8,128)}, u32[]{:S(2)}) copy-start(f32[1,128,64]{1,2,0:T(8,128)} %param.11) | copy-start | bytes 98308
  39.9 1.3 %collective-permute-start.3 = (f32[32,512]{1,0:T(8,128)S(1)}, f32[32,512]{1,0:T(8,128)S(1)}, u32[]{:S(2)}, u32[]{:S(2)}) collective-permute-start(f32[32,512]{1,0:T(8,128)S(1)} %get-tuple-element.55), channel_id=1, source_target_pairs={{0,16},{16,0},{1,17},{17,1},{2,18},{18,2},{3,19},{19,3},{4,20},{20... | collective-permute-start | bytes 196616 | tf_op jit(solution)/shard_map/ppermute | solution.py:54
  41.4 9.6 %collective-permute-start.6 = (bf16[32,640]{1,0:T(8,128)(2,1)S(1)}, bf16[32,640]{1,0:T(8,128)(2,1)S(1)}, u32[]{:S(2)}, u32[]{:S(2)}) collective-permute-start(bf16[32,640]{1,0:T(8,128)(2,1)S(1)} %combine_branches.1.refs_0_), channel_id=1, source_target_pairs={{0,3},{1,2},{2,1},{3,0},{4,7},{5,6},{6,5},{7,4},{8,11},{9,10},{10,... | collective-permute-start | bytes 122888 | tf_op jit(solution)/shard_map/ppermute | solution.py:54
  43.9 9.4 %collective-permute-start.5 = (bf16[32,640]{1,0:T(8,128)(2,1)S(1)}, bf16[32,640]{1,0:T(8,128)(2,1)S(1)}, u32[]{:S(2)}, u32[]{:S(2)}) collective-permute-start(bf16[32,640]{1,0:T(8,128)(2,1)S(1)} %combine_branches.1.refs_0_), channel_id=1, source_target_pairs={{0,2},{1,3},{2,0},{3,1},{4,6},{5,7},{6,4},{7,5},{8,10},{9,11},{10,... | collective-permute-start | bytes 122888 | tf_op jit(solution)/shard_map/ppermute | solution.py:54
  50.8 4.0 %collective-permute-start.4 = (bf16[32,640]{1,0:T(8,128)(2,1)S(1)}, bf16[32,640]{1,0:T(8,128)(2,1)S(1)}, u32[]{:S(2)}, u32[]{:S(2)}) collective-permute-start(bf16[32,640]{1,0:T(8,128)(2,1)S(1)} %combine_branches.1.refs_0_), channel_id=1, source_target_pairs={{0,1},{1,0},{2,3},{3,2},{4,5},{5,4},{6,7},{7,6},{8,9},{9,8},{10,11... | collective-permute-start | bytes 122888 | tf_op jit(solution)/shard_map/ppermute | solution.py:54
  55.0 1.3 %collective-permute-start.7 = (f32[40,512]{1,0:T(8,128)S(1)}, f32[40,512]{1,0:T(8,128)S(1)}, u32[]{:S(2)}, u32[]{:S(2)}) collective-permute-start(f32[40,512]{1,0:T(8,128)S(1)} %gather_guided.1.refs_3_), channel_id=1, source_target_pairs={{0,16},{16,0},{1,17},{17,1},{2,18},{18,2},{3,19},{19,3},{4,20},{20... | collective-permute-start | bytes 245768 | tf_op jit(solution)/shard_map/ppermute | solution.py:54
  60.2 3.2 %collective-permute-start.11 = (f32[64,512]{1,0:T(8,128)S(1)}, f32[64,512]{1,0:T(8,128)S(1)}, u32[]{:S(2)}, u32[]{:S(2)}) collective-permute-start(f32[64,512]{1,0:T(8,128)S(1)} %get-tuple-element.63), channel_id=1, source_target_pairs={{0,16},{16,0},{1,17},{17,1},{2,18},{18,2},{3,19},{19,3},{4,20},{20... | collective-permute-start | bytes 393224 | tf_op jit(solution)/shard_map/ppermute | solution.py:54
  60.3 36.0 %collective-permute-start.8 = (bf16[1,336,384]{2,1,0:T(8,128)(2,1)S(1)}, bf16[1,336,384]{2,1,0:T(8,128)(2,1)S(1)}, u32[]{:S(2)}, u32[]{:S(2)}) collective-permute-start(bf16[1,336,384]{2,1,0:T(8,128)(2,1)S(1)} %get-tuple-element.60), channel_id=1, source_target_pairs={{0,1},{1,0},{2,3},{3,2},{4,5},{5,4},{6,7},{7,6},{8,9},{9,8},{10,11... | collective-permute-start | bytes 774152 | tf_op jit(solution)/shard_map/ppermute | solution.py:54
  61.3 35.1 %collective-permute-start.9 = (bf16[1,336,384]{2,1,0:T(8,128)(2,1)S(1)}, bf16[1,336,384]{2,1,0:T(8,128)(2,1)S(1)}, u32[]{:S(2)}, u32[]{:S(2)}) collective-permute-start(bf16[1,336,384]{2,1,0:T(8,128)(2,1)S(1)} %get-tuple-element.61), channel_id=1, source_target_pairs={{0,2},{1,3},{2,0},{3,1},{4,6},{5,7},{6,4},{7,5},{8,10},{9,11},{10,... | collective-permute-start | bytes 774152 | tf_op jit(solution)/shard_map/ppermute | solution.py:54
  72.4 6.2 %collective-permute-start.12 = (bf16[1,464,128]{2,1,0:T(8,128)(2,1)S(1)}, bf16[1,464,128]{2,1,0:T(8,128)(2,1)S(1)}, u32[]{:S(2)}, u32[]{:S(2)}) collective-permute-start(bf16[1,464,128]{2,1,0:T(8,128)(2,1)S(1)} %get-tuple-element.69), channel_id=1, source_target_pairs={{0,1},{1,0},{2,3},{3,2},{4,5},{5,4},{6,7},{7,6},{8,9},{9,8},{10,11... | collective-permute-start | bytes 356360 | tf_op jit(solution)/shard_map/ppermute | solution.py:54
  72.9 23.9 %collective-permute-start.10 = (bf16[1,336,384]{2,1,0:T(8,128)(2,1)S(1)}, bf16[1,336,384]{2,1,0:T(8,128)(2,1)S(1)}, u32[]{:S(2)}, u32[]{:S(2)}) collective-permute-start(bf16[1,336,384]{2,1,0:T(8,128)(2,1)S(1)} %get-tuple-element.62), channel_id=1, source_target_pairs={{0,3},{1,2},{2,1},{3,0},{4,7},{5,6},{6,5},{7,4},{8,11},{9,10},{10,... | collective-permute-start | bytes 774152 | tf_op jit(solution)/shard_map/ppermute | solution.py:54
  74.9 20.9 %collective-permute-start.13 = (bf16[1,464,128]{2,1,0:T(8,128)(2,1)S(1)}, bf16[1,464,128]{2,1,0:T(8,128)(2,1)S(1)}, u32[]{:S(2)}, u32[]{:S(2)}) collective-permute-start(bf16[1,464,128]{2,1,0:T(8,128)(2,1)S(1)} %get-tuple-element.70), channel_id=1, source_target_pairs={{0,2},{1,3},{2,0},{3,1},{4,6},{5,7},{6,4},{7,5},{8,10},{9,11},{10,... | collective-permute-start | bytes 356360 | tf_op jit(solution)/shard_map/ppermute | solution.py:54
  78.6 17.2 %collective-permute-start.14 = (bf16[1,464,128]{2,1,0:T(8,128)(2,1)S(1)}, bf16[1,464,128]{2,1,0:T(8,128)(2,1)S(1)}, u32[]{:S(2)}, u32[]{:S(2)}) collective-permute-start(bf16[1,464,128]{2,1,0:T(8,128)(2,1)S(1)} %get-tuple-element.71), channel_id=1, source_target_pairs={{0,3},{1,2},{2,1},{3,0},{4,7},{5,6},{6,5},{7,4},{8,11},{9,10},{10,... | collective-permute-start | bytes 356360 | tf_op jit(solution)/shard_map/ppermute | solution.py:54
  95.8 2.7 %collective-permute-start.15 = (bf16[1,464,128]{2,1,0:T(8,128)(2,1)S(1)}, bf16[1,464,128]{2,1,0:T(8,128)(2,1)S(1)}, u32[]{:S(2)}, u32[]{:S(2)}) collective-permute-start(bf16[1,464,128]{2,1,0:T(8,128)(2,1)S(1)} %get-tuple-element.75.refs_4_.refs_0_), channel_id=1, source_target_pairs={{0,16},{16,0},{1,17},{17,1},{2,18},{18,2},{3,19},{19,3},{4,20},{20... | collective-permute-start | bytes 356360 | tf_op jit(solution)/shard_map/ppermute | solution.py:54
  95.8 2.7 %collective-permute-start.16 = (bf16[1,464,128]{2,1,0:T(8,128)(2,1)S(1)}, bf16[1,464,128]{2,1,0:T(8,128)(2,1)S(1)}, u32[]{:S(2)}, u32[]{:S(2)}) collective-permute-start(bf16[1,464,128]{2,1,0:T(8,128)(2,1)S(1)} %collective-permute-done.12.refs_5_.refs_1_), channel_id=1, source_target_pairs={{0,16},{16,0},{1,17},{17,1},{2,18},{18,2},{3,19},{19,3},{4,20},{20... | collective-permute-start | bytes 356360 | tf_op jit(solution)/shard_map/ppermute | solution.py:54
  96.3 2.2 %collective-permute-start.17 = (bf16[1,464,128]{2,1,0:T(8,128)(2,1)S(1)}, bf16[1,464,128]{2,1,0:T(8,128)(2,1)S(1)}, u32[]{:S(2)}, u32[]{:S(2)}) collective-permute-start(bf16[1,464,128]{2,1,0:T(8,128)(2,1)S(1)} %collective-permute-done.13.refs_6_.refs_2_), channel_id=1, source_target_pairs={{0,16},{16,0},{1,17},{17,1},{2,18},{18,2},{3,19},{19,3},{4,20},{20... | collective-permute-start | bytes 356360 | tf_op jit(solution)/shard_map/ppermute | solution.py:54
  96.4 2.1 %collective-permute-start.18 = (bf16[1,464,128]{2,1,0:T(8,128)(2,1)S(1)}, bf16[1,464,128]{2,1,0:T(8,128)(2,1)S(1)}, u32[]{:S(2)}, u32[]{:S(2)}) collective-permute-start(bf16[1,464,128]{2,1,0:T(8,128)(2,1)S(1)} %collective-permute-done.14.refs_7_.refs_3_), channel_id=1, source_target_pairs={{0,16},{16,0},{1,17},{17,1},{2,18},{18,2},{3,19},{19,3},{4,20},{20... | collective-permute-start | bytes 356360 | tf_op jit(solution)/shard_map/ppermute | solution.py:54

commit v6 on v5

--- a/solution.py
+++ b/solution.py
@@ -126,14 +126,19 @@
         return lax.axis_index("seq") // self.copies
 
 
+def far_first(blocks):
+    own, near, *far = blocks
+    far, near = lax.optimization_barrier((far, near))
+    return [own, near] + list(far)
+
+
 def spread(size, blocks):
-    found = [mirror(blocks[k], "seq", k) for k in reversed(range(1, size.parts))]
-    return [blocks[0]] + found[::-1]
+    return [blocks[0]] + [mirror(blocks[k], "seq", k) for k in range(1, size.parts)]
 
 
 def exchange(size, blocks):
     if size.mirrored:
-        return spread(size, blocks)
+        return far_first(spread(size, blocks))
     return [lax.all_to_all(blocks[0], "seq", split_axis=0, concat_axis=0, tiled=True)]
 
 
@@ -641,9 +646,11 @@
     noise_wide, old_wide = noise[0].T, old_velocity[0].T
     text = txt_kv[0, 0]
     if size.mirrored:
-        away = list(range(1, size.parts))
-        sent = pack(size, slots, text, away, 60 * MIB)
-        blocks = [mirror(block, "seq", k) for k, block in zip(away, sent)]
+        first = min(2, size.parts - 1)
+        rest = [k for k in range(1, size.parts) if k != first]
+        packed = dict(zip([first], pack(size, slots, text, [first], 60 * MIB)))
+        packed.update(zip(rest, pack(size, slots, text, rest, 60 * MIB) if rest else []))
+        blocks = [mirror(packed[k], "seq", k) for k in range(1, size.parts)]
     else:
         blocks = exchange(size, pack(size, slots, text, list(range(size.parts)), 48 * MIB))
 
@@ -652,7 +659,7 @@
     if size.mirrored:
         stats, near, words = lax.optimization_barrier((stats, slots, text))
         blocks = list(pack(size, near, words, [0], 16 * MIB)) + blocks
-        blocks = lax.optimization_barrier(blocks)
+        blocks = far_first(blocks)
 
     *saved, part = forward(size, strength, blocks, wide)
     if size.mirrored:
@@ -685,7 +692,7 @@
         ratio = found
     if size.late:
         homes = [exchange(size, sent[0])]
-        homes.append(exchange(size, join_readout(size, readout_part, sent[1])))
+        homes.append(spread(size, join_readout(size, readout_part, sent[1])))
         joined = homes[1]
         found = joined + [mirror(x, "cfg", 1) for x in joined]
         token_grads, text_grads = home(size, wide, homes)

time: 99.6 us -> 97.1 us (0.975)
  waiting for transfers between devices: 40.6 us -> 36.1 us
  Pallas kernels: 12.2 us -> 13.7 us
    ppermute x19, waiting for transfers between devices: 40.6 us -> 36.1 us  [mirror(): return lax.ppermute(x, axis, [(i, i ^ apart) for i in range(count)])]
    pallas_call x2 -> x3, Pallas kernels: 2.97 us -> 4.51 us  [pack(): pl.pallas_call(functools.partial(pack_kernel, size, which), in_specs=[ANY...]
  transfers between devices with their start and end apart: 19 -> 19, of which waited for: 8 -> 8; matrix products, arithmetic and copies ran while one was open for 0% -> 0% of each run, Pallas kernels for 2% -> 4%
where the time goes in v6:
time: 97.1 us; the launch traced here: 96.9 us
  waiting for transfers between devices  36.1 us (37%)
  starting transfers between devices  25.4 us (26%)
  blocking collectives  18.9 us (19%)
  Pallas kernels  13.7 us (14%)
  between operations  2.75 us (3%)
    ppermute x19, waiting for transfers between devices, mirror(): return lax.ppermute(x, axis, [(i, i ^ apart) for i in range(count)])  36.1 us
    ppermute x19, starting transfers between devices, mirror(): return lax.ppermute(x, axis, [(i, i ^ apart) for i in range(count)])  25.4 us
    psum x1, blocking collectives, on_device(): stats = lax.psum(jnp.where(mine, rewards[0], 0.0), 'img')  9.91 us
    all_gather x1, blocking collectives, join_readout(): held = lax.all_gather(sent, 'img', axis=0)  9 us
    pallas_call x3, Pallas kernels, pack(): pl.pallas_call(functools.partial(pack_kernel, size, which), in_specs=[ANY...  4.51 us
    pallas_call x1, Pallas kernels, backward(): pl.pallas_call(functools.partial(backward_kernel, size), in_specs=specs +...  3.89 us
    pallas_call x1, Pallas kernels, forward(): pl.pallas_call(functools.partial(forward_kernel, size), in_specs=[SMEM] +...  2.52 us
  transfers between devices with their start and end apart: 19, of which 8 were waited for; matrix products, arithmetic and copies ran while one was open for 0% of the time, Pallas kernels for 4%

profile of v6, /device:TPU:0, one launch (start us, length us, event | category | flops | bytes accessed | tf_op | source)
XLA Modules:
  0.0 96.9 jit_solution(8557046625818580326)
XLA Ops:
  0.6 0.0 copy-start
  0.6 0.0 copy-start.2
  0.7 2.0 %pack_tokens.4 = bf16[1,400,512]{2,1,0:T(8,128)(2,1)} custom-call(bf16[3,128,2048]{2,1,0:T(8,128)(2,1)} %bitcast.23, bf16[8,2,2048]{2,1,0:T(2,128)(2,1)} %bitcast.30), custom_call_target="tpu_custom_call" | custom-call | tf_op jit(solution)/shard_map/pack_tokens/pallas_call | solution.py:197
  2.6 0.0 copy-start.1
  2.6 4.1 %collective-permute-start = (bf16[1,400,512]{2,1,0:T(8,128)(2,1)}, bf16[1,400,512]{2,1,0:T(8,128)(2,1)S(1)}, u32[]{:S(2)}, u32[]{:S(2)}) collective-permute-start(bf16[1,400,512]{2,1,0:T(8,128)(2,1)} %pack_tokens.4), channel_id=1, source_target_pairs={{0,2},{1,3},{2,0},{3,1},{4,6},{5,7},{6,4},{7,5},{8,10},{9,11},{10,... | collective-permute-start | bytes 1228808 | tf_op jit(solution)/shard_map/ppermute | solution.py:54
  6.8 2.1 %pack_tokens.5 = (bf16[1,400,512]{2,1,0:T(8,128)(2,1)}, bf16[1,400,512]{2,1,0:T(8,128)(2,1)}) custom-call(bf16[3,128,2048]{2,1,0:T(8,128)(2,1)} %bitcast.24, bf16[8,2,2048]{2,1,0:T(2,128)(2,1)} %bitcast.31), custom_call_target="tpu_custom_call" | custom-call | tf_op jit(solution)/shard_map/pack_tokens/pallas_call | solution.py:197
  8.9 1.4 %collective-permute-start.1 = (bf16[1,400,512]{2,1,0:T(8,128)(2,1)}, bf16[1,400,512]{2,1,0:T(8,128)(2,1)S(1)}, u32[]{:S(2)}, u32[]{:S(2)}) collective-permute-start(bf16[1,400,512]{2,1,0:T(8,128)(2,1)} %get-tuple-element.48), channel_id=1, source_target_pairs={{0,3},{1,2},{2,1},{3,0},{4,7},{5,6},{6,5},{7,4},{8,11},{9,10},{10,... | collective-permute-start | bytes 1228808 | tf_op jit(solution)/shard_map/ppermute | solution.py:54
  10.3 0.3 collective-permute-start.2
  11.3 9.9 %psum.7.refs_2_ = f32[4]{0:T(128)S(1)} all-reduce(f32[4]{0:T(128)S(1)} %compare_select_fusion), channel_id=1, replica_groups=mesh['cfg'=2,'img'=4,'seq'=4] {'img'}, use_global_device_ids=true, to_apply=%region_0.1 | all-reduce | flops 4 | bytes 32 | tf_op jit(solution)/shard_map/psum | solution.py:658
  21.8 0.0 copy-done
  21.8 0.0 copy-done.2
  21.8 0.0 copy-start.3
  21.9 0.0 copy-start.4
  21.9 0.4 pack_tokens.3.refs_0_.refs_5_
  22.3 12.6 %collective-permute-done.refs_2_.refs_7_ = bf16[1,400,512]{2,1,0:T(8,128)(2,1)S(1)} collective-permute-done((bf16[1,400,512]{2,1,0:T(8,128)(2,1)}, bf16[1,400,512]{2,1,0:T(8,128)(2,1)S(1)}, u32[]{:S(2)}, u32[]{:S(2)}) %collective-permute-start) | collective-permute-done | bytes 409632 | tf_op jit(solution)/shard_map/ppermute | solution.py:54
  34.9 0.0 collective-permute-done.1.refs_3_.refs_8_
  34.9 2.7 %collective-permute-done.2.refs_1_.refs_6_ = bf16[1,400,512]{2,1,0:T(8,128)(2,1)S(1)} collective-permute-done((bf16[1,400,512]{2,1,0:T(8,128)(2,1)}, bf16[1,400,512]{2,1,0:T(8,128)(2,1)S(1)}, u32[]{:S(2)}, u32[]{:S(2)}) %collective-permute-start.2) | collective-permute-done | bytes 409632 | tf_op jit(solution)/shard_map/ppermute | solution.py:54
  37.5 0.0 copy-done.1
  37.5 2.5 %attention_forward.1 = (bf16[4,544,512]{2,1,0:T(8,128)(2,1)S(1)}, f32[4,64,512]{2,1,0:T(8,128)S(1)}, f32[4,1,512]{2,1,0:T(1,128)S(1)}, f32[32,512]{1,0:T(8,128)S(1)}, f32[32,512]{1,0:T(8,128)S(1)}) custom-call(f32[1]{0:T(128)} %bitcast.21.guidance, bf16[1,400,512]{2,1,0:T(8,128)(2,1)S(1)} %pack_tokens.3.refs_0_.refs_5_, ...), custom_call_target="tpu_custom_call" | custom-call | tf_op jit(solution)/shard_map/attention_forward/pallas_call | solution.py:298
  40.1 0.1 collective-permute-start.3
  40.8 0.6 collective-permute-done.3.other
  41.4 0.0 copy-done.3
  41.4 0.0 copy-done.4
  41.4 0.1 combine_branches.1.refs_0_
  41.5 3.6 %collective-permute-start.6 = (bf16[32,640]{1,0:T(8,128)(2,1)S(1)}, bf16[32,640]{1,0:T(8,128)(2,1)S(1)}, u32[]{:S(2)}, u32[]{:S(2)}) collective-permute-start(bf16[32,640]{1,0:T(8,128)(2,1)S(1)} %combine_branches.1.refs_0_), channel_id=1, source_target_pairs={{0,3},{1,2},{2,1},{3,0},{4,7},{5,6},{6,5},{7,4},{8,11},{9,10},{10,... | collective-permute-start | bytes 122888 | tf_op jit(solution)/shard_map/ppermute | solution.py:54
  45.1 4.5 %collective-permute-start.5 = (bf16[32,640]{1,0:T(8,128)(2,1)S(1)}, bf16[32,640]{1,0:T(8,128)(2,1)S(1)}, u32[]{:S(2)}, u32[]{:S(2)}) collective-permute-start(bf16[32,640]{1,0:T(8,128)(2,1)S(1)} %combine_branches.1.refs_0_), channel_id=1, source_target_pairs={{0,2},{1,3},{2,0},{3,1},{4,6},{5,7},{6,4},{7,5},{8,10},{9,11},{10,... | collective-permute-start | bytes 122888 | tf_op jit(solution)/shard_map/ppermute | solution.py:54
  49.6 0.5 collective-permute-start.4
  50.1 0.0 collective-permute-done.6.refs_3_
  50.1 2.2 %collective-permute-done.5.refs_2_ = bf16[32,640]{1,0:T(8,128)(2,1)S(1)} collective-permute-done((bf16[32,640]{1,0:T(8,128)(2,1)S(1)}, bf16[32,640]{1,0:T(8,128)(2,1)S(1)}, u32[]{:S(2)}, u32[]{:S(2)}) %collective-permute-start.5) | collective-permute-done | bytes 40992 | tf_op jit(solution)/shard_map/ppermute | solution.py:54
  52.3 1.3 %collective-permute-done.4.refs_1_ = bf16[32,640]{1,0:T(8,128)(2,1)S(1)} collective-permute-done((bf16[32,640]{1,0:T(8,128)(2,1)S(1)}, bf16[32,640]{1,0:T(8,128)(2,1)S(1)}, u32[]{:S(2)}, u32[]{:S(2)}) %collective-permute-start.4) | collective-permute-done | bytes 40992 | tf_op jit(solution)/shard_map/ppermute | solution.py:54
  53.6 0.2 gather_guided.1.refs_3_
  53.8 0.1 collective-permute-start.7
  53.8 1.3 %collective-permute-done.7.refs_4_ = f32[40,512]{1,0:T(8,128)S(1)} collective-permute-done((f32[40,512]{1,0:T(8,128)S(1)}, f32[40,512]{1,0:T(8,128)S(1)}, u32[]{:S(2)}, u32[]{:S(2)}) %collective-permute-start.7) | collective-permute-done | bytes 81952 | tf_op jit(solution)/shard_map/ppermute | solution.py:54
  55.1 3.9 %attention_backward.1 = (f32[1,1]{1,0:T(1,128)}, f32[64,512]{1,0:T(8,128)S(1)}, bf16[1,336,384]{2,1,0:T(8,128)(2,1)S(1)}, bf16[1,336,384]{2,1,0:T(8,128)(2,1)S(1...) custom-call(f32[1]{0:T(128)S(6)} %copy.12.rate.refs_0_, ...), custom_call_target="tpu_custom_call" | custom-call | tf_op jit(solution)/shard_map/attention_backward/pallas_call | solution.py:518
  59.0 0.2 collective-permute-start.11
  59.1 1.8 %collective-permute-start.8 = (bf16[1,336,384]{2,1,0:T(8,128)(2,1)S(1)}, bf16[1,336,384]{2,1,0:T(8,128)(2,1)S(1)}, u32[]{:S(2)}, u32[]{:S(2)}) collective-permute-start(bf16[1,336,384]{2,1,0:T(8,128)(2,1)S(1)} %get-tuple-element.59), channel_id=1, source_target_pairs={{0,2},{1,3},{2,0},{3,1},{4,6},{5,7},{6,4},{7,5},{8,10},{9,11},{10,... | collective-permute-start | bytes 774152 | tf_op jit(solution)/shard_map/ppermute | solution.py:54
  61.0 1.9 %collective-permute-start.9 = (bf16[1,336,384]{2,1,0:T(8,128)(2,1)S(1)}, bf16[1,336,384]{2,1,0:T(8,128)(2,1)S(1)}, u32[]{:S(2)}, u32[]{:S(2)}) collective-permute-start(bf16[1,336,384]{2,1,0:T(8,128)(2,1)S(1)} %get-tuple-element.60), channel_id=1, source_target_pairs={{0,3},{1,2},{2,1},{3,0},{4,7},{5,6},{6,5},{7,4},{8,11},{9,10},{10,... | collective-permute-start | bytes 774152 | tf_op jit(solution)/shard_map/ppermute | solution.py:54
  62.9 0.0 collective-permute-done.11
  62.9 9.0 %all-gather = bf16[256,512]{1,0:T(8,128)(2,1)S(1)} all-gather(bf16[64,512]{1,0:T(8,128)(2,1)S(1)} %add_convert_fusion), channel_id=2, replica_groups=mesh['cfg'=2,'img'=4,'seq'=4] {'img'}, dimensions={0}, use_global_device_ids=true | all-gather | bytes 327680 | tf_op jit(solution)/shard_map/all_gather | solution.py:601
  72.0 0.1 collective-permute-start.12
  72.0 2.0 %collective-permute-start.10 = (bf16[1,336,384]{2,1,0:T(8,128)(2,1)S(1)}, bf16[1,336,384]{2,1,0:T(8,128)(2,1)S(1)}, u32[]{:S(2)}, u32[]{:S(2)}) collective-permute-start(bf16[1,336,384]{2,1,0:T(8,128)(2,1)S(1)} %get-tuple-element.61), channel_id=1, source_target_pairs={{0,1},{1,0},{2,3},{3,2},{4,5},{5,4},{6,7},{7,6},{8,9},{9,8},{10,11... | collective-permute-start | bytes 774152 | tf_op jit(solution)/shard_map/ppermute | solution.py:54
  74.1 1.1 %collective-permute-start.13 = (bf16[1,464,128]{2,1,0:T(8,128)(2,1)S(1)}, bf16[1,464,128]{2,1,0:T(8,128)(2,1)S(1)}, u32[]{:S(2)}, u32[]{:S(2)}) collective-permute-start(bf16[1,464,128]{2,1,0:T(8,128)(2,1)S(1)} %get-tuple-element.72), channel_id=1, source_target_pairs={{0,2},{1,3},{2,0},{3,1},{4,6},{5,7},{6,4},{7,5},{8,10},{9,11},{10,... | collective-permute-start | bytes 356360 | tf_op jit(solution)/shard_map/ppermute | solution.py:54
  75.2 7.0 %collective-permute-done.12.refs_5_.refs_1_ = bf16[1,464,128]{2,1,0:T(8,128)(2,1)S(1)} collective-permute-done((bf16[1,464,128]{2,1,0:T(8,128)(2,1)S(1)}, bf16[1,464,128]{2,1,0:T(8,128)(2,1)S(1)}, u32[]{:S(2)}, u32[]{:S(2)}) %collective-permute-start.12) | collective-permute-done | bytes 118816 | tf_op jit(solution)/shard_map/ppermute | solution.py:54
  82.2 2.7 %collective-permute-start.14 = (bf16[1,464,128]{2,1,0:T(8,128)(2,1)S(1)}, bf16[1,464,128]{2,1,0:T(8,128)(2,1)S(1)}, u32[]{:S(2)}, u32[]{:S(2)}) collective-permute-start(bf16[1,464,128]{2,1,0:T(8,128)(2,1)S(1)} %get-tuple-element.73), channel_id=1, source_target_pairs={{0,3},{1,2},{2,1},{3,0},{4,7},{5,6},{6,5},{7,4},{8,11},{9,10},{10,... | collective-permute-start | bytes 356360 | tf_op jit(solution)/shard_map/ppermute | solution.py:54
  84.9 8.4 %collective-permute-done.13.refs_6_.refs_2_ = bf16[1,464,128]{2,1,0:T(8,128)(2,1)S(1)} collective-permute-done((bf16[1,464,128]{2,1,0:T(8,128)(2,1)S(1)}, bf16[1,464,128]{2,1,0:T(8,128)(2,1)S(1)}, u32[]{:S(2)}, u32[]{:S(2)}) %collective-permute-start.13) | collective-permute-done | bytes 118816 | tf_op jit(solution)/shard_map/ppermute | solution.py:54
  93.3 0.0 collective-permute-start.15
  93.4 0.0 collective-permute-done.14.refs_7_.refs_3_
  93.4 0.5 collective-permute-start.16
  93.9 0.0 collective-permute-done.8.refs_2_
  93.9 0.1 collective-permute-start.17
  93.9 0.0 collective-permute-done.9.refs_3_
  93.9 0.4 collective-permute-start.18
  94.4 0.0 collective-permute-done.10.refs_1_
  94.4 1.6 %home_tokens.1 = (bf16[3,128,2048]{2,1,0:T(8,128)(2,1)}, bf16[8,2,2048]{2,1,0:T(2,128)(2,1)}) custom-call(bf16[64,2048]{1,0:T(8,128)(2,1)S(1)} %bitcast.28, bf16[1,336,384]{2,1,0:T(8,128)(2,1)S(1)} %get-tuple-element.58.refs_0_, bf16[1,336,384]{2,1,0:T(8,128)(2,1)S(1)} %collective-permute-done.10.refs_1_, ...), custom_call_target="tpu_custom_call" | custom-call | tf_op jit(solution)/shard_map/home_tokens/pallas_call | solution.py:576
  96.0 0.0 collective-permute-done.15.refs_4_
  96.0 0.0 collective-permute-done.16.refs_5_
  96.0 0.0 collective-permute-done.17.refs_6_
  96.0 0.0 collective-permute-done.18.refs_7_
  96.0 0.9 place_readout_grad.1
  (3 shorter events, 0.1 us)
Async XLA Ops:
  0.6 21.2 %copy-start = (bf16[1,1,128,3,2048]{4,2,3,1,0:T(8,128)(2,1)S(1)}, bf16[1,1,128,3,2048]{4,2,3,1,0:T(8,128)(2,1)}, u32[]{:S(2)}) copy-start(bf16[1,1,128,3,2048]{4,2,3,1,0:T(8,128)(2,1)} %param.8) | copy-start | bytes 4718596
  0.6 21.2 %copy-start.2 = (bf16[1,1,8,2,2048]{4,3,2,1,0:T(2,128)(2,1)S(1)}, bf16[1,1,8,2,2048]{4,3,2,1,0:T(2,128)(2,1)}, u32[]{:S(2)}) copy-start(bf16[1,1,8,2,2048]{4,3,2,1,0:T(2,128)(2,1)} %param.9) | copy-start | bytes 196612
  2.6 34.9 %copy-start.1 = (bf16[2048,64]{0,1:T(8,128)(2,1)S(1)}, bf16[2048,64]{0,1:T(8,128)(2,1)}, u32[]{:S(2)}) copy-start(bf16[2048,64]{0,1:T(8,128)(2,1)} %param.10) | copy-start | bytes 786436
  2.6 32.2 %collective-permute-start = (bf16[1,400,512]{2,1,0:T(8,128)(2,1)}, bf16[1,400,512]{2,1,0:T(8,128)(2,1)S(1)}, u32[]{:S(2)}, u32[]{:S(2)}) collective-permute-start(bf16[1,400,512]{2,1,0:T(8,128)(2,1)} %pack_tokens.4), channel_id=1, source_target_pairs={{0,2},{1,3},{2,0},{3,1},{4,6},{5,7},{6,4},{7,5},{8,10},{9,11},{10,... | collective-permute-start | bytes 1228808 | tf_op jit(solution)/shard_map/ppermute | solution.py:54
  8.9 26.0 %collective-permute-start.1 = (bf16[1,400,512]{2,1,0:T(8,128)(2,1)}, bf16[1,400,512]{2,1,0:T(8,128)(2,1)S(1)}, u32[]{:S(2)}, u32[]{:S(2)}) collective-permute-start(bf16[1,400,512]{2,1,0:T(8,128)(2,1)} %get-tuple-element.48), channel_id=1, source_target_pairs={{0,3},{1,2},{2,1},{3,0},{4,7},{5,6},{6,5},{7,4},{8,11},{9,10},{10,... | collective-permute-start | bytes 1228808 | tf_op jit(solution)/shard_map/ppermute | solution.py:54
  10.3 27.2 %collective-permute-start.2 = (bf16[1,400,512]{2,1,0:T(8,128)(2,1)}, bf16[1,400,512]{2,1,0:T(8,128)(2,1)S(1)}, u32[]{:S(2)}, u32[]{:S(2)}) collective-permute-start(bf16[1,400,512]{2,1,0:T(8,128)(2,1)} %get-tuple-element.49), channel_id=1, source_target_pairs={{0,1},{1,0},{2,3},{3,2},{4,5},{5,4},{6,7},{7,6},{8,9},{9,8},{10,11... | collective-permute-start | bytes 1228808 | tf_op jit(solution)/shard_map/ppermute | solution.py:54
  21.8 19.5 %copy-start.3 = (f32[1,128,64]{1,2,0:T(8,128)S(1)}, f32[1,128,64]{1,2,0:T(8,128)}, u32[]{:S(2)}) copy-start(f32[1,128,64]{1,2,0:T(8,128)} %param.12) | copy-start | bytes 98308
  21.9 19.5 %copy-start.4 = (f32[1,128,64]{1,2,0:T(8,128)S(1)}, f32[1,128,64]{1,2,0:T(8,128)}, u32[]{:S(2)}) copy-start(f32[1,128,64]{1,2,0:T(8,128)} %param.11) | copy-start | bytes 98308
  40.1 1.3 %collective-permute-start.3 = (f32[32,512]{1,0:T(8,128)S(1)}, f32[32,512]{1,0:T(8,128)S(1)}, u32[]{:S(2)}, u32[]{:S(2)}) collective-permute-start(f32[32,512]{1,0:T(8,128)S(1)} %get-tuple-element.54), channel_id=1, source_target_pairs={{0,16},{16,0},{1,17},{17,1},{2,18},{18,2},{3,19},{19,3},{4,20},{20... | collective-permute-start | bytes 196616 | tf_op jit(solution)/shard_map/ppermute | solution.py:54
  41.5 8.5 %collective-permute-start.6 = (bf16[32,640]{1,0:T(8,128)(2,1)S(1)}, bf16[32,640]{1,0:T(8,128)(2,1)S(1)}, u32[]{:S(2)}, u32[]{:S(2)}) collective-permute-start(bf16[32,640]{1,0:T(8,128)(2,1)S(1)} %combine_branches.1.refs_0_), channel_id=1, source_target_pairs={{0,3},{1,2},{2,1},{3,0},{4,7},{5,6},{6,5},{7,4},{8,11},{9,10},{10,... | collective-permute-start | bytes 122888 | tf_op jit(solution)/shard_map/ppermute | solution.py:54
  45.1 7.2 %collective-permute-start.5 = (bf16[32,640]{1,0:T(8,128)(2,1)S(1)}, bf16[32,640]{1,0:T(8,128)(2,1)S(1)}, u32[]{:S(2)}, u32[]{:S(2)}) collective-permute-start(bf16[32,640]{1,0:T(8,128)(2,1)S(1)} %combine_branches.1.refs_0_), channel_id=1, source_target_pairs={{0,2},{1,3},{2,0},{3,1},{4,6},{5,7},{6,4},{7,5},{8,10},{9,11},{10,... | collective-permute-start | bytes 122888 | tf_op jit(solution)/shard_map/ppermute | solution.py:54
  49.6 4.0 %collective-permute-start.4 = (bf16[32,640]{1,0:T(8,128)(2,1)S(1)}, bf16[32,640]{1,0:T(8,128)(2,1)S(1)}, u32[]{:S(2)}, u32[]{:S(2)}) collective-permute-start(bf16[32,640]{1,0:T(8,128)(2,1)S(1)} %combine_branches.1.refs_0_), channel_id=1, source_target_pairs={{0,1},{1,0},{2,3},{3,2},{4,5},{5,4},{6,7},{7,6},{8,9},{9,8},{10,11... | collective-permute-start | bytes 122888 | tf_op jit(solution)/shard_map/ppermute | solution.py:54
  53.8 1.3 %collective-permute-start.7 = (f32[40,512]{1,0:T(8,128)S(1)}, f32[40,512]{1,0:T(8,128)S(1)}, u32[]{:S(2)}, u32[]{:S(2)}) collective-permute-start(f32[40,512]{1,0:T(8,128)S(1)} %gather_guided.1.refs_3_), channel_id=1, source_target_pairs={{0,16},{16,0},{1,17},{17,1},{2,18},{18,2},{3,19},{19,3},{4,20},{20... | collective-permute-start | bytes 245768 | tf_op jit(solution)/shard_map/ppermute | solution.py:54
  59.0 3.9 %collective-permute-start.11 = (f32[64,512]{1,0:T(8,128)S(1)}, f32[64,512]{1,0:T(8,128)S(1)}, u32[]{:S(2)}, u32[]{:S(2)}) collective-permute-start(f32[64,512]{1,0:T(8,128)S(1)} %get-tuple-element.65), channel_id=1, source_target_pairs={{0,16},{16,0},{1,17},{17,1},{2,18},{18,2},{3,19},{19,3},{4,20},{20... | collective-permute-start | bytes 393224 | tf_op jit(solution)/shard_map/ppermute | solution.py:54
  59.1 34.7 %collective-permute-start.8 = (bf16[1,336,384]{2,1,0:T(8,128)(2,1)S(1)}, bf16[1,336,384]{2,1,0:T(8,128)(2,1)S(1)}, u32[]{:S(2)}, u32[]{:S(2)}) collective-permute-start(bf16[1,336,384]{2,1,0:T(8,128)(2,1)S(1)} %get-tuple-element.59), channel_id=1, source_target_pairs={{0,2},{1,3},{2,0},{3,1},{4,6},{5,7},{6,4},{7,5},{8,10},{9,11},{10,... | collective-permute-start | bytes 774152 | tf_op jit(solution)/shard_map/ppermute | solution.py:54
  61.0 33.0 %collective-permute-start.9 = (bf16[1,336,384]{2,1,0:T(8,128)(2,1)S(1)}, bf16[1,336,384]{2,1,0:T(8,128)(2,1)S(1)}, u32[]{:S(2)}, u32[]{:S(2)}) collective-permute-start(bf16[1,336,384]{2,1,0:T(8,128)(2,1)S(1)} %get-tuple-element.60), channel_id=1, source_target_pairs={{0,3},{1,2},{2,1},{3,0},{4,7},{5,6},{6,5},{7,4},{8,11},{9,10},{10,... | collective-permute-start | bytes 774152 | tf_op jit(solution)/shard_map/ppermute | solution.py:54
  72.0 10.3 %collective-permute-start.12 = (bf16[1,464,128]{2,1,0:T(8,128)(2,1)S(1)}, bf16[1,464,128]{2,1,0:T(8,128)(2,1)S(1)}, u32[]{:S(2)}, u32[]{:S(2)}) collective-permute-start(bf16[1,464,128]{2,1,0:T(8,128)(2,1)S(1)} %get-tuple-element.71), channel_id=1, source_target_pairs={{0,1},{1,0},{2,3},{3,2},{4,5},{5,4},{6,7},{7,6},{8,9},{9,8},{10,11... | collective-permute-start | bytes 356360 | tf_op jit(solution)/shard_map/ppermute | solution.py:54
  72.0 22.3 %collective-permute-start.10 = (bf16[1,336,384]{2,1,0:T(8,128)(2,1)S(1)}, bf16[1,336,384]{2,1,0:T(8,128)(2,1)S(1)}, u32[]{:S(2)}, u32[]{:S(2)}) collective-permute-start(bf16[1,336,384]{2,1,0:T(8,128)(2,1)S(1)} %get-tuple-element.61), channel_id=1, source_target_pairs={{0,1},{1,0},{2,3},{3,2},{4,5},{5,4},{6,7},{7,6},{8,9},{9,8},{10,11... | collective-permute-start | bytes 774152 | tf_op jit(solution)/shard_map/ppermute | solution.py:54
  74.1 19.3 %collective-permute-start.13 = (bf16[1,464,128]{2,1,0:T(8,128)(2,1)S(1)}, bf16[1,464,128]{2,1,0:T(8,128)(2,1)S(1)}, u32[]{:S(2)}, u32[]{:S(2)}) collective-permute-start(bf16[1,464,128]{2,1,0:T(8,128)(2,1)S(1)} %get-tuple-element.72), channel_id=1, source_target_pairs={{0,2},{1,3},{2,0},{3,1},{4,6},{5,7},{6,4},{7,5},{8,10},{9,11},{10,... | collective-permute-start | bytes 356360 | tf_op jit(solution)/shard_map/ppermute | solution.py:54
  82.2 11.1 %collective-permute-start.14 = (bf16[1,464,128]{2,1,0:T(8,128)(2,1)S(1)}, bf16[1,464,128]{2,1,0:T(8,128)(2,1)S(1)}, u32[]{:S(2)}, u32[]{:S(2)}) collective-permute-start(bf16[1,464,128]{2,1,0:T(8,128)(2,1)S(1)} %get-tuple-element.73), channel_id=1, source_target_pairs={{0,3},{1,2},{2,1},{3,0},{4,7},{5,6},{6,5},{7,4},{8,11},{9,10},{10,... | collective-permute-start | bytes 356360 | tf_op jit(solution)/shard_map/ppermute | solution.py:54
  93.3 2.7 %collective-permute-start.15 = (bf16[1,464,128]{2,1,0:T(8,128)(2,1)S(1)}, bf16[1,464,128]{2,1,0:T(8,128)(2,1)S(1)}, u32[]{:S(2)}, u32[]{:S(2)}) collective-permute-start(bf16[1,464,128]{2,1,0:T(8,128)(2,1)S(1)} %get-tuple-element.77.refs_4_.refs_0_), channel_id=1, source_target_pairs={{0,16},{16,0},{1,17},{17,1},{2,18},{18,2},{3,19},{19,3},{4,20},{20... | collective-permute-start | bytes 356360 | tf_op jit(solution)/shard_map/ppermute | solution.py:54
  93.4 2.7 %collective-permute-start.16 = (bf16[1,464,128]{2,1,0:T(8,128)(2,1)S(1)}, bf16[1,464,128]{2,1,0:T(8,128)(2,1)S(1)}, u32[]{:S(2)}, u32[]{:S(2)}) collective-permute-start(bf16[1,464,128]{2,1,0:T(8,128)(2,1)S(1)} %collective-permute-done.12.refs_5_.refs_1_), channel_id=1, source_target_pairs={{0,16},{16,0},{1,17},{17,1},{2,18},{18,2},{3,19},{19,3},{4,20},{20... | collective-permute-start | bytes 356360 | tf_op jit(solution)/shard_map/ppermute | solution.py:54
  93.9 2.2 %collective-permute-start.17 = (bf16[1,464,128]{2,1,0:T(8,128)(2,1)S(1)}, bf16[1,464,128]{2,1,0:T(8,128)(2,1)S(1)}, u32[]{:S(2)}, u32[]{:S(2)}) collective-permute-start(bf16[1,464,128]{2,1,0:T(8,128)(2,1)S(1)} %collective-permute-done.13.refs_6_.refs_2_), channel_id=1, source_target_pairs={{0,16},{16,0},{1,17},{17,1},{2,18},{18,2},{3,19},{19,3},{4,20},{20... | collective-permute-start | bytes 356360 | tf_op jit(solution)/shard_map/ppermute | solution.py:54
  93.9 2.1 %collective-permute-start.18 = (bf16[1,464,128]{2,1,0:T(8,128)(2,1)S(1)}, bf16[1,464,128]{2,1,0:T(8,128)(2,1)S(1)}, u32[]{:S(2)}, u32[]{:S(2)}) collective-permute-start(bf16[1,464,128]{2,1,0:T(8,128)(2,1)S(1)} %collective-permute-done.14.refs_7_.refs_3_), channel_id=1, source_target_pairs={{0,16},{16,0},{1,17},{17,1},{2,18},{18,2},{3,19},{19,3},{4,20},{20... | collective-permute-start | bytes 356360 | tf_op jit(solution)/shard_map/ppermute | solution.py:54

commit v7 on v6

--- a/solution.py
+++ b/solution.py
@@ -211,6 +211,14 @@
     )(slots, text)
 
 
+def slice_tokens(size, slots, text, slot):
+    start = (size.base() ^ slot) * size.width
+    tokens = lax.dynamic_slice_in_dim(slots, start, size.width, 2)
+    words = lax.dynamic_slice_in_dim(text, start, size.width, 2).transpose(1, 0, 2)
+    parts = [tokens.reshape(3 * size.rows, size.width), words.reshape(2 * size.txt, size.width)]
+    return jnp.concatenate(parts, axis=0)[None]
+
+
 def lanes_of(head):
     return slice(head * HEAD_DIM, (head + 1) * HEAD_DIM)
 
@@ -648,7 +656,7 @@
     if size.mirrored:
         first = min(2, size.parts - 1)
         rest = [k for k in range(1, size.parts) if k != first]
-        packed = dict(zip([first], pack(size, slots, text, [first], 60 * MIB)))
+        packed = {first: slice_tokens(size, slots, text, first)}
         packed.update(zip(rest, pack(size, slots, text, rest, 60 * MIB) if rest else []))
         blocks = [mirror(packed[k], "seq", k) for k in range(1, size.parts)]
     else:

time: 97.1 us -> 96.9 us (level)
  Pallas kernels: 13.7 us -> 11.8 us
  local copies, waits for them, and re-layouts: 0.03 us -> 1.92 us
    pallas_call x3 -> x2, Pallas kernels: 4.51 us -> 2.58 us  [pack(): pl.pallas_call(functools.partial(pack_kernel, size, which), in_specs=[ANY...]
    another operation x0 -> x1, local copies, waits for them, and re-layouts: none -> 1.15 us
where the time goes in v7:
time: 96.9 us; the launch traced here: 96.6 us
  waiting for transfers between devices  36.1 us (37%)
  starting transfers between devices  25.1 us (26%)
  blocking collectives  18.9 us (20%)
  Pallas kernels  11.8 us (12%)
  between operations  2.77 us (3%)
  local copies, waits for them, and re-layouts  1.92 us (2%)
    ppermute x19, waiting for transfers between devices, mirror(): return lax.ppermute(x, axis, [(i, i ^ apart) for i in range(count)])  36.1 us
    ppermute x19, starting transfers between devices, mirror(): return lax.ppermute(x, axis, [(i, i ^ apart) for i in range(count)])  25.1 us
    psum x1, blocking collectives, on_device(): stats = lax.psum(jnp.where(mine, rewards[0], 0.0), 'img')  9.91 us
    all_gather x1, blocking collectives, join_readout(): held = lax.all_gather(sent, 'img', axis=0)  8.99 us
    pallas_call x1, Pallas kernels, backward(): pl.pallas_call(functools.partial(backward_kernel, size), in_specs=specs +...  3.86 us
    pallas_call x2, Pallas kernels, pack(): pl.pallas_call(functools.partial(pack_kernel, size, which), in_specs=[ANY...  2.58 us
    pallas_call x1, Pallas kernels, forward(): pl.pallas_call(functools.partial(forward_kernel, size), in_specs=[SMEM] +...  2.5 us
  transfers between devices with their start and end apart: 19, of which 8 were waited for; matrix products, arithmetic and copies ran while one was open for 0% of the time, Pallas kernels for 4%

profile of v7, /device:TPU:0, one launch (start us, length us, event | category | flops | bytes accessed | tf_op | source)
XLA Modules:
  0.0 96.6 jit_solution(5267323789509926752)
XLA Ops:
  0.6 0.7 constant_dynamic-slice_fusion
  1.4 0.0 copy-start
  1.4 0.0 copy-start.2
  1.4 1.1 %constant_dynamic-slice_fusion.1 = bf16[1,1,128,3,512]{4,2,3,1,0:T(8,128)(2,1)S(1)} fusion(bf16[1,1,128,3,2048]{4,2,3,1,0:T(8,128)(2,1)} %param.8, s32[]{:T(128)S(6)} %select_n.9), kind=kLoop, calls=%fused_computation.5 | loop fusion | bytes 786436 | tf_op jit(solution)/shard_map/dynamic-slice.2
  2.6 4.1 %collective-permute-start = (bf16[1,400,512]{2,1,0:T(8,128)(2,1)S(1)}, bf16[1,400,512]{2,1,0:T(8,128)(2,1)S(1)}, u32[]{:S(2)}, u32[]{:S(2)}) collective-permute-start(bf16[1,400,512]{2,1,0:T(8,128)(2,1)S(1)} %maximum_bitcast_fusion), channel_id=1, source_target_pairs={{0,2},{1,3},{2,0},{3,1},{4,6},{5,7},{6,4},{7,5},{8,10},{9,11},{10,... | collective-permute-start | bytes 1228808 | tf_op jit(solution)/shard_map/ppermute | solution.py:54
  6.7 0.0 copy-start.1
  6.7 2.2 %pack_tokens.3 = (bf16[1,400,512]{2,1,0:T(8,128)(2,1)}, bf16[1,400,512]{2,1,0:T(8,128)(2,1)}) custom-call(bf16[3,128,2048]{2,1,0:T(8,128)(2,1)} %bitcast.37, bf16[8,2,2048]{2,1,0:T(2,128)(2,1)} %bitcast.43), custom_call_target="tpu_custom_call" | custom-call | tf_op jit(solution)/shard_map/pack_tokens/pallas_call | solution.py:197
  8.9 1.4 %collective-permute-start.1 = (bf16[1,400,512]{2,1,0:T(8,128)(2,1)}, bf16[1,400,512]{2,1,0:T(8,128)(2,1)S(1)}, u32[]{:S(2)}, u32[]{:S(2)}) collective-permute-start(bf16[1,400,512]{2,1,0:T(8,128)(2,1)} %get-tuple-element.48), channel_id=1, source_target_pairs={{0,3},{1,2},{2,1},{3,0},{4,7},{5,6},{6,5},{7,4},{8,11},{9,10},{10,... | collective-permute-start | bytes 1228808 | tf_op jit(solution)/shard_map/ppermute | solution.py:54
  10.3 0.3 collective-permute-start.2
  11.3 9.9 %psum.7.refs_2_ = f32[4]{0:T(128)S(1)} all-reduce(f32[4]{0:T(128)S(1)} %compare_select_fusion), channel_id=1, replica_groups=mesh['cfg'=2,'img'=4,'seq'=4] {'img'}, use_global_device_ids=true, to_apply=%region_0.1 | all-reduce | flops 4 | bytes 32 | tf_op jit(solution)/shard_map/psum | solution.py:666
  21.8 0.0 copy-done
  21.8 0.0 copy-done.2
  21.8 0.0 copy-start.3
  21.9 0.0 copy-start.4
  21.9 0.4 pack_tokens.2.refs_0_.refs_5_
  22.3 12.3 %collective-permute-done.refs_2_.refs_7_ = bf16[1,400,512]{2,1,0:T(8,128)(2,1)S(1)} collective-permute-done((bf16[1,400,512]{2,1,0:T(8,128)(2,1)S(1)}, bf16[1,400,512]{2,1,0:T(8,128)(2,1)S(1)}, u32[]{:S(2)}, u32[]{:S(2)}) %collective-permute-start) | collective-permute-done | bytes 409632 | tf_op jit(solution)/shard_map/ppermute | solution.py:54
  34.6 0.0 collective-permute-done.1.refs_3_.refs_8_
  34.6 2.9 %collective-permute-done.2.refs_1_.refs_6_ = bf16[1,400,512]{2,1,0:T(8,128)(2,1)S(1)} collective-permute-done((bf16[1,400,512]{2,1,0:T(8,128)(2,1)}, bf16[1,400,512]{2,1,0:T(8,128)(2,1)S(1)}, u32[]{:S(2)}, u32[]{:S(2)}) %collective-permute-start.2) | collective-permute-done | bytes 409632 | tf_op jit(solution)/shard_map/ppermute | solution.py:54
  37.5 0.0 copy-done.1
  37.5 2.5 %attention_forward.1 = (bf16[4,544,512]{2,1,0:T(8,128)(2,1)S(1)}, f32[4,64,512]{2,1,0:T(8,128)S(1)}, f32[4,1,512]{2,1,0:T(1,128)S(1)}, f32[32,512]{1,0:T(8,128)S(1)}, f32[32,512]{1,0:T(8,128)S(1)}) custom-call(f32[1]{0:T(128)} %bitcast.35.guidance, bf16[1,400,512]{2,1,0:T(8,128)(2,1)S(1)} %pack_tokens.2.refs_0_.refs_5_, ...), custom_call_target="tpu_custom_call" | custom-call | tf_op jit(solution)/shard_map/attention_forward/pallas_call | solution.py:306
  40.1 0.1 collective-permute-start.3
  40.8 0.6 collective-permute-done.3.other
  41.4 0.0 copy-done.3
  41.4 0.0 copy-done.4
  41.4 0.1 combine_branches.1.refs_0_
  41.5 3.6 %collective-permute-start.6 = (bf16[32,640]{1,0:T(8,128)(2,1)S(1)}, bf16[32,640]{1,0:T(8,128)(2,1)S(1)}, u32[]{:S(2)}, u32[]{:S(2)}) collective-permute-start(bf16[32,640]{1,0:T(8,128)(2,1)S(1)} %combine_branches.1.refs_0_), channel_id=1, source_target_pairs={{0,3},{1,2},{2,1},{3,0},{4,7},{5,6},{6,5},{7,4},{8,11},{9,10},{10,... | collective-permute-start | bytes 122888 | tf_op jit(solution)/shard_map/ppermute | solution.py:54
  45.1 4.2 %collective-permute-start.5 = (bf16[32,640]{1,0:T(8,128)(2,1)S(1)}, bf16[32,640]{1,0:T(8,128)(2,1)S(1)}, u32[]{:S(2)}, u32[]{:S(2)}) collective-permute-start(bf16[32,640]{1,0:T(8,128)(2,1)S(1)} %combine_branches.1.refs_0_), channel_id=1, source_target_pairs={{0,2},{1,3},{2,0},{3,1},{4,6},{5,7},{6,4},{7,5},{8,10},{9,11},{10,... | collective-permute-start | bytes 122888 | tf_op jit(solution)/shard_map/ppermute | solution.py:54
  49.3 0.5 collective-permute-start.4
  49.8 0.0 collective-permute-done.6.refs_3_
  49.8 2.2 %collective-permute-done.5.refs_2_ = bf16[32,640]{1,0:T(8,128)(2,1)S(1)} collective-permute-done((bf16[32,640]{1,0:T(8,128)(2,1)S(1)}, bf16[32,640]{1,0:T(8,128)(2,1)S(1)}, u32[]{:S(2)}, u32[]{:S(2)}) %collective-permute-start.5) | collective-permute-done | bytes 40992 | tf_op jit(solution)/shard_map/ppermute | solution.py:54
  52.0 1.3 %collective-permute-done.4.refs_1_ = bf16[32,640]{1,0:T(8,128)(2,1)S(1)} collective-permute-done((bf16[32,640]{1,0:T(8,128)(2,1)S(1)}, bf16[32,640]{1,0:T(8,128)(2,1)S(1)}, u32[]{:S(2)}, u32[]{:S(2)}) %collective-permute-start.4) | collective-permute-done | bytes 40992 | tf_op jit(solution)/shard_map/ppermute | solution.py:54
  53.3 0.2 gather_guided.1.refs_3_
  53.5 0.1 collective-permute-start.7
  53.6 1.3 %collective-permute-done.7.refs_4_ = f32[40,512]{1,0:T(8,128)S(1)} collective-permute-done((f32[40,512]{1,0:T(8,128)S(1)}, f32[40,512]{1,0:T(8,128)S(1)}, u32[]{:S(2)}, u32[]{:S(2)}) %collective-permute-start.7) | collective-permute-done | bytes 81952 | tf_op jit(solution)/shard_map/ppermute | solution.py:54
  54.8 3.9 %attention_backward.1 = (f32[1,1]{1,0:T(1,128)}, f32[64,512]{1,0:T(8,128)S(1)}, bf16[1,336,384]{2,1,0:T(8,128)(2,1)S(1)}, bf16[1,336,384]{2,1,0:T(8,128)(2,1)S(1...) custom-call(f32[1]{0:T(128)S(6)} %copy.16.rate.refs_0_, ...), custom_call_target="tpu_custom_call" | custom-call | tf_op jit(solution)/shard_map/attention_backward/pallas_call | solution.py:526
  58.7 0.2 collective-permute-start.11
  58.9 1.8 %collective-permute-start.8 = (bf16[1,336,384]{2,1,0:T(8,128)(2,1)S(1)}, bf16[1,336,384]{2,1,0:T(8,128)(2,1)S(1)}, u32[]{:S(2)}, u32[]{:S(2)}) collective-permute-start(bf16[1,336,384]{2,1,0:T(8,128)(2,1)S(1)} %get-tuple-element.59), channel_id=1, source_target_pairs={{0,2},{1,3},{2,0},{3,1},{4,6},{5,7},{6,4},{7,5},{8,10},{9,11},{10,... | collective-permute-start | bytes 774152 | tf_op jit(solution)/shard_map/ppermute | solution.py:54
  60.7 1.9 %collective-permute-start.9 = (bf16[1,336,384]{2,1,0:T(8,128)(2,1)S(1)}, bf16[1,336,384]{2,1,0:T(8,128)(2,1)S(1)}, u32[]{:S(2)}, u32[]{:S(2)}) collective-permute-start(bf16[1,336,384]{2,1,0:T(8,128)(2,1)S(1)} %get-tuple-element.60), channel_id=1, source_target_pairs={{0,3},{1,2},{2,1},{3,0},{4,7},{5,6},{6,5},{7,4},{8,11},{9,10},{10,... | collective-permute-start | bytes 774152 | tf_op jit(solution)/shard_map/ppermute | solution.py:54
  62.6 0.0 collective-permute-done.11
  62.6 9.0 %all-gather = bf16[256,512]{1,0:T(8,128)(2,1)S(1)} all-gather(bf16[64,512]{1,0:T(8,128)(2,1)S(1)} %add_convert_fusion), channel_id=2, replica_groups=mesh['cfg'=2,'img'=4,'seq'=4] {'img'}, dimensions={0}, use_global_device_ids=true | all-gather | bytes 327680 | tf_op jit(solution)/shard_map/all_gather | solution.py:609
  71.7 0.1 collective-permute-start.12
  71.8 2.0 %collective-permute-start.10 = (bf16[1,336,384]{2,1,0:T(8,128)(2,1)S(1)}, bf16[1,336,384]{2,1,0:T(8,128)(2,1)S(1)}, u32[]{:S(2)}, u32[]{:S(2)}) collective-permute-start(bf16[1,336,384]{2,1,0:T(8,128)(2,1)S(1)} %get-tuple-element.61), channel_id=1, source_target_pairs={{0,1},{1,0},{2,3},{3,2},{4,5},{5,4},{6,7},{7,6},{8,9},{9,8},{10,11... | collective-permute-start | bytes 774152 | tf_op jit(solution)/shard_map/ppermute | solution.py:54
  73.8 1.1 %collective-permute-start.13 = (bf16[1,464,128]{2,1,0:T(8,128)(2,1)S(1)}, bf16[1,464,128]{2,1,0:T(8,128)(2,1)S(1)}, u32[]{:S(2)}, u32[]{:S(2)}) collective-permute-start(bf16[1,464,128]{2,1,0:T(8,128)(2,1)S(1)} %get-tuple-element.72), channel_id=1, source_target_pairs={{0,2},{1,3},{2,0},{3,1},{4,6},{5,7},{6,4},{7,5},{8,10},{9,11},{10,... | collective-permute-start | bytes 356360 | tf_op jit(solution)/shard_map/ppermute | solution.py:54
  74.9 7.0 %collective-permute-done.12.refs_5_.refs_1_ = bf16[1,464,128]{2,1,0:T(8,128)(2,1)S(1)} collective-permute-done((bf16[1,464,128]{2,1,0:T(8,128)(2,1)S(1)}, bf16[1,464,128]{2,1,0:T(8,128)(2,1)S(1)}, u32[]{:S(2)}, u32[]{:S(2)}) %collective-permute-start.12) | collective-permute-done | bytes 118816 | tf_op jit(solution)/shard_map/ppermute | solution.py:54
  81.9 2.7 %collective-permute-start.14 = (bf16[1,464,128]{2,1,0:T(8,128)(2,1)S(1)}, bf16[1,464,128]{2,1,0:T(8,128)(2,1)S(1)}, u32[]{:S(2)}, u32[]{:S(2)}) collective-permute-start(bf16[1,464,128]{2,1,0:T(8,128)(2,1)S(1)} %get-tuple-element.73), channel_id=1, source_target_pairs={{0,3},{1,2},{2,1},{3,0},{4,7},{5,6},{6,5},{7,4},{8,11},{9,10},{10,... | collective-permute-start | bytes 356360 | tf_op jit(solution)/shard_map/ppermute | solution.py:54
  84.6 8.4 %collective-permute-done.13.refs_6_.refs_2_ = bf16[1,464,128]{2,1,0:T(8,128)(2,1)S(1)} collective-permute-done((bf16[1,464,128]{2,1,0:T(8,128)(2,1)S(1)}, bf16[1,464,128]{2,1,0:T(8,128)(2,1)S(1)}, u32[]{:S(2)}, u32[]{:S(2)}) %collective-permute-start.13) | collective-permute-done | bytes 118816 | tf_op jit(solution)/shard_map/ppermute | solution.py:54
  93.1 0.0 collective-permute-start.15
  93.1 0.0 collective-permute-done.14.refs_7_.refs_3_
  93.1 0.5 collective-permute-start.16
  93.6 0.0 collective-permute-done.8.refs_2_
  93.6 0.1 collective-permute-start.17
  93.7 0.0 collective-permute-done.9.refs_3_
  93.7 0.4 collective-permute-start.18
  94.1 0.0 collective-permute-done.10.refs_1_
  94.1 1.6 %home_tokens.1 = (bf16[3,128,2048]{2,1,0:T(8,128)(2,1)}, bf16[8,2,2048]{2,1,0:T(2,128)(2,1)}) custom-call(bf16[64,2048]{1,0:T(8,128)(2,1)S(1)} %bitcast.41, bf16[1,336,384]{2,1,0:T(8,128)(2,1)S(1)} %get-tuple-element.58.refs_0_, bf16[1,336,384]{2,1,0:T(8,128)(2,1)S(1)} %collective-permute-done.10.refs_1_, ...), custom_call_target="tpu_custom_call" | custom-call | tf_op jit(solution)/shard_map/home_tokens/pallas_call | solution.py:584
  95.7 0.0 collective-permute-done.15.refs_4_
  95.7 0.0 collective-permute-done.16.refs_5_
  95.7 0.0 collective-permute-done.17.refs_6_
  95.7 0.0 collective-permute-done.18.refs_7_
  95.8 0.9 place_readout_grad.1
  (5 shorter events, 0.1 us)
Async XLA Ops:
  1.4 20.4 %copy-start = (bf16[1,1,128,3,2048]{4,2,3,1,0:T(8,128)(2,1)S(1)}, bf16[1,1,128,3,2048]{4,2,3,1,0:T(8,128)(2,1)}, u32[]{:S(2)}) copy-start(bf16[1,1,128,3,2048]{4,2,3,1,0:T(8,128)(2,1)} %param.8) | copy-start | bytes 4718596
  1.4 20.4 %copy-start.2 = (bf16[1,1,8,2,2048]{4,3,2,1,0:T(2,128)(2,1)S(1)}, bf16[1,1,8,2,2048]{4,3,2,1,0:T(2,128)(2,1)}, u32[]{:S(2)}) copy-start(bf16[1,1,8,2,2048]{4,3,2,1,0:T(2,128)(2,1)} %param.9) | copy-start | bytes 196612
  2.6 32.0 %collective-permute-start = (bf16[1,400,512]{2,1,0:T(8,128)(2,1)S(1)}, bf16[1,400,512]{2,1,0:T(8,128)(2,1)S(1)}, u32[]{:S(2)}, u32[]{:S(2)}) collective-permute-start(bf16[1,400,512]{2,1,0:T(8,128)(2,1)S(1)} %maximum_bitcast_fusion), channel_id=1, source_target_pairs={{0,2},{1,3},{2,0},{3,1},{4,6},{5,7},{6,4},{7,5},{8,10},{9,11},{10,... | collective-permute-start | bytes 1228808 | tf_op jit(solution)/shard_map/ppermute | solution.py:54
  6.7 30.8 %copy-start.1 = (bf16[2048,64]{0,1:T(8,128)(2,1)S(1)}, bf16[2048,64]{0,1:T(8,128)(2,1)}, u32[]{:S(2)}) copy-start(bf16[2048,64]{0,1:T(8,128)(2,1)} %param.10) | copy-start | bytes 786436
  8.9 25.7 %collective-permute-start.1 = (bf16[1,400,512]{2,1,0:T(8,128)(2,1)}, bf16[1,400,512]{2,1,0:T(8,128)(2,1)S(1)}, u32[]{:S(2)}, u32[]{:S(2)}) collective-permute-start(bf16[1,400,512]{2,1,0:T(8,128)(2,1)} %get-tuple-element.48), channel_id=1, source_target_pairs={{0,3},{1,2},{2,1},{3,0},{4,7},{5,6},{6,5},{7,4},{8,11},{9,10},{10,... | collective-permute-start | bytes 1228808 | tf_op jit(solution)/shard_map/ppermute | solution.py:54
  10.3 27.2 %collective-permute-start.2 = (bf16[1,400,512]{2,1,0:T(8,128)(2,1)}, bf16[1,400,512]{2,1,0:T(8,128)(2,1)S(1)}, u32[]{:S(2)}, u32[]{:S(2)}) collective-permute-start(bf16[1,400,512]{2,1,0:T(8,128)(2,1)} %get-tuple-element.49), channel_id=1, source_target_pairs={{0,1},{1,0},{2,3},{3,2},{4,5},{5,4},{6,7},{7,6},{8,9},{9,8},{10,11... | collective-permute-start | bytes 1228808 | tf_op jit(solution)/shard_map/ppermute | solution.py:54
  21.8 19.5 %copy-start.3 = (f32[1,128,64]{1,2,0:T(8,128)S(1)}, f32[1,128,64]{1,2,0:T(8,128)}, u32[]{:S(2)}) copy-start(f32[1,128,64]{1,2,0:T(8,128)} %param.12) | copy-start | bytes 98308
  21.9 19.5 %copy-start.4 = (f32[1,128,64]{1,2,0:T(8,128)S(1)}, f32[1,128,64]{1,2,0:T(8,128)}, u32[]{:S(2)}) copy-start(f32[1,128,64]{1,2,0:T(8,128)} %param.11) | copy-start | bytes 98308
  40.1 1.3 %collective-permute-start.3 = (f32[32,512]{1,0:T(8,128)S(1)}, f32[32,512]{1,0:T(8,128)S(1)}, u32[]{:S(2)}, u32[]{:S(2)}) collective-permute-start(f32[32,512]{1,0:T(8,128)S(1)} %get-tuple-element.54), channel_id=1, source_target_pairs={{0,16},{16,0},{1,17},{17,1},{2,18},{18,2},{3,19},{19,3},{4,20},{20... | collective-permute-start | bytes 196616 | tf_op jit(solution)/shard_map/ppermute | solution.py:54
  41.5 8.3 %collective-permute-start.6 = (bf16[32,640]{1,0:T(8,128)(2,1)S(1)}, bf16[32,640]{1,0:T(8,128)(2,1)S(1)}, u32[]{:S(2)}, u32[]{:S(2)}) collective-permute-start(bf16[32,640]{1,0:T(8,128)(2,1)S(1)} %combine_branches.1.refs_0_), channel_id=1, source_target_pairs={{0,3},{1,2},{2,1},{3,0},{4,7},{5,6},{6,5},{7,4},{8,11},{9,10},{10,... | collective-permute-start | bytes 122888 | tf_op jit(solution)/shard_map/ppermute | solution.py:54
  45.1 6.9 %collective-permute-start.5 = (bf16[32,640]{1,0:T(8,128)(2,1)S(1)}, bf16[32,640]{1,0:T(8,128)(2,1)S(1)}, u32[]{:S(2)}, u32[]{:S(2)}) collective-permute-start(bf16[32,640]{1,0:T(8,128)(2,1)S(1)} %combine_branches.1.refs_0_), channel_id=1, source_target_pairs={{0,2},{1,3},{2,0},{3,1},{4,6},{5,7},{6,4},{7,5},{8,10},{9,11},{10,... | collective-permute-start | bytes 122888 | tf_op jit(solution)/shard_map/ppermute | solution.py:54
  49.3 4.0 %collective-permute-start.4 = (bf16[32,640]{1,0:T(8,128)(2,1)S(1)}, bf16[32,640]{1,0:T(8,128)(2,1)S(1)}, u32[]{:S(2)}, u32[]{:S(2)}) collective-permute-start(bf16[32,640]{1,0:T(8,128)(2,1)S(1)} %combine_branches.1.refs_0_), channel_id=1, source_target_pairs={{0,1},{1,0},{2,3},{3,2},{4,5},{5,4},{6,7},{7,6},{8,9},{9,8},{10,11... | collective-permute-start | bytes 122888 | tf_op jit(solution)/shard_map/ppermute | solution.py:54
  53.5 1.3 %collective-permute-start.7 = (f32[40,512]{1,0:T(8,128)S(1)}, f32[40,512]{1,0:T(8,128)S(1)}, u32[]{:S(2)}, u32[]{:S(2)}) collective-permute-start(f32[40,512]{1,0:T(8,128)S(1)} %gather_guided.1.refs_3_), channel_id=1, source_target_pairs={{0,16},{16,0},{1,17},{17,1},{2,18},{18,2},{3,19},{19,3},{4,20},{20... | collective-permute-start | bytes 245768 | tf_op jit(solution)/shard_map/ppermute | solution.py:54
  58.7 3.9 %collective-permute-start.11 = (f32[64,512]{1,0:T(8,128)S(1)}, f32[64,512]{1,0:T(8,128)S(1)}, u32[]{:S(2)}, u32[]{:S(2)}) collective-permute-start(f32[64,512]{1,0:T(8,128)S(1)} %get-tuple-element.65), channel_id=1, source_target_pairs={{0,16},{16,0},{1,17},{17,1},{2,18},{18,2},{3,19},{19,3},{4,20},{20... | collective-permute-start | bytes 393224 | tf_op jit(solution)/shard_map/ppermute | solution.py:54
  58.9 34.7 %collective-permute-start.8 = (bf16[1,336,384]{2,1,0:T(8,128)(2,1)S(1)}, bf16[1,336,384]{2,1,0:T(8,128)(2,1)S(1)}, u32[]{:S(2)}, u32[]{:S(2)}) collective-permute-start(bf16[1,336,384]{2,1,0:T(8,128)(2,1)S(1)} %get-tuple-element.59), channel_id=1, source_target_pairs={{0,2},{1,3},{2,0},{3,1},{4,6},{5,7},{6,4},{7,5},{8,10},{9,11},{10,... | collective-permute-start | bytes 774152 | tf_op jit(solution)/shard_map/ppermute | solution.py:54
  60.7 33.0 %collective-permute-start.9 = (bf16[1,336,384]{2,1,0:T(8,128)(2,1)S(1)}, bf16[1,336,384]{2,1,0:T(8,128)(2,1)S(1)}, u32[]{:S(2)}, u32[]{:S(2)}) collective-permute-start(bf16[1,336,384]{2,1,0:T(8,128)(2,1)S(1)} %get-tuple-element.60), channel_id=1, source_target_pairs={{0,3},{1,2},{2,1},{3,0},{4,7},{5,6},{6,5},{7,4},{8,11},{9,10},{10,... | collective-permute-start | bytes 774152 | tf_op jit(solution)/shard_map/ppermute | solution.py:54
  71.7 10.2 %collective-permute-start.12 = (bf16[1,464,128]{2,1,0:T(8,128)(2,1)S(1)}, bf16[1,464,128]{2,1,0:T(8,128)(2,1)S(1)}, u32[]{:S(2)}, u32[]{:S(2)}) collective-permute-start(bf16[1,464,128]{2,1,0:T(8,128)(2,1)S(1)} %get-tuple-element.71), channel_id=1, source_target_pairs={{0,1},{1,0},{2,3},{3,2},{4,5},{5,4},{6,7},{7,6},{8,9},{9,8},{10,11... | collective-permute-start | bytes 356360 | tf_op jit(solution)/shard_map/ppermute | solution.py:54
  71.8 22.3 %collective-permute-start.10 = (bf16[1,336,384]{2,1,0:T(8,128)(2,1)S(1)}, bf16[1,336,384]{2,1,0:T(8,128)(2,1)S(1)}, u32[]{:S(2)}, u32[]{:S(2)}) collective-permute-start(bf16[1,336,384]{2,1,0:T(8,128)(2,1)S(1)} %get-tuple-element.61), channel_id=1, source_target_pairs={{0,1},{1,0},{2,3},{3,2},{4,5},{5,4},{6,7},{7,6},{8,9},{9,8},{10,11... | collective-permute-start | bytes 774152 | tf_op jit(solution)/shard_map/ppermute | solution.py:54
  73.8 19.3 %collective-permute-start.13 = (bf16[1,464,128]{2,1,0:T(8,128)(2,1)S(1)}, bf16[1,464,128]{2,1,0:T(8,128)(2,1)S(1)}, u32[]{:S(2)}, u32[]{:S(2)}) collective-permute-start(bf16[1,464,128]{2,1,0:T(8,128)(2,1)S(1)} %get-tuple-element.72), channel_id=1, source_target_pairs={{0,2},{1,3},{2,0},{3,1},{4,6},{5,7},{6,4},{7,5},{8,10},{9,11},{10,... | collective-permute-start | bytes 356360 | tf_op jit(solution)/shard_map/ppermute | solution.py:54
  81.9 11.1 %collective-permute-start.14 = (bf16[1,464,128]{2,1,0:T(8,128)(2,1)S(1)}, bf16[1,464,128]{2,1,0:T(8,128)(2,1)S(1)}, u32[]{:S(2)}, u32[]{:S(2)}) collective-permute-start(bf16[1,464,128]{2,1,0:T(8,128)(2,1)S(1)} %get-tuple-element.73), channel_id=1, source_target_pairs={{0,3},{1,2},{2,1},{3,0},{4,7},{5,6},{6,5},{7,4},{8,11},{9,10},{10,... | collective-permute-start | bytes 356360 | tf_op jit(solution)/shard_map/ppermute | solution.py:54
  93.1 2.7 %collective-permute-start.15 = (bf16[1,464,128]{2,1,0:T(8,128)(2,1)S(1)}, bf16[1,464,128]{2,1,0:T(8,128)(2,1)S(1)}, u32[]{:S(2)}, u32[]{:S(2)}) collective-permute-start(bf16[1,464,128]{2,1,0:T(8,128)(2,1)S(1)} %get-tuple-element.77.refs_4_.refs_0_), channel_id=1, source_target_pairs={{0,16},{16,0},{1,17},{17,1},{2,18},{18,2},{3,19},{19,3},{4,20},{20... | collective-permute-start | bytes 356360 | tf_op jit(solution)/shard_map/ppermute | solution.py:54
  93.1 2.7 %collective-permute-start.16 = (bf16[1,464,128]{2,1,0:T(8,128)(2,1)S(1)}, bf16[1,464,128]{2,1,0:T(8,128)(2,1)S(1)}, u32[]{:S(2)}, u32[]{:S(2)}) collective-permute-start(bf16[1,464,128]{2,1,0:T(8,128)(2,1)S(1)} %collective-permute-done.12.refs_5_.refs_1_), channel_id=1, source_target_pairs={{0,16},{16,0},{1,17},{17,1},{2,18},{18,2},{3,19},{19,3},{4,20},{20... | collective-permute-start | bytes 356360 | tf_op jit(solution)/shard_map/ppermute | solution.py:54
  93.6 2.2 %collective-permute-start.17 = (bf16[1,464,128]{2,1,0:T(8,128)(2,1)S(1)}, bf16[1,464,128]{2,1,0:T(8,128)(2,1)S(1)}, u32[]{:S(2)}, u32[]{:S(2)}) collective-permute-start(bf16[1,464,128]{2,1,0:T(8,128)(2,1)S(1)} %collective-permute-done.13.refs_6_.refs_2_), channel_id=1, source_target_pairs={{0,16},{16,0},{1,17},{17,1},{2,18},{18,2},{3,19},{19,3},{4,20},{20... | collective-permute-start | bytes 356360 | tf_op jit(solution)/shard_map/ppermute | solution.py:54
  93.7 2.1 %collective-permute-start.18 = (bf16[1,464,128]{2,1,0:T(8,128)(2,1)S(1)}, bf16[1,464,128]{2,1,0:T(8,128)(2,1)S(1)}, u32[]{:S(2)}, u32[]{:S(2)}) collective-permute-start(bf16[1,464,128]{2,1,0:T(8,128)(2,1)S(1)} %collective-permute-done.14.refs_7_.refs_3_), channel_id=1, source_target_pairs={{0,16},{16,0},{1,17},{17,1},{2,18},{18,2},{3,19},{19,3},{4,20},{20... | collective-permute-start | bytes 356360 | tf_op jit(solution)/shard_map/ppermute | solution.py:54

commit v8 on v7

--- a/solution.py
+++ b/solution.py
@@ -138,7 +138,9 @@
 
 def exchange(size, blocks):
     if size.mirrored:
-        return far_first(spread(size, blocks))
+        own, near, *far = spread(size, blocks)
+        far, near = lax.optimization_barrier((far[::-1], near))
+        return [own, near] + list(far)[::-1]
     return [lax.all_to_all(blocks[0], "seq", split_axis=0, concat_axis=0, tiled=True)]
 
 

time: 96.9 us -> 96.8 us (level)
  no operation moved by 1% of the time
where the time goes in v8:
time: 96.8 us; the launch traced here: 96.5 us
  waiting for transfers between devices  35.5 us (37%)
  starting transfers between devices  25.6 us (26%)
  blocking collectives  18.9 us (20%)
  Pallas kernels  11.8 us (12%)
  between operations  2.76 us (3%)
  local copies, waits for them, and re-layouts  1.92 us (2%)
    ppermute x19, waiting for transfers between devices, mirror(): return lax.ppermute(x, axis, [(i, i ^ apart) for i in range(count)])  35.5 us
    ppermute x19, starting transfers between devices, mirror(): return lax.ppermute(x, axis, [(i, i ^ apart) for i in range(count)])  25.6 us
    psum x1, blocking collectives, on_device(): stats = lax.psum(jnp.where(mine, rewards[0], 0.0), 'img')  9.91 us
    all_gather x1, blocking collectives, join_readout(): held = lax.all_gather(sent, 'img', axis=0)  8.99 us
    pallas_call x1, Pallas kernels, backward(): pl.pallas_call(functools.partial(backward_kernel, size), in_specs=specs +...  3.86 us
    pallas_call x2, Pallas kernels, pack(): pl.pallas_call(functools.partial(pack_kernel, size, which), in_specs=[ANY...  2.58 us
    pallas_call x1, Pallas kernels, forward(): pl.pallas_call(functools.partial(forward_kernel, size), in_specs=[SMEM] +...  2.5 us
  transfers between devices with their start and end apart: 19, of which 8 were waited for; matrix products, arithmetic and copies ran while one was open for 0% of the time, Pallas kernels for 4%

profile of v8, /device:TPU:0, one launch (start us, length us, event | category | flops | bytes accessed | tf_op | source)
XLA Modules:
  0.0 96.5 jit_solution(9904129597343198601)
XLA Ops:
  0.6 0.7 constant_dynamic-slice_fusion
  1.4 0.0 copy-start
  1.4 0.0 copy-start.2
  1.4 1.1 %constant_dynamic-slice_fusion.1 = bf16[1,1,128,3,512]{4,2,3,1,0:T(8,128)(2,1)S(1)} fusion(bf16[1,1,128,3,2048]{4,2,3,1,0:T(8,128)(2,1)} %param.8, s32[]{:T(128)S(6)} %select_n.9), kind=kLoop, calls=%fused_computation.5 | loop fusion | bytes 786436 | tf_op jit(solution)/shard_map/dynamic-slice.2
  2.6 4.1 %collective-permute-start = (bf16[1,400,512]{2,1,0:T(8,128)(2,1)S(1)}, bf16[1,400,512]{2,1,0:T(8,128)(2,1)S(1)}, u32[]{:S(2)}, u32[]{:S(2)}) collective-permute-start(bf16[1,400,512]{2,1,0:T(8,128)(2,1)S(1)} %maximum_bitcast_fusion), channel_id=1, source_target_pairs={{0,2},{1,3},{2,0},{3,1},{4,6},{5,7},{6,4},{7,5},{8,10},{9,11},{10,... | collective-permute-start | bytes 1228808 | tf_op jit(solution)/shard_map/ppermute | solution.py:54
  6.7 0.0 copy-start.1
  6.7 2.2 %pack_tokens.3 = (bf16[1,400,512]{2,1,0:T(8,128)(2,1)}, bf16[1,400,512]{2,1,0:T(8,128)(2,1)}) custom-call(bf16[3,128,2048]{2,1,0:T(8,128)(2,1)} %bitcast.37, bf16[8,2,2048]{2,1,0:T(2,128)(2,1)} %bitcast.43), custom_call_target="tpu_custom_call" | custom-call | tf_op jit(solution)/shard_map/pack_tokens/pallas_call | solution.py:199
  8.9 1.4 %collective-permute-start.1 = (bf16[1,400,512]{2,1,0:T(8,128)(2,1)}, bf16[1,400,512]{2,1,0:T(8,128)(2,1)S(1)}, u32[]{:S(2)}, u32[]{:S(2)}) collective-permute-start(bf16[1,400,512]{2,1,0:T(8,128)(2,1)} %get-tuple-element.48), channel_id=1, source_target_pairs={{0,3},{1,2},{2,1},{3,0},{4,7},{5,6},{6,5},{7,4},{8,11},{9,10},{10,... | collective-permute-start | bytes 1228808 | tf_op jit(solution)/shard_map/ppermute | solution.py:54
  10.3 0.3 collective-permute-start.2
  11.3 9.9 %psum.7.refs_2_ = f32[4]{0:T(128)S(1)} all-reduce(f32[4]{0:T(128)S(1)} %compare_select_fusion), channel_id=1, replica_groups=mesh['cfg'=2,'img'=4,'seq'=4] {'img'}, use_global_device_ids=true, to_apply=%region_0.1 | all-reduce | flops 4 | bytes 32 | tf_op jit(solution)/shard_map/psum | solution.py:668
  21.8 0.0 copy-done
  21.8 0.0 copy-done.2
  21.8 0.0 copy-start.3
  21.9 0.0 copy-start.4
  21.9 0.4 pack_tokens.2.refs_0_.refs_5_
  22.3 12.3 %collective-permute-done.refs_2_.refs_7_ = bf16[1,400,512]{2,1,0:T(8,128)(2,1)S(1)} collective-permute-done((bf16[1,400,512]{2,1,0:T(8,128)(2,1)S(1)}, bf16[1,400,512]{2,1,0:T(8,128)(2,1)S(1)}, u32[]{:S(2)}, u32[]{:S(2)}) %collective-permute-start) | collective-permute-done | bytes 409632 | tf_op jit(solution)/shard_map/ppermute | solution.py:54
  34.6 0.0 collective-permute-done.1.refs_3_.refs_8_
  34.6 2.9 %collective-permute-done.2.refs_1_.refs_6_ = bf16[1,400,512]{2,1,0:T(8,128)(2,1)S(1)} collective-permute-done((bf16[1,400,512]{2,1,0:T(8,128)(2,1)}, bf16[1,400,512]{2,1,0:T(8,128)(2,1)S(1)}, u32[]{:S(2)}, u32[]{:S(2)}) %collective-permute-start.2) | collective-permute-done | bytes 409632 | tf_op jit(solution)/shard_map/ppermute | solution.py:54
  37.5 0.0 copy-done.1
  37.5 2.5 %attention_forward.1 = (bf16[4,544,512]{2,1,0:T(8,128)(2,1)S(1)}, f32[4,64,512]{2,1,0:T(8,128)S(1)}, f32[4,1,512]{2,1,0:T(1,128)S(1)}, f32[32,512]{1,0:T(8,128)S(1)}, f32[32,512]{1,0:T(8,128)S(1)}) custom-call(f32[1]{0:T(128)} %bitcast.35.guidance, bf16[1,400,512]{2,1,0:T(8,128)(2,1)S(1)} %pack_tokens.2.refs_0_.refs_5_, ...), custom_call_target="tpu_custom_call" | custom-call | tf_op jit(solution)/shard_map/attention_forward/pallas_call | solution.py:308
  40.1 0.1 collective-permute-start.3
  40.8 0.6 collective-permute-done.3.other
  41.4 0.0 copy-done.3
  41.4 0.0 copy-done.4
  41.4 0.1 combine_branches.1.refs_0_
  41.5 3.6 %collective-permute-start.6 = (bf16[32,640]{1,0:T(8,128)(2,1)S(1)}, bf16[32,640]{1,0:T(8,128)(2,1)S(1)}, u32[]{:S(2)}, u32[]{:S(2)}) collective-permute-start(bf16[32,640]{1,0:T(8,128)(2,1)S(1)} %combine_branches.1.refs_0_), channel_id=1, source_target_pairs={{0,3},{1,2},{2,1},{3,0},{4,7},{5,6},{6,5},{7,4},{8,11},{9,10},{10,... | collective-permute-start | bytes 122888 | tf_op jit(solution)/shard_map/ppermute | solution.py:54
  45.1 4.2 %collective-permute-start.5 = (bf16[32,640]{1,0:T(8,128)(2,1)S(1)}, bf16[32,640]{1,0:T(8,128)(2,1)S(1)}, u32[]{:S(2)}, u32[]{:S(2)}) collective-permute-start(bf16[32,640]{1,0:T(8,128)(2,1)S(1)} %combine_branches.1.refs_0_), channel_id=1, source_target_pairs={{0,2},{1,3},{2,0},{3,1},{4,6},{5,7},{6,4},{7,5},{8,10},{9,11},{10,... | collective-permute-start | bytes 122888 | tf_op jit(solution)/shard_map/ppermute | solution.py:54
  49.3 0.5 collective-permute-start.4
  49.8 0.0 collective-permute-done.6.refs_3_
  49.8 2.2 %collective-permute-done.5.refs_2_ = bf16[32,640]{1,0:T(8,128)(2,1)S(1)} collective-permute-done((bf16[32,640]{1,0:T(8,128)(2,1)S(1)}, bf16[32,640]{1,0:T(8,128)(2,1)S(1)}, u32[]{:S(2)}, u32[]{:S(2)}) %collective-permute-start.5) | collective-permute-done | bytes 40992 | tf_op jit(solution)/shard_map/ppermute | solution.py:54
  52.0 1.3 %collective-permute-done.4.refs_1_ = bf16[32,640]{1,0:T(8,128)(2,1)S(1)} collective-permute-done((bf16[32,640]{1,0:T(8,128)(2,1)S(1)}, bf16[32,640]{1,0:T(8,128)(2,1)S(1)}, u32[]{:S(2)}, u32[]{:S(2)}) %collective-permute-start.4) | collective-permute-done | bytes 40992 | tf_op jit(solution)/shard_map/ppermute | solution.py:54
  53.3 0.2 gather_guided.1.refs_3_
  53.5 0.1 collective-permute-start.7
  53.6 1.3 %collective-permute-done.7.refs_4_ = f32[40,512]{1,0:T(8,128)S(1)} collective-permute-done((f32[40,512]{1,0:T(8,128)S(1)}, f32[40,512]{1,0:T(8,128)S(1)}, u32[]{:S(2)}, u32[]{:S(2)}) %collective-permute-start.7) | collective-permute-done | bytes 81952 | tf_op jit(solution)/shard_map/ppermute | solution.py:54
  54.8 3.9 %attention_backward.1 = (f32[1,1]{1,0:T(1,128)}, f32[64,512]{1,0:T(8,128)S(1)}, bf16[1,336,384]{2,1,0:T(8,128)(2,1)S(1)}, bf16[1,336,384]{2,1,0:T(8,128)(2,1)S(1...) custom-call(f32[1]{0:T(128)S(6)} %copy.16.rate.refs_0_, ...), custom_call_target="tpu_custom_call" | custom-call | tf_op jit(solution)/shard_map/attention_backward/pallas_call | solution.py:528
  58.7 0.2 collective-permute-start.11
  58.9 2.8 %collective-permute-start.8 = (bf16[1,336,384]{2,1,0:T(8,128)(2,1)S(1)}, bf16[1,336,384]{2,1,0:T(8,128)(2,1)S(1)}, u32[]{:S(2)}, u32[]{:S(2)}) collective-permute-start(bf16[1,336,384]{2,1,0:T(8,128)(2,1)S(1)} %get-tuple-element.59), channel_id=1, source_target_pairs={{0,3},{1,2},{2,1},{3,0},{4,7},{5,6},{6,5},{7,4},{8,11},{9,10},{10,... | collective-permute-start | bytes 774152 | tf_op jit(solution)/shard_map/ppermute | solution.py:54
  61.7 0.0 collective-permute-start.9
  61.7 0.0 collective-permute-done.11
  61.7 9.0 %all-gather = bf16[256,512]{1,0:T(8,128)(2,1)S(1)} all-gather(bf16[64,512]{1,0:T(8,128)(2,1)S(1)} %add_convert_fusion), channel_id=2, replica_groups=mesh['cfg'=2,'img'=4,'seq'=4] {'img'}, dimensions={0}, use_global_device_ids=true | all-gather | bytes 327680 | tf_op jit(solution)/shard_map/all_gather | solution.py:611
  70.8 1.6 %collective-permute-start.12 = (bf16[1,464,128]{2,1,0:T(8,128)(2,1)S(1)}, bf16[1,464,128]{2,1,0:T(8,128)(2,1)S(1)}, u32[]{:S(2)}, u32[]{:S(2)}) collective-permute-start(bf16[1,464,128]{2,1,0:T(8,128)(2,1)S(1)} %get-tuple-element.71), channel_id=1, source_target_pairs={{0,1},{1,0},{2,3},{3,2},{4,5},{5,4},{6,7},{7,6},{8,9},{9,8},{10,11... | collective-permute-start | bytes 356360 | tf_op jit(solution)/shard_map/ppermute | solution.py:54
  72.4 0.5 collective-permute-start.10
  72.9 2.9 %collective-permute-start.13 = (bf16[1,464,128]{2,1,0:T(8,128)(2,1)S(1)}, bf16[1,464,128]{2,1,0:T(8,128)(2,1)S(1)}, u32[]{:S(2)}, u32[]{:S(2)}) collective-permute-start(bf16[1,464,128]{2,1,0:T(8,128)(2,1)S(1)} %get-tuple-element.72), channel_id=1, source_target_pairs={{0,2},{1,3},{2,0},{3,1},{4,6},{5,7},{6,4},{7,5},{8,10},{9,11},{10,... | collective-permute-start | bytes 356360 | tf_op jit(solution)/shard_map/ppermute | solution.py:54
  75.8 1.2 %collective-permute-done.12.refs_5_.refs_1_ = bf16[1,464,128]{2,1,0:T(8,128)(2,1)S(1)} collective-permute-done((bf16[1,464,128]{2,1,0:T(8,128)(2,1)S(1)}, bf16[1,464,128]{2,1,0:T(8,128)(2,1)S(1)}, u32[]{:S(2)}, u32[]{:S(2)}) %collective-permute-start.12) | collective-permute-done | bytes 118816 | tf_op jit(solution)/shard_map/ppermute | solution.py:54
  77.0 2.3 %collective-permute-start.14 = (bf16[1,464,128]{2,1,0:T(8,128)(2,1)S(1)}, bf16[1,464,128]{2,1,0:T(8,128)(2,1)S(1)}, u32[]{:S(2)}, u32[]{:S(2)}) collective-permute-start(bf16[1,464,128]{2,1,0:T(8,128)(2,1)S(1)} %get-tuple-element.73), channel_id=1, source_target_pairs={{0,3},{1,2},{2,1},{3,0},{4,7},{5,6},{6,5},{7,4},{8,11},{9,10},{10,... | collective-permute-start | bytes 356360 | tf_op jit(solution)/shard_map/ppermute | solution.py:54
  79.3 13.7 %collective-permute-done.13.refs_6_.refs_2_ = bf16[1,464,128]{2,1,0:T(8,128)(2,1)S(1)} collective-permute-done((bf16[1,464,128]{2,1,0:T(8,128)(2,1)S(1)}, bf16[1,464,128]{2,1,0:T(8,128)(2,1)S(1)}, u32[]{:S(2)}, u32[]{:S(2)}) %collective-permute-start.13) | collective-permute-done | bytes 118816 | tf_op jit(solution)/shard_map/ppermute | solution.py:54
  92.9 0.0 collective-permute-start.15
  92.9 0.0 collective-permute-done.14.refs_7_.refs_3_
  93.0 0.5 collective-permute-start.16
  93.5 0.0 collective-permute-done.8.refs_3_
  93.5 0.1 collective-permute-start.17
  93.5 0.0 collective-permute-done.9.refs_2_
  93.5 0.4 collective-permute-start.18
  94.0 0.0 collective-permute-done.10.refs_1_
  94.0 1.6 %home_tokens.1 = (bf16[3,128,2048]{2,1,0:T(8,128)(2,1)}, bf16[8,2,2048]{2,1,0:T(2,128)(2,1)}) custom-call(bf16[64,2048]{1,0:T(8,128)(2,1)S(1)} %bitcast.41, bf16[1,336,384]{2,1,0:T(8,128)(2,1)S(1)} %get-tuple-element.58.refs_0_, bf16[1,336,384]{2,1,0:T(8,128)(2,1)S(1)} %collective-permute-done.10.refs_1_, ...), custom_call_target="tpu_custom_call" | custom-call | tf_op jit(solution)/shard_map/home_tokens/pallas_call | solution.py:586
  95.6 0.0 collective-permute-done.15.refs_4_
  95.6 0.0 collective-permute-done.16.refs_5_
  95.6 0.0 collective-permute-done.17.refs_6_
  95.6 0.0 collective-permute-done.18.refs_7_
  95.6 0.9 place_readout_grad.1
  (5 shorter events, 0.1 us)
Async XLA Ops:
  1.4 20.4 %copy-start = (bf16[1,1,128,3,2048]{4,2,3,1,0:T(8,128)(2,1)S(1)}, bf16[1,1,128,3,2048]{4,2,3,1,0:T(8,128)(2,1)}, u32[]{:S(2)}) copy-start(bf16[1,1,128,3,2048]{4,2,3,1,0:T(8,128)(2,1)} %param.8) | copy-start | bytes 4718596
  1.4 20.4 %copy-start.2 = (bf16[1,1,8,2,2048]{4,3,2,1,0:T(2,128)(2,1)S(1)}, bf16[1,1,8,2,2048]{4,3,2,1,0:T(2,128)(2,1)}, u32[]{:S(2)}) copy-start(bf16[1,1,8,2,2048]{4,3,2,1,0:T(2,128)(2,1)} %param.9) | copy-start | bytes 196612
  2.6 32.0 %collective-permute-start = (bf16[1,400,512]{2,1,0:T(8,128)(2,1)S(1)}, bf16[1,400,512]{2,1,0:T(8,128)(2,1)S(1)}, u32[]{:S(2)}, u32[]{:S(2)}) collective-permute-start(bf16[1,400,512]{2,1,0:T(8,128)(2,1)S(1)} %maximum_bitcast_fusion), channel_id=1, source_target_pairs={{0,2},{1,3},{2,0},{3,1},{4,6},{5,7},{6,4},{7,5},{8,10},{9,11},{10,... | collective-permute-start | bytes 1228808 | tf_op jit(solution)/shard_map/ppermute | solution.py:54
  6.7 30.8 %copy-start.1 = (bf16[2048,64]{0,1:T(8,128)(2,1)S(1)}, bf16[2048,64]{0,1:T(8,128)(2,1)}, u32[]{:S(2)}) copy-start(bf16[2048,64]{0,1:T(8,128)(2,1)} %param.10) | copy-start | bytes 786436
  8.9 25.7 %collective-permute-start.1 = (bf16[1,400,512]{2,1,0:T(8,128)(2,1)}, bf16[1,400,512]{2,1,0:T(8,128)(2,1)S(1)}, u32[]{:S(2)}, u32[]{:S(2)}) collective-permute-start(bf16[1,400,512]{2,1,0:T(8,128)(2,1)} %get-tuple-element.48), channel_id=1, source_target_pairs={{0,3},{1,2},{2,1},{3,0},{4,7},{5,6},{6,5},{7,4},{8,11},{9,10},{10,... | collective-permute-start | bytes 1228808 | tf_op jit(solution)/shard_map/ppermute | solution.py:54
  10.3 27.2 %collective-permute-start.2 = (bf16[1,400,512]{2,1,0:T(8,128)(2,1)}, bf16[1,400,512]{2,1,0:T(8,128)(2,1)S(1)}, u32[]{:S(2)}, u32[]{:S(2)}) collective-permute-start(bf16[1,400,512]{2,1,0:T(8,128)(2,1)} %get-tuple-element.49), channel_id=1, source_target_pairs={{0,1},{1,0},{2,3},{3,2},{4,5},{5,4},{6,7},{7,6},{8,9},{9,8},{10,11... | collective-permute-start | bytes 1228808 | tf_op jit(solution)/shard_map/ppermute | solution.py:54
  21.8 19.5 %copy-start.3 = (f32[1,128,64]{1,2,0:T(8,128)S(1)}, f32[1,128,64]{1,2,0:T(8,128)}, u32[]{:S(2)}) copy-start(f32[1,128,64]{1,2,0:T(8,128)} %param.12) | copy-start | bytes 98308
  21.9 19.5 %copy-start.4 = (f32[1,128,64]{1,2,0:T(8,128)S(1)}, f32[1,128,64]{1,2,0:T(8,128)}, u32[]{:S(2)}) copy-start(f32[1,128,64]{1,2,0:T(8,128)} %param.11) | copy-start | bytes 98308
  40.1 1.3 %collective-permute-start.3 = (f32[32,512]{1,0:T(8,128)S(1)}, f32[32,512]{1,0:T(8,128)S(1)}, u32[]{:S(2)}, u32[]{:S(2)}) collective-permute-start(f32[32,512]{1,0:T(8,128)S(1)} %get-tuple-element.54), channel_id=1, source_target_pairs={{0,16},{16,0},{1,17},{17,1},{2,18},{18,2},{3,19},{19,3},{4,20},{20... | collective-permute-start | bytes 196616 | tf_op jit(solution)/shard_map/ppermute | solution.py:54
  41.5 8.3 %collective-permute-start.6 = (bf16[32,640]{1,0:T(8,128)(2,1)S(1)}, bf16[32,640]{1,0:T(8,128)(2,1)S(1)}, u32[]{:S(2)}, u32[]{:S(2)}) collective-permute-start(bf16[32,640]{1,0:T(8,128)(2,1)S(1)} %combine_branches.1.refs_0_), channel_id=1, source_target_pairs={{0,3},{1,2},{2,1},{3,0},{4,7},{5,6},{6,5},{7,4},{8,11},{9,10},{10,... | collective-permute-start | bytes 122888 | tf_op jit(solution)/shard_map/ppermute | solution.py:54
  45.1 6.9 %collective-permute-start.5 = (bf16[32,640]{1,0:T(8,128)(2,1)S(1)}, bf16[32,640]{1,0:T(8,128)(2,1)S(1)}, u32[]{:S(2)}, u32[]{:S(2)}) collective-permute-start(bf16[32,640]{1,0:T(8,128)(2,1)S(1)} %combine_branches.1.refs_0_), channel_id=1, source_target_pairs={{0,2},{1,3},{2,0},{3,1},{4,6},{5,7},{6,4},{7,5},{8,10},{9,11},{10,... | collective-permute-start | bytes 122888 | tf_op jit(solution)/shard_map/ppermute | solution.py:54
  49.3 4.0 %collective-permute-start.4 = (bf16[32,640]{1,0:T(8,128)(2,1)S(1)}, bf16[32,640]{1,0:T(8,128)(2,1)S(1)}, u32[]{:S(2)}, u32[]{:S(2)}) collective-permute-start(bf16[32,640]{1,0:T(8,128)(2,1)S(1)} %combine_branches.1.refs_0_), channel_id=1, source_target_pairs={{0,1},{1,0},{2,3},{3,2},{4,5},{5,4},{6,7},{7,6},{8,9},{9,8},{10,11... | collective-permute-start | bytes 122888 | tf_op jit(solution)/shard_map/ppermute | solution.py:54
  53.5 1.3 %collective-permute-start.7 = (f32[40,512]{1,0:T(8,128)S(1)}, f32[40,512]{1,0:T(8,128)S(1)}, u32[]{:S(2)}, u32[]{:S(2)}) collective-permute-start(f32[40,512]{1,0:T(8,128)S(1)} %gather_guided.1.refs_3_), channel_id=1, source_target_pairs={{0,16},{16,0},{1,17},{17,1},{2,18},{18,2},{3,19},{19,3},{4,20},{20... | collective-permute-start | bytes 245768 | tf_op jit(solution)/shard_map/ppermute | solution.py:54
  58.7 3.0 %collective-permute-start.11 = (f32[64,512]{1,0:T(8,128)S(1)}, f32[64,512]{1,0:T(8,128)S(1)}, u32[]{:S(2)}, u32[]{:S(2)}) collective-permute-start(f32[64,512]{1,0:T(8,128)S(1)} %get-tuple-element.65), channel_id=1, source_target_pairs={{0,16},{16,0},{1,17},{17,1},{2,18},{18,2},{3,19},{19,3},{4,20},{20... | collective-permute-start | bytes 393224 | tf_op jit(solution)/shard_map/ppermute | solution.py:54
  58.9 34.6 %collective-permute-start.8 = (bf16[1,336,384]{2,1,0:T(8,128)(2,1)S(1)}, bf16[1,336,384]{2,1,0:T(8,128)(2,1)S(1)}, u32[]{:S(2)}, u32[]{:S(2)}) collective-permute-start(bf16[1,336,384]{2,1,0:T(8,128)(2,1)S(1)} %get-tuple-element.59), channel_id=1, source_target_pairs={{0,3},{1,2},{2,1},{3,0},{4,7},{5,6},{6,5},{7,4},{8,11},{9,10},{10,... | collective-permute-start | bytes 774152 | tf_op jit(solution)/shard_map/ppermute | solution.py:54
  61.7 31.8 %collective-permute-start.9 = (bf16[1,336,384]{2,1,0:T(8,128)(2,1)S(1)}, bf16[1,336,384]{2,1,0:T(8,128)(2,1)S(1)}, u32[]{:S(2)}, u32[]{:S(2)}) collective-permute-start(bf16[1,336,384]{2,1,0:T(8,128)(2,1)S(1)} %get-tuple-element.60), channel_id=1, source_target_pairs={{0,2},{1,3},{2,0},{3,1},{4,6},{5,7},{6,4},{7,5},{8,10},{9,11},{10,... | collective-permute-start | bytes 774152 | tf_op jit(solution)/shard_map/ppermute | solution.py:54
  70.8 6.2 %collective-permute-start.12 = (bf16[1,464,128]{2,1,0:T(8,128)(2,1)S(1)}, bf16[1,464,128]{2,1,0:T(8,128)(2,1)S(1)}, u32[]{:S(2)}, u32[]{:S(2)}) collective-permute-start(bf16[1,464,128]{2,1,0:T(8,128)(2,1)S(1)} %get-tuple-element.71), channel_id=1, source_target_pairs={{0,1},{1,0},{2,3},{3,2},{4,5},{5,4},{6,7},{7,6},{8,9},{9,8},{10,11... | collective-permute-start | bytes 356360 | tf_op jit(solution)/shard_map/ppermute | solution.py:54
  72.4 21.6 %collective-permute-start.10 = (bf16[1,336,384]{2,1,0:T(8,128)(2,1)S(1)}, bf16[1,336,384]{2,1,0:T(8,128)(2,1)S(1)}, u32[]{:S(2)}, u32[]{:S(2)}) collective-permute-start(bf16[1,336,384]{2,1,0:T(8,128)(2,1)S(1)} %get-tuple-element.61), channel_id=1, source_target_pairs={{0,1},{1,0},{2,3},{3,2},{4,5},{5,4},{6,7},{7,6},{8,9},{9,8},{10,11... | collective-permute-start | bytes 774152 | tf_op jit(solution)/shard_map/ppermute | solution.py:54
  72.9 20.1 %collective-permute-start.13 = (bf16[1,464,128]{2,1,0:T(8,128)(2,1)S(1)}, bf16[1,464,128]{2,1,0:T(8,128)(2,1)S(1)}, u32[]{:S(2)}, u32[]{:S(2)}) collective-permute-start(bf16[1,464,128]{2,1,0:T(8,128)(2,1)S(1)} %get-tuple-element.72), channel_id=1, source_target_pairs={{0,2},{1,3},{2,0},{3,1},{4,6},{5,7},{6,4},{7,5},{8,10},{9,11},{10,... | collective-permute-start | bytes 356360 | tf_op jit(solution)/shard_map/ppermute | solution.py:54
  77.0 15.9 %collective-permute-start.14 = (bf16[1,464,128]{2,1,0:T(8,128)(2,1)S(1)}, bf16[1,464,128]{2,1,0:T(8,128)(2,1)S(1)}, u32[]{:S(2)}, u32[]{:S(2)}) collective-permute-start(bf16[1,464,128]{2,1,0:T(8,128)(2,1)S(1)} %get-tuple-element.73), channel_id=1, source_target_pairs={{0,3},{1,2},{2,1},{3,0},{4,7},{5,6},{6,5},{7,4},{8,11},{9,10},{10,... | collective-permute-start | bytes 356360 | tf_op jit(solution)/shard_map/ppermute | solution.py:54
  92.9 2.7 %collective-permute-start.15 = (bf16[1,464,128]{2,1,0:T(8,128)(2,1)S(1)}, bf16[1,464,128]{2,1,0:T(8,128)(2,1)S(1)}, u32[]{:S(2)}, u32[]{:S(2)}) collective-permute-start(bf16[1,464,128]{2,1,0:T(8,128)(2,1)S(1)} %get-tuple-element.77.refs_4_.refs_0_), channel_id=1, source_target_pairs={{0,16},{16,0},{1,17},{17,1},{2,18},{18,2},{3,19},{19,3},{4,20},{20... | collective-permute-start | bytes 356360 | tf_op jit(solution)/shard_map/ppermute | solution.py:54
  93.0 2.7 %collective-permute-start.16 = (bf16[1,464,128]{2,1,0:T(8,128)(2,1)S(1)}, bf16[1,464,128]{2,1,0:T(8,128)(2,1)S(1)}, u32[]{:S(2)}, u32[]{:S(2)}) collective-permute-start(bf16[1,464,128]{2,1,0:T(8,128)(2,1)S(1)} %collective-permute-done.12.refs_5_.refs_1_), channel_id=1, source_target_pairs={{0,16},{16,0},{1,17},{17,1},{2,18},{18,2},{3,19},{19,3},{4,20},{20... | collective-permute-start | bytes 356360 | tf_op jit(solution)/shard_map/ppermute | solution.py:54
  93.5 2.2 %collective-permute-start.17 = (bf16[1,464,128]{2,1,0:T(8,128)(2,1)S(1)}, bf16[1,464,128]{2,1,0:T(8,128)(2,1)S(1)}, u32[]{:S(2)}, u32[]{:S(2)}) collective-permute-start(bf16[1,464,128]{2,1,0:T(8,128)(2,1)S(1)} %collective-permute-done.13.refs_6_.refs_2_), channel_id=1, source_target_pairs={{0,16},{16,0},{1,17},{17,1},{2,18},{18,2},{3,19},{19,3},{4,20},{20... | collective-permute-start | bytes 356360 | tf_op jit(solution)/shard_map/ppermute | solution.py:54
  93.5 2.1 %collective-permute-start.18 = (bf16[1,464,128]{2,1,0:T(8,128)(2,1)S(1)}, bf16[1,464,128]{2,1,0:T(8,128)(2,1)S(1)}, u32[]{:S(2)}, u32[]{:S(2)}) collective-permute-start(bf16[1,464,128]{2,1,0:T(8,128)(2,1)S(1)} %collective-permute-done.14.refs_7_.refs_3_), channel_id=1, source_target_pairs={{0,16},{16,0},{1,17},{17,1},{2,18},{18,2},{3,19},{19,3},{4,20},{20... | collective-permute-start | bytes 356360 | tf_op jit(solution)/shard_map/ppermute | solution.py:54

commit v9 on v8

--- a/solution.py
+++ b/solution.py
@@ -657,9 +657,10 @@
     text = txt_kv[0, 0]
     if size.mirrored:
         first = min(2, size.parts - 1)
-        rest = [k for k in range(1, size.parts) if k != first]
-        packed = {first: slice_tokens(size, slots, text, first)}
-        packed.update(zip(rest, pack(size, slots, text, rest, 60 * MIB) if rest else []))
+        far = [first] + [k for k in range(1, size.parts) if k not in (1, first)]
+        packed = {k: slice_tokens(size, slots, text, k) for k in far}
+        if 1 not in packed:
+            packed[1] = pack(size, slots, text, [1], 60 * MIB)[0]
         blocks = [mirror(packed[k], "seq", k) for k in range(1, size.parts)]
     else:
         blocks = exchange(size, pack(size, slots, text, list(range(size.parts)), 48 * MIB))

time: 96.8 us -> 97.3 us (level)
  local copies, waits for them, and re-layouts: 1.92 us -> 0.14 us
    another operation x1, local copies, waits for them, and re-layouts: 1.15 us -> 0.08 us
  transfers between devices with their start and end apart: 19 -> 19, of which waited for: 8 -> 8; matrix products, arithmetic and copies ran while one was open for 0% -> 1% of each run, Pallas kernels for 4% -> 2%
where the time goes in v9:
time: 97.3 us; the launch traced here: 97.1 us
  waiting for transfers between devices  36.2 us (37%)
  starting transfers between devices  26.5 us (27%)
  blocking collectives  19.1 us (20%)
  Pallas kernels  11.6 us (12%)
  between operations  2.76 us (3%)
    ppermute x19, waiting for transfers between devices, mirror(): return lax.ppermute(x, axis, [(i, i ^ apart) for i in range(count)])  36.2 us
    ppermute x19, starting transfers between devices, mirror(): return lax.ppermute(x, axis, [(i, i ^ apart) for i in range(count)])  26.5 us
    psum x1, blocking collectives, on_device(): stats = lax.psum(jnp.where(mine, rewards[0], 0.0), 'img')  10.1 us
    all_gather x1, blocking collectives, join_readout(): held = lax.all_gather(sent, 'img', axis=0)  9.01 us
    pallas_call x1, Pallas kernels, backward(): pl.pallas_call(functools.partial(backward_kernel, size), in_specs=specs +...  3.85 us
    pallas_call x1, Pallas kernels, forward(): pl.pallas_call(functools.partial(forward_kernel, size), in_specs=[SMEM] +...  2.5 us
    pallas_call x2, Pallas kernels, pack(): pl.pallas_call(functools.partial(pack_kernel, size, which), in_specs=[ANY...  2.4 us
  transfers between devices with their start and end apart: 19, of which 8 were waited for; matrix products, arithmetic and copies ran while one was open for 1% of the time, Pallas kernels for 2%

profile of v9, /device:TPU:0, one launch (start us, length us, event | category | flops | bytes accessed | tf_op | source)
XLA Modules:
  0.0 97.1 jit_solution(9511804218412407719)
XLA Ops:
  0.6 0.0 copy-start.2
  0.6 0.0 copy-start
  0.7 2.0 %pack_tokens.3 = bf16[1,400,512]{2,1,0:T(8,128)(2,1)} custom-call(bf16[3,128,2048]{2,1,0:T(8,128)(2,1)} %bitcast.51, bf16[8,2,2048]{2,1,0:T(2,128)(2,1)} %bitcast.57), custom_call_target="tpu_custom_call" | custom-call | tf_op jit(solution)/shard_map/pack_tokens/pallas_call | solution.py:199
  2.6 3.1 %collective-permute-start.2 = (bf16[1,400,512]{2,1,0:T(8,128)(2,1)}, bf16[1,400,512]{2,1,0:T(8,128)(2,1)S(1)}, u32[]{:S(2)}, u32[]{:S(2)}) collective-permute-start(bf16[1,400,512]{2,1,0:T(8,128)(2,1)} %pack_tokens.3), channel_id=1, source_target_pairs={{0,1},{1,0},{2,3},{3,2},{4,5},{5,4},{6,7},{7,6},{8,9},{9,8},{10,11... | collective-permute-start | bytes 1228808 | tf_op jit(solution)/shard_map/ppermute | solution.py:54
  5.7 0.0 copy-done.2
  5.8 0.0 copy-done
  5.8 0.1 constant_dynamic-slice_fusion.1
  5.9 0.0 copy-start.1
  5.9 2.7 %collective-permute-start = (bf16[1,400,512]{2,1,0:T(8,128)(2,1)S(1)}, bf16[1,400,512]{2,1,0:T(8,128)(2,1)S(1)}, u32[]{:S(2)}, u32[]{:S(2)}) collective-permute-start(bf16[1,400,512]{2,1,0:T(8,128)(2,1)S(1)} %maximum_bitcast_fusion), channel_id=1, source_target_pairs={{0,2},{1,3},{2,0},{3,1},{4,6},{5,7},{6,4},{7,5},{8,10},{9,11},{10,... | collective-permute-start | bytes 1228808 | tf_op jit(solution)/shard_map/ppermute | solution.py:54
  8.6 0.8 maximum_bitcast_fusion.1
  9.4 0.0 collective-permute-start.1
  10.0 10.1 %psum.7.refs_2_ = f32[4]{0:T(128)S(1)} all-reduce(f32[4]{0:T(128)S(1)} %compare_select_fusion), channel_id=1, replica_groups=mesh['cfg'=2,'img'=4,'seq'=4] {'img'}, use_global_device_ids=true, to_apply=%region_0.1 | all-reduce | flops 4 | bytes 32 | tf_op jit(solution)/shard_map/psum | solution.py:669
  20.8 0.0 copy-start.3
  20.8 0.0 copy-start.4
  20.8 0.4 pack_tokens.2.refs_0_.refs_5_
  21.3 2.1 %collective-permute-done.2.refs_1_.refs_6_ = bf16[1,400,512]{2,1,0:T(8,128)(2,1)S(1)} collective-permute-done((bf16[1,400,512]{2,1,0:T(8,128)(2,1)}, bf16[1,400,512]{2,1,0:T(8,128)(2,1)S(1)}, u32[]{:S(2)}, u32[]{:S(2)}) %collective-permute-start.2) | collective-permute-done | bytes 409632 | tf_op jit(solution)/shard_map/ppermute | solution.py:54
  23.4 13.4 %collective-permute-done.refs_2_.refs_7_ = bf16[1,400,512]{2,1,0:T(8,128)(2,1)S(1)} collective-permute-done((bf16[1,400,512]{2,1,0:T(8,128)(2,1)S(1)}, bf16[1,400,512]{2,1,0:T(8,128)(2,1)S(1)}, u32[]{:S(2)}, u32[]{:S(2)}) %collective-permute-start) | collective-permute-done | bytes 409632 | tf_op jit(solution)/shard_map/ppermute | solution.py:54
  36.8 0.0 collective-permute-done.1.refs_3_.refs_8_
  36.8 0.0 copy-done.1
  36.8 2.5 %attention_forward.1 = (bf16[4,544,512]{2,1,0:T(8,128)(2,1)S(1)}, f32[4,64,512]{2,1,0:T(8,128)S(1)}, f32[4,1,512]{2,1,0:T(1,128)S(1)}, f32[32,512]{1,0:T(8,128)S(1)}, f32[32,512]{1,0:T(8,128)S(1)}) custom-call(f32[1]{0:T(128)} %bitcast.49.guidance, bf16[1,400,512]{2,1,0:T(8,128)(2,1)S(1)} %pack_tokens.2.refs_0_.refs_5_, ...), custom_call_target="tpu_custom_call" | custom-call | tf_op jit(solution)/shard_map/attention_forward/pallas_call | solution.py:308
  39.3 0.1 collective-permute-start.3
  40.1 0.6 collective-permute-done.3.other
  40.7 0.0 copy-done.3
  40.7 0.0 copy-done.4
  40.7 0.1 combine_branches.1.refs_0_
  40.8 2.5 %collective-permute-start.6 = (bf16[32,640]{1,0:T(8,128)(2,1)S(1)}, bf16[32,640]{1,0:T(8,128)(2,1)S(1)}, u32[]{:S(2)}, u32[]{:S(2)}) collective-permute-start(bf16[32,640]{1,0:T(8,128)(2,1)S(1)} %combine_branches.1.refs_0_), channel_id=1, source_target_pairs={{0,3},{1,2},{2,1},{3,0},{4,7},{5,6},{6,5},{7,4},{8,11},{9,10},{10,... | collective-permute-start | bytes 122888 | tf_op jit(solution)/shard_map/ppermute | solution.py:54
  43.4 6.9 %collective-permute-start.5 = (bf16[32,640]{1,0:T(8,128)(2,1)S(1)}, bf16[32,640]{1,0:T(8,128)(2,1)S(1)}, u32[]{:S(2)}, u32[]{:S(2)}) collective-permute-start(bf16[32,640]{1,0:T(8,128)(2,1)S(1)} %combine_branches.1.refs_0_), channel_id=1, source_target_pairs={{0,2},{1,3},{2,0},{3,1},{4,6},{5,7},{6,4},{7,5},{8,10},{9,11},{10,... | collective-permute-start | bytes 122888 | tf_op jit(solution)/shard_map/ppermute | solution.py:54
  50.3 0.1 collective-permute-start.4
  50.4 0.0 collective-permute-done.6.refs_3_
  50.4 2.4 %collective-permute-done.5.refs_2_ = bf16[32,640]{1,0:T(8,128)(2,1)S(1)} collective-permute-done((bf16[32,640]{1,0:T(8,128)(2,1)S(1)}, bf16[32,640]{1,0:T(8,128)(2,1)S(1)}, u32[]{:S(2)}, u32[]{:S(2)}) %collective-permute-start.5) | collective-permute-done | bytes 40992 | tf_op jit(solution)/shard_map/ppermute | solution.py:54
  52.8 1.5 %collective-permute-done.4.refs_1_ = bf16[32,640]{1,0:T(8,128)(2,1)S(1)} collective-permute-done((bf16[32,640]{1,0:T(8,128)(2,1)S(1)}, bf16[32,640]{1,0:T(8,128)(2,1)S(1)}, u32[]{:S(2)}, u32[]{:S(2)}) %collective-permute-start.4) | collective-permute-done | bytes 40992 | tf_op jit(solution)/shard_map/ppermute | solution.py:54
  54.3 0.2 gather_guided.1.refs_3_
  54.4 0.1 collective-permute-start.7
  54.5 1.3 %collective-permute-done.7.refs_4_ = f32[40,512]{1,0:T(8,128)S(1)} collective-permute-done((f32[40,512]{1,0:T(8,128)S(1)}, f32[40,512]{1,0:T(8,128)S(1)}, u32[]{:S(2)}, u32[]{:S(2)}) %collective-permute-start.7) | collective-permute-done | bytes 81952 | tf_op jit(solution)/shard_map/ppermute | solution.py:54
  55.8 3.9 %attention_backward.1 = (f32[1,1]{1,0:T(1,128)}, f32[64,512]{1,0:T(8,128)S(1)}, bf16[1,336,384]{2,1,0:T(8,128)(2,1)S(1)}, bf16[1,336,384]{2,1,0:T(8,128)(2,1)S(1...) custom-call(f32[1]{0:T(128)S(6)} %copy.20.rate.refs_0_, ...), custom_call_target="tpu_custom_call" | custom-call | tf_op jit(solution)/shard_map/attention_backward/pallas_call | solution.py:528
  59.6 0.2 collective-permute-start.11
  59.8 2.5 %collective-permute-start.8 = (bf16[1,336,384]{2,1,0:T(8,128)(2,1)S(1)}, bf16[1,336,384]{2,1,0:T(8,128)(2,1)S(1)}, u32[]{:S(2)}, u32[]{:S(2)}) collective-permute-start(bf16[1,336,384]{2,1,0:T(8,128)(2,1)S(1)} %get-tuple-element.55), channel_id=1, source_target_pairs={{0,3},{1,2},{2,1},{3,0},{4,7},{5,6},{6,5},{7,4},{8,11},{9,10},{10,... | collective-permute-start | bytes 774152 | tf_op jit(solution)/shard_map/ppermute | solution.py:54
  62.3 0.0 collective-permute-start.9
  62.3 0.0 collective-permute-done.11
  62.3 9.0 %all-gather = bf16[256,512]{1,0:T(8,128)(2,1)S(1)} all-gather(bf16[64,512]{1,0:T(8,128)(2,1)S(1)} %add_convert_fusion), channel_id=2, replica_groups=mesh['cfg'=2,'img'=4,'seq'=4] {'img'}, dimensions={0}, use_global_device_ids=true | all-gather | bytes 327680 | tf_op jit(solution)/shard_map/all_gather | solution.py:611
  71.3 2.0 %collective-permute-start.12 = (bf16[1,464,128]{2,1,0:T(8,128)(2,1)S(1)}, bf16[1,464,128]{2,1,0:T(8,128)(2,1)S(1)}, u32[]{:S(2)}, u32[]{:S(2)}) collective-permute-start(bf16[1,464,128]{2,1,0:T(8,128)(2,1)S(1)} %get-tuple-element.67), channel_id=1, source_target_pairs={{0,1},{1,0},{2,3},{3,2},{4,5},{5,4},{6,7},{7,6},{8,9},{9,8},{10,11... | collective-permute-start | bytes 356360 | tf_op jit(solution)/shard_map/ppermute | solution.py:54
  73.3 0.1 collective-permute-start.10
  73.4 2.9 %collective-permute-start.13 = (bf16[1,464,128]{2,1,0:T(8,128)(2,1)S(1)}, bf16[1,464,128]{2,1,0:T(8,128)(2,1)S(1)}, u32[]{:S(2)}, u32[]{:S(2)}) collective-permute-start(bf16[1,464,128]{2,1,0:T(8,128)(2,1)S(1)} %get-tuple-element.68), channel_id=1, source_target_pairs={{0,2},{1,3},{2,0},{3,1},{4,6},{5,7},{6,4},{7,5},{8,10},{9,11},{10,... | collective-permute-start | bytes 356360 | tf_op jit(solution)/shard_map/ppermute | solution.py:54
  76.3 1.2 %collective-permute-done.12.refs_5_.refs_1_ = bf16[1,464,128]{2,1,0:T(8,128)(2,1)S(1)} collective-permute-done((bf16[1,464,128]{2,1,0:T(8,128)(2,1)S(1)}, bf16[1,464,128]{2,1,0:T(8,128)(2,1)S(1)}, u32[]{:S(2)}, u32[]{:S(2)}) %collective-permute-start.12) | collective-permute-done | bytes 118816 | tf_op jit(solution)/shard_map/ppermute | solution.py:54
  77.5 2.3 %collective-permute-start.14 = (bf16[1,464,128]{2,1,0:T(8,128)(2,1)S(1)}, bf16[1,464,128]{2,1,0:T(8,128)(2,1)S(1)}, u32[]{:S(2)}, u32[]{:S(2)}) collective-permute-start(bf16[1,464,128]{2,1,0:T(8,128)(2,1)S(1)} %get-tuple-element.69), channel_id=1, source_target_pairs={{0,3},{1,2},{2,1},{3,0},{4,7},{5,6},{6,5},{7,4},{8,11},{9,10},{10,... | collective-permute-start | bytes 356360 | tf_op jit(solution)/shard_map/ppermute | solution.py:54
  79.8 13.7 %collective-permute-done.13.refs_6_.refs_2_ = bf16[1,464,128]{2,1,0:T(8,128)(2,1)S(1)} collective-permute-done((bf16[1,464,128]{2,1,0:T(8,128)(2,1)S(1)}, bf16[1,464,128]{2,1,0:T(8,128)(2,1)S(1)}, u32[]{:S(2)}, u32[]{:S(2)}) %collective-permute-start.13) | collective-permute-done | bytes 118816 | tf_op jit(solution)/shard_map/ppermute | solution.py:54
  93.5 0.0 collective-permute-start.15
  93.5 0.0 collective-permute-done.14.refs_7_.refs_3_
  93.5 0.5 collective-permute-start.16
  94.1 0.0 collective-permute-done.8.refs_3_
  94.1 0.1 collective-permute-start.17
  94.1 0.0 collective-permute-done.9.refs_2_
  94.1 0.4 collective-permute-start.18
  94.6 0.0 collective-permute-done.10.refs_1_
  94.6 1.6 %home_tokens.1 = (bf16[3,128,2048]{2,1,0:T(8,128)(2,1)}, bf16[8,2,2048]{2,1,0:T(2,128)(2,1)}) custom-call(bf16[64,2048]{1,0:T(8,128)(2,1)S(1)} %bitcast.55, bf16[1,336,384]{2,1,0:T(8,128)(2,1)S(1)} %get-tuple-element.54.refs_0_, bf16[1,336,384]{2,1,0:T(8,128)(2,1)S(1)} %collective-permute-done.10.refs_1_, ...), custom_call_target="tpu_custom_call" | custom-call | tf_op jit(solution)/shard_map/home_tokens/pallas_call | solution.py:586
  96.2 0.0 collective-permute-done.15.refs_4_
  96.2 0.0 collective-permute-done.16.refs_5_
  96.2 0.0 collective-permute-done.17.refs_6_
  96.2 0.0 collective-permute-done.18.refs_7_
  96.2 0.9 place_readout_grad.1
  (7 shorter events, 0.1 us)
Async XLA Ops:
  0.6 5.1 %copy-start.2 = (bf16[1,1,8,2,2048]{4,3,2,1,0:T(2,128)(2,1)S(1)}, bf16[1,1,8,2,2048]{4,3,2,1,0:T(2,128)(2,1)}, u32[]{:S(2)}) copy-start(bf16[1,1,8,2,2048]{4,3,2,1,0:T(2,128)(2,1)} %param.9) | copy-start | bytes 196612
  0.6 5.1 %copy-start = (bf16[1,1,128,3,2048]{4,2,3,1,0:T(8,128)(2,1)S(1)}, bf16[1,1,128,3,2048]{4,2,3,1,0:T(8,128)(2,1)}, u32[]{:S(2)}) copy-start(bf16[1,1,128,3,2048]{4,2,3,1,0:T(8,128)(2,1)} %param.8) | copy-start | bytes 4718596
  2.6 20.8 %collective-permute-start.2 = (bf16[1,400,512]{2,1,0:T(8,128)(2,1)}, bf16[1,400,512]{2,1,0:T(8,128)(2,1)S(1)}, u32[]{:S(2)}, u32[]{:S(2)}) collective-permute-start(bf16[1,400,512]{2,1,0:T(8,128)(2,1)} %pack_tokens.3), channel_id=1, source_target_pairs={{0,1},{1,0},{2,3},{3,2},{4,5},{5,4},{6,7},{7,6},{8,9},{9,8},{10,11... | collective-permute-start | bytes 1228808 | tf_op jit(solution)/shard_map/ppermute | solution.py:54
  5.9 30.9 %copy-start.1 = (bf16[2048,64]{0,1:T(8,128)(2,1)S(1)}, bf16[2048,64]{0,1:T(8,128)(2,1)}, u32[]{:S(2)}) copy-start(bf16[2048,64]{0,1:T(8,128)(2,1)} %param.10) | copy-start | bytes 786436
  5.9 30.9 %collective-permute-start = (bf16[1,400,512]{2,1,0:T(8,128)(2,1)S(1)}, bf16[1,400,512]{2,1,0:T(8,128)(2,1)S(1)}, u32[]{:S(2)}, u32[]{:S(2)}) collective-permute-start(bf16[1,400,512]{2,1,0:T(8,128)(2,1)S(1)} %maximum_bitcast_fusion), channel_id=1, source_target_pairs={{0,2},{1,3},{2,0},{3,1},{4,6},{5,7},{6,4},{7,5},{8,10},{9,11},{10,... | collective-permute-start | bytes 1228808 | tf_op jit(solution)/shard_map/ppermute | solution.py:54
  9.4 27.5 %collective-permute-start.1 = (bf16[1,400,512]{2,1,0:T(8,128)(2,1)}, bf16[1,400,512]{2,1,0:T(8,128)(2,1)S(1)}, u32[]{:S(2)}, u32[]{:S(2)}) collective-permute-start(bf16[1,400,512]{2,1,0:T(8,128)(2,1)} %maximum_bitcast_fusion.1), channel_id=1, source_target_pairs={{0,3},{1,2},{2,1},{3,0},{4,7},{5,6},{6,5},{7,4},{8,11},{9,10},{10,... | collective-permute-start | bytes 1228808 | tf_op jit(solution)/shard_map/ppermute | solution.py:54
  20.8 19.9 %copy-start.3 = (f32[1,128,64]{1,2,0:T(8,128)S(1)}, f32[1,128,64]{1,2,0:T(8,128)}, u32[]{:S(2)}) copy-start(f32[1,128,64]{1,2,0:T(8,128)} %param.12) | copy-start | bytes 98308
  20.8 19.9 %copy-start.4 = (f32[1,128,64]{1,2,0:T(8,128)S(1)}, f32[1,128,64]{1,2,0:T(8,128)}, u32[]{:S(2)}) copy-start(f32[1,128,64]{1,2,0:T(8,128)} %param.11) | copy-start | bytes 98308
  39.3 1.3 %collective-permute-start.3 = (f32[32,512]{1,0:T(8,128)S(1)}, f32[32,512]{1,0:T(8,128)S(1)}, u32[]{:S(2)}, u32[]{:S(2)}) collective-permute-start(f32[32,512]{1,0:T(8,128)S(1)} %get-tuple-element.50), channel_id=1, source_target_pairs={{0,16},{16,0},{1,17},{17,1},{2,18},{18,2},{3,19},{19,3},{4,20},{20... | collective-permute-start | bytes 196616 | tf_op jit(solution)/shard_map/ppermute | solution.py:54
  40.8 9.6 %collective-permute-start.6 = (bf16[32,640]{1,0:T(8,128)(2,1)S(1)}, bf16[32,640]{1,0:T(8,128)(2,1)S(1)}, u32[]{:S(2)}, u32[]{:S(2)}) collective-permute-start(bf16[32,640]{1,0:T(8,128)(2,1)S(1)} %combine_branches.1.refs_0_), channel_id=1, source_target_pairs={{0,3},{1,2},{2,1},{3,0},{4,7},{5,6},{6,5},{7,4},{8,11},{9,10},{10,... | collective-permute-start | bytes 122888 | tf_op jit(solution)/shard_map/ppermute | solution.py:54
  43.4 9.4 %collective-permute-start.5 = (bf16[32,640]{1,0:T(8,128)(2,1)S(1)}, bf16[32,640]{1,0:T(8,128)(2,1)S(1)}, u32[]{:S(2)}, u32[]{:S(2)}) collective-permute-start(bf16[32,640]{1,0:T(8,128)(2,1)S(1)} %combine_branches.1.refs_0_), channel_id=1, source_target_pairs={{0,2},{1,3},{2,0},{3,1},{4,6},{5,7},{6,4},{7,5},{8,10},{9,11},{10,... | collective-permute-start | bytes 122888 | tf_op jit(solution)/shard_map/ppermute | solution.py:54
  50.3 4.0 %collective-permute-start.4 = (bf16[32,640]{1,0:T(8,128)(2,1)S(1)}, bf16[32,640]{1,0:T(8,128)(2,1)S(1)}, u32[]{:S(2)}, u32[]{:S(2)}) collective-permute-start(bf16[32,640]{1,0:T(8,128)(2,1)S(1)} %combine_branches.1.refs_0_), channel_id=1, source_target_pairs={{0,1},{1,0},{2,3},{3,2},{4,5},{5,4},{6,7},{7,6},{8,9},{9,8},{10,11... | collective-permute-start | bytes 122888 | tf_op jit(solution)/shard_map/ppermute | solution.py:54
  54.4 1.3 %collective-permute-start.7 = (f32[40,512]{1,0:T(8,128)S(1)}, f32[40,512]{1,0:T(8,128)S(1)}, u32[]{:S(2)}, u32[]{:S(2)}) collective-permute-start(f32[40,512]{1,0:T(8,128)S(1)} %gather_guided.1.refs_3_), channel_id=1, source_target_pairs={{0,16},{16,0},{1,17},{17,1},{2,18},{18,2},{3,19},{19,3},{4,20},{20... | collective-permute-start | bytes 245768 | tf_op jit(solution)/shard_map/ppermute | solution.py:54
  59.6 2.6 %collective-permute-start.11 = (f32[64,512]{1,0:T(8,128)S(1)}, f32[64,512]{1,0:T(8,128)S(1)}, u32[]{:S(2)}, u32[]{:S(2)}) collective-permute-start(f32[64,512]{1,0:T(8,128)S(1)} %get-tuple-element.61), channel_id=1, source_target_pairs={{0,16},{16,0},{1,17},{17,1},{2,18},{18,2},{3,19},{19,3},{4,20},{20... | collective-permute-start | bytes 393224 | tf_op jit(solution)/shard_map/ppermute | solution.py:54
  59.8 34.3 %collective-permute-start.8 = (bf16[1,336,384]{2,1,0:T(8,128)(2,1)S(1)}, bf16[1,336,384]{2,1,0:T(8,128)(2,1)S(1)}, u32[]{:S(2)}, u32[]{:S(2)}) collective-permute-start(bf16[1,336,384]{2,1,0:T(8,128)(2,1)S(1)} %get-tuple-element.55), channel_id=1, source_target_pairs={{0,3},{1,2},{2,1},{3,0},{4,7},{5,6},{6,5},{7,4},{8,11},{9,10},{10,... | collective-permute-start | bytes 774152 | tf_op jit(solution)/shard_map/ppermute | solution.py:54
  62.3 31.9 %collective-permute-start.9 = (bf16[1,336,384]{2,1,0:T(8,128)(2,1)S(1)}, bf16[1,336,384]{2,1,0:T(8,128)(2,1)S(1)}, u32[]{:S(2)}, u32[]{:S(2)}) collective-permute-start(bf16[1,336,384]{2,1,0:T(8,128)(2,1)S(1)} %get-tuple-element.56), channel_id=1, source_target_pairs={{0,2},{1,3},{2,0},{3,1},{4,6},{5,7},{6,4},{7,5},{8,10},{9,11},{10,... | collective-permute-start | bytes 774152 | tf_op jit(solution)/shard_map/ppermute | solution.py:54
  71.3 6.2 %collective-permute-start.12 = (bf16[1,464,128]{2,1,0:T(8,128)(2,1)S(1)}, bf16[1,464,128]{2,1,0:T(8,128)(2,1)S(1)}, u32[]{:S(2)}, u32[]{:S(2)}) collective-permute-start(bf16[1,464,128]{2,1,0:T(8,128)(2,1)S(1)} %get-tuple-element.67), channel_id=1, source_target_pairs={{0,1},{1,0},{2,3},{3,2},{4,5},{5,4},{6,7},{7,6},{8,9},{9,8},{10,11... | collective-permute-start | bytes 356360 | tf_op jit(solution)/shard_map/ppermute | solution.py:54
  73.3 21.3 %collective-permute-start.10 = (bf16[1,336,384]{2,1,0:T(8,128)(2,1)S(1)}, bf16[1,336,384]{2,1,0:T(8,128)(2,1)S(1)}, u32[]{:S(2)}, u32[]{:S(2)}) collective-permute-start(bf16[1,336,384]{2,1,0:T(8,128)(2,1)S(1)} %get-tuple-element.57), channel_id=1, source_target_pairs={{0,1},{1,0},{2,3},{3,2},{4,5},{5,4},{6,7},{7,6},{8,9},{9,8},{10,11... | collective-permute-start | bytes 774152 | tf_op jit(solution)/shard_map/ppermute | solution.py:54
  73.4 20.1 %collective-permute-start.13 = (bf16[1,464,128]{2,1,0:T(8,128)(2,1)S(1)}, bf16[1,464,128]{2,1,0:T(8,128)(2,1)S(1)}, u32[]{:S(2)}, u32[]{:S(2)}) collective-permute-start(bf16[1,464,128]{2,1,0:T(8,128)(2,1)S(1)} %get-tuple-element.68), channel_id=1, source_target_pairs={{0,2},{1,3},{2,0},{3,1},{4,6},{5,7},{6,4},{7,5},{8,10},{9,11},{10,... | collective-permute-start | bytes 356360 | tf_op jit(solution)/shard_map/ppermute | solution.py:54
  77.5 16.0 %collective-permute-start.14 = (bf16[1,464,128]{2,1,0:T(8,128)(2,1)S(1)}, bf16[1,464,128]{2,1,0:T(8,128)(2,1)S(1)}, u32[]{:S(2)}, u32[]{:S(2)}) collective-permute-start(bf16[1,464,128]{2,1,0:T(8,128)(2,1)S(1)} %get-tuple-element.69), channel_id=1, source_target_pairs={{0,3},{1,2},{2,1},{3,0},{4,7},{5,6},{6,5},{7,4},{8,11},{9,10},{10,... | collective-permute-start | bytes 356360 | tf_op jit(solution)/shard_map/ppermute | solution.py:54
  93.5 2.7 %collective-permute-start.15 = (bf16[1,464,128]{2,1,0:T(8,128)(2,1)S(1)}, bf16[1,464,128]{2,1,0:T(8,128)(2,1)S(1)}, u32[]{:S(2)}, u32[]{:S(2)}) collective-permute-start(bf16[1,464,128]{2,1,0:T(8,128)(2,1)S(1)} %get-tuple-element.73.refs_4_.refs_0_), channel_id=1, source_target_pairs={{0,16},{16,0},{1,17},{17,1},{2,18},{18,2},{3,19},{19,3},{4,20},{20... | collective-permute-start | bytes 356360 | tf_op jit(solution)/shard_map/ppermute | solution.py:54
  93.5 2.7 %collective-permute-start.16 = (bf16[1,464,128]{2,1,0:T(8,128)(2,1)S(1)}, bf16[1,464,128]{2,1,0:T(8,128)(2,1)S(1)}, u32[]{:S(2)}, u32[]{:S(2)}) collective-permute-start(bf16[1,464,128]{2,1,0:T(8,128)(2,1)S(1)} %collective-permute-done.12.refs_5_.refs_1_), channel_id=1, source_target_pairs={{0,16},{16,0},{1,17},{17,1},{2,18},{18,2},{3,19},{19,3},{4,20},{20... | collective-permute-start | bytes 356360 | tf_op jit(solution)/shard_map/ppermute | solution.py:54
  94.1 2.2 %collective-permute-start.17 = (bf16[1,464,128]{2,1,0:T(8,128)(2,1)S(1)}, bf16[1,464,128]{2,1,0:T(8,128)(2,1)S(1)}, u32[]{:S(2)}, u32[]{:S(2)}) collective-permute-start(bf16[1,464,128]{2,1,0:T(8,128)(2,1)S(1)} %collective-permute-done.13.refs_6_.refs_2_), channel_id=1, source_target_pairs={{0,16},{16,0},{1,17},{17,1},{2,18},{18,2},{3,19},{19,3},{4,20},{20... | collective-permute-start | bytes 356360 | tf_op jit(solution)/shard_map/ppermute | solution.py:54
  94.1 2.1 %collective-permute-start.18 = (bf16[1,464,128]{2,1,0:T(8,128)(2,1)S(1)}, bf16[1,464,128]{2,1,0:T(8,128)(2,1)S(1)}, u32[]{:S(2)}, u32[]{:S(2)}) collective-permute-start(bf16[1,464,128]{2,1,0:T(8,128)(2,1)S(1)} %collective-permute-done.14.refs_7_.refs_3_), channel_id=1, source_target_pairs={{0,16},{16,0},{1,17},{17,1},{2,18},{18,2},{3,19},{19,3},{4,20},{20... | collective-permute-start | bytes 356360 | tf_op jit(solution)/shard_map/ppermute | solution.py:54
